TPU v7x, 32 devices: a whole 2x2x4 slice. The times are simulated.
32 devices in a mesh: groups: 2 (over y), tensor: 4 (over z), dp: 2 (over x), pipe: 2 (over core).
Axes of the slice: x: 2, y: 2, z: 4, core: 2. Of those that a mesh axis runs over, the one named last changes fastest.
Arguments:
- tokens: bfloat16 [6144, 8192], P(('groups', 'dp', 'pipe'), 'tensor'), parts along dimension 0, may hold values from -6 to 6
- base_weight: bfloat16 [8192, 2048], P(None, 'tensor'), may hold values from -0.0625 to 0.0625
- adapter_a: bfloat16 [8, 64, 8192], P(('groups', 'dp'), None, 'tensor'), parts along dimension 0, may hold values from -0.0625 to 0.0625
- adapter_b: bfloat16 [8, 64, 2048], P(('groups', 'dp'), None, 'tensor'), parts along dimension 0, may hold values from -0.75 to 0.75
- cotangent: bfloat16 [6144, 2048], P(('groups', 'dp', 'pipe'), 'tensor'), parts along dimension 0, may hold values from -0.059814453 to 0.059814453
- block_tenant_index: int32 [48], P(('groups', 'dp', 'pipe')), parts along dimension 0, may hold values from 0 to 3
- block_fill: int32 [8, 6], P(('groups', 'dp', 'pipe')), parts along dimension 0, may hold values from 1 to 128, 512 in all within a row
Outputs:
- projection_output: bfloat16 [6144, 2048], P(('groups', 'dp', 'pipe'), 'tensor'), parts along dimension 0
- down_adapter_gradient: float32 [8, 64, 8192], P(('groups', 'dp'), None, 'tensor'), parts along dimension 0
- up_adapter_gradient: float32 [8, 64, 2048], P(('groups', 'dp'), None, 'tensor'), parts along dimension 0
There are 2 independent parts, one for each index of `groups`. A program takes and returns all parts, laid end to end along the dimension named above; an argument that names none is the same for every part. Nothing has to cross between parts.
Inputs may be any that keep to these rules, and one draw needn't show every extreme that they name: `block_fill`: the 6 numbers of one line sum to exactly 512.
All inputs are finite; a program needn't handle non-finite values.
Results may differ from a plain program's by a relative error of at most 0.015.
Values may be sent and summed in bfloat16 or wider, within the bound.
No kernel may reach another device: no remote copies, remote signals or barrier semaphores. Data moves between devices by JAX's collectives and lax.ppermute only.
A program may use at most 128 MiB of HBM per device.

v0:
```python
import jax
import jax.numpy as jnp
from jax import lax
from jax.sharding import PartitionSpec as P

ADAPTER_SCALE = 2.0


def body(tokens, base_weight, adapter_a, adapter_b, cotangent, block_tenant_index, block_fill):
    row_blocks = block_tenant_index.shape[0]
    total_rows = tokens.shape[0]
    block_row_length = total_rows // row_blocks
    local_feat = tokens.shape[1]
    output_columns = base_weight.shape[1]
    fill_rows = block_fill.reshape(-1)
    live_grid = jnp.arange(block_row_length, dtype=jnp.int32)[None, :] < fill_rows[:, None]
    active_row_mask = live_grid[:, :, None]
    every_down, every_up = (
        lax.all_gather(adapter_a, "dp", axis=0, tiled=True),
        lax.all_gather(adapter_b, "dp", axis=0, tiled=True),
    )
    chosen_down = every_down[block_tenant_index]
    chosen_up = every_up[block_tenant_index]
    tok_blocks = tokens.reshape(row_blocks, block_row_length, local_feat)
    cot_blocks = cotangent.reshape(row_blocks, block_row_length, output_columns)
    part_in = jnp.einsum(
        "bnd,brd->bnr", tok_blocks, chosen_down, preferred_element_type=jnp.float32
    )
    part_grad = jnp.einsum(
        "bne,bre->bnr", cot_blocks, chosen_up, preferred_element_type=jnp.float32
    )
    whole_in, whole_grad = (
        lax.psum(part_in.astype(jnp.bfloat16), "tensor").astype(jnp.float32),
        lax.psum(part_grad.astype(jnp.bfloat16), "tensor").astype(jnp.float32),
    )
    low_in = jnp.where(active_row_mask, whole_in, 0.0).astype(jnp.bfloat16)
    low_grad = jnp.where(active_row_mask, whole_grad, 0.0).astype(jnp.bfloat16)
    piece = lax.all_gather(tokens, "tensor", axis=1, tiled=True)
    count = piece.shape[1] // local_feat
    panel = base_weight
    panel = panel.reshape(count, local_feat, output_columns)
    split = piece.reshape(piece.shape[0], count, local_feat)
    part = jnp.einsum("nkf,kfe->nke", split, panel, preferred_element_type=jnp.float32)
    part = lax.optimization_barrier(part.astype(jnp.bfloat16)).astype(jnp.float32)
    base_output_used = jnp.sum(part, axis=1)
    low_rank_output = jnp.einsum(
        "bnr,bre->bne", low_in, chosen_up, preferred_element_type=jnp.float32
    )
    combined_output = (
        base_output_used.reshape(row_blocks, block_row_length, output_columns)
        + ADAPTER_SCALE * low_rank_output
    )
    projection_output = (
        jnp.where(active_row_mask, combined_output, 0.0)
        .astype(jnp.bfloat16)
        .reshape(total_rows, output_columns)
    )
    block_down_weight = jnp.einsum(
        "bnr,bnd->brd", low_grad, tok_blocks, preferred_element_type=jnp.float32
    )
    block_up_weight = jnp.einsum(
        "bnr,bne->bre", low_in, cot_blocks, preferred_element_type=jnp.float32
    )
    tenants = every_down.shape[0]
    selector = (
        jnp.arange(tenants, dtype=jnp.int32)[:, None] == block_tenant_index[None, :]
    ).astype(jnp.float32)
    dense_down_weight = ADAPTER_SCALE * jnp.einsum(
        "tb,brd->trd", selector, block_down_weight, precision=lax.Precision.HIGHEST
    )
    dense_up_weight = ADAPTER_SCALE * jnp.einsum(
        "tb,bre->tre", selector, block_up_weight, precision=lax.Precision.HIGHEST
    )
    share_down, share_up = (
        lax.psum_scatter(
            dense_down_weight.astype(jnp.bfloat16), ("dp", "pipe"), scatter_dimension=0, tiled=True
        ).astype(jnp.float32),
        lax.psum_scatter(
            dense_up_weight.astype(jnp.bfloat16), ("dp", "pipe"), scatter_dimension=0, tiled=True
        ).astype(jnp.float32),
    )
    down_adapter_gradient, up_adapter_gradient = (
        lax.all_gather(share_down.astype(jnp.bfloat16), "pipe", axis=0, tiled=True).astype(
            share_down.dtype
        ),
        lax.all_gather(share_up.astype(jnp.bfloat16), "pipe", axis=0, tiled=True).astype(
            share_up.dtype
        ),
    )
    return (projection_output, down_adapter_gradient, up_adapter_gradient)


def solution(mesh):
    placed = (
        P(("groups", "dp", "pipe"), "tensor"),
        P(None, "tensor"),
        P(("groups", "dp"), None, "tensor"),
        P(("groups", "dp"), None, "tensor"),
        P(("groups", "dp", "pipe"), "tensor"),
        P(("groups", "dp", "pipe")),
        P(("groups", "dp", "pipe"), None),
    )
    return jax.shard_map(
        body,
        mesh=mesh,
        in_specs=placed,
        out_specs=(
            P(("groups", "dp", "pipe"), "tensor"),
            P(("groups", "dp"), None, "tensor"),
            P(("groups", "dp"), None, "tensor"),
        ),
        check_vma=False,
    )
```

profile of v0, /device:TPU:0, one launch (start us, length us, event | category | flops | bytes accessed | tf_op | source)
XLA Modules:
  0.0 369.1 jit_solution(12119505016826863879)
XLA Ops:
  8.0 7.4 %all_gather.17 = bf16[4,64,512]{2,1,0:T(8,128)(2,1)S(1)} all-gather(bf16[2,64,512]{2,1,0:T(8,128)(2,1)} %param.10), channel_id=1, replica_groups=mesh['groups'=2,'tensor'=4,'dp'=2,'pipe'=2] {'dp'}, dimensions={0}, use_global_device_ids=true | all-gather | bytes 393216 | tf_op jit(solution)/shard_map/all_gather | solution.py:20
  16.6 1.0 fusion.10
  17.6 16.0 %all-gather.5.cloned.1.call-done = bf16[4,64,2048]{2,1,0:T(8,128)(2,1)} async-done(((bf16[2,64,2048]{2,1,0:T(8,128)(2,1)}), bf16[4,64,2048]{2,1,0:T(8,128)(2,1)}) %all-gather.5.cloned.1.call-update) | async-done | bytes 1048592 | tf_op jit(solution)/shard_map/all_gather | solution.py:19
  33.6 1.9 gather_fusion
  35.5 3.7 %fusion.9 = bf16[6,128,64]{1,2,0:T(8,128)(2,1)} fusion(bf16[6,64,2048]{2,1,0:T(8,128)(2,1)S(1)} %gather_fusion, bf16[6,128,2048]{2,1,0:T(8,128)(2,1)} %bitcast.28), kind=kOutput, calls=%fused_computation.13 | convolution fusion | flops 201375744 | bytes 4816896 | tf_op jit(solution)/shard_map/bnd,brd->bnr/dot_general | solution.py:26
  39.4 35.0 %all-reduce.3.cloned.1.call-done = (bf16[6,128,64]{1,2,0:T(8,128)(2,1)}, bf16[6,128,64]{1,2,0:T(8,128)(2,1)}) async-done(((bf16[6,128,64]{1,2,0:T(8,128)(2,1)}, bf16[6,128,64]{1,2,0:T(8,128)(2,1)}), (bf16[6,128,64]{1,2,0:T(8,128)(2,1)}, bf16[6,128,64]{1,2,0:T(8,128)(2,1)})) %all-reduce.3.cloned.1.call-update) | async-done | bytes 196624 | tf_op jit(solution)/shard_map/psum | solution.py:33
  74.3 1.2 fusion.15
  75.5 1.0 fusion.8
  76.6 0.7 copy.25
  77.4 2.5 fusion.12
  79.9 3.9 %fusion.5 = bf16[4,64,2048]{2,0,1:T(4,128)(2,1)S(1)} fusion(f32[6,64,2048]{2,1,0:T(8,128)S(1)} %fusion.12, s32[6]{0:T(128)S(1)} %copy-done.3), kind=kOutput, calls=%fused_computation.7 | convolution fusion | flops 38797336 | bytes 4194328 | tf_op jit(solution)/shard_map/tb,brd->trd/dot_general | solution.py:68
  83.8 1.5 copy.23
  85.4 4.7 %copy.18 = bf16[768,2048]{0,1:T(8,128)(2,1)} copy(bf16[768,2048]{1,0:T(8,128)(2,1)} %param.7) | data formatting | bytes 6291456 | tf_op args[0]
  90.2 7.2 %reduce-scatter.5.cloned.1.call-done = bf16[1,64,512]{2,1,0:T(8,128)(2,1)} async-done(((bf16[4,64,512]{2,1,0:T(8,128)(2,1)}), bf16[1,64,512]{2,1,0:T(8,128)(2,1)}) %reduce-scatter.5.cloned.1.call-update) | async-done | bytes 65552 | tf_op jit(solution)/shard_map/reduce_scatter | solution.py:78
  97.3 2.1 all_gather.19
  99.4 0.7 convert_element_type.68
  100.1 25.1 %reduce-scatter.3.cloned.1.call-done = bf16[1,64,2048]{2,1,0:T(8,128)(2,1)} async-done(((bf16[4,64,2048]{2,1,0:T(8,128)(2,1)}), bf16[1,64,2048]{2,1,0:T(8,128)(2,1)}) %reduce-scatter.3.cloned.1.call-update) | async-done | bytes 262160 | tf_op jit(solution)/shard_map/reduce_scatter | solution.py:75
  125.2 2.6 all_gather.18
  127.8 1.1 convert_element_type.66
  128.8 216.1 %all-gather.3.cloned.1.call-done = bf16[768,8192]{0,1:T(8,128)(2,1)} async-done(((bf16[768,2048]{0,1:T(8,128)(2,1)}), bf16[768,8192]{0,1:T(8,128)(2,1)}) %all-gather.3.cloned.1.call-update) | async-done | bytes 12582928 | tf_op jit(solution)/shard_map/all_gather | solution.py:38
  344.9 12.8 %convert_bitcast_fusion = bf16[768,4,512]{0,2,1:T(8,128)(2,1)S(1)} fusion(bf16[4,2048,512]{2,1,0:T(8,128)(2,1)} %bitcast.33, bf16[768,4,2048]{0,2,1:T(8,128)(2,1)} %bitcast.32), kind=kOutput, calls=%fused_computation.5 | convolution fusion | flops 6444023808 | bytes 24117248 | tf_op jit(solution)/shard_map/nkf,kfe->nke/dot_general | solution.py:43
  357.7 1.6 convert_reduce_fusion
  359.4 1.9 copy.21
  361.2 1.3 select_convert_fusion
  (24 shorter events, 2.3 us)
Async XLA Ops:
  7.2 9.4 %copy-start = (bf16[768,512]{1,0:T(8,128)(2,1)S(1)}, bf16[768,512]{1,0:T(8,128)(2,1)}, u32[]{:S(2)}) copy-start(bf16[768,512]{1,0:T(8,128)(2,1)} %param.11) | copy-start | bytes 2359300
  7.2 26.4 %all-gather.5.cloned.1.call-start = ((), (), s32[]{:S(2)}) async-start(), calls=%async_computation.3 | async-start | bytes 1572864 | tf_op jit(solution)/shard_map/all_gather | solution.py:19
  7.9 66.4 %all-reduce.3.cloned.1.call-start = ((), (), s32[]{:S(2)}) async-start(), calls=%async_computation.6 | async-start | bytes 393216 | tf_op jit(solution)/shard_map/psum | solution.py:33
  35.5 3.8 %copy-start.4 = (s32[1,6]{1,0:T(1,128)S(1)}, s32[1,6]{1,0:T(1,128)}, u32[]{:S(2)}) copy-start(s32[1,6]{1,0:T(1,128)} %param.13) | copy-start | bytes 76
  35.5 40.0 %copy-start.3 = (s32[6]{0:T(128)S(1)}, s32[6]{0:T(128)}, u32[]{:S(2)}) copy-start(s32[6]{0:T(128)} %param.12) | copy-start | bytes 76
  39.3 58.1 %reduce-scatter.5.cloned.1.call-start = ((), (), s32[]{:S(2)}) async-start(), calls=%async_computation.5 | async-start | bytes 327680 | tf_op jit(solution)/shard_map/reduce_scatter | solution.py:78
  74.3 3.1 copy-start.2
  77.3 47.9 %reduce-scatter.3.cloned.1.call-start = ((), (), s32[]{:S(2)}) async-start(), calls=%async_computation.4 | async-start | bytes 1310720 | tf_op jit(solution)/shard_map/reduce_scatter | solution.py:75
  85.4 259.6 %all-gather.3.cloned.1.call-start = ((), (), s32[]{:S(2)}) async-start(), calls=%async_computation.2 | async-start | bytes 15728640 | tf_op jit(solution)/shard_map/all_gather | solution.py:38
  357.7 3.5 copy-start.1
Sparse Core Ops, SparseCore 0:
  9.6 23.9 all-gather.4
  39.4 34.9 all-reduce.2
  77.5 19.7 reduce-scatter.4
  100.3 24.8 reduce-scatter.2
  126.7 218.1 all-gather.2
where the time goes:
time: 369 us
  waiting for transfers between devices  300 us (81%)
  matrix products  27.4 us (7%)
  between operations  13.9 us (4%)
  blocking collectives  12 us (3%)
  local copies, waits for them, and re-layouts  11.4 us (3%)
  other arithmetic  4.16 us (1%)
    all_gather x1, waiting for transfers between devices, body(): piece = lax.all_gather(tokens, 'tensor', axis=1, tiled=True)  216 us
    psum x1, waiting for transfers between devices, body(): lax.psum(part_in.astype(jnp.bfloat16), 'tensor').astype(jnp.float32)  35 us
    reduce_scatter x1, waiting for transfers between devices, body(): lax.psum_scatter(dense_down_weight.astype(jnp.bfloat16), ('dp', 'pipe'),...  25.1 us
    all_gather x1, waiting for transfers between devices, body(): lax.all_gather(adapter_a, 'dp', axis=0, tiled=True)  16 us
    dot_general x1, matrix products, body(): jnp.einsum('nkf,kfe->nke', split, panel, preferred_element_type=jnp.float32)  12.8 us
  transfers between devices with their start and end apart: 5, of which 5 were waited for; matrix products, arithmetic and copies ran while one was open for 5% of the time, Pallas kernels for 0%

commit v1 on v0

v1 whole, which is shorter than its diff:
```python
import functools

import jax
import jax.numpy as jnp
from jax import lax
from jax.sharding import PartitionSpec as P

ADAPTER_SCALE = 2.0
LIVE_ROWS = 512
BF16 = jnp.bfloat16
F32 = jnp.float32


def dot(a, b, contract):
    return lax.dot_general(a, b, ((contract[0:1], contract[1:2]), ((), ())), preferred_element_type=F32)


def shift(x, name, count, step):
    return lax.ppermute(x, name, [(i, (i + step) % count) for i in range(count)])


def flip(x, names, count, mask):
    return lax.ppermute(x, names, [(i, i ^ mask) for i in range(count)])


def gather_xy(piece, planes):
    return [piece] + [flip(piece, ("groups", "dp"), planes, m) for m in range(1, planes)]


def body(sizes, tokens, base_weight, adapter_a, adapter_b, cotangent, block_tenant_index, block_fill):
    n_t, n_dp, n_pipe = sizes["tensor"], sizes["dp"], sizes["pipe"]
    planes = sizes["groups"] * n_dp
    rows, feat = tokens.shape
    cols = base_weight.shape[1]
    half = cols // n_pipe
    blocks = block_tenant_index.shape[0]
    block = rows // blocks
    rank = adapter_a.shape[1]
    tenants = adapter_a.shape[0] * n_dp
    me_t, me_pipe = lax.axis_index("tensor"), lax.axis_index("pipe")
    q = lax.axis_index("groups") * n_dp + lax.axis_index("dp")
    part_rows = feat // planes

    received = []
    for s in range(1, n_t):
        k = (me_t + s) % n_t
        share = lax.dynamic_slice(base_weight, (k * feat + q * part_rows, me_pipe * half), (part_rows, half))
        received.append(shift(share, "tensor", n_t, s))

    all_a = lax.all_gather(adapter_a, "dp", axis=0, tiled=True).reshape(tenants * rank, feat)
    all_b = lax.all_gather(adapter_b, "dp", axis=0, tiled=True).reshape(tenants * rank, cols)

    fill = block_fill.reshape(-1)
    ends = jnp.cumsum(fill)
    starts = ends - fill
    inside = jnp.arange(block, dtype=jnp.int32)
    place = jnp.where(inside[None, :] < fill[:, None], starts[:, None] + inside[None, :], -1).reshape(rows)
    packed = jnp.arange(LIVE_ROWS, dtype=jnp.int32)
    pick = (packed[:, None] == place[None, :]).astype(BF16)
    tenant_of = jnp.sum(
        jnp.where((packed[:, None] >= starts[None, :]) & (packed[:, None] < ends[None, :]), block_tenant_index[None, :], 0),
        axis=1,
    )
    own = tenant_of[:, None] == jnp.arange(tenants * rank, dtype=jnp.int32)[None, :] // rank

    x = dot(pick, tokens, (1, 0)).astype(BF16)
    c = dot(pick, cotangent, (1, 0)).astype(BF16)
    x_other = flip(x, "pipe", n_pipe, 1)

    def fold(v):
        return jnp.sum(jnp.where(own, v, 0.0).reshape(LIVE_ROWS, tenants, rank), axis=1)

    low = jnp.concatenate([fold(dot(x, all_a, (1, 1))), fold(dot(c, all_b, (1, 1)))], axis=1).astype(BF16)
    low_sum = low.astype(F32)
    for s in range(1, n_t):
        low_sum = low_sum + shift(low, "tensor", n_t, s).astype(F32)
    low_sum = low_sum.astype(BF16)

    def spread(v):
        return jnp.where(own, jnp.concatenate([v] * tenants, axis=1), jnp.zeros((), BF16))

    low_in, low_grad = spread(low_sum[:, :rank]), spread(low_sum[:, rank:])
    down = (ADAPTER_SCALE * dot(low_grad, x, (0, 0))).astype(BF16)
    up = (ADAPTER_SCALE * dot(low_in, c, (0, 0))).astype(BF16)
    both = jnp.concatenate([down, up], axis=1).reshape(n_dp, tenants // n_dp * rank, feat + cols)
    me_dp = lax.axis_index("dp")
    mine = lax.dynamic_index_in_dim(both, me_dp, 0, keepdims=False).astype(F32)
    for s in range(1, n_dp):
        sent = lax.dynamic_index_in_dim(both, (me_dp + s) % n_dp, 0, keepdims=False)
        mine = mine + shift(sent, "dp", n_dp, s).astype(F32)
    mine = mine + flip(mine.astype(BF16), "pipe", n_pipe, 1).astype(F32)
    down_out = mine[:, :feat].reshape(tenants // n_dp, rank, feat)
    up_out = mine[:, feat:].reshape(tenants // n_dp, rank, cols)

    def columns_of(v):
        return [lax.dynamic_slice_in_dim(v, (q ^ m) * part_rows, part_rows, 1) for m in range(planes)]

    x_parts, other_parts = columns_of(x), columns_of(x_other)
    own_half = jnp.zeros((LIVE_ROWS, half), F32)
    other_half = jnp.zeros((LIVE_ROWS, half), F32)
    for s in range(1, n_t):
        panel = gather_xy(received[s - 1], planes)
        y = sum(dot(a, w, (1, 0)) for a, w in zip(x_parts, panel)).astype(BF16)
        y_other = sum(dot(a, w, (1, 0)) for a, w in zip(other_parts, panel)).astype(BF16)
        own_half = own_half + shift(y, "tensor", n_t, -s).astype(F32)
        pairs = [
            (i * n_pipe + p, ((i - s) % n_t) * n_pipe + (p ^ 1)) for i in range(n_t) for p in range(n_pipe)
        ]
        other_half = other_half + lax.ppermute(y_other, ("tensor", "pipe"), pairs).astype(F32)
    weight = lax.dynamic_slice_in_dim(base_weight, me_t * feat, feat, 0)
    base = dot(x, weight, (1, 0)).astype(BF16).astype(F32)
    first = me_pipe == 0
    base = base + jnp.concatenate(
        [jnp.where(first, own_half, other_half), jnp.where(first, other_half, own_half)], axis=1
    )
    out = (base + ADAPTER_SCALE * dot(low_in, all_b, (1, 0))).astype(BF16)
    out = dot(pick, out, (0, 0)).astype(BF16)
    return out, down_out, up_out


def solution(mesh):
    placed = (
        P(("groups", "dp", "pipe"), "tensor"),
        P(None, "tensor"),
        P(("groups", "dp"), None, "tensor"),
        P(("groups", "dp"), None, "tensor"),
        P(("groups", "dp", "pipe"), "tensor"),
        P(("groups", "dp", "pipe")),
        P(("groups", "dp", "pipe"), None),
    )
    return jax.shard_map(
        functools.partial(body, dict(mesh.shape)),
        mesh=mesh,
        in_specs=placed,
        out_specs=(
            P(("groups", "dp", "pipe"), "tensor"),
            P(("groups", "dp"), None, "tensor"),
            P(("groups", "dp"), None, "tensor"),
        ),
        check_vma=False,
    )
```

time: 369 us -> 167 us (0.45)
  the two profiles are of different devices: /device:TPU:0 before, /device:TPU:13 now
where the time goes in v1:
time: 167 us; the launch traced here: 166 us
  matrix products  59.1 us (35%)
  waiting for transfers between devices  44.3 us (27%)
  starting transfers between devices  26.7 us (16%)
  between operations  14.6 us (9%)
  other arithmetic  9.93 us (6%)
  blocking collectives  5.89 us (4%)
  local copies, waits for them, and re-layouts  5.47 us (3%)
    dot_general x32, matrix products, dot(): lax.dot_general(a, b, ((contract[0:1], contract[1:2]), ((), ())), preferr...  59.1 us
    ppermute x11, waiting for transfers between devices, flip(): return lax.ppermute(x, names, [(i, i ^ mask) for i in range(count)])  16.3 us
    ppermute x10, waiting for transfers between devices, shift(): lax.ppermute(x, name, [(i, (i + step) % count) for i in range(count)])  14.5 us
    ppermute x3, waiting for transfers between devices, body(): lax.ppermute(y_other, ('tensor', 'pipe'), pairs).astype(F32)  13.5 us
    ppermute x10, starting transfers between devices, shift(): lax.ppermute(x, name, [(i, (i + step) % count) for i in range(count)])  13.2 us
    ppermute x11, starting transfers between devices, flip(): return lax.ppermute(x, names, [(i, i ^ mask) for i in range(count)])  10.3 us
    all_gather x1, blocking collectives, body(): lax.all_gather(adapter_b, 'dp', axis=0, tiled=True)  5.89 us
  transfers between devices with their start and end apart: 25, of which 8 were waited for; matrix products, arithmetic and copies ran while one was open for 41% of the time, Pallas kernels for 0%

profile of v1, /device:TPU:13, one launch (start us, length us, event | category | flops | bytes accessed | tf_op | source)
XLA Modules:
  0.0 166.0 jit_solution(11322158692879559602)
XLA Ops:
  7.3 2.2 %fusion.114 = (bf16[512,256]{1,0:T(8,128)(2,1)}, bf16[512,256]{1,0:T(8,128)(2,1)}, bf16[512,256]{1,0:T(8,128)(2,1)}) fusion(bf16[8192,512]{1,0:T(8,128)(2,1)} %param.8, s32[]{:T(128)S(6)} %select_n.116, s32[]{:T(128)S(6)} %select_n.117, s32[]{:T(128)S(6)} %select_n.124, s32[]{:T(128)S(6)} %select_n.122), kind=kLoop, calls=%fused_computation.151 | loop fusion | bytes 1572880 | tf_op jit(solution)/shard_map/dynamic_slice | solution.py:47
  9.6 2.3 %collective-permute-start.5 = (bf16[512,256]{1,0:T(8,128)(2,1)}, bf16[512,256]{1,0:T(8,128)(2,1)S(1)}, u32[]{:S(2)}, u32[]{:S(2)}) collective-permute-start(bf16[512,256]{1,0:T(8,128)(2,1)} %get-tuple-element.5), channel_id=1, source_target_pairs={{0,8},{4,12},{8,0},{12,4},{1,9},{5,13},{9,1},{13,5},{2,10},{6,14},... | collective-permute-start | bytes 786440 | tf_op jit(solution)/shard_map/ppermute | solution.py:19
  11.9 2.2 %collective-permute-start = (bf16[512,256]{1,0:T(8,128)(2,1)}, bf16[512,256]{1,0:T(8,128)(2,1)}, u32[]{:S(2)}, u32[]{:S(2)}) collective-permute-start(bf16[512,256]{1,0:T(8,128)(2,1)} %get-tuple-element.3), channel_id=1, source_target_pairs={{0,4},{4,8},{8,12},{12,0},{1,5},{5,9},{9,13},{13,1},{2,6},{6,10},{... | collective-permute-start | bytes 786440 | tf_op jit(solution)/shard_map/ppermute | solution.py:19
  16.3 3.2 %convolution_convert_fusion = bf16[512,2048]{1,0:T(8,128)(2,1)} fusion(bf16[768,2048]{1,0:T(8,128)(2,1)S(1)} %copy-done, s32[768]{0:T(1024)S(1)} %select_bitcast_fusion), kind=kOutput, calls=%fused_computation | convolution fusion | flops 1612054528 | bytes 5245952 | tf_op jit(solution)/shard_map/dot_general | solution.py:15
  22.9 5.9 %all_gather.7 = bf16[4,64,512]{2,1,0:T(8,128)(2,1)S(1)} all-gather(bf16[2,64,512]{2,1,0:T(8,128)(2,1)S(1)} %copy-done.21), channel_id=1, replica_groups=mesh['groups'=2,'tensor'=4,'dp'=2,'pipe'=2] {'dp'}, dimensions={0}, use_global_device_ids=true | all-gather | bytes 393216 | tf_op jit(solution)/shard_map/all_gather | solution.py:51
  38.5 2.2 %fusion.69 = f32[512,256]{1,0:T(8,128)} fusion(bf16[512,256]{1,0:T(8,128)(2,1)} %collective-permute-done, bf16[512,2048]{1,0:T(8,128)(2,1)} %convolution_convert_fusion, s32[]{:T(128)S(6)} %select_n.114), kind=kOutput, calls=%fused_computation.93 | convolution fusion | flops 134217728 | bytes 1310724 | tf_op jit(solution)/shard_map/dot_general | solution.py:15
  40.7 11.5 %collective-permute-done.11 = bf16[512,256]{1,0:T(8,128)(2,1)S(1)} collective-permute-done((bf16[512,256]{1,0:T(8,128)(2,1)}, bf16[512,256]{1,0:T(8,128)(2,1)S(1)}, u32[]{:S(2)}, u32[]{:S(2)}) %collective-permute-start.11) | collective-permute-done | bytes 262176 | tf_op jit(solution)/shard_map/ppermute | solution.py:23
  55.6 2.3 %collective-permute-done.8 = bf16[512,256]{1,0:T(8,128)(2,1)S(1)} collective-permute-done((bf16[512,256]{1,0:T(8,128)(2,1)S(1)}, bf16[512,256]{1,0:T(8,128)(2,1)S(1)}, u32[]{:S(2)}, u32[]{:S(2)}) %collective-permute-start.8) | collective-permute-done | bytes 262176 | tf_op jit(solution)/shard_map/ppermute | solution.py:23
  59.1 2.1 %fusion.55 = f32[512,256]{1,0:T(8,128)} fusion(bf16[512,256]{1,0:T(8,128)(2,1)S(1)} %collective-permute-done.8, bf16[512,2048]{1,0:T(8,128)(2,1)} %convolution_convert_fusion, s32[]{:T(128)S(6)} %select_n.120), kind=kOutput, calls=%fused_computation.79 | convolution fusion | flops 134217728 | bytes 1310724 | tf_op jit(solution)/shard_map/dot_general | solution.py:15
  61.2 2.5 %collective-permute-done.6 = bf16[512,256]{1,0:T(8,128)(2,1)S(1)} collective-permute-done((bf16[512,256]{1,0:T(8,128)(2,1)S(1)}, bf16[512,256]{1,0:T(8,128)(2,1)S(1)}, u32[]{:S(2)}, u32[]{:S(2)}) %collective-permute-start.6) | collective-permute-done | bytes 262176 | tf_op jit(solution)/shard_map/ppermute | solution.py:23
  63.7 2.2 %convolution_add_fusion.9 = f32[512,256]{1,0:T(8,128)} fusion(f32[512,256]{1,0:T(8,128)S(1)} %fusion.67, bf16[512,256]{1,0:T(8,128)(2,1)S(1)} %collective-permute-done.6, bf16[512,2048]{1,0:T(8,128)(2,1)} %convolution_convert_fusion, s32[]{:T(128)S(6)} %select_n.118), kind=kOutput, calls=%fused_computation.35 | convolution fusion | flops 134348800 | bytes 1835012 | tf_op jit(solution)/shard_map/dot_general | solution.py:15
  68.7 3.4 %convolution_select_fusion = f32[512,256]{0,1:T(8,128)} fusion(bf16[512,2048]{1,0:T(8,128)(2,1)} %convolution_convert_fusion, bf16[256,2048]{1,0:T(8,128)(2,1)} %bitcast.72, s32[512]{0:T(512)S(1)} %select_reduce_fusion, s32[256]{0:T(256)S(1)} %and_select_fusion), kind=kOutput, calls=%fused_computation.18 | convolution fusion | flops 537133056 | bytes 3673088 | tf_op jit(solution)/shard_map/dot_general | solution.py:15
  75.6 2.1 %collective-permute-start.19 = (bf16[512,128]{0,1:T(8,128)(2,1)S(1)}, bf16[512,128]{0,1:T(8,128)(2,1)S(1)}, u32[]{:S(2)}, u32[]{:S(2)}) collective-permute-start(bf16[512,128]{0,1:T(8,128)(2,1)S(1)} %pad_maximum_fusion.1), channel_id=1, source_target_pairs={{0,4},{4,8},{8,12},{12,0},{1,5},{5,9},{9,13},{13,1},{2,6},{6,10},{... | collective-permute-start | bytes 393224 | tf_op jit(solution)/shard_map/ppermute | solution.py:19
  79.8 3.2 %collective-permute-done.20 = bf16[512,128]{0,1:T(8,128)(2,1)S(1)} collective-permute-done((bf16[512,128]{0,1:T(8,128)(2,1)S(1)}, bf16[512,128]{0,1:T(8,128)(2,1)S(1)}, u32[]{:S(2)}, u32[]{:S(2)}) %collective-permute-start.20) | collective-permute-done | bytes 131104 | tf_op jit(solution)/shard_map/ppermute | solution.py:19
  83.2 3.3 %collective-permute-done.19 = bf16[512,128]{0,1:T(8,128)(2,1)S(1)} collective-permute-done((bf16[512,128]{0,1:T(8,128)(2,1)S(1)}, bf16[512,128]{0,1:T(8,128)(2,1)S(1)}, u32[]{:S(2)}, u32[]{:S(2)}) %collective-permute-start.19) | collective-permute-done | bytes 131104 | tf_op jit(solution)/shard_map/ppermute | solution.py:19
  86.5 2.2 %collective-permute-start.14 = (bf16[512,256]{1,0:T(8,128)(2,1)S(1)}, bf16[512,256]{1,0:T(8,128)(2,1)S(1)}, u32[]{:S(2)}, u32[]{:S(2)}) collective-permute-start(bf16[512,256]{1,0:T(8,128)(2,1)S(1)} %copy-done.18), channel_id=1, source_target_pairs={{0,4},{4,8},{8,12},{12,0},{1,5},{5,9},{9,13},{13,1},{2,6},{6,10},{... | collective-permute-start | bytes 786440 | tf_op jit(solution)/shard_map/ppermute | solution.py:19
  89.2 2.3 %fusion = bf16[256,2048]{1,0:T(8,128)(2,1)S(1)} fusion(bf16[512,2048]{1,0:T(8,128)(2,1)} %convolution_convert_fusion, bf16[512,64]{0,1:T(8,128)(2,1)S(1)} %get-tuple-element.8, s32[512]{0:T(512)S(1)} %select_reduce_fusion, s32[256]{0:T(256)S(1)} %and_select_fusion), kind=kOutput, calls=%fused_computation.2 | convolution fusion | flops 539230208 | bytes 3214336 | tf_op jit(solution)/shard_map/dot_general | solution.py:15
  98.6 8.0 %collective-permute-done.22 = bf16[128,2560]{1,0:T(8,128)(2,1)S(1)} collective-permute-done((bf16[128,2560]{1,0:T(8,128)(2,1)S(1)}, bf16[128,2560]{1,0:T(8,128)(2,1)S(1)}, u32[]{:S(2)}, u32[]{:S(2)}) %collective-permute-start.22) | collective-permute-done | bytes 655392 | tf_op jit(solution)/shard_map/ppermute | solution.py:19
  107.6 2.4 %collective-permute-start.23 = (bf16[128,2560]{1,0:T(8,128)(2,1)}, bf16[128,2560]{1,0:T(8,128)(2,1)}, u32[]{:S(2)}, u32[]{:S(2)}) collective-permute-start(bf16[128,2560]{1,0:T(8,128)(2,1)} %fusion.21), channel_id=1, source_target_pairs={{0,1},{1,0},{2,3},{3,2},{4,5},{5,4},{6,7},{7,6},{8,9},{9,8},{10,11... | collective-permute-start | bytes 1966088 | tf_op jit(solution)/shard_map/ppermute | solution.py:23
  124.5 2.1 %fusion.26 = bf16[512,256]{1,0:T(8,128)(2,1)} fusion(f32[512,256]{1,0:T(8,128)S(1)} %fusion.37, f32[512,256]{1,0:T(8,128)S(1)} %convolution_add_fusion.3, bf16[512,256]{1,0:T(8,128)(2,1)} %collective-permute-done.7, bf16[512,2048]{1,0:T(8,128)(2,1)} %collective-permute-done.15, s32[]{:T(128)S(6)} %select_n.119), kind=kOutput, calls=%fused_computation.44 | convolution fusion | flops 134610944 | bytes 2097156 | tf_op jit(solution)/shard_map/dot_general | solution.py:15
  131.9 4.4 %fusion.10 = f32[512,512]{1,0:T(8,128)} fusion(bf16[512,2048]{1,0:T(8,128)(2,1)} %convolution_convert_fusion, bf16[8192,512]{1,0:T(8,128)(2,1)} %param.8, s32[]{:T(128)S(6)} %select_n.112), kind=kOutput, calls=%fused_computation.15 | convolution fusion | flops 1074266112 | bytes 5242884 | tf_op jit(solution)/shard_map/dot_general | solution.py:15
  136.3 11.5 %collective-permute-done.17 = bf16[512,256]{1,0:T(8,128)(2,1)} collective-permute-done((bf16[512,256]{1,0:T(8,128)(2,1)}, bf16[512,256]{1,0:T(8,128)(2,1)}, u32[]{:S(2)}, u32[]{:S(2)}) %collective-permute-start.17) | collective-permute-done | bytes 262176 | tf_op jit(solution)/shard_map/ppermute | solution.py:109
  149.8 2.5 %fusion.72 = (f32[512,256]{1,0:T(8,128)}, f32[512,256]{1,0:T(8,128)}) fusion(bf16[512,256]{1,0:T(8,128)(2,1)} %copy-done.19, bf16[512,256]{1,0:T(8,128)(2,1)} %copy-done.20, bf16[512,256]{1,0:T(8,128)(2,1)} %collective-permute-done.4, bf16[512,256]{1,0:T(8,128)(2,1)} %collective-permute-done.18, bf16[512,256]{1,0:T(8,128)(2,1)} %collective-permute-done.17, ...), kind=kLoop, calls=%fused_computation.96 | loop fusion | flops 1572864 | bytes 2621441 | tf_op jit(solution)/shard_map/jit(_where)/select_n | solution.py:114
  152.4 3.3 %fusion.5 = bf16[768,512]{1,0:T(8,128)(2,1)} fusion(bf16[256,512]{1,0:T(8,128)(2,1)S(1)} %bitcast.66, f32[512,512]{1,0:T(8,128)} %fusion.10, f32[512,256]{1,0:T(8,128)} %get-tuple-element.7, f32[512,256]{1,0:T(8,128)} %get-tuple-element.6, s32[768]{0:T(1024)S(1)} %select_bitcast_fusion, bf16[512,64]{0,1:T(8,128)(2,1)S(1)} %get-tuple-element.9, ...), kind=kOutput, calls=%fused_computation.8 | convolution fusion | flops 540278784 | bytes 3217408 | tf_op jit(solution)/shard_map/dot_general | solution.py:15
  (131 shorter events, 62.0 us)
Async XLA Ops:
  7.2 61.5 %all-gather.2.cloned.1.call-start = ((), (), s32[]{:S(2)}) async-start(), calls=%async_computation | async-start | bytes 1572864 | tf_op jit(solution)/shard_map/all_gather | solution.py:50
  9.4 22.3 %collective-permute-start.10 = (bf16[512,256]{1,0:T(8,128)(2,1)}, bf16[512,256]{1,0:T(8,128)(2,1)}, u32[]{:S(2)}, u32[]{:S(2)}) collective-permute-start(bf16[512,256]{1,0:T(8,128)(2,1)} %get-tuple-element.4), channel_id=1, source_target_pairs={{0,12},{4,0},{8,4},{12,8},{1,13},{5,1},{9,5},{13,9},{2,14},{6,2},{... | collective-permute-start | bytes 786440 | tf_op jit(solution)/shard_map/ppermute | solution.py:19
  9.6 25.1 %collective-permute-start.5 = (bf16[512,256]{1,0:T(8,128)(2,1)}, bf16[512,256]{1,0:T(8,128)(2,1)S(1)}, u32[]{:S(2)}, u32[]{:S(2)}) collective-permute-start(bf16[512,256]{1,0:T(8,128)(2,1)} %get-tuple-element.5), channel_id=1, source_target_pairs={{0,8},{4,12},{8,0},{12,4},{1,9},{5,13},{9,1},{13,5},{2,10},{6,14},... | collective-permute-start | bytes 786440 | tf_op jit(solution)/shard_map/ppermute | solution.py:19
  11.9 25.4 %collective-permute-start = (bf16[512,256]{1,0:T(8,128)(2,1)}, bf16[512,256]{1,0:T(8,128)(2,1)}, u32[]{:S(2)}, u32[]{:S(2)}) collective-permute-start(bf16[512,256]{1,0:T(8,128)(2,1)} %get-tuple-element.3), channel_id=1, source_target_pairs={{0,4},{4,8},{8,12},{12,0},{1,5},{5,9},{9,13},{13,1},{2,6},{6,10},{... | collective-permute-start | bytes 786440 | tf_op jit(solution)/shard_map/ppermute | solution.py:19
  19.5 90.5 %collective-permute-start.15 = (bf16[512,2048]{1,0:T(8,128)(2,1)}, bf16[512,2048]{1,0:T(8,128)(2,1)}, u32[]{:S(2)}, u32[]{:S(2)}) collective-permute-start(bf16[512,2048]{1,0:T(8,128)(2,1)} %convolution_convert_fusion), channel_id=1, source_target_pairs={{0,1},{1,0},{2,3},{3,2},{4,5},{5,4},{6,7},{7,6},{8,9},{9,8},{10,11... | collective-permute-start | bytes 6291464 | tf_op jit(solution)/shard_map/ppermute | solution.py:23
  31.8 22.1 %collective-permute-start.13 = (bf16[512,256]{1,0:T(8,128)(2,1)}, bf16[512,256]{1,0:T(8,128)(2,1)S(1)}, u32[]{:S(2)}, u32[]{:S(2)}) collective-permute-start(bf16[512,256]{1,0:T(8,128)(2,1)} %collective-permute-done.10), channel_id=1, source_target_pairs={{0,18},{2,16},{16,2},{18,0},{1,19},{3,17},{17,3},{19,1},{4,22},{6,... | collective-permute-start | bytes 786440 | tf_op jit(solution)/shard_map/ppermute | solution.py:23
  33.0 19.3 %collective-permute-start.11 = (bf16[512,256]{1,0:T(8,128)(2,1)}, bf16[512,256]{1,0:T(8,128)(2,1)S(1)}, u32[]{:S(2)}, u32[]{:S(2)}) collective-permute-start(bf16[512,256]{1,0:T(8,128)(2,1)} %collective-permute-done.10), channel_id=1, source_target_pairs={{0,2},{2,0},{16,18},{18,16},{1,3},{3,1},{17,19},{19,17},{4,6},{6,4... | collective-permute-start | bytes 786440 | tf_op jit(solution)/shard_map/ppermute | solution.py:23
  34.7 31.2 %collective-permute-start.12 = (bf16[512,256]{1,0:T(8,128)(2,1)}, bf16[512,256]{1,0:T(8,128)(2,1)S(1)}, u32[]{:S(2)}, u32[]{:S(2)}) collective-permute-start(bf16[512,256]{1,0:T(8,128)(2,1)} %collective-permute-done.10), channel_id=1, source_target_pairs={{0,16},{2,18},{16,0},{18,2},{1,17},{3,19},{17,1},{19,3},{4,20},{6,... | collective-permute-start | bytes 786440 | tf_op jit(solution)/shard_map/ppermute | solution.py:23
  37.3 20.6 %collective-permute-start.8 = (bf16[512,256]{1,0:T(8,128)(2,1)S(1)}, bf16[512,256]{1,0:T(8,128)(2,1)S(1)}, u32[]{:S(2)}, u32[]{:S(2)}) collective-permute-start(bf16[512,256]{1,0:T(8,128)(2,1)S(1)} %collective-permute-done.5), channel_id=1, source_target_pairs={{0,18},{2,16},{16,2},{18,0},{1,19},{3,17},{17,3},{19,1},{4,22},{6,... | collective-permute-start | bytes 786440 | tf_op jit(solution)/shard_map/ppermute | solution.py:23
  52.3 11.4 %collective-permute-start.6 = (bf16[512,256]{1,0:T(8,128)(2,1)S(1)}, bf16[512,256]{1,0:T(8,128)(2,1)S(1)}, u32[]{:S(2)}, u32[]{:S(2)}) collective-permute-start(bf16[512,256]{1,0:T(8,128)(2,1)S(1)} %collective-permute-done.5), channel_id=1, source_target_pairs={{0,2},{2,0},{16,18},{18,16},{1,3},{3,1},{17,19},{19,17},{4,6},{6,4... | collective-permute-start | bytes 786440 | tf_op jit(solution)/shard_map/ppermute | solution.py:23
  53.9 21.7 %collective-permute-start.7 = (bf16[512,256]{1,0:T(8,128)(2,1)S(1)}, bf16[512,256]{1,0:T(8,128)(2,1)}, u32[]{:S(2)}, u32[]{:S(2)}) collective-permute-start(bf16[512,256]{1,0:T(8,128)(2,1)S(1)} %collective-permute-done.5), channel_id=1, source_target_pairs={{0,16},{2,18},{16,0},{18,2},{1,17},{3,19},{17,1},{19,3},{4,20},{6,... | collective-permute-start | bytes 786440 | tf_op jit(solution)/shard_map/ppermute | solution.py:23
  57.9 33.8 %collective-permute-start.3 = (bf16[512,256]{1,0:T(8,128)(2,1)}, bf16[512,256]{1,0:T(8,128)(2,1)}, u32[]{:S(2)}, u32[]{:S(2)}) collective-permute-start(bf16[512,256]{1,0:T(8,128)(2,1)} %collective-permute-done), channel_id=1, source_target_pairs={{0,18},{2,16},{16,2},{18,0},{1,19},{3,17},{17,3},{19,1},{4,22},{6,... | collective-permute-start | bytes 786440 | tf_op jit(solution)/shard_map/ppermute | solution.py:23
  73.5 9.4 %collective-permute-start.20 = (bf16[512,128]{0,1:T(8,128)(2,1)S(1)}, bf16[512,128]{0,1:T(8,128)(2,1)S(1)}, u32[]{:S(2)}, u32[]{:S(2)}) collective-permute-start(bf16[512,128]{0,1:T(8,128)(2,1)S(1)} %pad_maximum_fusion.1), channel_id=1, source_target_pairs={{0,8},{4,12},{8,0},{12,4},{1,9},{5,13},{9,1},{13,5},{2,10},{6,14},... | collective-permute-start | bytes 393224 | tf_op jit(solution)/shard_map/ppermute | solution.py:19
  75.6 10.9 %collective-permute-start.19 = (bf16[512,128]{0,1:T(8,128)(2,1)S(1)}, bf16[512,128]{0,1:T(8,128)(2,1)S(1)}, u32[]{:S(2)}, u32[]{:S(2)}) collective-permute-start(bf16[512,128]{0,1:T(8,128)(2,1)S(1)} %pad_maximum_fusion.1), channel_id=1, source_target_pairs={{0,4},{4,8},{8,12},{12,0},{1,5},{5,9},{9,13},{13,1},{2,6},{6,10},{... | collective-permute-start | bytes 393224 | tf_op jit(solution)/shard_map/ppermute | solution.py:19
  79.5 14.1 %collective-permute-start.1 = (bf16[512,256]{1,0:T(8,128)(2,1)}, bf16[512,256]{1,0:T(8,128)(2,1)S(1)}, u32[]{:S(2)}, u32[]{:S(2)}) collective-permute-start(bf16[512,256]{1,0:T(8,128)(2,1)} %collective-permute-done), channel_id=1, source_target_pairs={{0,2},{2,0},{16,18},{18,16},{1,3},{3,1},{17,19},{19,17},{4,6},{6,4... | collective-permute-start | bytes 786440 | tf_op jit(solution)/shard_map/ppermute | solution.py:23
  82.9 13.5 %collective-permute-start.2 = (bf16[512,256]{1,0:T(8,128)(2,1)}, bf16[512,256]{1,0:T(8,128)(2,1)S(1)}, u32[]{:S(2)}, u32[]{:S(2)}) collective-permute-start(bf16[512,256]{1,0:T(8,128)(2,1)} %collective-permute-done), channel_id=1, source_target_pairs={{0,16},{2,18},{16,0},{18,2},{1,17},{3,19},{17,1},{19,3},{4,20},{6,... | collective-permute-start | bytes 786440 | tf_op jit(solution)/shard_map/ppermute | solution.py:23
  86.5 42.2 %collective-permute-start.14 = (bf16[512,256]{1,0:T(8,128)(2,1)S(1)}, bf16[512,256]{1,0:T(8,128)(2,1)S(1)}, u32[]{:S(2)}, u32[]{:S(2)}) collective-permute-start(bf16[512,256]{1,0:T(8,128)(2,1)S(1)} %copy-done.18), channel_id=1, source_target_pairs={{0,4},{4,8},{8,12},{12,0},{1,5},{5,9},{9,13},{13,1},{2,6},{6,10},{... | collective-permute-start | bytes 786440 | tf_op jit(solution)/shard_map/ppermute | solution.py:19
  91.7 14.8 %collective-permute-start.22 = (bf16[128,2560]{1,0:T(8,128)(2,1)S(1)}, bf16[128,2560]{1,0:T(8,128)(2,1)S(1)}, u32[]{:S(2)}, u32[]{:S(2)}) collective-permute-start(bf16[128,2560]{1,0:T(8,128)(2,1)S(1)} %dynamic-slice_bitcast_fusion), channel_id=1, source_target_pairs={{0,2},{2,0},{1,3},{3,1},{4,6},{6,4},{5,7},{7,5},{8,10},{10,8},{9,1... | collective-permute-start | bytes 1966088 | tf_op jit(solution)/shard_map/ppermute | solution.py:19
  93.6 36.9 %collective-permute-start.9 = (bf16[512,256]{1,0:T(8,128)(2,1)S(1)}, bf16[512,256]{1,0:T(8,128)(2,1)S(1)}, u32[]{:S(2)}, u32[]{:S(2)}) collective-permute-start(bf16[512,256]{1,0:T(8,128)(2,1)S(1)} %fusion.23), channel_id=1, source_target_pairs={{0,8},{4,12},{8,0},{12,4},{1,9},{5,13},{9,1},{13,5},{2,10},{6,14},... | collective-permute-start | bytes 786440 | tf_op jit(solution)/shard_map/ppermute | solution.py:19
  98.6 37.8 %collective-permute-start.4 = (bf16[512,256]{1,0:T(8,128)(2,1)}, bf16[512,256]{1,0:T(8,128)(2,1)}, u32[]{:S(2)}, u32[]{:S(2)}) collective-permute-start(bf16[512,256]{1,0:T(8,128)(2,1)} %fusion.22), channel_id=1, source_target_pairs={{0,12},{4,0},{8,4},{12,8},{1,13},{5,1},{9,5},{13,9},{2,14},{6,2},{... | collective-permute-start | bytes 786440 | tf_op jit(solution)/shard_map/ppermute | solution.py:19
  107.6 48.1 %collective-permute-start.23 = (bf16[128,2560]{1,0:T(8,128)(2,1)}, bf16[128,2560]{1,0:T(8,128)(2,1)}, u32[]{:S(2)}, u32[]{:S(2)}) collective-permute-start(bf16[128,2560]{1,0:T(8,128)(2,1)} %fusion.21), channel_id=1, source_target_pairs={{0,1},{1,0},{2,3},{3,2},{4,5},{5,4},{6,7},{7,6},{8,9},{9,8},{10,11... | collective-permute-start | bytes 1966088 | tf_op jit(solution)/shard_map/ppermute | solution.py:23
  116.2 20.1 %collective-permute-start.18 = (bf16[512,256]{1,0:T(8,128)(2,1)}, bf16[512,256]{1,0:T(8,128)(2,1)}, u32[]{:S(2)}, u32[]{:S(2)}) collective-permute-start(bf16[512,256]{1,0:T(8,128)(2,1)} %fusion.27), channel_id=1, source_target_pairs={{0,5},{1,4},{4,9},{5,8},{8,13},{9,12},{12,1},{13,0},{2,7},{3,6},{6... | collective-permute-start | bytes 786440 | tf_op jit(solution)/shard_map/ppermute | solution.py:109
  128.7 19.1 %collective-permute-start.17 = (bf16[512,256]{1,0:T(8,128)(2,1)}, bf16[512,256]{1,0:T(8,128)(2,1)}, u32[]{:S(2)}, u32[]{:S(2)}) collective-permute-start(bf16[512,256]{1,0:T(8,128)(2,1)} %fusion.26), channel_id=1, source_target_pairs={{0,9},{1,8},{4,13},{5,12},{8,1},{9,0},{12,5},{13,4},{2,11},{3,10},... | collective-permute-start | bytes 786440 | tf_op jit(solution)/shard_map/ppermute | solution.py:109
  130.5 19.3 %collective-permute-start.16 = (bf16[512,256]{1,0:T(8,128)(2,1)}, bf16[512,256]{1,0:T(8,128)(2,1)}, u32[]{:S(2)}, u32[]{:S(2)}) collective-permute-start(bf16[512,256]{1,0:T(8,128)(2,1)} %fusion.25), channel_id=1, source_target_pairs={{0,13},{1,12},{4,1},{5,0},{8,5},{9,4},{12,9},{13,8},{2,15},{3,14},... | collective-permute-start | bytes 786440 | tf_op jit(solution)/shard_map/ppermute | solution.py:109
  (27 other events, 182.4 us)
Sparse Core Ops, SparseCore 0:
  21.2 26.3 all-gather.1

commit v2 on v1

v2 whole, which is shorter than its diff:
```python
import functools

import jax
import jax.numpy as jnp
from jax import lax
from jax.experimental import pallas as pl
from jax.experimental.pallas import tpu as pltpu
from jax.sharding import PartitionSpec as P

ADAPTER_SCALE = 2.0
LIVE = 512
BF16 = jnp.bfloat16
F32 = jnp.float32
I32 = jnp.int32
MIB = 1 << 20
SMEM = pl.BlockSpec(memory_space=pltpu.SMEM)
VMEM = pl.BlockSpec(memory_space=pltpu.VMEM)


def shaped(shape, dtype):
    return jax.ShapeDtypeStruct(shape, dtype)


def dot(a, b, contract=(1, 0)):
    return lax.dot_general(a, b, ((contract[0:1], contract[1:2]), ((), ())), preferred_element_type=F32)


def shift(x, name, count, step):
    return lax.ppermute(x, name, [(i, (i + step) % count) for i in range(count)])


def flip(x, names, count, mask):
    return lax.ppermute(x, names, [(i, i ^ mask) for i in range(count)])


def params(mib):
    return pltpu.CompilerParams(vmem_limit_bytes=mib * MIB)


def cost(flops, bytes_accessed):
    return pl.CostEstimate(flops=flops, bytes_accessed=bytes_accessed, transcendentals=0)


def starts_of(fill_ref, blocks):
    starts, at = [], jnp.int32(0)
    for b in range(blocks):
        starts.append(at)
        at = at + fill_ref[0, b]
    return starts


def tenant_lanes(fill_ref, tenant_ref, blocks, lanes):
    row = lax.broadcasted_iota(I32, (LIVE, lanes), 0)
    tenant = jnp.zeros((LIVE, lanes), I32)
    for b, start in enumerate(starts_of(fill_ref, blocks)):
        tenant = jnp.where(row >= start, tenant_ref[b], tenant)
    return tenant


def pack_kernel(blocks, block, fill_ref, tok_ref, cot_ref, x_ref, c_ref, pick):
    @pl.when(pl.program_id(0) == 0)
    def _():
        row = lax.broadcasted_iota(I32, (LIVE, block), 0)
        col = lax.broadcasted_iota(I32, (LIVE, block), 1)
        for b, start in enumerate(starts_of(fill_ref, blocks)):
            hit = (row == col + start) & (col < fill_ref[0, b])
            pick[:, b * block : (b + 1) * block] = jnp.where(hit, 1.0, 0.0).astype(BF16)
        c_ref[...] = dot(pick[...], cot_ref[...]).astype(BF16)

    x_ref[...] = dot(pick[...], tok_ref[...]).astype(BF16)


def pack(fill, tokens, cotangent, blocks):
    rows, feat = tokens.shape
    cols = cotangent.shape[1]
    steps = 4 if feat % 512 == 0 else 1
    wide = feat // steps
    return pl.pallas_call(
        functools.partial(pack_kernel, blocks, rows // blocks),
        grid=(steps,),
        in_specs=[SMEM, pl.BlockSpec((rows, wide), lambda i: (0, i)), pl.BlockSpec((rows, cols), lambda i: (0, 0))],
        out_specs=[pl.BlockSpec((LIVE, wide), lambda i: (0, i)), pl.BlockSpec((LIVE, cols), lambda i: (0, 0))],
        out_shape=[shaped((LIVE, feat), BF16), shaped((LIVE, cols), BF16)],
        scratch_shapes=[pltpu.VMEM((LIVE, rows), BF16)],
        compiler_params=params(24),
        cost_estimate=cost(2 * LIVE * rows * (feat + cols), 2 * (LIVE + rows) * (feat + cols)),
        name="pack",
    )(fill, tokens, cotangent)


def owner_mask(tenant, lane, owner, rank):
    return tenant == 2 * owner + (lane >= rank).astype(I32)


def low_kernel(n_dp, rank, blocks, dp_ref, fill_ref, tenant_ref, x_ref, c_ref, *refs):
    a_refs, b_refs, out_ref = refs[:n_dp], refs[n_dp : 2 * n_dp], refs[2 * n_dp]
    lanes = 2 * rank
    tenant = tenant_lanes(fill_ref, tenant_ref, blocks, lanes)
    lane = lax.broadcasted_iota(I32, (LIVE, lanes), 1)
    low_in = jnp.zeros((LIVE, lanes), F32)
    low_grad = jnp.zeros((LIVE, lanes), F32)
    for s in range(n_dp):
        mask = owner_mask(tenant, lane, (dp_ref[0] + n_dp - s) % n_dp, rank)
        low_in = low_in + jnp.where(mask, dot(x_ref[...], a_refs[s][...], (1, 1)), 0.0)
        low_grad = low_grad + jnp.where(mask, dot(c_ref[...], b_refs[s][...], (1, 1)), 0.0)
    low_in = low_in + pltpu.roll(low_in, rank, 1)
    low_grad = low_grad + pltpu.roll(low_grad, rank, 1)
    out_ref[...] = jnp.where(lane < rank, low_in, low_grad).astype(BF16)


def low_part(dp, fill, tenant, x, c, a_list, b_list, blocks, rank):
    n_dp = len(a_list)
    width = x.shape[1] + c.shape[1]
    return pl.pallas_call(
        functools.partial(low_kernel, n_dp, rank, blocks),
        in_specs=[SMEM] * 3 + [VMEM] * (2 + 2 * n_dp),
        out_specs=VMEM,
        out_shape=shaped((LIVE, 2 * rank), BF16),
        compiler_params=params(24),
        cost_estimate=cost(4 * LIVE * rank * n_dp * width, 2 * LIVE * width + 4 * rank * n_dp * width),
        name="low_part",
    )(dp, fill, tenant, x, c, *a_list, *b_list)


def doubled(low, lane, rank):
    turned = pltpu.roll(low, rank, 1)
    return jnp.where(lane < rank, low, turned), jnp.where(lane < rank, turned, low)


def grad_kernel(n_dp, n_t, rank, blocks, dp_ref, fill_ref, tenant_ref, x_ref, c_ref, *refs):
    lows, low_ref, own_ref, sends = refs[:n_t], refs[n_t], refs[n_t + 1], refs[n_t + 2 :]
    lanes = 2 * rank
    feat = x_ref.shape[1]
    total = lows[0][...].astype(F32)
    for ref in lows[1:]:
        total = total + ref[...].astype(F32)
    low_ref[...] = total.astype(BF16)
    total = total.astype(BF16).astype(F32)
    tenant = tenant_lanes(fill_ref, tenant_ref, blocks, lanes)
    lane = lax.broadcasted_iota(I32, (LIVE, lanes), 1)
    low_in, low_grad = doubled(total, lane, rank)
    for s in range(n_dp):
        mask = owner_mask(tenant, lane, (dp_ref[0] + s) % n_dp, rank)
        target = own_ref if s == 0 else sends[s - 1]
        grad_t = jnp.transpose(jnp.where(mask, ADAPTER_SCALE * low_grad, 0.0)).astype(BF16)
        in_t = jnp.transpose(jnp.where(mask, ADAPTER_SCALE * low_in, 0.0)).astype(BF16)
        target[:, :feat] = dot(grad_t, x_ref[...]).astype(target.dtype)
        target[:, feat:] = dot(in_t, c_ref[...]).astype(target.dtype)


def grads(dp, fill, tenant, x, c, lows, n_dp, blocks, rank):
    n_t = len(lows)
    width = x.shape[1] + c.shape[1]
    return pl.pallas_call(
        functools.partial(grad_kernel, n_dp, n_t, rank, blocks),
        in_specs=[SMEM] * 3 + [VMEM] * (2 + n_t),
        out_specs=[VMEM] * (1 + n_dp),
        out_shape=[shaped((LIVE, 2 * rank), BF16), shaped((2 * rank, width), F32)]
        + [shaped((2 * rank, width), BF16)] * (n_dp - 1),
        compiler_params=params(32),
        cost_estimate=cost(4 * LIVE * rank * n_dp * width, 2 * LIVE * width + 4 * rank * n_dp * width),
        name="grads",
    )(dp, fill, tenant, x, c, *lows)


def panel_kernel(count, place_ref, *refs):
    xs, others = refs[:count], refs[count : 2 * count]
    pieces, y_ref, y_other_ref = refs[2 * count : 3 * count], refs[3 * count], refs[3 * count + 1]
    for part, out in ((xs, y_ref), (others, y_other_ref)):
        total = dot(part[0][...], pieces[0][...])
        for a, w in zip(part[1:], pieces[1:]):
            total = total + dot(a[...], w[...])
        out[...] = total.astype(BF16)


def panel_product(place, x, x_other, pieces):
    count = len(pieces)
    deep, half = pieces[0].shape
    x_specs = [pl.BlockSpec((LIVE, deep), functools.partial(lambda m, i, place: (0, place[0] ^ m), m)) for m in range(count)]
    whole = lambda i, place: (0, 0)
    return pl.pallas_call(
        functools.partial(panel_kernel, count),
        grid_spec=pltpu.PrefetchScalarGridSpec(
            num_scalar_prefetch=1,
            grid=(1,),
            in_specs=x_specs * 2 + [pl.BlockSpec((deep, half), whole)] * count,
            out_specs=[pl.BlockSpec((LIVE, half), whole)] * 2,
        ),
        out_shape=[shaped((LIVE, half), BF16)] * 2,
        compiler_params=params(24),
        cost_estimate=cost(4 * LIVE * count * deep * half, 4 * LIVE * count * deep + 2 * count * deep * half),
        name="panel",
    )(place, *([x] * count), *([x_other] * count), *pieces)


def base_kernel(n_dp, rank, blocks, at_ref, dp_ref, fill_ref, tenant_ref, x_ref, w_ref, low_ref, *refs):
    b_refs, out_ref = refs[:n_dp], refs[n_dp]
    lanes = 2 * rank
    tenant = tenant_lanes(fill_ref, tenant_ref, blocks, lanes)
    lane = lax.broadcasted_iota(I32, (LIVE, lanes), 1)
    low_in, _ = doubled(low_ref[...].astype(F32), lane, rank)
    total = dot(x_ref[...], w_ref[...])
    for s in range(n_dp):
        mask = owner_mask(tenant, lane, (dp_ref[0] + n_dp - s) % n_dp, rank)
        total = total + dot(jnp.where(mask, ADAPTER_SCALE * low_in, 0.0).astype(BF16), b_refs[s][...])
    out_ref[...] = total


def base_product(at, dp, fill, tenant, x, base_weight, low, b_list, blocks, rank):
    n_dp = len(b_list)
    feat, cols = x.shape[1], base_weight.shape[1]
    whole = lambda i, at: (0, 0)
    return pl.pallas_call(
        functools.partial(base_kernel, n_dp, rank, blocks),
        grid_spec=pltpu.PrefetchScalarGridSpec(
            num_scalar_prefetch=1,
            grid=(1,),
            in_specs=[SMEM] * 3
            + [pl.BlockSpec((LIVE, feat), whole), pl.BlockSpec((feat, cols), lambda i, at: (at[0], 0)), pl.BlockSpec((LIVE, 2 * rank), whole)]
            + [pl.BlockSpec((2 * rank, cols), whole)] * n_dp,
            out_specs=pl.BlockSpec((LIVE, cols), whole),
        ),
        out_shape=shaped((LIVE, cols), F32),
        compiler_params=params(24),
        cost_estimate=cost(2 * LIVE * feat * cols, 2 * feat * (LIVE + cols) + 4 * LIVE * cols),
        name="base",
    )(at, dp, fill, tenant, x, base_weight, low, *b_list)


def out_kernel(count, blocks, block, core_ref, fill_ref, base_ref, *refs):
    owns, others, out_ref, held = refs[:count], refs[count : 2 * count], refs[2 * count], refs[2 * count + 1]
    half = owns[0].shape[1]

    def total(parts):
        value = parts[0][...].astype(F32)
        for part in parts[1:]:
            value = value + part[...].astype(F32)
        return value

    own, other = total(owns), total(others)
    first = core_ref[0] == 0
    held[:, :half] = (base_ref[:, :half] + jnp.where(first, own, other)).astype(BF16)
    held[:, half:] = (base_ref[:, half:] + jnp.where(first, other, own)).astype(BF16)
    row = lax.broadcasted_iota(I32, (block, LIVE), 0)
    col = lax.broadcasted_iota(I32, (block, LIVE), 1)
    for b, start in enumerate(starts_of(fill_ref, blocks)):
        hit = (col == row + start) & (row < fill_ref[0, b])
        pick = jnp.where(hit, 1.0, 0.0).astype(BF16)
        out_ref[b * block : (b + 1) * block, :] = dot(pick, held[...]).astype(BF16)


def finish(core, fill, base, owns, others, rows, blocks):
    cols = base.shape[1]
    count = len(owns)
    return pl.pallas_call(
        functools.partial(out_kernel, count, blocks, rows // blocks),
        in_specs=[SMEM] * 2 + [VMEM] * (1 + 2 * count),
        out_specs=VMEM,
        out_shape=shaped((rows, cols), BF16),
        scratch_shapes=[pltpu.VMEM((LIVE, cols), BF16)],
        compiler_params=params(24),
        cost_estimate=cost(2 * LIVE * rows * cols, 4 * LIVE * cols + 2 * LIVE * cols * count + 2 * rows * cols),
        name="finish",
    )(core, fill, base, *owns, *others)


def body(sizes, tokens, base_weight, adapter_a, adapter_b, cotangent, block_tenant_index, block_fill):
    n_t, n_dp, n_pipe = sizes["tensor"], sizes["dp"], sizes["pipe"]
    planes = sizes["groups"] * n_dp
    rows, feat = tokens.shape
    cols = base_weight.shape[1]
    half = cols // n_pipe
    blocks = block_tenant_index.shape[0]
    pair, rank = adapter_a.shape[:2]
    me_t, me_pipe, me_dp = lax.axis_index("tensor"), lax.axis_index("pipe"), lax.axis_index("dp")
    q = lax.axis_index("groups") * n_dp + me_dp
    part_rows = feat // planes
    scalar = lambda v: v.astype(I32).reshape(1)
    dp, core, at, place = scalar(me_dp), scalar(me_pipe), scalar(me_t), scalar(q)

    received = []
    for s in range(1, n_t):
        k = (me_t + s) % n_t
        share = lax.dynamic_slice(base_weight, (k * feat + q * part_rows, me_pipe * half), (part_rows, half))
        received.append(shift(share, "tensor", n_t, s))

    own_a, own_b = adapter_a.reshape(pair * rank, feat), adapter_b.reshape(pair * rank, cols)
    a_list = [own_a] + [shift(own_a, "dp", n_dp, s) for s in range(1, n_dp)]
    b_list = [own_b] + [shift(own_b, "dp", n_dp, s) for s in range(1, n_dp)]

    x, c = pack(block_fill, tokens, cotangent, blocks)
    x_other = flip(x, "pipe", n_pipe, 1)

    low = low_part(dp, block_fill, block_tenant_index, x, c, a_list, b_list, blocks, rank)
    lows = [low] + [shift(low, "tensor", n_t, s) for s in range(1, n_t)]
    low_sum, mine, *sends = grads(dp, block_fill, block_tenant_index, x, c, lows, n_dp, blocks, rank)
    for s in range(1, n_dp):
        mine = mine + shift(sends[s - 1], "dp", n_dp, s).astype(F32)
    mine = mine + flip(mine.astype(BF16), "pipe", n_pipe, 1).astype(F32)
    down_out = mine[:, :feat].reshape(pair, rank, feat)
    up_out = mine[:, feat:].reshape(pair, rank, cols)

    owns, others = [], []
    for s in range(1, n_t):
        if planes == 4:
            pieces = [received[s - 1]] + [flip(received[s - 1], ("groups", "dp"), planes, m) for m in range(1, planes)]
            y, y_other = panel_product(place, x, x_other, pieces)
        else:
            panel = lax.all_gather(received[s - 1], ("groups", "dp"), axis=0, tiled=True)
            y, y_other = panel_product(jnp.zeros_like(place), x, x_other, [panel])
        pairs = [
            (i * n_pipe + p, ((i - s) % n_t) * n_pipe + (p ^ 1)) for i in range(n_t) for p in range(n_pipe)
        ]
        owns.append(shift(y, "tensor", n_t, -s))
        others.append(lax.ppermute(y_other, ("tensor", "pipe"), pairs))
    base = base_product(at, dp, block_fill, block_tenant_index, x, base_weight, low_sum, b_list, blocks, rank)
    out = finish(core, block_fill, base, owns, others, rows, blocks)
    return out, down_out, up_out


def solution(mesh):
    placed = (
        P(("groups", "dp", "pipe"), "tensor"),
        P(None, "tensor"),
        P(("groups", "dp"), None, "tensor"),
        P(("groups", "dp"), None, "tensor"),
        P(("groups", "dp", "pipe"), "tensor"),
        P(("groups", "dp", "pipe")),
        P(("groups", "dp", "pipe"), None),
    )
    return jax.shard_map(
        functools.partial(body, dict(mesh.shape)),
        mesh=mesh,
        in_specs=placed,
        out_specs=(
            P(("groups", "dp", "pipe"), "tensor"),
            P(("groups", "dp"), None, "tensor"),
            P(("groups", "dp"), None, "tensor"),
        ),
        check_vma=False,
    )
```

time: 167 us -> 145 us (0.87)
  matrix products: 59.1 us -> 0 us
  waiting for transfers between devices: 44.3 us -> 71.7 us
  Pallas kernels: 0 us -> 21.1 us
  starting transfers between devices: 26.7 us -> 43.9 us
  between operations: 14.6 us -> 0.79 us
  other arithmetic: 9.93 us -> 0.31 us
  blocking collectives: 5.89 us -> 0 us
    dot_general x32 -> x0, matrix products: 59.1 us -> none  [dot(): lax.dot_general(a, b, ((contract[0:1], contract[1:2]), ((), ())), preferr...]
    ppermute x10 -> x12, waiting for transfers between devices: 14.5 us -> 57.6 us  [shift(): lax.ppermute(x, name, [(i, (i + step) % count) for i in range(count)])]
    pallas_call x0 -> x8, Pallas kernels: none -> 21.1 us  [the longest x3 8.65 us: panel_product(): pl.pallas_call(functools.partial(panel_kernel, count), grid_spec=pltpu.Pr...]
    ppermute x11, waiting for transfers between devices: 16.3 us -> 2.96 us  [flip(): return lax.ppermute(x, names, [(i, i ^ mask) for i in range(count)])]
    ppermute x10 -> x12, starting transfers between devices: 13.2 us -> 21.4 us  [shift(): lax.ppermute(x, name, [(i, (i + step) % count) for i in range(count)])]
    ppermute x11, starting transfers between devices: 10.3 us -> 16.4 us  [flip(): return lax.ppermute(x, names, [(i, i ^ mask) for i in range(count)])]
    all_gather x1 -> x0, blocking collectives: 5.89 us -> none  [body(): lax.all_gather(adapter_b, 'dp', axis=0, tiled=True)]
    select_n x3 -> x0, other arithmetic: 3.27 us -> none  [the longest x1 2.54 us: body(): jnp.where(first, own_half, other_half)]
  transfers between devices with their start and end apart: 25 -> 26, of which waited for: 8 -> 13; matrix products, arithmetic and copies ran while one was open for 41% -> 2% of each run, Pallas kernels for 0% -> 13%
where the time goes in v2:
time: 145 us; the launch traced here: 144 us
  waiting for transfers between devices  71.7 us (49%)
  starting transfers between devices  43.9 us (30%)
  Pallas kernels  21.1 us (15%)
  local copies, waits for them, and re-layouts  6.62 us (5%)
    ppermute x12, waiting for transfers between devices, shift(): lax.ppermute(x, name, [(i, (i + step) % count) for i in range(count)])  57.6 us
    ppermute x12, starting transfers between devices, shift(): lax.ppermute(x, name, [(i, (i + step) % count) for i in range(count)])  21.4 us
    ppermute x11, starting transfers between devices, flip(): return lax.ppermute(x, names, [(i, i ^ mask) for i in range(count)])  16.4 us
    ppermute x3, waiting for transfers between devices, body(): others.append(lax.ppermute(y_other, ('tensor', 'pipe'), pairs))  11.2 us
    pallas_call x3, Pallas kernels, panel_product(): pl.pallas_call(functools.partial(panel_kernel, count), grid_spec=pltpu.Pr...  8.65 us
    ppermute x3, starting transfers between devices, body(): others.append(lax.ppermute(y_other, ('tensor', 'pipe'), pairs))  6.14 us
    pallas_call x1, Pallas kernels, pack(): pl.pallas_call(functools.partial(pack_kernel, blocks, rows // blocks), gr...  3.78 us
    unnamed x18, local copies, waits for them, and re-layouts  3.7 us
  transfers between devices with their start and end apart: 26, of which 13 were waited for; matrix products, arithmetic and copies ran while one was open for 2% of the time, Pallas kernels for 13%

profile of v2, /device:TPU:13, one launch (start us, length us, event | category | flops | bytes accessed | tf_op | source)
XLA Modules:
  0.0 144.5 jit_solution(8541813071436320387)
XLA Ops:
  2.6 1.9 %copy-done.5 = bf16[768,2048]{1,0:T(8,128)(2,1)S(1)} copy-done((bf16[768,2048]{1,0:T(8,128)(2,1)S(1)}, bf16[768,2048]{1,0:T(8,128)(2,1)}, u32[]{:S(2)}) %copy-start.5) | copy-done | bytes 3145752
  5.6 3.8 %pack.1 = (bf16[512,2048]{1,0:T(8,128)(2,1)S(1)}, bf16[512,512]{1,0:T(8,128)(2,1)S(1)}) custom-call(s32[1,6]{1,0:T(1,128)S(1)} %copy-done.2, bf16[768,2048]{1,0:T(8,128)(2,1)S(1)} %copy-done.5, bf16[768,512]{1,0:T(8,128)(2,1)S(1)} %copy-done.6), custom_call_target="tpu_custom_call" | custom-call | flops 2013265920 | bytes 6553600 | tf_op jit(solution)/shard_map/pack/pallas_call | solution.py:78
  10.7 5.8 %collective-permute-done.1.refs_3_.refs_1_ = bf16[128,512]{1,0:T(8,128)(2,1)S(1)} collective-permute-done((bf16[128,512]{1,0:T(8,128)(2,1)S(1)}, bf16[128,512]{1,0:T(8,128)(2,1)S(1)}, u32[]{:S(2)}, u32[]{:S(2)}) %collective-permute-start.1) | collective-permute-done | bytes 131104 | tf_op jit(solution)/shard_map/ppermute | solution.py:29
  16.6 2.7 %low_part.1.refs_0_ = bf16[512,128]{1,0:T(8,128)(2,1)S(1)} custom-call(s32[1]{0:T(128)} %bitcast.2.dp_ref, s32[1,6]{1,0:T(1,128)S(1)} %copy-done.3, s32[6]{0:T(128)S(1)} %copy-done.4, bf16[512,2048]{1,0:T(8,128)(2,1)S(1)} %get-tuple-element.14.x_ref.refs_0_.refs_1_.refs_2_.refs_3_, bf16[512,512]{1,0:T(8,128)(2,1)S(1)} %get-tuple-element.15.c_ref, ...), custom_call_target="tpu_custom_call" | custom-call | flops 671088640 | bytes 3932160 | tf_op jit(solution)/shard_map/low_part/pallas_call | solution.py:114
  23.1 3.2 %collective-permute-done.3.refs_2_ = bf16[512,128]{1,0:T(8,128)(2,1)S(1)} collective-permute-done((bf16[512,128]{1,0:T(8,128)(2,1)S(1)}, bf16[512,128]{1,0:T(8,128)(2,1)S(1)}, u32[]{:S(2)}, u32[]{:S(2)}) %collective-permute-start.3) | collective-permute-done | bytes 131104 | tf_op jit(solution)/shard_map/ppermute | solution.py:29
  26.3 7.8 %collective-permute-done.4.refs_3_ = bf16[512,128]{1,0:T(8,128)(2,1)S(1)} collective-permute-done((bf16[512,128]{1,0:T(8,128)(2,1)S(1)}, bf16[512,128]{1,0:T(8,128)(2,1)S(1)}, u32[]{:S(2)}, u32[]{:S(2)}) %collective-permute-start.4) | collective-permute-done | bytes 131104 | tf_op jit(solution)/shard_map/ppermute | solution.py:29
  34.1 1.7 %grads.1 = (bf16[512,128]{1,0:T(8,128)(2,1)S(1)}, f32[128,2560]{1,0:T(8,128)S(1)}, bf16[128,2560]{1,0:T(8,128)(2,1)S(1)}) custom-call(s32[1]{0:T(128)} %bitcast.2.dp_ref, s32[1,6]{1,0:T(1,128)S(1)} %copy-done.3, s32[6]{0:T(128)S(1)} %copy-done.4, bf16[512,2048]{1,0:T(8,128)(2,1)S(1)} %get-tuple-element.14.x_ref.refs_0_.refs_1_.refs_2_.refs_3_, ...), custom_call_target="tpu_custom_call" | custom-call | flops 671088640 | bytes 3932160 | tf_op jit(solution)/shard_map/grads/pallas_call | solution.py:154
  39.7 7.2 %collective-permute-done.16.refs_8_ = bf16[512,256]{1,0:T(8,128)(2,1)S(1)} collective-permute-done((bf16[512,256]{1,0:T(8,128)(2,1)S(1)}, bf16[512,256]{1,0:T(8,128)(2,1)S(1)}, u32[]{:S(2)}, u32[]{:S(2)}) %collective-permute-start.16) | collective-permute-done | bytes 262176 | tf_op jit(solution)/shard_map/ppermute | solution.py:29
  47.1 8.4 %collective-permute-done.11.refs_8_ = bf16[512,256]{1,0:T(8,128)(2,1)S(1)} collective-permute-done((bf16[512,256]{1,0:T(8,128)(2,1)S(1)}, bf16[512,256]{1,0:T(8,128)(2,1)S(1)}, u32[]{:S(2)}, u32[]{:S(2)}) %collective-permute-start.11) | collective-permute-done | bytes 262176 | tf_op jit(solution)/shard_map/ppermute | solution.py:29
  55.7 5.4 %collective-permute-done.6.refs_8_ = bf16[512,256]{1,0:T(8,128)(2,1)S(1)} collective-permute-done((bf16[512,256]{1,0:T(8,128)(2,1)S(1)}, bf16[512,256]{1,0:T(8,128)(2,1)S(1)}, u32[]{:S(2)}, u32[]{:S(2)}) %collective-permute-start.6) | collective-permute-done | bytes 262176 | tf_op jit(solution)/shard_map/ppermute | solution.py:29
  63.9 8.9 %collective-permute-start.25 = (bf16[128,2560]{1,0:T(8,128)(2,1)S(1)}, bf16[128,2560]{1,0:T(8,128)(2,1)S(1)}, u32[]{:S(2)}, u32[]{:S(2)}) collective-permute-start(bf16[128,2560]{1,0:T(8,128)(2,1)S(1)} %fusion), channel_id=1, source_target_pairs={{0,1},{1,0},{2,3},{3,2},{4,5},{5,4},{6,7},{7,6},{8,9},{9,8},{10,11... | collective-permute-start | bytes 1966088 | tf_op jit(solution)/shard_map/ppermute | solution.py:33
  72.8 1.6 %collective-permute-start.14 = (bf16[512,256]{1,0:T(8,128)(2,1)S(1)}, bf16[512,256]{1,0:T(8,128)(2,1)S(1)}, u32[]{:S(2)}, u32[]{:S(2)}) collective-permute-start(bf16[512,256]{1,0:T(8,128)(2,1)S(1)} %collective-permute-done.11.refs_8_), channel_id=1, source_target_pairs={{0,18},{2,16},{16,2},{18,0},{1,19},{3,17},{17,3},{19,1},{4,22},{6,... | collective-permute-start | bytes 786440 | tf_op jit(solution)/shard_map/ppermute | solution.py:33
  77.7 3.0 %panel.5 = (bf16[512,256]{1,0:T(8,128)(2,1)S(1)}, bf16[512,256]{1,0:T(8,128)(2,1)S(1)}) custom-call(s32[1]{0:T(128)} %bitcast.5.place_ref, bf16[512,2048]{1,0:T(8,128)(2,1)S(1)} %get-tuple-element.14.x_ref.refs_0_.refs_1_.refs_2_.refs_3_, bf16[512,2048]{1,0:T(8,128)(2,1)S(1)} %get-tuple-element.14.x_ref.refs_0_.refs_1_.refs_2_.refs_3_, ...), custom_call_target="tpu_custom_call" | custom-call | flops 1073741824 | bytes 5242880 | tf_op jit(solution)/shard_map/panel/pallas_call | solution.py:181
  82.0 4.8 %collective-permute-start.20 = (bf16[512,256]{1,0:T(8,128)(2,1)S(1)}, bf16[512,256]{1,0:T(8,128)(2,1)S(1)}, u32[]{:S(2)}, u32[]{:S(2)}) collective-permute-start(bf16[512,256]{1,0:T(8,128)(2,1)S(1)} %get-tuple-element.19), channel_id=1, source_target_pairs={{0,4},{4,8},{8,12},{12,0},{1,5},{5,9},{9,13},{13,1},{2,6},{6,10},{... | collective-permute-start | bytes 786440 | tf_op jit(solution)/shard_map/ppermute | solution.py:29
  86.8 2.1 %base.1.base_ref = f32[512,512]{1,0:T(8,128)S(1)} custom-call(s32[1]{0:T(128)} %bitcast.1.at_ref, s32[1]{0:T(128)} %bitcast.2.dp_ref, s32[1,6]{1,0:T(1,128)S(1)} %copy-done.3, s32[6]{0:T(128)S(1)} %copy-done.4, bf16[512,2048]{1,0:T(8,128)(2,1)S(1)} %get-tuple-element.14.x_ref.refs_0_.refs_1_.refs_2_.refs_3_, bf16[8192,512]{1,0:T(8,128)(2,1)S(1)} %bitcast.9, ...), custom_call_target="tpu_custom_call" | custom-call | flops 1073741824 | bytes 5242880 | tf_op jit(solution)/shard_map/base/pallas_call | solution.py:213
  88.9 2.8 %panel.4 = (bf16[512,256]{1,0:T(8,128)(2,1)S(1)}, bf16[512,256]{1,0:T(8,128)(2,1)S(1)}) custom-call(s32[1]{0:T(128)} %bitcast.5.place_ref, bf16[512,2048]{1,0:T(8,128)(2,1)S(1)} %get-tuple-element.14.x_ref.refs_0_.refs_1_.refs_2_.refs_3_, bf16[512,2048]{1,0:T(8,128)(2,1)S(1)} %get-tuple-element.14.x_ref.refs_0_.refs_1_.refs_2_.refs_3_, ...), custom_call_target="tpu_custom_call" | custom-call | flops 1073741824 | bytes 5242880 | tf_op jit(solution)/shard_map/panel/pallas_call | solution.py:181
  91.8 3.3 %collective-permute-start.23 = (bf16[512,256]{1,0:T(8,128)(2,1)S(1)}, bf16[512,256]{1,0:T(8,128)(2,1)S(1)}, u32[]{:S(2)}, u32[]{:S(2)}) collective-permute-start(bf16[512,256]{1,0:T(8,128)(2,1)S(1)} %get-tuple-element.22), channel_id=1, source_target_pairs={{0,5},{1,4},{4,9},{5,8},{8,13},{9,12},{12,1},{13,0},{2,7},{3,6},{6... | collective-permute-start | bytes 786440 | tf_op jit(solution)/shard_map/ppermute | solution.py:315
  95.1 7.1 %collective-permute-start.15 = (bf16[512,256]{1,0:T(8,128)(2,1)S(1)}, bf16[512,256]{1,0:T(8,128)(2,1)S(1)}, u32[]{:S(2)}, u32[]{:S(2)}) collective-permute-start(bf16[512,256]{1,0:T(8,128)(2,1)S(1)} %get-tuple-element.18), channel_id=1, source_target_pairs={{0,8},{4,12},{8,0},{12,4},{1,9},{5,13},{9,1},{13,5},{2,10},{6,14},... | collective-permute-start | bytes 786440 | tf_op jit(solution)/shard_map/ppermute | solution.py:29
  102.3 2.8 %panel.3 = (bf16[512,256]{1,0:T(8,128)(2,1)S(1)}, bf16[512,256]{1,0:T(8,128)(2,1)S(1)}) custom-call(s32[1]{0:T(128)} %bitcast.5.place_ref, bf16[512,2048]{1,0:T(8,128)(2,1)S(1)} %get-tuple-element.14.x_ref.refs_0_.refs_1_.refs_2_.refs_3_, bf16[512,2048]{1,0:T(8,128)(2,1)S(1)} %get-tuple-element.14.x_ref.refs_0_.refs_1_.refs_2_.refs_3_, ...), custom_call_target="tpu_custom_call" | custom-call | flops 1073741824 | bytes 5242880 | tf_op jit(solution)/shard_map/panel/pallas_call | solution.py:181
  106.5 2.8 %collective-permute-start.21 = (bf16[512,256]{1,0:T(8,128)(2,1)S(1)}, bf16[512,256]{1,0:T(8,128)(2,1)S(1)}, u32[]{:S(2)}, u32[]{:S(2)}) collective-permute-start(bf16[512,256]{1,0:T(8,128)(2,1)S(1)} %get-tuple-element.20), channel_id=1, source_target_pairs={{0,13},{1,12},{4,1},{5,0},{8,5},{9,4},{12,9},{13,8},{2,15},{3,14},... | collective-permute-start | bytes 786440 | tf_op jit(solution)/shard_map/ppermute | solution.py:315
  111.3 19.6 %collective-permute-done.15.refs_1_ = bf16[512,256]{1,0:T(8,128)(2,1)S(1)} collective-permute-done((bf16[512,256]{1,0:T(8,128)(2,1)S(1)}, bf16[512,256]{1,0:T(8,128)(2,1)S(1)}, u32[]{:S(2)}, u32[]{:S(2)}) %collective-permute-start.15) | collective-permute-done | bytes 262176 | tf_op jit(solution)/shard_map/ppermute | solution.py:29
  130.9 5.6 %collective-permute-done.22.refs_4_ = bf16[512,256]{1,0:T(8,128)(2,1)S(1)} collective-permute-done((bf16[512,256]{1,0:T(8,128)(2,1)S(1)}, bf16[512,256]{1,0:T(8,128)(2,1)S(1)}, u32[]{:S(2)}, u32[]{:S(2)}) %collective-permute-start.22) | collective-permute-done | bytes 262176 | tf_op jit(solution)/shard_map/ppermute | solution.py:315
  136.6 5.6 %collective-permute-done.21.refs_3_ = bf16[512,256]{1,0:T(8,128)(2,1)S(1)} collective-permute-done((bf16[512,256]{1,0:T(8,128)(2,1)S(1)}, bf16[512,256]{1,0:T(8,128)(2,1)S(1)}, u32[]{:S(2)}, u32[]{:S(2)}) %collective-permute-start.21) | collective-permute-done | bytes 262176 | tf_op jit(solution)/shard_map/ppermute | solution.py:315
  142.2 2.2 %finish.1 = bf16[768,512]{1,0:T(8,128)(2,1)} custom-call(s32[1]{0:T(128)} %bitcast.core_ref, s32[1,6]{1,0:T(1,128)S(1)} %copy-done.3, f32[512,512]{1,0:T(8,128)S(1)} %base.1.base_ref, bf16[512,256]{1,0:T(8,128)(2,1)S(1)} %collective-permute-done.10.refs_0_, bf16[512,256]{1,0:T(8,128)(2,1)S(1)} %collective-permute-done.15.refs_1_, ...), custom_call_target="tpu_custom_call" | custom-call | flops 402653184 | bytes 3407872 | tf_op jit(solution)/shard_map/finish/pallas_call | solution.py:255
  (60 shorter events, 23.5 us)
Async XLA Ops:
  0.7 15.9 %collective-permute-start = (bf16[128,2048]{1,0:T(8,128)(2,1)}, bf16[128,2048]{1,0:T(8,128)(2,1)}, u32[]{:S(2)}, u32[]{:S(2)}) collective-permute-start(bf16[128,2048]{1,0:T(8,128)(2,1)} %bitcast.13), channel_id=1, source_target_pairs={{0,2},{2,0},{1,3},{3,1},{4,6},{6,4},{5,7},{7,5},{8,10},{10,8},{9,1... | collective-permute-start | bytes 1572872 | tf_op jit(solution)/shard_map/ppermute | solution.py:29
  9.4 67.2 %collective-permute-start.5 = (bf16[512,2048]{1,0:T(8,128)(2,1)S(1)}, bf16[512,2048]{1,0:T(8,128)(2,1)}, u32[]{:S(2)}, u32[]{:S(2)}) collective-permute-start(bf16[512,2048]{1,0:T(8,128)(2,1)S(1)} %get-tuple-element.14.x_ref.refs_0_.refs_1_.refs_2_.refs_3_), channel_id=1, source_target_pairs={{0,1},{1,0},{2,3},{3,2},{4,5},{5,4},{6,7},{7,6},{8,9},{9,8},{10,11... | collective-permute-start | bytes 6291464 | tf_op jit(solution)/shard_map/ppermute | solution.py:33
  10.4 6.1 %collective-permute-start.1 = (bf16[128,512]{1,0:T(8,128)(2,1)S(1)}, bf16[128,512]{1,0:T(8,128)(2,1)S(1)}, u32[]{:S(2)}, u32[]{:S(2)}) collective-permute-start(bf16[128,512]{1,0:T(8,128)(2,1)S(1)} %bitcast.10), channel_id=1, source_target_pairs={{0,2},{2,0},{1,3},{3,1},{4,6},{6,4},{5,7},{7,5},{8,10},{10,8},{9,1... | collective-permute-start | bytes 393224 | tf_op jit(solution)/shard_map/ppermute | solution.py:29
  21.7 12.4 %collective-permute-start.4 = (bf16[512,128]{1,0:T(8,128)(2,1)S(1)}, bf16[512,128]{1,0:T(8,128)(2,1)S(1)}, u32[]{:S(2)}, u32[]{:S(2)}) collective-permute-start(bf16[512,128]{1,0:T(8,128)(2,1)S(1)} %low_part.1.refs_0_), channel_id=1, source_target_pairs={{0,12},{4,0},{8,4},{12,8},{1,13},{5,1},{9,5},{13,9},{2,14},{6,2},{... | collective-permute-start | bytes 393224 | tf_op jit(solution)/shard_map/ppermute | solution.py:29
  35.7 26.8 %collective-permute-start.24 = (bf16[128,2560]{1,0:T(8,128)(2,1)S(1)}, bf16[128,2560]{1,0:T(8,128)(2,1)S(1)}, u32[]{:S(2)}, u32[]{:S(2)}) collective-permute-start(bf16[128,2560]{1,0:T(8,128)(2,1)S(1)} %get-tuple-element.24), channel_id=1, source_target_pairs={{0,2},{2,0},{1,3},{3,1},{4,6},{6,4},{5,7},{7,5},{8,10},{10,8},{9,1... | collective-permute-start | bytes 1966088 | tf_op jit(solution)/shard_map/ppermute | solution.py:29
  38.2 8.7 %collective-permute-start.16 = (bf16[512,256]{1,0:T(8,128)(2,1)S(1)}, bf16[512,256]{1,0:T(8,128)(2,1)S(1)}, u32[]{:S(2)}, u32[]{:S(2)}) collective-permute-start(bf16[512,256]{1,0:T(8,128)(2,1)S(1)} %get-tuple-element.25), channel_id=1, source_target_pairs={{0,12},{4,0},{8,4},{12,8},{1,13},{5,1},{9,5},{13,9},{2,14},{6,2},{... | collective-permute-start | bytes 786440 | tf_op jit(solution)/shard_map/ppermute | solution.py:29
  38.2 17.3 %collective-permute-start.11 = (bf16[512,256]{1,0:T(8,128)(2,1)S(1)}, bf16[512,256]{1,0:T(8,128)(2,1)S(1)}, u32[]{:S(2)}, u32[]{:S(2)}) collective-permute-start(bf16[512,256]{1,0:T(8,128)(2,1)S(1)} %get-tuple-element.27), channel_id=1, source_target_pairs={{0,8},{4,12},{8,0},{12,4},{1,9},{5,13},{9,1},{13,5},{2,10},{6,14},... | collective-permute-start | bytes 786440 | tf_op jit(solution)/shard_map/ppermute | solution.py:29
  38.7 22.5 %collective-permute-start.6 = (bf16[512,256]{1,0:T(8,128)(2,1)S(1)}, bf16[512,256]{1,0:T(8,128)(2,1)S(1)}, u32[]{:S(2)}, u32[]{:S(2)}) collective-permute-start(bf16[512,256]{1,0:T(8,128)(2,1)S(1)} %get-tuple-element.26), channel_id=1, source_target_pairs={{0,4},{4,8},{8,12},{12,0},{1,5},{5,9},{9,13},{13,1},{2,6},{6,10},{... | collective-permute-start | bytes 786440 | tf_op jit(solution)/shard_map/ppermute | solution.py:29
  46.9 14.5 %collective-permute-start.17 = (bf16[512,256]{1,0:T(8,128)(2,1)S(1)}, bf16[512,256]{1,0:T(8,128)(2,1)S(1)}, u32[]{:S(2)}, u32[]{:S(2)}) collective-permute-start(bf16[512,256]{1,0:T(8,128)(2,1)S(1)} %collective-permute-done.16.refs_8_), channel_id=1, source_target_pairs={{0,2},{2,0},{16,18},{18,16},{1,3},{3,1},{17,19},{19,17},{4,6},{6,4... | collective-permute-start | bytes 786440 | tf_op jit(solution)/shard_map/ppermute | solution.py:33
  55.5 8.4 %collective-permute-start.18 = (bf16[512,256]{1,0:T(8,128)(2,1)S(1)}, bf16[512,256]{1,0:T(8,128)(2,1)S(1)}, u32[]{:S(2)}, u32[]{:S(2)}) collective-permute-start(bf16[512,256]{1,0:T(8,128)(2,1)S(1)} %collective-permute-done.16.refs_8_), channel_id=1, source_target_pairs={{0,16},{2,18},{16,0},{18,2},{1,17},{3,19},{17,1},{19,3},{4,20},{6,... | collective-permute-start | bytes 786440 | tf_op jit(solution)/shard_map/ppermute | solution.py:33
  61.1 11.7 %collective-permute-start.19 = (bf16[512,256]{1,0:T(8,128)(2,1)S(1)}, bf16[512,256]{1,0:T(8,128)(2,1)S(1)}, u32[]{:S(2)}, u32[]{:S(2)}) collective-permute-start(bf16[512,256]{1,0:T(8,128)(2,1)S(1)} %collective-permute-done.16.refs_8_), channel_id=1, source_target_pairs={{0,18},{2,16},{16,2},{18,0},{1,19},{3,17},{17,3},{19,1},{4,22},{6,... | collective-permute-start | bytes 786440 | tf_op jit(solution)/shard_map/ppermute | solution.py:33
  61.3 13.7 %collective-permute-start.12 = (bf16[512,256]{1,0:T(8,128)(2,1)S(1)}, bf16[512,256]{1,0:T(8,128)(2,1)S(1)}, u32[]{:S(2)}, u32[]{:S(2)}) collective-permute-start(bf16[512,256]{1,0:T(8,128)(2,1)S(1)} %collective-permute-done.11.refs_8_), channel_id=1, source_target_pairs={{0,2},{2,0},{16,18},{18,16},{1,3},{3,1},{17,19},{19,17},{4,6},{6,4... | collective-permute-start | bytes 786440 | tf_op jit(solution)/shard_map/ppermute | solution.py:33
  62.6 13.8 %collective-permute-start.13 = (bf16[512,256]{1,0:T(8,128)(2,1)S(1)}, bf16[512,256]{1,0:T(8,128)(2,1)S(1)}, u32[]{:S(2)}, u32[]{:S(2)}) collective-permute-start(bf16[512,256]{1,0:T(8,128)(2,1)S(1)} %collective-permute-done.11.refs_8_), channel_id=1, source_target_pairs={{0,16},{2,18},{16,0},{18,2},{1,17},{3,19},{17,1},{19,3},{4,20},{6,... | collective-permute-start | bytes 786440 | tf_op jit(solution)/shard_map/ppermute | solution.py:33
  63.9 41.2 %collective-permute-start.25 = (bf16[128,2560]{1,0:T(8,128)(2,1)S(1)}, bf16[128,2560]{1,0:T(8,128)(2,1)S(1)}, u32[]{:S(2)}, u32[]{:S(2)}) collective-permute-start(bf16[128,2560]{1,0:T(8,128)(2,1)S(1)} %fusion), channel_id=1, source_target_pairs={{0,1},{1,0},{2,3},{3,2},{4,5},{5,4},{6,7},{7,6},{8,9},{9,8},{10,11... | collective-permute-start | bytes 1966088 | tf_op jit(solution)/shard_map/ppermute | solution.py:33
  72.8 9.2 %collective-permute-start.14 = (bf16[512,256]{1,0:T(8,128)(2,1)S(1)}, bf16[512,256]{1,0:T(8,128)(2,1)S(1)}, u32[]{:S(2)}, u32[]{:S(2)}) collective-permute-start(bf16[512,256]{1,0:T(8,128)(2,1)S(1)} %collective-permute-done.11.refs_8_), channel_id=1, source_target_pairs={{0,18},{2,16},{16,2},{18,0},{1,19},{3,17},{17,3},{19,1},{4,22},{6,... | collective-permute-start | bytes 786440 | tf_op jit(solution)/shard_map/ppermute | solution.py:33
  75.1 16.7 %collective-permute-start.7 = (bf16[512,256]{1,0:T(8,128)(2,1)S(1)}, bf16[512,256]{1,0:T(8,128)(2,1)S(1)}, u32[]{:S(2)}, u32[]{:S(2)}) collective-permute-start(bf16[512,256]{1,0:T(8,128)(2,1)S(1)} %collective-permute-done.6.refs_8_), channel_id=1, source_target_pairs={{0,2},{2,0},{16,18},{18,16},{1,3},{3,1},{17,19},{19,17},{4,6},{6,4... | collective-permute-start | bytes 786440 | tf_op jit(solution)/shard_map/ppermute | solution.py:33
  76.3 18.8 %collective-permute-start.8 = (bf16[512,256]{1,0:T(8,128)(2,1)S(1)}, bf16[512,256]{1,0:T(8,128)(2,1)S(1)}, u32[]{:S(2)}, u32[]{:S(2)}) collective-permute-start(bf16[512,256]{1,0:T(8,128)(2,1)S(1)} %collective-permute-done.6.refs_8_), channel_id=1, source_target_pairs={{0,16},{2,18},{16,0},{18,2},{1,17},{3,19},{17,1},{19,3},{4,20},{6,... | collective-permute-start | bytes 786440 | tf_op jit(solution)/shard_map/ppermute | solution.py:33
  76.6 25.6 %collective-permute-start.9 = (bf16[512,256]{1,0:T(8,128)(2,1)S(1)}, bf16[512,256]{1,0:T(8,128)(2,1)S(1)}, u32[]{:S(2)}, u32[]{:S(2)}) collective-permute-start(bf16[512,256]{1,0:T(8,128)(2,1)S(1)} %collective-permute-done.6.refs_8_), channel_id=1, source_target_pairs={{0,18},{2,16},{16,2},{18,0},{1,19},{3,17},{17,3},{19,1},{4,22},{6,... | collective-permute-start | bytes 786440 | tf_op jit(solution)/shard_map/ppermute | solution.py:33
  82.0 24.4 %collective-permute-start.20 = (bf16[512,256]{1,0:T(8,128)(2,1)S(1)}, bf16[512,256]{1,0:T(8,128)(2,1)S(1)}, u32[]{:S(2)}, u32[]{:S(2)}) collective-permute-start(bf16[512,256]{1,0:T(8,128)(2,1)S(1)} %get-tuple-element.19), channel_id=1, source_target_pairs={{0,4},{4,8},{8,12},{12,0},{1,5},{5,9},{9,13},{13,1},{2,6},{6,10},{... | collective-permute-start | bytes 786440 | tf_op jit(solution)/shard_map/ppermute | solution.py:29
  91.8 19.4 %collective-permute-start.23 = (bf16[512,256]{1,0:T(8,128)(2,1)S(1)}, bf16[512,256]{1,0:T(8,128)(2,1)S(1)}, u32[]{:S(2)}, u32[]{:S(2)}) collective-permute-start(bf16[512,256]{1,0:T(8,128)(2,1)S(1)} %get-tuple-element.22), channel_id=1, source_target_pairs={{0,5},{1,4},{4,9},{5,8},{8,13},{9,12},{12,1},{13,0},{2,7},{3,6},{6... | collective-permute-start | bytes 786440 | tf_op jit(solution)/shard_map/ppermute | solution.py:315
  95.1 35.7 %collective-permute-start.15 = (bf16[512,256]{1,0:T(8,128)(2,1)S(1)}, bf16[512,256]{1,0:T(8,128)(2,1)S(1)}, u32[]{:S(2)}, u32[]{:S(2)}) collective-permute-start(bf16[512,256]{1,0:T(8,128)(2,1)S(1)} %get-tuple-element.18), channel_id=1, source_target_pairs={{0,8},{4,12},{8,0},{12,4},{1,9},{5,13},{9,1},{13,5},{2,10},{6,14},... | collective-permute-start | bytes 786440 | tf_op jit(solution)/shard_map/ppermute | solution.py:29
  102.3 34.2 %collective-permute-start.22 = (bf16[512,256]{1,0:T(8,128)(2,1)S(1)}, bf16[512,256]{1,0:T(8,128)(2,1)S(1)}, u32[]{:S(2)}, u32[]{:S(2)}) collective-permute-start(bf16[512,256]{1,0:T(8,128)(2,1)S(1)} %get-tuple-element.21), channel_id=1, source_target_pairs={{0,9},{1,8},{4,13},{5,12},{8,1},{9,0},{12,5},{13,4},{2,11},{3,10},... | collective-permute-start | bytes 786440 | tf_op jit(solution)/shard_map/ppermute | solution.py:315
  105.1 31.5 %collective-permute-start.10 = (bf16[512,256]{1,0:T(8,128)(2,1)S(1)}, bf16[512,256]{1,0:T(8,128)(2,1)S(1)}, u32[]{:S(2)}, u32[]{:S(2)}) collective-permute-start(bf16[512,256]{1,0:T(8,128)(2,1)S(1)} %get-tuple-element.17), channel_id=1, source_target_pairs={{0,12},{4,0},{8,4},{12,8},{1,13},{5,1},{9,5},{13,9},{2,14},{6,2},{... | collective-permute-start | bytes 786440 | tf_op jit(solution)/shard_map/ppermute | solution.py:29
  106.5 35.7 %collective-permute-start.21 = (bf16[512,256]{1,0:T(8,128)(2,1)S(1)}, bf16[512,256]{1,0:T(8,128)(2,1)S(1)}, u32[]{:S(2)}, u32[]{:S(2)}) collective-permute-start(bf16[512,256]{1,0:T(8,128)(2,1)S(1)} %get-tuple-element.20), channel_id=1, source_target_pairs={{0,13},{1,12},{4,1},{5,0},{8,5},{9,4},{12,9},{13,8},{2,15},{3,14},... | collective-permute-start | bytes 786440 | tf_op jit(solution)/shard_map/ppermute | solution.py:315
  (11 other events, 78.9 us)

commit v3 on v2

--- a/solution.py
+++ b/solution.py
@@ -38,7 +38,11 @@
 
 
 def cost(flops, bytes_accessed):
-    return pl.CostEstimate(flops=flops, bytes_accessed=bytes_accessed, transcendentals=0)
+    return pl.CostEstimate(flops=1, bytes_accessed=1, transcendentals=0)
+
+
+def after(x, *others):
+    return lax.optimization_barrier((x, *others))[0]
 
 
 def starts_of(fill_ref, blocks):
@@ -55,6 +59,42 @@
     for b, start in enumerate(starts_of(fill_ref, blocks)):
         tenant = jnp.where(row >= start, tenant_ref[b], tenant)
     return tenant
+
+
+def shares_kernel(count, at_ref, w_ref, a_ref, b_ref, *refs):
+    outs, both, sems = refs[:count], refs[count], refs[count + 1]
+    deep, half = outs[0].shape
+    feat = a_ref.shape[1]
+    col = pl.multiple_of(at_ref[count], 128)
+    copies = []
+    for s in range(count):
+        source = w_ref.at[pl.ds(pl.multiple_of(at_ref[s], 16), deep), pl.ds(col, half)]
+        copies.append(pltpu.make_async_copy(source, outs[s], sems.at[s]))
+    copies.append(pltpu.make_async_copy(a_ref, both.at[:, :feat], sems.at[count]))
+    copies.append(pltpu.make_async_copy(b_ref, both.at[:, feat:], sems.at[count + 1]))
+    for copy in copies:
+        copy.start()
+    for copy in copies:
+        copy.wait()
+
+
+def shares_of(rows_at, col_at, base_weight, a, b, deep, half):
+    if half % 128 or deep % 16:
+        blocks = [lax.dynamic_slice(base_weight, (row, col_at), (deep, half)) for row in rows_at]
+        return blocks, jnp.concatenate([a, b], axis=1)
+    count = len(rows_at)
+    shapes = [shaped((deep, half), BF16)] * count + [shaped((a.shape[0], a.shape[1] + b.shape[1]), BF16)]
+    *blocks, both = pl.pallas_call(
+        functools.partial(shares_kernel, count),
+        in_specs=[SMEM] + [pl.BlockSpec(memory_space=pl.ANY)] * 3,
+        out_specs=[VMEM] * (count + 1),
+        out_shape=shapes,
+        scratch_shapes=[pltpu.SemaphoreType.DMA((count + 2,))],
+        compiler_params=params(8),
+        cost_estimate=cost(0, 4 * (count * deep * half + shapes[-1].size)),
+        name="shares",
+    )(jnp.stack([*rows_at, col_at]).astype(I32), base_weight, a, b)
+    return blocks, both
 
 
 def pack_kernel(blocks, block, fill_ref, tok_ref, cot_ref, x_ref, c_ref, pick):
@@ -93,7 +133,8 @@
 
 
 def low_kernel(n_dp, rank, blocks, dp_ref, fill_ref, tenant_ref, x_ref, c_ref, *refs):
-    a_refs, b_refs, out_ref = refs[:n_dp], refs[n_dp : 2 * n_dp], refs[2 * n_dp]
+    ab_refs, out_ref = refs[:n_dp], refs[n_dp]
+    feat = x_ref.shape[1]
     lanes = 2 * rank
     tenant = tenant_lanes(fill_ref, tenant_ref, blocks, lanes)
     lane = lax.broadcasted_iota(I32, (LIVE, lanes), 1)
@@ -101,25 +142,25 @@
     low_grad = jnp.zeros((LIVE, lanes), F32)
     for s in range(n_dp):
         mask = owner_mask(tenant, lane, (dp_ref[0] + n_dp - s) % n_dp, rank)
-        low_in = low_in + jnp.where(mask, dot(x_ref[...], a_refs[s][...], (1, 1)), 0.0)
-        low_grad = low_grad + jnp.where(mask, dot(c_ref[...], b_refs[s][...], (1, 1)), 0.0)
+        low_in = low_in + jnp.where(mask, dot(x_ref[...], ab_refs[s][:, :feat], (1, 1)), 0.0)
+        low_grad = low_grad + jnp.where(mask, dot(c_ref[...], ab_refs[s][:, feat:], (1, 1)), 0.0)
     low_in = low_in + pltpu.roll(low_in, rank, 1)
     low_grad = low_grad + pltpu.roll(low_grad, rank, 1)
     out_ref[...] = jnp.where(lane < rank, low_in, low_grad).astype(BF16)
 
 
-def low_part(dp, fill, tenant, x, c, a_list, b_list, blocks, rank):
-    n_dp = len(a_list)
+def low_part(dp, fill, tenant, x, c, ab_list, blocks, rank):
+    n_dp = len(ab_list)
     width = x.shape[1] + c.shape[1]
     return pl.pallas_call(
         functools.partial(low_kernel, n_dp, rank, blocks),
-        in_specs=[SMEM] * 3 + [VMEM] * (2 + 2 * n_dp),
+        in_specs=[SMEM] * 3 + [VMEM] * (2 + n_dp),
         out_specs=VMEM,
         out_shape=shaped((LIVE, 2 * rank), BF16),
         compiler_params=params(24),
         cost_estimate=cost(4 * LIVE * rank * n_dp * width, 2 * LIVE * width + 4 * rank * n_dp * width),
         name="low_part",
-    )(dp, fill, tenant, x, c, *a_list, *b_list)
+    )(dp, fill, tenant, x, c, *ab_list)
 
 
 def doubled(low, lane, rank):
@@ -163,38 +204,56 @@
     )(dp, fill, tenant, x, c, *lows)
 
 
-def panel_kernel(count, place_ref, *refs):
-    xs, others = refs[:count], refs[count : 2 * count]
-    pieces, y_ref, y_other_ref = refs[2 * count : 3 * count], refs[3 * count], refs[3 * count + 1]
-    for part, out in ((xs, y_ref), (others, y_other_ref)):
-        total = dot(part[0][...], pieces[0][...])
-        for a, w in zip(part[1:], pieces[1:]):
-            total = total + dot(a[...], w[...])
+def panel_kernel(order, sources, place_ref, *refs):
+    pieces, outs = refs[sources:-sources], refs[-sources:]
+    for source, out in zip(refs[:sources], outs):
+        total, at = None, 0
+        deep = source.shape[1] // len(order)
+        for piece in pieces:
+            for i in range(piece.shape[0] // deep):
+                col = pl.multiple_of((place_ref[0] ^ order[at]) * deep, min(deep, 128))
+                term = dot(source[:, pl.ds(col, deep)], piece[i * deep : (i + 1) * deep, :])
+                total = term if total is None else total + term
+                at += 1
         out[...] = total.astype(BF16)
 
 
-def panel_product(place, x, x_other, pieces):
-    count = len(pieces)
-    deep, half = pieces[0].shape
-    x_specs = [pl.BlockSpec((LIVE, deep), functools.partial(lambda m, i, place: (0, place[0] ^ m), m)) for m in range(count)]
-    whole = lambda i, place: (0, 0)
-    return pl.pallas_call(
-        functools.partial(panel_kernel, count),
-        grid_spec=pltpu.PrefetchScalarGridSpec(
-            num_scalar_prefetch=1,
-            grid=(1,),
-            in_specs=x_specs * 2 + [pl.BlockSpec((deep, half), whole)] * count,
-            out_specs=[pl.BlockSpec((LIVE, half), whole)] * 2,
-        ),
-        out_shape=[shaped((LIVE, half), BF16)] * 2,
+def panel_product(order, place, sources, pieces):
+    feat, half = sources[0].shape[1], pieces[0].shape[1]
+    count = len(sources)
+    return pl.pallas_call(
+        functools.partial(panel_kernel, order, count),
+        in_specs=[SMEM] + [VMEM] * (count + len(pieces)),
+        out_specs=[VMEM] * count,
+        out_shape=[shaped((LIVE, half), BF16)] * count,
         compiler_params=params(24),
-        cost_estimate=cost(4 * LIVE * count * deep * half, 4 * LIVE * count * deep + 2 * count * deep * half),
+        cost_estimate=cost(2 * count * LIVE * feat * half, 2 * count * LIVE * feat + 2 * feat * half),
         name="panel",
-    )(place, *([x] * count), *([x_other] * count), *pieces)
+    )(place, *sources, *pieces)
+
+
+def settle_kernel(own_ref, got_ref, down_ref, up_ref):
+    pair, rank, feat = down_ref.shape
+    for t in range(pair):
+        total = own_ref[t * rank : (t + 1) * rank, :] + got_ref[t * rank : (t + 1) * rank, :].astype(F32)
+        down_ref[t], up_ref[t] = total[:, :feat], total[:, feat:]
+
+
+def settle(own, got, pair, feat):
+    rank, width = own.shape[0] // pair, own.shape[1]
+    return pl.pallas_call(
+        settle_kernel,
+        in_specs=[VMEM] * 2,
+        out_specs=[VMEM] * 2,
+        out_shape=[shaped((pair, rank, feat), F32), shaped((pair, rank, width - feat), F32)],
+        compiler_params=params(16),
+        cost_estimate=cost(own.size, 10 * own.size),
+        name="settle",
+    )(own, got)
 
 
 def base_kernel(n_dp, rank, blocks, at_ref, dp_ref, fill_ref, tenant_ref, x_ref, w_ref, low_ref, *refs):
-    b_refs, out_ref = refs[:n_dp], refs[n_dp]
+    ab_refs, out_ref = refs[:n_dp], refs[n_dp]
     lanes = 2 * rank
     tenant = tenant_lanes(fill_ref, tenant_ref, blocks, lanes)
     lane = lax.broadcasted_iota(I32, (LIVE, lanes), 1)
@@ -202,12 +261,12 @@
     total = dot(x_ref[...], w_ref[...])
     for s in range(n_dp):
         mask = owner_mask(tenant, lane, (dp_ref[0] + n_dp - s) % n_dp, rank)
-        total = total + dot(jnp.where(mask, ADAPTER_SCALE * low_in, 0.0).astype(BF16), b_refs[s][...])
+        total = total + dot(jnp.where(mask, ADAPTER_SCALE * low_in, 0.0).astype(BF16), ab_refs[s][...])
     out_ref[...] = total
 
 
-def base_product(at, dp, fill, tenant, x, base_weight, low, b_list, blocks, rank):
-    n_dp = len(b_list)
+def base_product(at, dp, fill, tenant, x, base_weight, low, ab_list, blocks, rank):
+    n_dp = len(ab_list)
     feat, cols = x.shape[1], base_weight.shape[1]
     whole = lambda i, at: (0, 0)
     return pl.pallas_call(
@@ -217,14 +276,14 @@
             grid=(1,),
             in_specs=[SMEM] * 3
             + [pl.BlockSpec((LIVE, feat), whole), pl.BlockSpec((feat, cols), lambda i, at: (at[0], 0)), pl.BlockSpec((LIVE, 2 * rank), whole)]
-            + [pl.BlockSpec((2 * rank, cols), whole)] * n_dp,
+            + [pl.BlockSpec((2 * rank, cols), lambda i, at: (0, feat // cols))] * n_dp,
             out_specs=pl.BlockSpec((LIVE, cols), whole),
         ),
         out_shape=shaped((LIVE, cols), F32),
         compiler_params=params(24),
         cost_estimate=cost(2 * LIVE * feat * cols, 2 * feat * (LIVE + cols) + 4 * LIVE * cols),
         name="base",
-    )(at, dp, fill, tenant, x, base_weight, low, *b_list)
+    )(at, dp, fill, tenant, x, base_weight, low, *ab_list)
 
 
 def out_kernel(count, blocks, block, core_ref, fill_ref, base_ref, *refs):
@@ -278,42 +337,69 @@
     scalar = lambda v: v.astype(I32).reshape(1)
     dp, core, at, place = scalar(me_dp), scalar(me_pipe), scalar(me_t), scalar(q)
 
-    received = []
-    for s in range(1, n_t):
-        k = (me_t + s) % n_t
-        share = lax.dynamic_slice(base_weight, (k * feat + q * part_rows, me_pipe * half), (part_rows, half))
-        received.append(shift(share, "tensor", n_t, s))
-
+    steps = list(range(1, n_t))
     own_a, own_b = adapter_a.reshape(pair * rank, feat), adapter_b.reshape(pair * rank, cols)
-    a_list = [own_a] + [shift(own_a, "dp", n_dp, s) for s in range(1, n_dp)]
-    b_list = [own_b] + [shift(own_b, "dp", n_dp, s) for s in range(1, n_dp)]
-
-    x, c = pack(block_fill, tokens, cotangent, blocks)
-    x_other = flip(x, "pipe", n_pipe, 1)
-
-    low = low_part(dp, block_fill, block_tenant_index, x, c, a_list, b_list, blocks, rank)
-    lows = [low] + [shift(low, "tensor", n_t, s) for s in range(1, n_t)]
+    rows_at = [(me_t + s) % n_t * feat + q * part_rows for s in steps]
+    blocks_w, own_ab = shares_of(rows_at, me_pipe * half, base_weight, own_a, own_b, part_rows, half)
+    shares = dict(zip(steps, blocks_w))
+    lead = n_t // 2
+    received = {lead: shift(shares[lead], "tensor", n_t, lead)}
+    ab_list = [own_ab] + [shift(own_ab, "dp", n_dp, s) for s in range(1, n_dp)]
+
+    fill = after(block_fill, shares[lead])
+    x, c = pack(fill, tokens, cotangent, blocks)
+    rest = [s for s in steps if s != lead][::-1]
+    for s in rest:
+        received[s] = shift(shares[s], "tensor", n_t, s)
+
+    def gathered(piece, first, low=None):
+        if planes != 4:
+            return [lax.all_gather(piece, ("groups", "dp"), axis=0, tiled=True)], [0]
+        if first is None:
+            near = [flip(piece, ("groups", "dp"), planes, m) for m in (1, 2)]
+            return [piece, *near, flip(after(piece, received[rest[0]]), ("groups", "dp"), planes, 3)], [0, 1, 2, 3]
+        stack = jnp.concatenate([piece, flip(piece, ("groups", "dp"), planes, first)], axis=0)
+        stack = after(stack, low)
+        return [stack, flip(stack, ("groups", "dp"), planes, 3 - first)], [0, first, 3 - first, 3]
+
+    def send_back(s, y, y_other):
+        pairs = [(i * n_pipe + p, ((i - s) % n_t) * n_pipe + (p ^ 1)) for i in range(n_t) for p in range(n_pipe)]
+        return shift(y, "tensor", n_t, -s), lax.ppermute(y_other, ("tensor", "pipe"), pairs)
+
+    low = low_part(dp, block_fill, block_tenant_index, x, c, ab_list, blocks, rank)
+    panel_at = place if planes == 4 else jnp.zeros_like(place)
+    pieces, order = gathered(received[lead], None)
+    x_other = flip(after(x, received[lead]), "pipe", n_pipe, 1)
+    pieces = [after(pieces[0], *[received[s] for s in rest]), *pieces[1:]]
+    (y,) = panel_product(order, panel_at, [x], pieces)
+    received.update((s, after(received[s], y)) for s in rest)
+    (y_other,) = panel_product(order, panel_at, [x_other], pieces)
+    owns, others = zip(send_back(lead, y, y_other))
+
+    low = after(low, x_other, y, *[received[s] for s in rest])
+    mask = 1
+    while 2 * mask < n_t:
+        low = (low.astype(F32) + flip(low, "tensor", n_t, mask).astype(F32)).astype(BF16)
+        mask *= 2
+    final_low = after(low, owns[0], y_other)
+    lows = [final_low] + ([flip(final_low, "tensor", n_t, mask)] if n_t > 1 else [])
+
+    last = []
+    for i, s in enumerate(rest):
+        pieces, order = gathered(received[s], 1 + i % 2, low)
+        last += pieces
+        y, y_other = panel_product(order, panel_at, [x, x_other], pieces)
+        if i > 0:
+            y, y_other = lax.optimization_barrier((y, y_other, owns[0], others[0]))[:2]
+        own, other = send_back(s, y, y_other)
+        owns, others = [*owns, own], [*others, other]
+
     low_sum, mine, *sends = grads(dp, block_fill, block_tenant_index, x, c, lows, n_dp, blocks, rank)
     for s in range(1, n_dp):
-        mine = mine + shift(sends[s - 1], "dp", n_dp, s).astype(F32)
-    mine = mine + flip(mine.astype(BF16), "pipe", n_pipe, 1).astype(F32)
-    down_out = mine[:, :feat].reshape(pair, rank, feat)
-    up_out = mine[:, feat:].reshape(pair, rank, cols)
-
-    owns, others = [], []
-    for s in range(1, n_t):
-        if planes == 4:
-            pieces = [received[s - 1]] + [flip(received[s - 1], ("groups", "dp"), planes, m) for m in range(1, planes)]
-            y, y_other = panel_product(place, x, x_other, pieces)
-        else:
-            panel = lax.all_gather(received[s - 1], ("groups", "dp"), axis=0, tiled=True)
-            y, y_other = panel_product(jnp.zeros_like(place), x, x_other, [panel])
-        pairs = [
-            (i * n_pipe + p, ((i - s) % n_t) * n_pipe + (p ^ 1)) for i in range(n_t) for p in range(n_pipe)
-        ]
-        owns.append(shift(y, "tensor", n_t, -s))
-        others.append(lax.ppermute(y_other, ("tensor", "pipe"), pairs))
-    base = base_product(at, dp, block_fill, block_tenant_index, x, base_weight, low_sum, b_list, blocks, rank)
+        mine = mine + after(shift(after(sends[s - 1], *last), "dp", n_dp, s), y).astype(F32)
+    down_out, up_out = settle(mine, flip(mine.astype(BF16), "pipe", n_pipe, 1), pair, feat)
+
+    base = base_product(at, dp, block_fill, block_tenant_index, x, base_weight, low_sum, ab_list, blocks, rank)
     out = finish(core, block_fill, base, owns, others, rows, blocks)
     return out, down_out, up_out
 

time: 145 us -> 136 us (0.938)
  the two profiles are of different devices: /device:TPU:13 before, /device:TPU:0 now
where the time goes in v3:
time: 136 us
  waiting for transfers between devices  84.5 us (62%)
  starting transfers between devices  27.2 us (20%)
  Pallas kernels  17.8 us (13%)
  local copies, waits for them, and re-layouts  5.35 us (4%)
    ppermute x8, waiting for transfers between devices, shift(): lax.ppermute(x, name, [(i, (i + step) % count) for i in range(count)])  37.2 us
    ppermute x11, waiting for transfers between devices, flip(): return lax.ppermute(x, names, [(i, i ^ mask) for i in range(count)])  27.3 us
    ppermute x3, waiting for transfers between devices, send_back(): lax.ppermute(y_other, ('tensor', 'pipe'), pairs)  20 us
    ppermute x8, starting transfers between devices, shift(): lax.ppermute(x, name, [(i, (i + step) % count) for i in range(count)])  14.8 us
    ppermute x11, starting transfers between devices, flip(): return lax.ppermute(x, names, [(i, i ^ mask) for i in range(count)])  8.78 us
    unnamed x18, local copies, waits for them, and re-layouts  5.35 us
    pallas_call x4, Pallas kernels, panel_product(): pl.pallas_call(functools.partial(panel_kernel, order, count), in_specs=[S...  3.93 us
    pallas_call x1, Pallas kernels, pack(): pl.pallas_call(functools.partial(pack_kernel, blocks, rows // blocks), gr...  3.79 us
  transfers between devices with their start and end apart: 22, of which 16 were waited for; matrix products, arithmetic and copies ran while one was open for 0% of the time, Pallas kernels for 12%

profile of v3, /device:TPU:0, one launch (start us, length us, event | category | flops | bytes accessed | tf_op | source)
XLA Modules:
  0.0 136.1 jit_solution(3890332315198685519)
XLA Ops:
  0.8 3.4 %copy-done = bf16[8192,512]{1,0:T(8,128)(2,1)S(1)} copy-done((bf16[8192,512]{1,0:T(8,128)(2,1)S(1)}, bf16[8192,512]{1,0:T(8,128)(2,1)}, u32[]{:S(2)}) %copy-start) | copy-done | bytes 8388632
  6.8 4.1 %collective-permute-start.1 = (bf16[512,256]{1,0:T(8,128)(2,1)S(1)}, bf16[512,256]{1,0:T(8,128)(2,1)S(1)}, u32[]{:S(2)}, u32[]{:S(2)}) collective-permute-start(bf16[512,256]{1,0:T(8,128)(2,1)S(1)} %get-tuple-element.32), channel_id=1, source_target_pairs={{0,8},{4,12},{8,0},{12,4},{1,9},{5,13},{9,1},{13,5},{2,10},{6,14},... | collective-permute-start | bytes 786440 | tf_op jit(solution)/shard_map/ppermute | solution.py:29
  10.9 3.8 %pack.1 = (bf16[512,2048]{1,0:T(8,128)(2,1)S(1)}, bf16[512,512]{1,0:T(8,128)(2,1)S(1)}) custom-call(s32[1,6]{1,0:T(1,128)S(1)} %copy-done.5, bf16[768,2048]{1,0:T(8,128)(2,1)S(1)} %copy-done.1, bf16[768,512]{1,0:T(8,128)(2,1)S(1)} %copy-done.2), custom_call_target="tpu_custom_call" | custom-call | flops 1 | bytes 1 | tf_op jit(solution)/shard_map/pack/pallas_call | solution.py:118
  14.7 8.1 %collective-permute-done.1.refs_1_ = bf16[512,256]{1,0:T(8,128)(2,1)S(1)} collective-permute-done((bf16[512,256]{1,0:T(8,128)(2,1)S(1)}, bf16[512,256]{1,0:T(8,128)(2,1)S(1)}, u32[]{:S(2)}, u32[]{:S(2)}) %collective-permute-start.1) | collective-permute-done | bytes 262176 | tf_op jit(solution)/shard_map/ppermute | solution.py:29
  22.8 3.6 %collective-permute-start.3 = (bf16[512,256]{1,0:T(8,128)(2,1)S(1)}, bf16[512,256]{1,0:T(8,128)(2,1)S(1)}, u32[]{:S(2)}, u32[]{:S(2)}) collective-permute-start(bf16[512,256]{1,0:T(8,128)(2,1)S(1)} %get-tuple-element.38), channel_id=1, source_target_pairs={{0,12},{4,0},{8,4},{12,8},{1,13},{5,1},{9,5},{13,9},{2,14},{6,2},{... | collective-permute-start | bytes 786440 | tf_op jit(solution)/shard_map/ppermute | solution.py:29
  27.9 5.2 %collective-permute-done.3 = bf16[512,256]{1,0:T(8,128)(2,1)S(1)} collective-permute-done((bf16[512,256]{1,0:T(8,128)(2,1)S(1)}, bf16[512,256]{1,0:T(8,128)(2,1)S(1)}, u32[]{:S(2)}, u32[]{:S(2)}) %collective-permute-start.3) | collective-permute-done | bytes 262176 | tf_op jit(solution)/shard_map/ppermute | solution.py:29
  33.0 2.4 %collective-permute-start.7 = (bf16[512,256]{1,0:T(8,128)(2,1)S(1)}, bf16[512,256]{1,0:T(8,128)(2,1)S(1)}, u32[]{:S(2)}, u32[]{:S(2)}) collective-permute-start(bf16[512,256]{1,0:T(8,128)(2,1)S(1)} %collective-permute-done.1.refs_1_), channel_id=1, source_target_pairs={{0,18},{2,16},{16,2},{18,0},{1,19},{3,17},{17,3},{19,1},{4,22},{6,... | collective-permute-start | bytes 786440 | tf_op jit(solution)/shard_map/ppermute | solution.py:33
  36.0 3.0 %collective-permute-done.4 = bf16[512,256]{1,0:T(8,128)(2,1)S(1)} collective-permute-done((bf16[512,256]{1,0:T(8,128)(2,1)S(1)}, bf16[512,256]{1,0:T(8,128)(2,1)S(1)}, u32[]{:S(2)}, u32[]{:S(2)}) %collective-permute-start.4) | collective-permute-done | bytes 262176 | tf_op jit(solution)/shard_map/ppermute | solution.py:29
  40.5 10.1 %collective-permute-done.7.refs_4_ = bf16[512,256]{1,0:T(8,128)(2,1)S(1)} collective-permute-done((bf16[512,256]{1,0:T(8,128)(2,1)S(1)}, bf16[512,256]{1,0:T(8,128)(2,1)S(1)}, u32[]{:S(2)}, u32[]{:S(2)}) %collective-permute-start.7) | collective-permute-done | bytes 262176 | tf_op jit(solution)/shard_map/ppermute | solution.py:33
  50.5 3.9 %collective-permute-done.5.refs_2_ = bf16[512,256]{1,0:T(8,128)(2,1)S(1)} collective-permute-done((bf16[512,256]{1,0:T(8,128)(2,1)S(1)}, bf16[512,256]{1,0:T(8,128)(2,1)S(1)}, u32[]{:S(2)}, u32[]{:S(2)}) %collective-permute-start.5) | collective-permute-done | bytes 262176 | tf_op jit(solution)/shard_map/ppermute | solution.py:33
  58.3 2.2 %low_part.1 = bf16[512,128]{1,0:T(8,128)(2,1)S(1)} custom-call(s32[1]{0:T(128)} %bitcast.2.dp_ref, s32[1,6]{1,0:T(1,128)S(1)} %copy-done.5, s32[6]{0:T(128)S(1)} %copy-done.6, bf16[512,2048]{1,0:T(8,128)(2,1)S(1)} %get-tuple-element.37.x_ref.refs_0_, bf16[512,512]{1,0:T(8,128)(2,1)S(1)} %get-tuple-element.35.c_ref, ...), custom_call_target="tpu_custom_call" | custom-call | flops 1 | bytes 1 | tf_op jit(solution)/shard_map/low_part/pallas_call | solution.py:155
  60.5 2.3 %collective-permute-done.11 = bf16[512,256]{1,0:T(8,128)(2,1)S(1)} collective-permute-done((bf16[512,256]{1,0:T(8,128)(2,1)S(1)}, bf16[512,256]{1,0:T(8,128)(2,1)S(1)}, u32[]{:S(2)}, u32[]{:S(2)}) %collective-permute-start.11) | collective-permute-done | bytes 262176 | tf_op jit(solution)/shard_map/ppermute | solution.py:33
  66.6 2.1 %collective-permute-start.9 = (bf16[512,256]{1,0:T(8,128)(2,1)S(1)}, bf16[512,256]{1,0:T(8,128)(2,1)S(1)}, u32[]{:S(2)}, u32[]{:S(2)}) collective-permute-start(bf16[512,256]{1,0:T(8,128)(2,1)S(1)} %panel.4), channel_id=1, source_target_pairs={{0,8},{4,12},{8,0},{12,4},{1,9},{5,13},{9,1},{13,5},{2,10},{6,14},... | collective-permute-start | bytes 786440 | tf_op jit(solution)/shard_map/ppermute | solution.py:29
  69.5 9.3 %collective-permute-done.9.refs_0_ = bf16[512,256]{1,0:T(8,128)(2,1)S(1)} collective-permute-done((bf16[512,256]{1,0:T(8,128)(2,1)S(1)}, bf16[512,256]{1,0:T(8,128)(2,1)S(1)}, u32[]{:S(2)}, u32[]{:S(2)}) %collective-permute-start.9) | collective-permute-done | bytes 262176 | tf_op jit(solution)/shard_map/ppermute | solution.py:29
  78.8 8.4 %collective-permute-done.10.refs_1_ = bf16[512,128]{1,0:T(8,128)(2,1)S(1)} collective-permute-done((bf16[512,128]{1,0:T(8,128)(2,1)S(1)}, bf16[512,128]{1,0:T(8,128)(2,1)S(1)}, u32[]{:S(2)}, u32[]{:S(2)}) %collective-permute-start.10) | collective-permute-done | bytes 131104 | tf_op jit(solution)/shard_map/ppermute | solution.py:33
  91.7 11.7 %collective-permute-done.16.refs_3_ = bf16[512,256]{1,0:T(8,128)(2,1)S(1)} collective-permute-done((bf16[512,256]{1,0:T(8,128)(2,1)S(1)}, bf16[512,256]{1,0:T(8,128)(2,1)S(1)}, u32[]{:S(2)}, u32[]{:S(2)}) %collective-permute-start.16) | collective-permute-done | bytes 262176 | tf_op jit(solution)/shard_map/ppermute | solution.py:367
  103.4 2.1 %collective-permute-done.20 = bf16[128,2560]{1,0:T(8,128)(2,1)S(1)} collective-permute-done((bf16[128,2560]{1,0:T(8,128)(2,1)S(1)}, bf16[128,2560]{1,0:T(8,128)(2,1)S(1)}, u32[]{:S(2)}, u32[]{:S(2)}) %collective-permute-start.20) | collective-permute-done | bytes 655392 | tf_op jit(solution)/shard_map/ppermute | solution.py:29
  107.1 3.6 %collective-permute-start.19 = (bf16[512,256]{1,0:T(8,128)(2,1)S(1)}, bf16[512,256]{1,0:T(8,128)(2,1)S(1)}, u32[]{:S(2)}, u32[]{:S(2)}) collective-permute-start(bf16[512,256]{1,0:T(8,128)(2,1)S(1)} %get-tuple-element.54), channel_id=1, source_target_pairs={{0,13},{1,12},{4,1},{5,0},{8,5},{9,4},{12,9},{13,8},{2,15},{3,14},... | collective-permute-start | bytes 786440 | tf_op jit(solution)/shard_map/ppermute | solution.py:367
  112.6 2.1 %base.1.base_ref = f32[512,512]{1,0:T(8,128)S(1)} custom-call(s32[1]{0:T(128)} %bitcast.1.at_ref, s32[1]{0:T(128)} %bitcast.2.dp_ref, s32[1,6]{1,0:T(1,128)S(1)} %copy-done.5, s32[6]{0:T(128)S(1)} %copy-done.6, bf16[512,2048]{1,0:T(8,128)(2,1)S(1)} %get-tuple-element.37.x_ref.refs_0_, bf16[8192,512]{1,0:T(8,128)(2,1)S(1)} %bitcast.11, ...), custom_call_target="tpu_custom_call" | custom-call | flops 1 | bytes 1 | tf_op jit(solution)/shard_map/base/pallas_call | solution.py:272
  114.7 3.3 %collective-permute-done.13.refs_1_ = bf16[512,256]{1,0:T(8,128)(2,1)S(1)} collective-permute-done((bf16[512,256]{1,0:T(8,128)(2,1)S(1)}, bf16[512,256]{1,0:T(8,128)(2,1)S(1)}, u32[]{:S(2)}, u32[]{:S(2)}) %collective-permute-start.13) | collective-permute-done | bytes 262176 | tf_op jit(solution)/shard_map/ppermute | solution.py:29
  118.1 4.8 %collective-permute-done.18.refs_4_ = bf16[512,256]{1,0:T(8,128)(2,1)S(1)} collective-permute-done((bf16[512,256]{1,0:T(8,128)(2,1)S(1)}, bf16[512,256]{1,0:T(8,128)(2,1)S(1)}, u32[]{:S(2)}, u32[]{:S(2)}) %collective-permute-start.18) | collective-permute-done | bytes 262176 | tf_op jit(solution)/shard_map/ppermute | solution.py:367
  122.9 3.5 %collective-permute-done.19.refs_5_ = bf16[512,256]{1,0:T(8,128)(2,1)S(1)} collective-permute-done((bf16[512,256]{1,0:T(8,128)(2,1)S(1)}, bf16[512,256]{1,0:T(8,128)(2,1)S(1)}, u32[]{:S(2)}, u32[]{:S(2)}) %collective-permute-start.19) | collective-permute-done | bytes 262176 | tf_op jit(solution)/shard_map/ppermute | solution.py:367
  126.4 6.2 %collective-permute-done.17.refs_2_ = bf16[512,256]{1,0:T(8,128)(2,1)S(1)} collective-permute-done((bf16[512,256]{1,0:T(8,128)(2,1)S(1)}, bf16[512,256]{1,0:T(8,128)(2,1)S(1)}, u32[]{:S(2)}, u32[]{:S(2)}) %collective-permute-start.17) | collective-permute-done | bytes 262176 | tf_op jit(solution)/shard_map/ppermute | solution.py:29
  132.6 2.2 %finish.1 = bf16[768,512]{1,0:T(8,128)(2,1)} custom-call(s32[1]{0:T(128)} %bitcast.core_ref, s32[1,6]{1,0:T(1,128)S(1)} %copy-done.5, f32[512,512]{1,0:T(8,128)S(1)} %base.1.base_ref, bf16[512,256]{1,0:T(8,128)(2,1)S(1)} %collective-permute-done.9.refs_0_, bf16[512,256]{1,0:T(8,128)(2,1)S(1)} %collective-permute-done.13.refs_1_, ...), custom_call_target="tpu_custom_call" | custom-call | flops 1 | bytes 1 | tf_op jit(solution)/shard_map/finish/pallas_call | solution.py:314
  (55 shorter events, 23.8 us)
Async XLA Ops:
  6.8 16.0 %collective-permute-start.1 = (bf16[512,256]{1,0:T(8,128)(2,1)S(1)}, bf16[512,256]{1,0:T(8,128)(2,1)S(1)}, u32[]{:S(2)}, u32[]{:S(2)}) collective-permute-start(bf16[512,256]{1,0:T(8,128)(2,1)S(1)} %get-tuple-element.32), channel_id=1, source_target_pairs={{0,8},{4,12},{8,0},{12,4},{1,9},{5,13},{9,1},{13,5},{2,10},{6,14},... | collective-permute-start | bytes 786440 | tf_op jit(solution)/shard_map/ppermute | solution.py:29
  22.8 37.6 %collective-permute-start.2 = (bf16[512,2048]{1,0:T(8,128)(2,1)S(1)}, bf16[512,2048]{1,0:T(8,128)(2,1)S(1)}, u32[]{:S(2)}, u32[]{:S(2)}) collective-permute-start(bf16[512,2048]{1,0:T(8,128)(2,1)S(1)} %get-tuple-element.37.x_ref.refs_0_), channel_id=1, source_target_pairs={{0,1},{1,0},{2,3},{3,2},{4,5},{5,4},{6,7},{7,6},{8,9},{9,8},{10,11... | collective-permute-start | bytes 6291464 | tf_op jit(solution)/shard_map/ppermute | solution.py:33
  22.8 10.2 %collective-permute-start.3 = (bf16[512,256]{1,0:T(8,128)(2,1)S(1)}, bf16[512,256]{1,0:T(8,128)(2,1)S(1)}, u32[]{:S(2)}, u32[]{:S(2)}) collective-permute-start(bf16[512,256]{1,0:T(8,128)(2,1)S(1)} %get-tuple-element.38), channel_id=1, source_target_pairs={{0,12},{4,0},{8,4},{12,8},{1,13},{5,1},{9,5},{13,9},{2,14},{6,2},{... | collective-permute-start | bytes 786440 | tf_op jit(solution)/shard_map/ppermute | solution.py:29
  26.4 12.6 %collective-permute-start.4 = (bf16[512,256]{1,0:T(8,128)(2,1)S(1)}, bf16[512,256]{1,0:T(8,128)(2,1)S(1)}, u32[]{:S(2)}, u32[]{:S(2)}) collective-permute-start(bf16[512,256]{1,0:T(8,128)(2,1)S(1)} %get-tuple-element.39), channel_id=1, source_target_pairs={{0,4},{4,8},{8,12},{12,0},{1,5},{5,9},{9,13},{13,1},{2,6},{6,10},{... | collective-permute-start | bytes 786440 | tf_op jit(solution)/shard_map/ppermute | solution.py:29
  26.4 31.9 %collective-permute-start = (bf16[128,2560]{1,0:T(8,128)(2,1)S(1)}, bf16[128,2560]{1,0:T(8,128)(2,1)S(1)}, u32[]{:S(2)}, u32[]{:S(2)}) collective-permute-start(bf16[128,2560]{1,0:T(8,128)(2,1)S(1)} %get-tuple-element.36.refs_0_), channel_id=1, source_target_pairs={{0,2},{2,0},{1,3},{3,1},{4,6},{6,4},{5,7},{7,5},{8,10},{10,8},{9,1... | collective-permute-start | bytes 1966088 | tf_op jit(solution)/shard_map/ppermute | solution.py:29
  33.0 17.5 %collective-permute-start.7 = (bf16[512,256]{1,0:T(8,128)(2,1)S(1)}, bf16[512,256]{1,0:T(8,128)(2,1)S(1)}, u32[]{:S(2)}, u32[]{:S(2)}) collective-permute-start(bf16[512,256]{1,0:T(8,128)(2,1)S(1)} %collective-permute-done.1.refs_1_), channel_id=1, source_target_pairs={{0,18},{2,16},{16,2},{18,0},{1,19},{3,17},{17,3},{19,1},{4,22},{6,... | collective-permute-start | bytes 786440 | tf_op jit(solution)/shard_map/ppermute | solution.py:33
  35.5 15.0 %collective-permute-start.6 = (bf16[512,256]{1,0:T(8,128)(2,1)S(1)}, bf16[512,256]{1,0:T(8,128)(2,1)S(1)}, u32[]{:S(2)}, u32[]{:S(2)}) collective-permute-start(bf16[512,256]{1,0:T(8,128)(2,1)S(1)} %collective-permute-done.1.refs_1_), channel_id=1, source_target_pairs={{0,16},{2,18},{16,0},{18,2},{1,17},{3,19},{17,1},{19,3},{4,20},{6,... | collective-permute-start | bytes 786440 | tf_op jit(solution)/shard_map/ppermute | solution.py:33
  39.0 15.5 %collective-permute-start.5 = (bf16[512,256]{1,0:T(8,128)(2,1)S(1)}, bf16[512,256]{1,0:T(8,128)(2,1)S(1)}, u32[]{:S(2)}, u32[]{:S(2)}) collective-permute-start(bf16[512,256]{1,0:T(8,128)(2,1)S(1)} %collective-permute-done.1.refs_1_), channel_id=1, source_target_pairs={{0,2},{2,0},{16,18},{18,16},{1,3},{3,1},{17,19},{19,17},{4,6},{6,4... | collective-permute-start | bytes 786440 | tf_op jit(solution)/shard_map/ppermute | solution.py:33
  55.2 7.7 %collective-permute-start.11 = (bf16[512,256]{1,0:T(8,128)(2,1)S(1)}, bf16[512,256]{1,0:T(8,128)(2,1)S(1)}, u32[]{:S(2)}, u32[]{:S(2)}) collective-permute-start(bf16[512,256]{1,0:T(8,128)(2,1)S(1)} %collective-permute-done.3), channel_id=1, source_target_pairs={{0,2},{2,0},{16,18},{18,16},{1,3},{3,1},{17,19},{19,17},{4,6},{6,4... | collective-permute-start | bytes 786440 | tf_op jit(solution)/shard_map/ppermute | solution.py:33
  56.8 7.3 %collective-permute-start.14 = (bf16[512,256]{1,0:T(8,128)(2,1)S(1)}, bf16[512,256]{1,0:T(8,128)(2,1)S(1)}, u32[]{:S(2)}, u32[]{:S(2)}) collective-permute-start(bf16[512,256]{1,0:T(8,128)(2,1)S(1)} %collective-permute-done.4), channel_id=1, source_target_pairs={{0,16},{2,18},{16,0},{18,2},{1,17},{3,19},{17,1},{19,3},{4,20},{6,... | collective-permute-start | bytes 786440 | tf_op jit(solution)/shard_map/ppermute | solution.py:33
  60.5 5.0 %collective-permute-start.8 = (bf16[512,128]{1,0:T(8,128)(2,1)S(1)}, bf16[512,128]{1,0:T(8,128)(2,1)S(1)}, u32[]{:S(2)}, u32[]{:S(2)}) collective-permute-start(bf16[512,128]{1,0:T(8,128)(2,1)S(1)} %low_part.1), channel_id=1, source_target_pairs={{0,4},{4,0},{8,12},{12,8},{1,5},{5,1},{9,13},{13,9},{2,6},{6,2},{1... | collective-permute-start | bytes 393224 | tf_op jit(solution)/shard_map/ppermute | solution.py:33
  65.5 23.3 %collective-permute-start.12 = (bf16[1024,256]{1,0:T(8,128)(2,1)S(1)}, bf16[1024,256]{1,0:T(8,128)(2,1)S(1)}, u32[]{:S(2)}, u32[]{:S(2)}) collective-permute-start(bf16[1024,256]{1,0:T(8,128)(2,1)S(1)} %pad_maximum_fusion.refs_2_), channel_id=1, source_target_pairs={{0,16},{2,18},{16,0},{18,2},{1,17},{3,19},{17,1},{19,3},{4,20},{6,... | collective-permute-start | bytes 1572872 | tf_op jit(solution)/shard_map/ppermute | solution.py:33
  66.1 22.8 %collective-permute-start.15 = (bf16[1024,256]{1,0:T(8,128)(2,1)S(1)}, bf16[1024,256]{1,0:T(8,128)(2,1)S(1)}, u32[]{:S(2)}, u32[]{:S(2)}) collective-permute-start(bf16[1024,256]{1,0:T(8,128)(2,1)S(1)} %pad_maximum_fusion.1.refs_2_), channel_id=1, source_target_pairs={{0,2},{2,0},{16,18},{18,16},{1,3},{3,1},{17,19},{19,17},{4,6},{6,4... | collective-permute-start | bytes 1572872 | tf_op jit(solution)/shard_map/ppermute | solution.py:33
  66.6 12.2 %collective-permute-start.9 = (bf16[512,256]{1,0:T(8,128)(2,1)S(1)}, bf16[512,256]{1,0:T(8,128)(2,1)S(1)}, u32[]{:S(2)}, u32[]{:S(2)}) collective-permute-start(bf16[512,256]{1,0:T(8,128)(2,1)S(1)} %panel.4), channel_id=1, source_target_pairs={{0,8},{4,12},{8,0},{12,4},{1,9},{5,13},{9,1},{13,5},{2,10},{6,14},... | collective-permute-start | bytes 786440 | tf_op jit(solution)/shard_map/ppermute | solution.py:29
  78.8 8.4 %collective-permute-start.10 = (bf16[512,128]{1,0:T(8,128)(2,1)S(1)}, bf16[512,128]{1,0:T(8,128)(2,1)S(1)}, u32[]{:S(2)}, u32[]{:S(2)}) collective-permute-start(bf16[512,128]{1,0:T(8,128)(2,1)S(1)} %add_convert_fusion.refs_0_), channel_id=1, source_target_pairs={{0,8},{4,12},{8,0},{12,4},{1,9},{5,13},{9,1},{13,5},{2,10},{6,14},... | collective-permute-start | bytes 393224 | tf_op jit(solution)/shard_map/ppermute | solution.py:33
  87.2 25.4 %slice-start = ((s8[8388608]{0:T(1024)(128)(4,1)}), s8[4194304]{0:T(1024)(128)(4,1)S(1)}, s32[]{:S(2)}) async-start(s8[8388608]{0:T(1024)(128)(4,1)} %bitcast.10), calls=%async_computation | async-start | bytes 8388608
  88.9 16.6 %collective-permute-start.20 = (bf16[128,2560]{1,0:T(8,128)(2,1)S(1)}, bf16[128,2560]{1,0:T(8,128)(2,1)S(1)}, u32[]{:S(2)}, u32[]{:S(2)}) collective-permute-start(bf16[128,2560]{1,0:T(8,128)(2,1)S(1)} %get-tuple-element.57), channel_id=1, source_target_pairs={{0,2},{2,0},{1,3},{3,1},{4,6},{6,4},{5,7},{7,5},{8,10},{10,8},{9,1... | collective-permute-start | bytes 1966088 | tf_op jit(solution)/shard_map/ppermute | solution.py:29
  90.5 12.9 %collective-permute-start.16 = (bf16[512,256]{1,0:T(8,128)(2,1)S(1)}, bf16[512,256]{1,0:T(8,128)(2,1)S(1)}, u32[]{:S(2)}, u32[]{:S(2)}) collective-permute-start(bf16[512,256]{1,0:T(8,128)(2,1)S(1)} %panel.5), channel_id=1, source_target_pairs={{0,9},{1,8},{4,13},{5,12},{8,1},{9,0},{12,5},{13,4},{2,11},{3,10},... | collective-permute-start | bytes 786440 | tf_op jit(solution)/shard_map/ppermute | solution.py:367
  105.5 7.2 %slice-start.1 = ((s8[8388608]{0:T(1024)(128)(4,1)}), s8[4194304]{0:T(1024)(128)(4,1)S(1)}, s32[]{:S(2)}) async-start(s8[8388608]{0:T(1024)(128)(4,1)} %bitcast.10), calls=%async_computation.1 | async-start | bytes 8388608
  105.6 29.2 %collective-permute-start.21 = (bf16[128,2560]{1,0:T(8,128)(2,1)S(1)}, bf16[128,2560]{1,0:T(8,128)(2,1)S(1)}, u32[]{:S(2)}, u32[]{:S(2)}) collective-permute-start(bf16[128,2560]{1,0:T(8,128)(2,1)S(1)} %get-tuple-element.61), channel_id=1, source_target_pairs={{0,1},{1,0},{2,3},{3,2},{4,5},{5,4},{6,7},{7,6},{8,9},{9,8},{10,11... | collective-permute-start | bytes 1966088 | tf_op jit(solution)/shard_map/ppermute | solution.py:33
  107.0 11.1 %collective-permute-start.13 = (bf16[512,256]{1,0:T(8,128)(2,1)S(1)}, bf16[512,256]{1,0:T(8,128)(2,1)S(1)}, u32[]{:S(2)}, u32[]{:S(2)}) collective-permute-start(bf16[512,256]{1,0:T(8,128)(2,1)S(1)} %get-tuple-element.48), channel_id=1, source_target_pairs={{0,4},{4,8},{8,12},{12,0},{1,5},{5,9},{9,13},{13,1},{2,6},{6,10},{... | collective-permute-start | bytes 786440 | tf_op jit(solution)/shard_map/ppermute | solution.py:29
  107.0 15.9 %collective-permute-start.18 = (bf16[512,256]{1,0:T(8,128)(2,1)S(1)}, bf16[512,256]{1,0:T(8,128)(2,1)S(1)}, u32[]{:S(2)}, u32[]{:S(2)}) collective-permute-start(bf16[512,256]{1,0:T(8,128)(2,1)S(1)} %get-tuple-element.53), channel_id=1, source_target_pairs={{0,5},{1,4},{4,9},{5,8},{8,13},{9,12},{12,1},{13,0},{2,7},{3,6},{6... | collective-permute-start | bytes 786440 | tf_op jit(solution)/shard_map/ppermute | solution.py:367
  107.1 19.3 %collective-permute-start.19 = (bf16[512,256]{1,0:T(8,128)(2,1)S(1)}, bf16[512,256]{1,0:T(8,128)(2,1)S(1)}, u32[]{:S(2)}, u32[]{:S(2)}) collective-permute-start(bf16[512,256]{1,0:T(8,128)(2,1)S(1)} %get-tuple-element.54), channel_id=1, source_target_pairs={{0,13},{1,12},{4,1},{5,0},{8,5},{9,4},{12,9},{13,8},{2,15},{3,14},... | collective-permute-start | bytes 786440 | tf_op jit(solution)/shard_map/ppermute | solution.py:367
  110.7 21.9 %collective-permute-start.17 = (bf16[512,256]{1,0:T(8,128)(2,1)S(1)}, bf16[512,256]{1,0:T(8,128)(2,1)S(1)}, u32[]{:S(2)}, u32[]{:S(2)}) collective-permute-start(bf16[512,256]{1,0:T(8,128)(2,1)S(1)} %get-tuple-element.52), channel_id=1, source_target_pairs={{0,12},{4,0},{8,4},{12,8},{1,13},{5,1},{9,5},{13,9},{2,14},{6,2},{... | collective-permute-start | bytes 786440 | tf_op jit(solution)/shard_map/ppermute | solution.py:29
  (7 other events, 23.6 us)

commit v4 on v3

--- a/solution.py
+++ b/solution.py
@@ -90,7 +90,7 @@
         out_specs=[VMEM] * (count + 1),
         out_shape=shapes,
         scratch_shapes=[pltpu.SemaphoreType.DMA((count + 2,))],
-        compiler_params=params(8),
+        compiler_params=params(56),
         cost_estimate=cost(0, 4 * (count * deep * half + shapes[-1].size)),
         name="shares",
     )(jnp.stack([*rows_at, col_at]).astype(I32), base_weight, a, b)
@@ -352,14 +352,12 @@
     for s in rest:
         received[s] = shift(shares[s], "tensor", n_t, s)
 
-    def gathered(piece, first, low=None):
+    def gathered(piece, first):
         if planes != 4:
             return [lax.all_gather(piece, ("groups", "dp"), axis=0, tiled=True)], [0]
         if first is None:
-            near = [flip(piece, ("groups", "dp"), planes, m) for m in (1, 2)]
-            return [piece, *near, flip(after(piece, received[rest[0]]), ("groups", "dp"), planes, 3)], [0, 1, 2, 3]
+            return [piece] + [flip(piece, ("groups", "dp"), planes, m) for m in range(1, 4)], [0, 1, 2, 3]
         stack = jnp.concatenate([piece, flip(piece, ("groups", "dp"), planes, first)], axis=0)
-        stack = after(stack, low)
         return [stack, flip(stack, ("groups", "dp"), planes, 3 - first)], [0, first, 3 - first, 3]
 
     def send_back(s, y, y_other):
@@ -369,35 +367,31 @@
     low = low_part(dp, block_fill, block_tenant_index, x, c, ab_list, blocks, rank)
     panel_at = place if planes == 4 else jnp.zeros_like(place)
     pieces, order = gathered(received[lead], None)
-    x_other = flip(after(x, received[lead]), "pipe", n_pipe, 1)
-    pieces = [after(pieces[0], *[received[s] for s in rest]), *pieces[1:]]
+    x_other = flip(after(x, *pieces, *received.values(), *ab_list[1:]), "pipe", n_pipe, 1)
     (y,) = panel_product(order, panel_at, [x], pieces)
     received.update((s, after(received[s], y)) for s in rest)
     (y_other,) = panel_product(order, panel_at, [x_other], pieces)
     owns, others = zip(send_back(lead, y, y_other))
 
-    low = after(low, x_other, y, *[received[s] for s in rest])
+    low = after(low, owns[0], y_other)
     mask = 1
     while 2 * mask < n_t:
         low = (low.astype(F32) + flip(low, "tensor", n_t, mask).astype(F32)).astype(BF16)
         mask *= 2
-    final_low = after(low, owns[0], y_other)
-    lows = [final_low] + ([flip(final_low, "tensor", n_t, mask)] if n_t > 1 else [])
+    lows = [low] + ([flip(low, "tensor", n_t, mask)] if n_t > 1 else [])
 
     last = []
     for i, s in enumerate(rest):
-        pieces, order = gathered(received[s], 1 + i % 2, low)
-        last += pieces
+        pieces, order = gathered(received[s], 1 + i % 2)
         y, y_other = panel_product(order, panel_at, [x, x_other], pieces)
-        if i > 0:
-            y, y_other = lax.optimization_barrier((y, y_other, owns[0], others[0]))[:2]
+        last += [y, y_other]
         own, other = send_back(s, y, y_other)
         owns, others = [*owns, own], [*others, other]
 
     low_sum, mine, *sends = grads(dp, block_fill, block_tenant_index, x, c, lows, n_dp, blocks, rank)
     for s in range(1, n_dp):
-        mine = mine + after(shift(after(sends[s - 1], *last), "dp", n_dp, s), y).astype(F32)
-    down_out, up_out = settle(mine, flip(mine.astype(BF16), "pipe", n_pipe, 1), pair, feat)
+        mine = mine + shift(after(sends[s - 1], *last, others[0]), "dp", n_dp, s).astype(F32)
+    down_out, up_out = settle(mine, flip(after(mine.astype(BF16), *owns[1:], others[1]), "pipe", n_pipe, 1), pair, feat)
 
     base = base_product(at, dp, block_fill, block_tenant_index, x, base_weight, low_sum, ab_list, blocks, rank)
     out = finish(core, block_fill, base, owns, others, rows, blocks)

time: 136 us -> 115 us (0.85)
  waiting for transfers between devices: 84.5 us -> 67.7 us
  local copies, waits for them, and re-layouts: 5.35 us -> 0.11 us
  Pallas kernels: 17.8 us -> 20.7 us
  starting transfers between devices: 27.2 us -> 25 us
    ppermute x3, waiting for transfers between devices: 20 us -> 5.77 us  [send_back(): lax.ppermute(y_other, ('tensor', 'pipe'), pairs)]
    unnamed x18 -> x16, local copies, waits for them, and re-layouts: 5.35 us -> 0.07 us
    ppermute x3, starting transfers between devices: 3.64 us -> 0.2 us  [send_back(): lax.ppermute(y_other, ('tensor', 'pipe'), pairs)]
    pallas_call x1, Pallas kernels: 0.71 us -> 3.63 us  [shares_of(): pl.pallas_call(functools.partial(shares_kernel, count), in_specs=[SMEM] +...]
    ppermute x8, waiting for transfers between devices: 37.2 us -> 35.6 us  [shift(): lax.ppermute(x, name, [(i, (i + step) % count) for i in range(count)])]
    ppermute x8, starting transfers between devices: 14.8 us -> 16.4 us  [shift(): lax.ppermute(x, name, [(i, (i + step) % count) for i in range(count)])]
  transfers between devices with their start and end apart: 22 -> 22, of which waited for: 16 -> 11; matrix products, arithmetic and copies ran while one was open for 0% -> 0% of each run, Pallas kernels for 12% -> 14%
where the time goes in v4:
time: 115 us
  waiting for transfers between devices  67.7 us (59%)
  starting transfers between devices  25 us (22%)
  Pallas kernels  20.7 us (18%)
    ppermute x8, waiting for transfers between devices, shift(): lax.ppermute(x, name, [(i, (i + step) % count) for i in range(count)])  35.6 us
    ppermute x11, waiting for transfers between devices, flip(): return lax.ppermute(x, names, [(i, i ^ mask) for i in range(count)])  26.3 us
    ppermute x8, starting transfers between devices, shift(): lax.ppermute(x, name, [(i, (i + step) % count) for i in range(count)])  16.4 us
    ppermute x11, starting transfers between devices, flip(): return lax.ppermute(x, names, [(i, i ^ mask) for i in range(count)])  8.4 us
    ppermute x3, waiting for transfers between devices, send_back(): lax.ppermute(y_other, ('tensor', 'pipe'), pairs)  5.77 us
    pallas_call x4, Pallas kernels, panel_product(): pl.pallas_call(functools.partial(panel_kernel, order, count), in_specs=[S...  3.94 us
    pallas_call x1, Pallas kernels, pack(): pl.pallas_call(functools.partial(pack_kernel, blocks, rows // blocks), gr...  3.79 us
    pallas_call x1, Pallas kernels, shares_of(): pl.pallas_call(functools.partial(shares_kernel, count), in_specs=[SMEM] +...  3.63 us
  transfers between devices with their start and end apart: 22, of which 11 were waited for; matrix products, arithmetic and copies ran while one was open for 0% of the time, Pallas kernels for 14%

profile of v4, /device:TPU:0, one launch (start us, length us, event | category | flops | bytes accessed | tf_op | source)
XLA Modules:
  0.0 115.2 jit_solution(6862378248987519)
XLA Ops:
  1.3 3.6 %shares.1 = (bf16[512,256]{1,0:T(8,128)(2,1)}, bf16[512,256]{1,0:T(8,128)(2,1)}, bf16[512,256]{1,0:T(8,128)(2,1)}, bf16[128,2560]{1,0:T(8,128)(2,1)}) custom-call(s32[4]{0:T(128)} %pad_add_fusion.at_ref, bf16[8192,512]{1,0:T(8,128)(2,1)} %w_ref.3, bf16[128,2048]{1,0:T(8,128)(2,1)} %bitcast.12, bf16[128,512]{1,0:T(8,128)(2,1)} %bitcast.13), custom_call_target="tpu_custom_call" | custom-call | flops 1 | bytes 1 | tf_op jit(solution)/shard_map/shares/pallas_call | solution.py:87
  5.0 3.0 %collective-permute-start = (bf16[128,2560]{1,0:T(8,128)(2,1)}, bf16[128,2560]{1,0:T(8,128)(2,1)S(1)}, u32[]{:S(2)}, u32[]{:S(2)}) collective-permute-start(bf16[128,2560]{1,0:T(8,128)(2,1)} %get-tuple-element.29.refs_0_), channel_id=1, source_target_pairs={{0,2},{2,0},{1,3},{3,1},{4,6},{6,4},{5,7},{7,5},{8,10},{10,8},{9,1... | collective-permute-start | bytes 1966088 | tf_op jit(solution)/shard_map/ppermute | solution.py:29
  8.0 2.6 %collective-permute-start.1 = (bf16[512,256]{1,0:T(8,128)(2,1)}, bf16[512,256]{1,0:T(8,128)(2,1)S(1)}, u32[]{:S(2)}, u32[]{:S(2)}) collective-permute-start(bf16[512,256]{1,0:T(8,128)(2,1)} %get-tuple-element.25), channel_id=1, source_target_pairs={{0,8},{4,12},{8,0},{12,4},{1,9},{5,13},{9,1},{13,5},{2,10},{6,14},... | collective-permute-start | bytes 786440 | tf_op jit(solution)/shard_map/ppermute | solution.py:29
  10.6 1.6 %collective-permute-start.7 = (bf16[512,256]{1,0:T(8,128)(2,1)}, bf16[512,256]{1,0:T(8,128)(2,1)S(1)}, u32[]{:S(2)}, u32[]{:S(2)}) collective-permute-start(bf16[512,256]{1,0:T(8,128)(2,1)} %get-tuple-element.31), channel_id=1, source_target_pairs={{0,4},{4,8},{8,12},{12,0},{1,5},{5,9},{9,13},{13,1},{2,6},{6,10},{... | collective-permute-start | bytes 786440 | tf_op jit(solution)/shard_map/ppermute | solution.py:29
  12.1 2.2 %collective-permute-start.6 = (bf16[512,256]{1,0:T(8,128)(2,1)}, bf16[512,256]{1,0:T(8,128)(2,1)S(1)}, u32[]{:S(2)}, u32[]{:S(2)}) collective-permute-start(bf16[512,256]{1,0:T(8,128)(2,1)} %get-tuple-element.30), channel_id=1, source_target_pairs={{0,12},{4,0},{8,4},{12,8},{1,13},{5,1},{9,5},{13,9},{2,14},{6,2},{... | collective-permute-start | bytes 786440 | tf_op jit(solution)/shard_map/ppermute | solution.py:29
  14.4 14.9 %collective-permute-done.1.refs_1_ = bf16[512,256]{1,0:T(8,128)(2,1)S(1)} collective-permute-done((bf16[512,256]{1,0:T(8,128)(2,1)}, bf16[512,256]{1,0:T(8,128)(2,1)S(1)}, u32[]{:S(2)}, u32[]{:S(2)}) %collective-permute-start.1) | collective-permute-done | bytes 262176 | tf_op jit(solution)/shard_map/ppermute | solution.py:29
  29.7 1.6 %collective-permute-start.3 = (bf16[512,256]{1,0:T(8,128)(2,1)S(1)}, bf16[512,256]{1,0:T(8,128)(2,1)S(1)}, u32[]{:S(2)}, u32[]{:S(2)}) collective-permute-start(bf16[512,256]{1,0:T(8,128)(2,1)S(1)} %collective-permute-done.1.refs_1_), channel_id=1, source_target_pairs={{0,16},{2,18},{16,0},{18,2},{1,17},{3,19},{17,1},{19,3},{4,20},{6,... | collective-permute-start | bytes 786440 | tf_op jit(solution)/shard_map/ppermute | solution.py:33
  32.8 3.8 %pack.1 = (bf16[512,2048]{1,0:T(8,128)(2,1)S(1)}, bf16[512,512]{1,0:T(8,128)(2,1)S(1)}) custom-call(s32[1,6]{1,0:T(1,128)S(1)} %copy-done.3, bf16[768,2048]{1,0:T(8,128)(2,1)S(1)} %copy-done, bf16[768,512]{1,0:T(8,128)(2,1)S(1)} %copy-done.2), custom_call_target="tpu_custom_call" | custom-call | flops 1 | bytes 1 | tf_op jit(solution)/shard_map/pack/pallas_call | solution.py:118
  38.1 2.1 %collective-permute-done.3.refs_3_ = bf16[512,256]{1,0:T(8,128)(2,1)S(1)} collective-permute-done((bf16[512,256]{1,0:T(8,128)(2,1)S(1)}, bf16[512,256]{1,0:T(8,128)(2,1)S(1)}, u32[]{:S(2)}, u32[]{:S(2)}) %collective-permute-start.3) | collective-permute-done | bytes 262176 | tf_op jit(solution)/shard_map/ppermute | solution.py:33
  40.2 1.6 %collective-permute-done.4.refs_4_ = bf16[512,256]{1,0:T(8,128)(2,1)S(1)} collective-permute-done((bf16[512,256]{1,0:T(8,128)(2,1)S(1)}, bf16[512,256]{1,0:T(8,128)(2,1)S(1)}, u32[]{:S(2)}, u32[]{:S(2)}) %collective-permute-start.4) | collective-permute-done | bytes 262176 | tf_op jit(solution)/shard_map/ppermute | solution.py:33
  45.0 3.4 %collective-permute-start.5 = (bf16[512,256]{1,0:T(8,128)(2,1)S(1)}, bf16[512,256]{1,0:T(8,128)(2,1)S(1)}, u32[]{:S(2)}, u32[]{:S(2)}) collective-permute-start(bf16[512,256]{1,0:T(8,128)(2,1)S(1)} %panel.4), channel_id=1, source_target_pairs={{0,8},{4,12},{8,0},{12,4},{1,9},{5,13},{9,1},{13,5},{2,10},{6,14},... | collective-permute-start | bytes 786440 | tf_op jit(solution)/shard_map/ppermute | solution.py:29
  48.4 3.0 %collective-permute-done.14 = bf16[512,256]{1,0:T(8,128)(2,1)S(1)} collective-permute-done((bf16[512,256]{1,0:T(8,128)(2,1)S(1)}, bf16[512,256]{1,0:T(8,128)(2,1)S(1)}, u32[]{:S(2)}, u32[]{:S(2)}) %collective-permute-start.14) | collective-permute-done | bytes 262176 | tf_op jit(solution)/shard_map/ppermute | solution.py:33
  52.3 1.6 %collective-permute-start.12 = (bf16[1024,256]{1,0:T(8,128)(2,1)S(1)}, bf16[1024,256]{1,0:T(8,128)(2,1)S(1)}, u32[]{:S(2)}, u32[]{:S(2)}) collective-permute-start(bf16[1024,256]{1,0:T(8,128)(2,1)S(1)} %constant_dynamic-update-slice_fusion.refs_2_), channel_id=1, source_target_pairs={{0,16},{2,18},{16,0},{18,2},{1,17},{3,19},{17,1},{19,3},{4,20},{6,... | collective-permute-start | bytes 1572872 | tf_op jit(solution)/shard_map/ppermute | solution.py:33
  53.9 2.2 %low_part.1 = bf16[512,128]{1,0:T(8,128)(2,1)S(1)} custom-call(s32[1]{0:T(128)} %bitcast.2.dp_ref, s32[1,6]{1,0:T(1,128)S(1)} %copy-done.3, s32[6]{0:T(128)S(1)} %copy-done.4, bf16[512,2048]{1,0:T(8,128)(2,1)S(1)} %get-tuple-element.32.x_ref.refs_0_, bf16[512,512]{1,0:T(8,128)(2,1)S(1)} %get-tuple-element.28.c_ref, bf16[128,2560]{1,0:T(8,128)(2,1)S(1)} %copy-done.1, ...), custom_call_target="tpu_custom_call" | custom-call | flops 1 | bytes 1 | tf_op jit(solution)/shard_map/low_part/pallas_call | solution.py:155
  56.8 3.6 %collective-permute-done.5.refs_0_ = bf16[512,256]{1,0:T(8,128)(2,1)S(1)} collective-permute-done((bf16[512,256]{1,0:T(8,128)(2,1)S(1)}, bf16[512,256]{1,0:T(8,128)(2,1)S(1)}, u32[]{:S(2)}, u32[]{:S(2)}) %collective-permute-start.5) | collective-permute-done | bytes 262176 | tf_op jit(solution)/shard_map/ppermute | solution.py:29
  60.4 6.4 %collective-permute-done.9 = bf16[512,128]{1,0:T(8,128)(2,1)S(1)} collective-permute-done((bf16[512,128]{1,0:T(8,128)(2,1)S(1)}, bf16[512,128]{1,0:T(8,128)(2,1)S(1)}, u32[]{:S(2)}, u32[]{:S(2)}) %collective-permute-start.9) | collective-permute-done | bytes 131104 | tf_op jit(solution)/shard_map/ppermute | solution.py:33
  69.5 11.6 %collective-permute-done.10.refs_1_ = bf16[512,128]{1,0:T(8,128)(2,1)S(1)} collective-permute-done((bf16[512,128]{1,0:T(8,128)(2,1)S(1)}, bf16[512,128]{1,0:T(8,128)(2,1)S(1)}, u32[]{:S(2)}, u32[]{:S(2)}) %collective-permute-start.10) | collective-permute-done | bytes 131104 | tf_op jit(solution)/shard_map/ppermute | solution.py:33
  81.1 1.7 %grads.1 = (bf16[512,128]{1,0:T(8,128)(2,1)S(1)}, f32[128,2560]{1,0:T(8,128)S(1)}, bf16[128,2560]{1,0:T(8,128)(2,1)S(1)}) custom-call(s32[1]{0:T(128)} %bitcast.2.dp_ref, s32[1,6]{1,0:T(1,128)S(1)} %copy-done.3, s32[6]{0:T(128)S(1)} %copy-done.4, bf16[512,2048]{1,0:T(8,128)(2,1)S(1)} %get-tuple-element.32.x_ref.refs_0_, ...), custom_call_target="tpu_custom_call" | custom-call | flops 1 | bytes 1 | tf_op jit(solution)/shard_map/grads/pallas_call | solution.py:195
  82.8 1.6 %collective-permute-start.20 = (bf16[128,2560]{1,0:T(8,128)(2,1)S(1)}, bf16[128,2560]{1,0:T(8,128)(2,1)S(1)}, u32[]{:S(2)}, u32[]{:S(2)}) collective-permute-start(bf16[128,2560]{1,0:T(8,128)(2,1)S(1)} %get-tuple-element.43), channel_id=1, source_target_pairs={{0,2},{2,0},{1,3},{3,1},{4,6},{6,4},{5,7},{7,5},{8,10},{10,8},{9,1... | collective-permute-start | bytes 1966088 | tf_op jit(solution)/shard_map/ppermute | solution.py:29
  86.4 13.2 %collective-permute-done.20 = bf16[128,2560]{1,0:T(8,128)(2,1)S(1)} collective-permute-done((bf16[128,2560]{1,0:T(8,128)(2,1)S(1)}, bf16[128,2560]{1,0:T(8,128)(2,1)S(1)}, u32[]{:S(2)}, u32[]{:S(2)}) %collective-permute-start.20) | collective-permute-done | bytes 655392 | tf_op jit(solution)/shard_map/ppermute | solution.py:29
  99.8 3.8 %collective-permute-done.16.refs_2_ = bf16[512,256]{1,0:T(8,128)(2,1)S(1)} collective-permute-done((bf16[512,256]{1,0:T(8,128)(2,1)S(1)}, bf16[512,256]{1,0:T(8,128)(2,1)S(1)}, u32[]{:S(2)}, u32[]{:S(2)}) %collective-permute-start.16) | collective-permute-done | bytes 262176 | tf_op jit(solution)/shard_map/ppermute | solution.py:29
  103.9 2.1 %base.1.base_ref = f32[512,512]{1,0:T(8,128)S(1)} custom-call(s32[1]{0:T(128)} %bitcast.1.at_ref, s32[1]{0:T(128)} %bitcast.2.dp_ref, s32[1,6]{1,0:T(1,128)S(1)} %copy-done.3, s32[6]{0:T(128)S(1)} %copy-done.4, bf16[512,2048]{1,0:T(8,128)(2,1)S(1)} %get-tuple-element.32.x_ref.refs_0_, bf16[8192,512]{1,0:T(8,128)(2,1)S(1)} %bitcast.11, ...), custom_call_target="tpu_custom_call" | custom-call | flops 1 | bytes 1 | tf_op jit(solution)/shard_map/base/pallas_call | solution.py:272
  106.0 5.8 %collective-permute-done.19.refs_5_ = bf16[512,256]{1,0:T(8,128)(2,1)S(1)} collective-permute-done((bf16[512,256]{1,0:T(8,128)(2,1)S(1)}, bf16[512,256]{1,0:T(8,128)(2,1)S(1)}, u32[]{:S(2)}, u32[]{:S(2)}) %collective-permute-start.19) | collective-permute-done | bytes 262176 | tf_op jit(solution)/shard_map/ppermute | solution.py:365
  111.8 2.2 %finish.1 = bf16[768,512]{1,0:T(8,128)(2,1)} custom-call(s32[1]{0:T(128)} %bitcast.core_ref, s32[1,6]{1,0:T(1,128)S(1)} %copy-done.3, f32[512,512]{1,0:T(8,128)S(1)} %base.1.base_ref, bf16[512,256]{1,0:T(8,128)(2,1)S(1)} %collective-permute-done.5.refs_0_, bf16[512,256]{1,0:T(8,128)(2,1)S(1)} %collective-permute-done.13.refs_1_, ...), custom_call_target="tpu_custom_call" | custom-call | flops 1 | bytes 1 | tf_op jit(solution)/shard_map/finish/pallas_call | solution.py:314
  (53 shorter events, 15.1 us)
Async XLA Ops:
  5.0 36.9 %collective-permute-start = (bf16[128,2560]{1,0:T(8,128)(2,1)}, bf16[128,2560]{1,0:T(8,128)(2,1)S(1)}, u32[]{:S(2)}, u32[]{:S(2)}) collective-permute-start(bf16[128,2560]{1,0:T(8,128)(2,1)} %get-tuple-element.29.refs_0_), channel_id=1, source_target_pairs={{0,2},{2,0},{1,3},{3,1},{4,6},{6,4},{5,7},{7,5},{8,10},{10,8},{9,1... | collective-permute-start | bytes 1966088 | tf_op jit(solution)/shard_map/ppermute | solution.py:29
  8.0 21.3 %collective-permute-start.1 = (bf16[512,256]{1,0:T(8,128)(2,1)}, bf16[512,256]{1,0:T(8,128)(2,1)S(1)}, u32[]{:S(2)}, u32[]{:S(2)}) collective-permute-start(bf16[512,256]{1,0:T(8,128)(2,1)} %get-tuple-element.25), channel_id=1, source_target_pairs={{0,8},{4,12},{8,0},{12,4},{1,9},{5,13},{9,1},{13,5},{2,10},{6,14},... | collective-permute-start | bytes 786440 | tf_op jit(solution)/shard_map/ppermute | solution.py:29
  10.6 20.8 %collective-permute-start.7 = (bf16[512,256]{1,0:T(8,128)(2,1)}, bf16[512,256]{1,0:T(8,128)(2,1)S(1)}, u32[]{:S(2)}, u32[]{:S(2)}) collective-permute-start(bf16[512,256]{1,0:T(8,128)(2,1)} %get-tuple-element.31), channel_id=1, source_target_pairs={{0,4},{4,8},{8,12},{12,0},{1,5},{5,9},{9,13},{13,1},{2,6},{6,10},{... | collective-permute-start | bytes 786440 | tf_op jit(solution)/shard_map/ppermute | solution.py:29
  12.1 24.5 %collective-permute-start.6 = (bf16[512,256]{1,0:T(8,128)(2,1)}, bf16[512,256]{1,0:T(8,128)(2,1)S(1)}, u32[]{:S(2)}, u32[]{:S(2)}) collective-permute-start(bf16[512,256]{1,0:T(8,128)(2,1)} %get-tuple-element.30), channel_id=1, source_target_pairs={{0,12},{4,0},{8,4},{12,8},{1,13},{5,1},{9,5},{13,9},{2,14},{6,2},{... | collective-permute-start | bytes 786440 | tf_op jit(solution)/shard_map/ppermute | solution.py:29
  29.3 8.8 %collective-permute-start.2 = (bf16[512,256]{1,0:T(8,128)(2,1)S(1)}, bf16[512,256]{1,0:T(8,128)(2,1)S(1)}, u32[]{:S(2)}, u32[]{:S(2)}) collective-permute-start(bf16[512,256]{1,0:T(8,128)(2,1)S(1)} %collective-permute-done.1.refs_1_), channel_id=1, source_target_pairs={{0,2},{2,0},{16,18},{18,16},{1,3},{3,1},{17,19},{19,17},{4,6},{6,4... | collective-permute-start | bytes 786440 | tf_op jit(solution)/shard_map/ppermute | solution.py:33
  29.7 10.5 %collective-permute-start.3 = (bf16[512,256]{1,0:T(8,128)(2,1)S(1)}, bf16[512,256]{1,0:T(8,128)(2,1)S(1)}, u32[]{:S(2)}, u32[]{:S(2)}) collective-permute-start(bf16[512,256]{1,0:T(8,128)(2,1)S(1)} %collective-permute-done.1.refs_1_), channel_id=1, source_target_pairs={{0,16},{2,18},{16,0},{18,2},{1,17},{3,19},{17,1},{19,3},{4,20},{6,... | collective-permute-start | bytes 786440 | tf_op jit(solution)/shard_map/ppermute | solution.py:33
  31.3 10.5 %collective-permute-start.4 = (bf16[512,256]{1,0:T(8,128)(2,1)S(1)}, bf16[512,256]{1,0:T(8,128)(2,1)S(1)}, u32[]{:S(2)}, u32[]{:S(2)}) collective-permute-start(bf16[512,256]{1,0:T(8,128)(2,1)S(1)} %collective-permute-done.1.refs_1_), channel_id=1, source_target_pairs={{0,18},{2,16},{16,2},{18,0},{1,19},{3,17},{17,3},{19,1},{4,22},{6,... | collective-permute-start | bytes 786440 | tf_op jit(solution)/shard_map/ppermute | solution.py:33
  41.9 14.2 %collective-permute-start.8 = (bf16[512,2048]{1,0:T(8,128)(2,1)S(1)}, bf16[512,2048]{1,0:T(8,128)(2,1)S(1)}, u32[]{:S(2)}, u32[]{:S(2)}) collective-permute-start(bf16[512,2048]{1,0:T(8,128)(2,1)S(1)} %get-tuple-element.32.x_ref.refs_0_), channel_id=1, source_target_pairs={{0,1},{1,0},{2,3},{3,2},{4,5},{5,4},{6,7},{7,6},{8,9},{9,8},{10,11... | collective-permute-start | bytes 6291464 | tf_op jit(solution)/shard_map/ppermute | solution.py:33
  42.6 8.8 %collective-permute-start.14 = (bf16[512,256]{1,0:T(8,128)(2,1)S(1)}, bf16[512,256]{1,0:T(8,128)(2,1)S(1)}, u32[]{:S(2)}, u32[]{:S(2)}) collective-permute-start(bf16[512,256]{1,0:T(8,128)(2,1)S(1)} %collective-permute-done.7), channel_id=1, source_target_pairs={{0,16},{2,18},{16,0},{18,2},{1,17},{3,19},{17,1},{19,3},{4,20},{6,... | collective-permute-start | bytes 786440 | tf_op jit(solution)/shard_map/ppermute | solution.py:33
  43.5 8.8 %collective-permute-start.11 = (bf16[512,256]{1,0:T(8,128)(2,1)S(1)}, bf16[512,256]{1,0:T(8,128)(2,1)S(1)}, u32[]{:S(2)}, u32[]{:S(2)}) collective-permute-start(bf16[512,256]{1,0:T(8,128)(2,1)S(1)} %collective-permute-done.6), channel_id=1, source_target_pairs={{0,2},{2,0},{16,18},{18,16},{1,3},{3,1},{17,19},{19,17},{4,6},{6,4... | collective-permute-start | bytes 786440 | tf_op jit(solution)/shard_map/ppermute | solution.py:33
  45.0 15.4 %collective-permute-start.5 = (bf16[512,256]{1,0:T(8,128)(2,1)S(1)}, bf16[512,256]{1,0:T(8,128)(2,1)S(1)}, u32[]{:S(2)}, u32[]{:S(2)}) collective-permute-start(bf16[512,256]{1,0:T(8,128)(2,1)S(1)} %panel.4), channel_id=1, source_target_pairs={{0,8},{4,12},{8,0},{12,4},{1,9},{5,13},{9,1},{13,5},{2,10},{6,14},... | collective-permute-start | bytes 786440 | tf_op jit(solution)/shard_map/ppermute | solution.py:29
  51.4 15.5 %collective-permute-start.15 = (bf16[1024,256]{1,0:T(8,128)(2,1)S(1)}, bf16[1024,256]{1,0:T(8,128)(2,1)S(1)}, u32[]{:S(2)}, u32[]{:S(2)}) collective-permute-start(bf16[1024,256]{1,0:T(8,128)(2,1)S(1)} %constant_dynamic-update-slice_fusion.2.refs_2_), channel_id=1, source_target_pairs={{0,2},{2,0},{16,18},{18,16},{1,3},{3,1},{17,19},{19,17},{4,6},{6,4... | collective-permute-start | bytes 1572872 | tf_op jit(solution)/shard_map/ppermute | solution.py:33
  52.3 15.9 %collective-permute-start.12 = (bf16[1024,256]{1,0:T(8,128)(2,1)S(1)}, bf16[1024,256]{1,0:T(8,128)(2,1)S(1)}, u32[]{:S(2)}, u32[]{:S(2)}) collective-permute-start(bf16[1024,256]{1,0:T(8,128)(2,1)S(1)} %constant_dynamic-update-slice_fusion.refs_2_), channel_id=1, source_target_pairs={{0,16},{2,18},{16,0},{18,2},{1,17},{3,19},{17,1},{19,3},{4,20},{6,... | collective-permute-start | bytes 1572872 | tf_op jit(solution)/shard_map/ppermute | solution.py:33
  60.4 6.4 %collective-permute-start.9 = (bf16[512,128]{1,0:T(8,128)(2,1)S(1)}, bf16[512,128]{1,0:T(8,128)(2,1)S(1)}, u32[]{:S(2)}, u32[]{:S(2)}) collective-permute-start(bf16[512,128]{1,0:T(8,128)(2,1)S(1)} %low_part.1), channel_id=1, source_target_pairs={{0,4},{4,0},{8,12},{12,8},{1,5},{5,1},{9,13},{13,9},{2,6},{6,2},{1... | collective-permute-start | bytes 393224 | tf_op jit(solution)/shard_map/ppermute | solution.py:33
  60.4 22.4 %collective-permute-start.17 = (bf16[512,256]{1,0:T(8,128)(2,1)S(1)}, bf16[512,256]{1,0:T(8,128)(2,1)S(1)}, u32[]{:S(2)}, u32[]{:S(2)}) collective-permute-start(bf16[512,256]{1,0:T(8,128)(2,1)S(1)} %panel.5), channel_id=1, source_target_pairs={{0,9},{1,8},{4,13},{5,12},{8,1},{9,0},{12,5},{13,4},{2,11},{3,10},... | collective-permute-start | bytes 786440 | tf_op jit(solution)/shard_map/ppermute | solution.py:365
  66.9 14.3 %collective-permute-start.10 = (bf16[512,128]{1,0:T(8,128)(2,1)S(1)}, bf16[512,128]{1,0:T(8,128)(2,1)S(1)}, u32[]{:S(2)}, u32[]{:S(2)}) collective-permute-start(bf16[512,128]{1,0:T(8,128)(2,1)S(1)} %add_convert_fusion.refs_0_), channel_id=1, source_target_pairs={{0,8},{4,12},{8,0},{12,4},{1,9},{5,13},{9,1},{13,5},{2,10},{6,14},... | collective-permute-start | bytes 393224 | tf_op jit(solution)/shard_map/ppermute | solution.py:33
  67.0 36.9 %slice-start = ((s8[8388608]{0:T(1024)(128)(4,1)}), s8[4194304]{0:T(1024)(128)(4,1)S(1)}, s32[]{:S(2)}) async-start(s8[8388608]{0:T(1024)(128)(4,1)} %bitcast.10), calls=%async_computation | async-start | bytes 8388608
  68.2 35.6 %slice-start.1 = ((s8[8388608]{0:T(1024)(128)(4,1)}), s8[4194304]{0:T(1024)(128)(4,1)S(1)}, s32[]{:S(2)}) async-start(s8[8388608]{0:T(1024)(128)(4,1)} %bitcast.10), calls=%async_computation.1 | async-start | bytes 8388608
  82.8 16.8 %collective-permute-start.20 = (bf16[128,2560]{1,0:T(8,128)(2,1)S(1)}, bf16[128,2560]{1,0:T(8,128)(2,1)S(1)}, u32[]{:S(2)}, u32[]{:S(2)}) collective-permute-start(bf16[128,2560]{1,0:T(8,128)(2,1)S(1)} %get-tuple-element.43), channel_id=1, source_target_pairs={{0,2},{2,0},{1,3},{3,1},{4,6},{6,4},{5,7},{7,5},{8,10},{10,8},{9,1... | collective-permute-start | bytes 1966088 | tf_op jit(solution)/shard_map/ppermute | solution.py:29
  84.4 19.3 %collective-permute-start.16 = (bf16[512,256]{1,0:T(8,128)(2,1)S(1)}, bf16[512,256]{1,0:T(8,128)(2,1)S(1)}, u32[]{:S(2)}, u32[]{:S(2)}) collective-permute-start(bf16[512,256]{1,0:T(8,128)(2,1)S(1)} %get-tuple-element.38), channel_id=1, source_target_pairs={{0,12},{4,0},{8,4},{12,8},{1,13},{5,1},{9,5},{13,9},{2,14},{6,2},{... | collective-permute-start | bytes 786440 | tf_op jit(solution)/shard_map/ppermute | solution.py:29
  85.7 18.0 %collective-permute-start.13 = (bf16[512,256]{1,0:T(8,128)(2,1)S(1)}, bf16[512,256]{1,0:T(8,128)(2,1)S(1)}, u32[]{:S(2)}, u32[]{:S(2)}) collective-permute-start(bf16[512,256]{1,0:T(8,128)(2,1)S(1)} %get-tuple-element.36), channel_id=1, source_target_pairs={{0,4},{4,8},{8,12},{12,0},{1,5},{5,9},{9,13},{13,1},{2,6},{6,10},{... | collective-permute-start | bytes 786440 | tf_op jit(solution)/shard_map/ppermute | solution.py:29
  86.4 17.3 %collective-permute-start.18 = (bf16[512,256]{1,0:T(8,128)(2,1)S(1)}, bf16[512,256]{1,0:T(8,128)(2,1)S(1)}, u32[]{:S(2)}, u32[]{:S(2)}) collective-permute-start(bf16[512,256]{1,0:T(8,128)(2,1)S(1)} %get-tuple-element.39), channel_id=1, source_target_pairs={{0,5},{1,4},{4,9},{5,8},{8,13},{9,12},{12,1},{13,0},{2,7},{3,6},{6... | collective-permute-start | bytes 786440 | tf_op jit(solution)/shard_map/ppermute | solution.py:365
  103.7 10.3 %collective-permute-start.21 = (bf16[128,2560]{1,0:T(8,128)(2,1)S(1)}, bf16[128,2560]{1,0:T(8,128)(2,1)S(1)}, u32[]{:S(2)}, u32[]{:S(2)}) collective-permute-start(bf16[128,2560]{1,0:T(8,128)(2,1)S(1)} %get-tuple-element.44), channel_id=1, source_target_pairs={{0,1},{1,0},{2,3},{3,2},{4,5},{5,4},{6,7},{7,6},{8,9},{9,8},{10,11... | collective-permute-start | bytes 1966088 | tf_op jit(solution)/shard_map/ppermute | solution.py:33
  103.7 8.1 %collective-permute-start.19 = (bf16[512,256]{1,0:T(8,128)(2,1)S(1)}, bf16[512,256]{1,0:T(8,128)(2,1)S(1)}, u32[]{:S(2)}, u32[]{:S(2)}) collective-permute-start(bf16[512,256]{1,0:T(8,128)(2,1)S(1)} %get-tuple-element.40), channel_id=1, source_target_pairs={{0,13},{1,12},{4,1},{5,0},{8,5},{9,4},{12,9},{13,8},{2,15},{3,14},... | collective-permute-start | bytes 786440 | tf_op jit(solution)/shard_map/ppermute | solution.py:365
  (5 other events, 117.0 us)

commit v5 on v4

--- a/solution.py
+++ b/solution.py
@@ -59,42 +59,6 @@
     for b, start in enumerate(starts_of(fill_ref, blocks)):
         tenant = jnp.where(row >= start, tenant_ref[b], tenant)
     return tenant
-
-
-def shares_kernel(count, at_ref, w_ref, a_ref, b_ref, *refs):
-    outs, both, sems = refs[:count], refs[count], refs[count + 1]
-    deep, half = outs[0].shape
-    feat = a_ref.shape[1]
-    col = pl.multiple_of(at_ref[count], 128)
-    copies = []
-    for s in range(count):
-        source = w_ref.at[pl.ds(pl.multiple_of(at_ref[s], 16), deep), pl.ds(col, half)]
-        copies.append(pltpu.make_async_copy(source, outs[s], sems.at[s]))
-    copies.append(pltpu.make_async_copy(a_ref, both.at[:, :feat], sems.at[count]))
-    copies.append(pltpu.make_async_copy(b_ref, both.at[:, feat:], sems.at[count + 1]))
-    for copy in copies:
-        copy.start()
-    for copy in copies:
-        copy.wait()
-
-
-def shares_of(rows_at, col_at, base_weight, a, b, deep, half):
-    if half % 128 or deep % 16:
-        blocks = [lax.dynamic_slice(base_weight, (row, col_at), (deep, half)) for row in rows_at]
-        return blocks, jnp.concatenate([a, b], axis=1)
-    count = len(rows_at)
-    shapes = [shaped((deep, half), BF16)] * count + [shaped((a.shape[0], a.shape[1] + b.shape[1]), BF16)]
-    *blocks, both = pl.pallas_call(
-        functools.partial(shares_kernel, count),
-        in_specs=[SMEM] + [pl.BlockSpec(memory_space=pl.ANY)] * 3,
-        out_specs=[VMEM] * (count + 1),
-        out_shape=shapes,
-        scratch_shapes=[pltpu.SemaphoreType.DMA((count + 2,))],
-        compiler_params=params(56),
-        cost_estimate=cost(0, 4 * (count * deep * half + shapes[-1].size)),
-        name="shares",
-    )(jnp.stack([*rows_at, col_at]).astype(I32), base_weight, a, b)
-    return blocks, both
 
 
 def pack_kernel(blocks, block, fill_ref, tok_ref, cot_ref, x_ref, c_ref, pick):
@@ -169,7 +133,7 @@
 
 
 def grad_kernel(n_dp, n_t, rank, blocks, dp_ref, fill_ref, tenant_ref, x_ref, c_ref, *refs):
-    lows, low_ref, own_ref, sends = refs[:n_t], refs[n_t], refs[n_t + 1], refs[n_t + 2 :]
+    lows, low_ref, out_ref = refs[:n_t], refs[n_t], refs[n_t + 1]
     lanes = 2 * rank
     feat = x_ref.shape[1]
     total = lows[0][...].astype(F32)
@@ -182,11 +146,10 @@
     low_in, low_grad = doubled(total, lane, rank)
     for s in range(n_dp):
         mask = owner_mask(tenant, lane, (dp_ref[0] + s) % n_dp, rank)
-        target = own_ref if s == 0 else sends[s - 1]
         grad_t = jnp.transpose(jnp.where(mask, ADAPTER_SCALE * low_grad, 0.0)).astype(BF16)
         in_t = jnp.transpose(jnp.where(mask, ADAPTER_SCALE * low_in, 0.0)).astype(BF16)
-        target[:, :feat] = dot(grad_t, x_ref[...]).astype(target.dtype)
-        target[:, feat:] = dot(in_t, c_ref[...]).astype(target.dtype)
+        out_ref[s * lanes : (s + 1) * lanes, :feat] = dot(grad_t, x_ref[...]).astype(BF16)
+        out_ref[s * lanes : (s + 1) * lanes, feat:] = dot(in_t, c_ref[...]).astype(BF16)
 
 
 def grads(dp, fill, tenant, x, c, lows, n_dp, blocks, rank):
@@ -195,41 +158,48 @@
     return pl.pallas_call(
         functools.partial(grad_kernel, n_dp, n_t, rank, blocks),
         in_specs=[SMEM] * 3 + [VMEM] * (2 + n_t),
-        out_specs=[VMEM] * (1 + n_dp),
-        out_shape=[shaped((LIVE, 2 * rank), BF16), shaped((2 * rank, width), F32)]
-        + [shaped((2 * rank, width), BF16)] * (n_dp - 1),
+        out_specs=[VMEM] * 2,
+        out_shape=[shaped((LIVE, 2 * rank), BF16), shaped((n_dp * 2 * rank, width), BF16)],
         compiler_params=params(32),
         cost_estimate=cost(4 * LIVE * rank * n_dp * width, 2 * LIVE * width + 4 * rank * n_dp * width),
         name="grads",
     )(dp, fill, tenant, x, c, *lows)
 
 
-def panel_kernel(order, sources, place_ref, *refs):
-    pieces, outs = refs[sources:-sources], refs[-sources:]
-    for source, out in zip(refs[:sources], outs):
-        total, at = None, 0
-        deep = source.shape[1] // len(order)
-        for piece in pieces:
-            for i in range(piece.shape[0] // deep):
-                col = pl.multiple_of((place_ref[0] ^ order[at]) * deep, min(deep, 128))
-                term = dot(source[:, pl.ds(col, deep)], piece[i * deep : (i + 1) * deep, :])
-                total = term if total is None else total + term
-                at += 1
-        out[...] = total.astype(BF16)
-
-
-def panel_product(order, place, sources, pieces):
-    feat, half = sources[0].shape[1], pieces[0].shape[1]
-    count = len(sources)
-    return pl.pallas_call(
-        functools.partial(panel_kernel, order, count),
-        in_specs=[SMEM] + [VMEM] * (count + len(pieces)),
-        out_specs=[VMEM] * count,
-        out_shape=[shaped((LIVE, half), BF16)] * count,
-        compiler_params=params(24),
-        cost_estimate=cost(2 * count * LIVE * feat * half, 2 * count * LIVE * feat + 2 * feat * half),
+def panel_kernel(order, count, split, place_ref, x_ref, other_ref, *refs):
+    pieces, refs = refs[:count], refs[count:]
+    half = refs[-1].shape[1]
+    panels = pieces[0].shape[1] // half
+    if split:
+        adds, outs = refs[:-2], [refs[-2:]]
+    else:
+        adds, outs = refs[:-panels], [(ref.at[:LIVE, :], ref.at[LIVE:, :]) for ref in refs[-panels:]]
+    deep = x_ref.shape[1] // len(order)
+    for n, source in enumerate((x_ref, other_ref)):
+        total = None
+        for piece, m in zip(pieces, order):
+            col = pl.multiple_of((place_ref[0] ^ m) * deep, min(deep, 128))
+            term = dot(source[:, pl.ds(col, deep)], piece[...])
+            total = term if total is None else total + term
+        for i, out in enumerate(outs):
+            value = total[:, i * half : (i + 1) * half]
+            if i < len(adds):
+                value = value + adds[i][n * LIVE : (n + 1) * LIVE, :].astype(F32)
+            out[n][...] = value.astype(BF16)
+
+
+def panel_product(order, place, x, x_other, pieces, half, adds=(), split=False):
+    feat, wide = x.shape[1], pieces[0].shape[1]
+    shapes = [shaped((LIVE, half), BF16)] * 2 if split else [shaped((2 * LIVE, half), BF16)] * (wide // half)
+    return pl.pallas_call(
+        functools.partial(panel_kernel, order, len(pieces), split),
+        in_specs=[SMEM] + [VMEM] * (2 + len(pieces) + len(adds)),
+        out_specs=[VMEM] * len(shapes),
+        out_shape=shapes,
+        compiler_params=params(24),
+        cost_estimate=cost(4 * LIVE * feat * wide, 4 * LIVE * feat + 2 * feat * wide),
         name="panel",
-    )(place, *sources, *pieces)
+    )(place, x, x_other, *pieces, *adds)
 
 
 def settle_kernel(own_ref, got_ref, down_ref, up_ref):
@@ -286,17 +256,36 @@
     )(at, dp, fill, tenant, x, base_weight, low, *ab_list)
 
 
+def swap_kernel(*refs):
+    ins, out_ref = refs[:-1], refs[-1]
+    total = ins[0][LIVE:, :].astype(F32)
+    for ref in ins[1:]:
+        total = total + ref[LIVE:, :].astype(F32)
+    out_ref[...] = total.astype(BF16)
+
+
+def other_rows(parts):
+    half = parts[0].shape[1]
+    return pl.pallas_call(
+        swap_kernel,
+        in_specs=[VMEM] * len(parts),
+        out_specs=VMEM,
+        out_shape=shaped((LIVE, half), BF16),
+        compiler_params=params(24),
+        cost_estimate=cost(LIVE * half, 2 * LIVE * half * len(parts)),
+        name="other_rows",
+    )(*parts)
+
+
 def out_kernel(count, blocks, block, core_ref, fill_ref, base_ref, *refs):
-    owns, others, out_ref, held = refs[:count], refs[count : 2 * count], refs[2 * count], refs[2 * count + 1]
-    half = owns[0].shape[1]
-
-    def total(parts):
-        value = parts[0][...].astype(F32)
-        for part in parts[1:]:
-            value = value + part[...].astype(F32)
-        return value
-
-    own, other = total(owns), total(others)
+    parts, rest, out_ref, held = refs[:count], refs[count:-2], refs[-2], refs[-1]
+    half = rest[0].shape[1]
+    own = parts[0][:LIVE, :].astype(F32)
+    for part in parts[1:]:
+        own = own + part[:LIVE, :].astype(F32)
+    other = rest[0][...].astype(F32)
+    for part in rest[1:]:
+        other = other + part[...].astype(F32)
     first = core_ref[0] == 0
     held[:, :half] = (base_ref[:, :half] + jnp.where(first, own, other)).astype(BF16)
     held[:, half:] = (base_ref[:, half:] + jnp.where(first, other, own)).astype(BF16)
@@ -308,19 +297,19 @@
         out_ref[b * block : (b + 1) * block, :] = dot(pick, held[...]).astype(BF16)
 
 
-def finish(core, fill, base, owns, others, rows, blocks):
+def finish(core, fill, base, parts, others, rows, blocks):
     cols = base.shape[1]
-    count = len(owns)
+    count = len(parts)
     return pl.pallas_call(
         functools.partial(out_kernel, count, blocks, rows // blocks),
-        in_specs=[SMEM] * 2 + [VMEM] * (1 + 2 * count),
+        in_specs=[SMEM] * 2 + [VMEM] * (1 + count + len(others)),
         out_specs=VMEM,
         out_shape=shaped((rows, cols), BF16),
         scratch_shapes=[pltpu.VMEM((LIVE, cols), BF16)],
         compiler_params=params(24),
         cost_estimate=cost(2 * LIVE * rows * cols, 4 * LIVE * cols + 2 * LIVE * cols * count + 2 * rows * cols),
         name="finish",
-    )(core, fill, base, *owns, *others)
+    )(core, fill, base, *parts, *others)
 
 
 def body(sizes, tokens, base_weight, adapter_a, adapter_b, cotangent, block_tenant_index, block_fill):
@@ -337,64 +326,72 @@
     scalar = lambda v: v.astype(I32).reshape(1)
     dp, core, at, place = scalar(me_dp), scalar(me_pipe), scalar(me_t), scalar(q)
 
-    steps = list(range(1, n_t))
     own_a, own_b = adapter_a.reshape(pair * rank, feat), adapter_b.reshape(pair * rank, cols)
-    rows_at = [(me_t + s) % n_t * feat + q * part_rows for s in steps]
-    blocks_w, own_ab = shares_of(rows_at, me_pipe * half, base_weight, own_a, own_b, part_rows, half)
-    shares = dict(zip(steps, blocks_w))
-    lead = n_t // 2
-    received = {lead: shift(shares[lead], "tensor", n_t, lead)}
+    own_ab = jnp.concatenate([own_a, own_b], axis=1)
     ab_list = [own_ab] + [shift(own_ab, "dp", n_dp, s) for s in range(1, n_dp)]
-
-    fill = after(block_fill, shares[lead])
-    x, c = pack(fill, tokens, cotangent, blocks)
-    rest = [s for s in steps if s != lead][::-1]
-    for s in rest:
-        received[s] = shift(shares[s], "tensor", n_t, s)
-
-    def gathered(piece, first):
+    panel_at = place if planes == 4 else jnp.zeros_like(place)
+
+    def share(k):
+        return lax.dynamic_slice(base_weight, (k * feat + q * part_rows, me_pipe * half), (part_rows, half))
+
+    def gathered(piece):
         if planes != 4:
             return [lax.all_gather(piece, ("groups", "dp"), axis=0, tiled=True)], [0]
-        if first is None:
-            return [piece] + [flip(piece, ("groups", "dp"), planes, m) for m in range(1, 4)], [0, 1, 2, 3]
-        stack = jnp.concatenate([piece, flip(piece, ("groups", "dp"), planes, first)], axis=0)
-        return [stack, flip(stack, ("groups", "dp"), planes, 3 - first)], [0, first, 3 - first, 3]
-
-    def send_back(s, y, y_other):
-        pairs = [(i * n_pipe + p, ((i - s) % n_t) * n_pipe + (p ^ 1)) for i in range(n_t) for p in range(n_pipe)]
-        return shift(y, "tensor", n_t, -s), lax.ppermute(y_other, ("tensor", "pipe"), pairs)
-
-    low = low_part(dp, block_fill, block_tenant_index, x, c, ab_list, blocks, rank)
-    panel_at = place if planes == 4 else jnp.zeros_like(place)
-    pieces, order = gathered(received[lead], None)
-    x_other = flip(after(x, *pieces, *received.values(), *ab_list[1:]), "pipe", n_pipe, 1)
-    (y,) = panel_product(order, panel_at, [x], pieces)
-    received.update((s, after(received[s], y)) for s in rest)
-    (y_other,) = panel_product(order, panel_at, [x_other], pieces)
-    owns, others = zip(send_back(lead, y, y_other))
-
-    low = after(low, owns[0], y_other)
-    mask = 1
-    while 2 * mask < n_t:
-        low = (low.astype(F32) + flip(low, "tensor", n_t, mask).astype(F32)).astype(BF16)
-        mask *= 2
-    lows = [low] + ([flip(low, "tensor", n_t, mask)] if n_t > 1 else [])
-
-    last = []
-    for i, s in enumerate(rest):
-        pieces, order = gathered(received[s], 1 + i % 2)
-        y, y_other = panel_product(order, panel_at, [x, x_other], pieces)
-        last += [y, y_other]
-        own, other = send_back(s, y, y_other)
-        owns, others = [*owns, own], [*others, other]
-
-    low_sum, mine, *sends = grads(dp, block_fill, block_tenant_index, x, c, lows, n_dp, blocks, rank)
-    for s in range(1, n_dp):
-        mine = mine + shift(after(sends[s - 1], *last, others[0]), "dp", n_dp, s).astype(F32)
-    down_out, up_out = settle(mine, flip(after(mine.astype(BF16), *owns[1:], others[1]), "pipe", n_pipe, 1), pair, feat)
+        return [piece] + [flip(piece, ("groups", "dp"), planes, m) for m in range(1, 4)], [0, 1, 2, 3]
+
+    def low_sums(low):
+        mask = 1
+        while 2 * mask < n_t:
+            low = (low.astype(F32) + flip(low, "tensor", n_t, mask).astype(F32)).astype(BF16)
+            mask *= 2
+        return [low] + ([flip(low, "tensor", n_t, mask)] if n_t > 1 else [])
+
+    def gradients(x, c, lows):
+        low_sum, grad = grads(dp, block_fill, block_tenant_index, x, c, lows, n_dp, blocks, rank)
+        grad = grad.astype(F32) + flip(grad, "pipe", n_pipe, 1).astype(F32)
+        mine, *sends = jnp.split(grad, n_dp, axis=0)
+        return low_sum, mine, [send.astype(BF16) for send in sends]
+
+    if n_t == 4:
+        share_3 = share(me_t ^ 3)
+        weight = {3: flip(share_3, "tensor", n_t, 3), 1: flip(share(me_t ^ 1), "tensor", n_t, 1)}
+        weight[2] = flip(after(share(me_t ^ 2), weight[3]), "tensor", n_t, 2)
+        x, c = pack(after(block_fill, share_3), tokens, cotangent, blocks)
+        x_other = flip(after(x, weight[3], weight[1], *ab_list[1:]), "pipe", n_pipe, 1)
+        low = low_part(dp, block_fill, block_tenant_index, x, c, ab_list, blocks, rank)
+        low = (low.astype(F32) + flip(low, "tensor", n_t, 1).astype(F32)).astype(BF16)
+        pieces, order = gathered(weight[3])
+        pieces[0] = after(pieces[0], weight[1], weight[2], low)
+        (y,) = panel_product(order, panel_at, x, x_other, pieces, half)
+        add = flip(y, "tensor", n_t, 1)
+        pieces, order = gathered(after(weight[2], y))
+        (y_2,) = panel_product(order, panel_at, x, x_other, pieces, half, adds=[add])
+        low_sum, mine, sends = gradients(x, c, [after(low, y_2), flip(after(low, y), "tensor", n_t, 2)])
+        pieces, order = gathered(after(weight[1], *pieces))
+        y_1, y_1_other = panel_product(order, panel_at, x, x_other, pieces, half, split=True)
+        parts = [flip(y_2, "tensor", n_t, 2)]
+        others = [flip(other_rows(parts), "pipe", n_pipe, 1)]
+        parts.append(flip(y_1, "tensor", n_t, 1))
+        others.append(flip(y_1_other, ("tensor", "pipe"), n_t * n_pipe, n_pipe + 1))
+    else:
+        x, c = pack(block_fill, tokens, cotangent, blocks)
+        x_other = flip(x, "pipe", n_pipe, 1)
+        low = low_part(dp, block_fill, block_tenant_index, x, c, ab_list, blocks, rank)
+        low_sum, mine, sends = gradients(x, c, low_sums(low))
+        steps = range(1, n_t)
+        weights = [shift(share((me_t + s) % n_t), "tensor", n_t, s) for s in steps]
+        pieces, order = gathered(jnp.concatenate(weights, axis=1))
+        ys = panel_product(order, panel_at, x, x_other, pieces, half)
+        parts = [shift(y, "tensor", n_t, -s) for s, y in zip(steps, ys)]
+        others = [flip(other_rows(parts), "pipe", n_pipe, 1)]
+    sends = [after(send, *pieces) for send in sends]
+    got = [shift(send, "dp", n_dp, s + 1) for s, send in enumerate(sends)]
+    for recv in got[:-1]:
+        mine = mine + recv.astype(F32)
+    down_out, up_out = settle(mine, got[-1], pair, feat)
 
     base = base_product(at, dp, block_fill, block_tenant_index, x, base_weight, low_sum, ab_list, blocks, rank)
-    out = finish(core, block_fill, base, owns, others, rows, blocks)
+    out = finish(core, block_fill, base, parts, others, rows, blocks)
     return out, down_out, up_out
 
 

time: 115 us -> 105 us (0.913)
  waiting for transfers between devices: 67.7 us -> 55.1 us
  Pallas kernels: 20.7 us -> 16.8 us
  local copies, waits for them, and re-layouts: 0.11 us -> 3.23 us
  starting transfers between devices: 25 us -> 27.2 us
    ppermute x8 -> x2, waiting for transfers between devices: 35.6 us -> 0.01 us  [shift(): lax.ppermute(x, name, [(i, (i + step) % count) for i in range(count)])]
    ppermute x11 -> x21, waiting for transfers between devices: 26.3 us -> 55.1 us  [flip(): return lax.ppermute(x, names, [(i, i ^ mask) for i in range(count)])]
    ppermute x11 -> x21, starting transfers between devices: 8.4 us -> 23.7 us  [flip(): return lax.ppermute(x, names, [(i, i ^ mask) for i in range(count)])]
    ppermute x8 -> x2, starting transfers between devices: 16.4 us -> 3.58 us  [shift(): lax.ppermute(x, name, [(i, (i + step) % count) for i in range(count)])]
    ppermute x3 -> x0, waiting for transfers between devices: 5.77 us -> none  [send_back(): lax.ppermute(y_other, ('tensor', 'pipe'), pairs)]
    pallas_call x5 -> x4, Pallas kernels: 7.57 us -> 3.77 us  [the longest x3 3.75 us: panel_product(): pl.pallas_call(functools.partial(panel_kernel, order, len(pieces), split)...]
    unnamed x16 -> x12, local copies, waits for them, and re-layouts: 0.07 us -> 1.91 us
    concatenate x0 -> x1, other arithmetic: none -> 1.22 us  [body(): own_ab = jnp.concatenate([own_a, own_b], axis=1)]
  transfers between devices with their start and end apart: 22 -> 23, of which waited for: 11 -> 13; matrix products, arithmetic and copies ran while one was open for 0% -> 2% of each run, Pallas kernels for 14% -> 12%
where the time goes in v5:
time: 105 us
  waiting for transfers between devices  55.1 us (52%)
  starting transfers between devices  27.2 us (26%)
  Pallas kernels  16.8 us (16%)
  local copies, waits for them, and re-layouts  3.23 us (3%)
  other arithmetic  1.62 us (2%)
    ppermute x21, waiting for transfers between devices, flip(): return lax.ppermute(x, names, [(i, i ^ mask) for i in range(count)])  55.1 us
    ppermute x21, starting transfers between devices, flip(): return lax.ppermute(x, names, [(i, i ^ mask) for i in range(count)])  23.7 us
    pallas_call x1, Pallas kernels, pack(): pl.pallas_call(functools.partial(pack_kernel, blocks, rows // blocks), gr...  3.78 us
    pallas_call x3, Pallas kernels, panel_product(): pl.pallas_call(functools.partial(panel_kernel, order, len(pieces), split)...  3.75 us
    ppermute x2, starting transfers between devices, shift(): lax.ppermute(x, name, [(i, (i + step) % count) for i in range(count)])  3.58 us
    pallas_call x1, Pallas kernels, low_part(): pl.pallas_call(functools.partial(low_kernel, n_dp, rank, blocks), in_spec...  2.16 us
    pallas_call x1, Pallas kernels, finish(): pl.pallas_call(functools.partial(out_kernel, count, blocks, rows // block...  2.14 us
    pallas_call x1, Pallas kernels, base_product(): pl.pallas_call(functools.partial(base_kernel, n_dp, rank, blocks), grid_s...  2.12 us
  transfers between devices with their start and end apart: 23, of which 13 were waited for; matrix products, arithmetic and copies ran while one was open for 2% of the time, Pallas kernels for 12%

profile of v5, /device:TPU:0, one launch (start us, length us, event | category | flops | bytes accessed | tf_op | source)
XLA Modules:
  0.0 104.8 jit_solution(18104604924554621023)
XLA Ops:
  1.9 3.0 %collective-permute-start = (bf16[128,2560]{1,0:T(8,128)(2,1)S(1)}, bf16[128,2560]{1,0:T(8,128)(2,1)S(1)}, u32[]{:S(2)}, u32[]{:S(2)}) collective-permute-start(bf16[128,2560]{1,0:T(8,128)(2,1)S(1)} %pad_maximum_fusion.refs_0_), channel_id=1, source_target_pairs={{0,2},{2,0},{1,3},{3,1},{4,6},{6,4},{5,7},{7,5},{8,10},{10,8},{9,1... | collective-permute-start | bytes 1966088 | tf_op jit(solution)/shard_map/ppermute | solution.py:29
  6.1 3.7 %collective-permute-start.2 = (bf16[512,256]{1,0:T(8,128)(2,1)S(1)}, bf16[512,256]{1,0:T(8,128)(2,1)S(1)}, u32[]{:S(2)}, u32[]{:S(2)}) collective-permute-start(bf16[512,256]{1,0:T(8,128)(2,1)S(1)} %get-tuple-element.39), channel_id=1, source_target_pairs={{0,12},{4,8},{8,4},{12,0},{1,13},{5,9},{9,5},{13,1},{2,14},{6,10},... | collective-permute-start | bytes 786440 | tf_op jit(solution)/shard_map/ppermute | solution.py:33
  9.7 1.9 %copy-done = bf16[768,2048]{1,0:T(8,128)(2,1)S(1)} copy-done((bf16[768,2048]{1,0:T(8,128)(2,1)S(1)}, bf16[768,2048]{1,0:T(8,128)(2,1)}, u32[]{:S(2)}) %copy-start) | copy-done | bytes 3145752
  11.6 3.8 %pack.1 = (bf16[512,2048]{1,0:T(8,128)(2,1)S(1)}, bf16[512,512]{1,0:T(8,128)(2,1)S(1)}) custom-call(s32[1,6]{1,0:T(1,128)S(1)} %copy-done.2, bf16[768,2048]{1,0:T(8,128)(2,1)S(1)} %copy-done, bf16[768,512]{1,0:T(8,128)(2,1)S(1)} %copy-done.1), custom_call_target="tpu_custom_call" | custom-call | flops 1 | bytes 1 | tf_op jit(solution)/shard_map/pack/pallas_call | solution.py:82
  15.4 1.8 %collective-permute-done.2.refs_0_ = bf16[512,256]{1,0:T(8,128)(2,1)S(1)} collective-permute-done((bf16[512,256]{1,0:T(8,128)(2,1)S(1)}, bf16[512,256]{1,0:T(8,128)(2,1)S(1)}, u32[]{:S(2)}, u32[]{:S(2)}) %collective-permute-start.2) | collective-permute-done | bytes 262176 | tf_op jit(solution)/shard_map/ppermute | solution.py:33
  17.2 4.3 %collective-permute-done.3.refs_0_ = bf16[512,256]{1,0:T(8,128)(2,1)S(1)} collective-permute-done((bf16[512,256]{1,0:T(8,128)(2,1)S(1)}, bf16[512,256]{1,0:T(8,128)(2,1)S(1)}, u32[]{:S(2)}, u32[]{:S(2)}) %collective-permute-start.3) | collective-permute-done | bytes 262176 | tf_op jit(solution)/shard_map/ppermute | solution.py:33
  21.5 2.2 %low_part.1 = bf16[512,128]{1,0:T(8,128)(2,1)S(1)} custom-call(s32[1]{0:T(128)} %bitcast.2.dp_ref, s32[1,6]{1,0:T(1,128)S(1)} %copy-done.2, s32[6]{0:T(128)S(1)} %copy-done.3, bf16[512,2048]{1,0:T(8,128)(2,1)S(1)} %get-tuple-element.23.x_ref, bf16[512,512]{1,0:T(8,128)(2,1)S(1)} %get-tuple-element.22.c_ref, bf16[128,2560]{1,0:T(8,128)(2,1)S(1)} %pad_maximum_fusion.refs_0_, ...), custom_call_target="tpu_custom_call" | custom-call | flops 1 | bytes 1 | tf_op jit(solution)/shard_map/low_part/pallas_call | solution.py:119
  23.7 1.7 %collective-permute-start.1 = (bf16[512,128]{1,0:T(8,128)(2,1)S(1)}, bf16[512,128]{1,0:T(8,128)(2,1)S(1)}, u32[]{:S(2)}, u32[]{:S(2)}) collective-permute-start(bf16[512,128]{1,0:T(8,128)(2,1)S(1)} %low_part.1), channel_id=1, source_target_pairs={{0,4},{4,0},{8,12},{12,8},{1,5},{5,1},{9,13},{13,9},{2,6},{6,2},{1... | collective-permute-start | bytes 393224 | tf_op jit(solution)/shard_map/ppermute | solution.py:33
  26.3 1.5 %collective-permute-start.6 = (bf16[512,256]{1,0:T(8,128)(2,1)S(1)}, bf16[512,256]{1,0:T(8,128)(2,1)S(1)}, u32[]{:S(2)}, u32[]{:S(2)}) collective-permute-start(bf16[512,256]{1,0:T(8,128)(2,1)S(1)} %collective-permute-done.2.refs_0_), channel_id=1, source_target_pairs={{0,2},{2,0},{16,18},{18,16},{1,3},{3,1},{17,19},{19,17},{4,6},{6,4... | collective-permute-start | bytes 786440 | tf_op jit(solution)/shard_map/ppermute | solution.py:33
  27.8 1.5 %collective-permute-start.7 = (bf16[512,256]{1,0:T(8,128)(2,1)S(1)}, bf16[512,256]{1,0:T(8,128)(2,1)S(1)}, u32[]{:S(2)}, u32[]{:S(2)}) collective-permute-start(bf16[512,256]{1,0:T(8,128)(2,1)S(1)} %collective-permute-done.2.refs_0_), channel_id=1, source_target_pairs={{0,16},{2,18},{16,0},{18,2},{1,17},{3,19},{17,1},{19,3},{4,20},{6,... | collective-permute-start | bytes 786440 | tf_op jit(solution)/shard_map/ppermute | solution.py:33
  30.6 2.4 %collective-permute-start.8 = (bf16[512,256]{1,0:T(8,128)(2,1)S(1)}, bf16[512,256]{1,0:T(8,128)(2,1)S(1)}, u32[]{:S(2)}, u32[]{:S(2)}) collective-permute-start(bf16[512,256]{1,0:T(8,128)(2,1)S(1)} %collective-permute-done.2.refs_0_), channel_id=1, source_target_pairs={{0,18},{2,16},{16,2},{18,0},{1,19},{3,17},{17,3},{19,1},{4,22},{6,... | collective-permute-start | bytes 786440 | tf_op jit(solution)/shard_map/ppermute | solution.py:33
  33.1 7.3 %collective-permute-done.5.refs_0_ = bf16[512,256]{1,0:T(8,128)(2,1)S(1)} collective-permute-done((bf16[512,256]{1,0:T(8,128)(2,1)S(1)}, bf16[512,256]{1,0:T(8,128)(2,1)S(1)}, u32[]{:S(2)}, u32[]{:S(2)}) %collective-permute-start.5) | collective-permute-done | bytes 262176 | tf_op jit(solution)/shard_map/ppermute | solution.py:33
  46.5 2.6 %collective-permute-start.13 = (bf16[512,128]{1,0:T(8,128)(2,1)S(1)}, bf16[512,128]{1,0:T(8,128)(2,1)S(1)}, u32[]{:S(2)}, u32[]{:S(2)}) collective-permute-start(bf16[512,128]{1,0:T(8,128)(2,1)S(1)} %add_convert_fusion.refs_0_), channel_id=1, source_target_pairs={{0,8},{4,12},{8,0},{12,4},{1,9},{5,13},{9,1},{13,5},{2,10},{6,14},... | collective-permute-start | bytes 393224 | tf_op jit(solution)/shard_map/ppermute | solution.py:33
  49.1 3.2 %collective-permute-done.9.refs_1_ = bf16[512,256]{1,0:T(8,128)(2,1)S(1)} collective-permute-done((bf16[512,256]{1,0:T(8,128)(2,1)S(1)}, bf16[512,256]{1,0:T(8,128)(2,1)S(1)}, u32[]{:S(2)}, u32[]{:S(2)}) %collective-permute-start.9) | collective-permute-done | bytes 262176 | tf_op jit(solution)/shard_map/ppermute | solution.py:33
  52.3 4.4 %collective-permute-done.10.refs_2_ = bf16[512,256]{1,0:T(8,128)(2,1)S(1)} collective-permute-done((bf16[512,256]{1,0:T(8,128)(2,1)S(1)}, bf16[512,256]{1,0:T(8,128)(2,1)S(1)}, u32[]{:S(2)}, u32[]{:S(2)}) %collective-permute-start.10) | collective-permute-done | bytes 262176 | tf_op jit(solution)/shard_map/ppermute | solution.py:33
  59.4 1.6 %grads.1 = (bf16[512,128]{1,0:T(8,128)(2,1)S(1)}, bf16[256,2560]{1,0:T(8,128)(2,1)S(1)}) custom-call(s32[1]{0:T(128)} %bitcast.2.dp_ref, s32[1,6]{1,0:T(1,128)S(1)} %copy-done.2, s32[6]{0:T(128)S(1)} %copy-done.3, bf16[512,2048]{1,0:T(8,128)(2,1)S(1)} %get-tuple-element.23.x_ref, bf16[512,512]{1,0:T(8,128)(2,1)S(1)} %get-tuple-element.22.c_ref, ...), custom_call_target="tpu_custom_call" | custom-call | flops 1 | bytes 1 | tf_op jit(solution)/shard_map/grads/pallas_call | solution.py:158
  61.1 1.5 %collective-permute-start.15 = (bf16[512,256]{1,0:T(8,128)(2,1)S(1)}, bf16[512,256]{1,0:T(8,128)(2,1)S(1)}, u32[]{:S(2)}, u32[]{:S(2)}) collective-permute-start(bf16[512,256]{1,0:T(8,128)(2,1)S(1)} %collective-permute-done.3.refs_0_), channel_id=1, source_target_pairs={{0,2},{2,0},{16,18},{18,16},{1,3},{3,1},{17,19},{19,17},{4,6},{6,4... | collective-permute-start | bytes 786440 | tf_op jit(solution)/shard_map/ppermute | solution.py:33
  66.0 4.3 %collective-permute-done.15.refs_1_ = bf16[512,256]{1,0:T(8,128)(2,1)S(1)} collective-permute-done((bf16[512,256]{1,0:T(8,128)(2,1)S(1)}, bf16[512,256]{1,0:T(8,128)(2,1)S(1)}, u32[]{:S(2)}, u32[]{:S(2)}) %collective-permute-start.15) | collective-permute-done | bytes 262176 | tf_op jit(solution)/shard_map/ppermute | solution.py:33
  70.3 6.3 %collective-permute-done.16.refs_2_ = bf16[512,256]{1,0:T(8,128)(2,1)S(1)} collective-permute-done((bf16[512,256]{1,0:T(8,128)(2,1)S(1)}, bf16[512,256]{1,0:T(8,128)(2,1)S(1)}, u32[]{:S(2)}, u32[]{:S(2)}) %collective-permute-start.16) | collective-permute-done | bytes 262176 | tf_op jit(solution)/shard_map/ppermute | solution.py:33
  79.3 11.1 %collective-permute-done.14.refs_0_ = bf16[1024,256]{1,0:T(8,128)(2,1)S(1)} collective-permute-done((bf16[1024,256]{1,0:T(8,128)(2,1)S(1)}, bf16[1024,256]{1,0:T(8,128)(2,1)S(1)}, u32[]{:S(2)}, u32[]{:S(2)}) %collective-permute-start.14) | collective-permute-done | bytes 524320 | tf_op jit(solution)/shard_map/ppermute | solution.py:33
  90.5 2.1 %base.1.base_ref = f32[512,512]{1,0:T(8,128)S(1)} custom-call(s32[1]{0:T(128)} %bitcast.1.at_ref, s32[1]{0:T(128)} %bitcast.2.dp_ref, s32[1,6]{1,0:T(1,128)S(1)} %copy-done.2, s32[6]{0:T(128)S(1)} %copy-done.3, bf16[512,2048]{1,0:T(8,128)(2,1)S(1)} %get-tuple-element.23.x_ref, bf16[8192,512]{1,0:T(8,128)(2,1)S(1)} %bitcast.7, ...), custom_call_target="tpu_custom_call" | custom-call | flops 1 | bytes 1 | tf_op jit(solution)/shard_map/base/pallas_call | solution.py:242
  92.6 3.4 %collective-permute-done.18.refs_1_ = bf16[512,256]{1,0:T(8,128)(2,1)S(1)} collective-permute-done((bf16[512,256]{1,0:T(8,128)(2,1)S(1)}, bf16[512,256]{1,0:T(8,128)(2,1)S(1)}, u32[]{:S(2)}, u32[]{:S(2)}) %collective-permute-start.18) | collective-permute-done | bytes 262176 | tf_op jit(solution)/shard_map/ppermute | solution.py:33
  95.9 5.4 %collective-permute-done.20.refs_3_ = bf16[512,256]{1,0:T(8,128)(2,1)S(1)} collective-permute-done((bf16[512,256]{1,0:T(8,128)(2,1)S(1)}, bf16[512,256]{1,0:T(8,128)(2,1)S(1)}, u32[]{:S(2)}, u32[]{:S(2)}) %collective-permute-start.20) | collective-permute-done | bytes 262176 | tf_op jit(solution)/shard_map/ppermute | solution.py:33
  101.4 2.1 %finish.1 = bf16[768,512]{1,0:T(8,128)(2,1)} custom-call(s32[1]{0:T(128)} %bitcast.core_ref, s32[1,6]{1,0:T(1,128)S(1)} %copy-done.2, f32[512,512]{1,0:T(8,128)S(1)} %base.1.base_ref, bf16[1024,256]{1,0:T(8,128)(2,1)S(1)} %collective-permute-done.14.refs_0_, bf16[512,256]{1,0:T(8,128)(2,1)S(1)} %collective-permute-done.18.refs_1_, ...), custom_call_target="tpu_custom_call" | custom-call | flops 1 | bytes 1 | tf_op jit(solution)/shard_map/finish/pallas_call | solution.py:303
  (51 shorter events, 21.0 us)
Async XLA Ops:
  1.9 19.6 %collective-permute-start = (bf16[128,2560]{1,0:T(8,128)(2,1)S(1)}, bf16[128,2560]{1,0:T(8,128)(2,1)S(1)}, u32[]{:S(2)}, u32[]{:S(2)}) collective-permute-start(bf16[128,2560]{1,0:T(8,128)(2,1)S(1)} %pad_maximum_fusion.refs_0_), channel_id=1, source_target_pairs={{0,2},{2,0},{1,3},{3,1},{4,6},{6,4},{5,7},{7,5},{8,10},{10,8},{9,1... | collective-permute-start | bytes 1966088 | tf_op jit(solution)/shard_map/ppermute | solution.py:29
  6.1 11.1 %collective-permute-start.2 = (bf16[512,256]{1,0:T(8,128)(2,1)S(1)}, bf16[512,256]{1,0:T(8,128)(2,1)S(1)}, u32[]{:S(2)}, u32[]{:S(2)}) collective-permute-start(bf16[512,256]{1,0:T(8,128)(2,1)S(1)} %get-tuple-element.39), channel_id=1, source_target_pairs={{0,12},{4,8},{8,4},{12,0},{1,13},{5,9},{9,5},{13,1},{2,14},{6,10},... | collective-permute-start | bytes 786440 | tf_op jit(solution)/shard_map/ppermute | solution.py:33
  9.7 11.7 %collective-permute-start.3 = (bf16[512,256]{1,0:T(8,128)(2,1)S(1)}, bf16[512,256]{1,0:T(8,128)(2,1)S(1)}, u32[]{:S(2)}, u32[]{:S(2)}) collective-permute-start(bf16[512,256]{1,0:T(8,128)(2,1)S(1)} %get-tuple-element.38), channel_id=1, source_target_pairs={{0,4},{4,0},{8,12},{12,8},{1,5},{5,1},{9,13},{13,9},{2,6},{6,2},{1... | collective-permute-start | bytes 786440 | tf_op jit(solution)/shard_map/ppermute | solution.py:33
  21.5 19.8 %collective-permute-start.4 = (bf16[512,2048]{1,0:T(8,128)(2,1)S(1)}, bf16[512,2048]{1,0:T(8,128)(2,1)S(1)}, u32[]{:S(2)}, u32[]{:S(2)}) collective-permute-start(bf16[512,2048]{1,0:T(8,128)(2,1)S(1)} %get-tuple-element.23.x_ref), channel_id=1, source_target_pairs={{0,1},{1,0},{2,3},{3,2},{4,5},{5,4},{6,7},{7,6},{8,9},{9,8},{10,11... | collective-permute-start | bytes 6291464 | tf_op jit(solution)/shard_map/ppermute | solution.py:33
  23.7 7.0 %collective-permute-start.1 = (bf16[512,128]{1,0:T(8,128)(2,1)S(1)}, bf16[512,128]{1,0:T(8,128)(2,1)S(1)}, u32[]{:S(2)}, u32[]{:S(2)}) collective-permute-start(bf16[512,128]{1,0:T(8,128)(2,1)S(1)} %low_part.1), channel_id=1, source_target_pairs={{0,4},{4,0},{8,12},{12,8},{1,5},{5,1},{9,13},{13,9},{2,6},{6,2},{1... | collective-permute-start | bytes 393224 | tf_op jit(solution)/shard_map/ppermute | solution.py:33
  25.4 15.0 %collective-permute-start.5 = (bf16[512,256]{1,0:T(8,128)(2,1)S(1)}, bf16[512,256]{1,0:T(8,128)(2,1)S(1)}, u32[]{:S(2)}, u32[]{:S(2)}) collective-permute-start(bf16[512,256]{1,0:T(8,128)(2,1)S(1)} %get-tuple-element.24), channel_id=1, source_target_pairs={{0,8},{4,12},{8,0},{12,4},{1,9},{5,13},{9,1},{13,5},{2,10},{6,14},... | collective-permute-start | bytes 786440 | tf_op jit(solution)/shard_map/ppermute | solution.py:33
  26.3 14.1 %collective-permute-start.6 = (bf16[512,256]{1,0:T(8,128)(2,1)S(1)}, bf16[512,256]{1,0:T(8,128)(2,1)S(1)}, u32[]{:S(2)}, u32[]{:S(2)}) collective-permute-start(bf16[512,256]{1,0:T(8,128)(2,1)S(1)} %collective-permute-done.2.refs_0_), channel_id=1, source_target_pairs={{0,2},{2,0},{16,18},{18,16},{1,3},{3,1},{17,19},{19,17},{4,6},{6,4... | collective-permute-start | bytes 786440 | tf_op jit(solution)/shard_map/ppermute | solution.py:33
  27.8 13.5 %collective-permute-start.7 = (bf16[512,256]{1,0:T(8,128)(2,1)S(1)}, bf16[512,256]{1,0:T(8,128)(2,1)S(1)}, u32[]{:S(2)}, u32[]{:S(2)}) collective-permute-start(bf16[512,256]{1,0:T(8,128)(2,1)S(1)} %collective-permute-done.2.refs_0_), channel_id=1, source_target_pairs={{0,16},{2,18},{16,0},{18,2},{1,17},{3,19},{17,1},{19,3},{4,20},{6,... | collective-permute-start | bytes 786440 | tf_op jit(solution)/shard_map/ppermute | solution.py:33
  30.6 10.6 %collective-permute-start.8 = (bf16[512,256]{1,0:T(8,128)(2,1)S(1)}, bf16[512,256]{1,0:T(8,128)(2,1)S(1)}, u32[]{:S(2)}, u32[]{:S(2)}) collective-permute-start(bf16[512,256]{1,0:T(8,128)(2,1)S(1)} %collective-permute-done.2.refs_0_), channel_id=1, source_target_pairs={{0,18},{2,16},{16,2},{18,0},{1,19},{3,17},{17,3},{19,1},{4,22},{6,... | collective-permute-start | bytes 786440 | tf_op jit(solution)/shard_map/ppermute | solution.py:33
  42.5 15.6 %collective-permute-start.12 = (bf16[1024,256]{1,0:T(8,128)(2,1)S(1)}, bf16[1024,256]{1,0:T(8,128)(2,1)S(1)}, u32[]{:S(2)}, u32[]{:S(2)}) collective-permute-start(bf16[1024,256]{1,0:T(8,128)(2,1)S(1)} %panel.3), channel_id=1, source_target_pairs={{0,4},{4,0},{8,12},{12,8},{1,5},{5,1},{9,13},{13,9},{2,6},{6,2},{1... | collective-permute-start | bytes 1572872 | tf_op jit(solution)/shard_map/ppermute | solution.py:33
  43.0 9.2 %collective-permute-start.9 = (bf16[512,256]{1,0:T(8,128)(2,1)S(1)}, bf16[512,256]{1,0:T(8,128)(2,1)S(1)}, u32[]{:S(2)}, u32[]{:S(2)}) collective-permute-start(bf16[512,256]{1,0:T(8,128)(2,1)S(1)} %collective-permute-done.5.refs_0_), channel_id=1, source_target_pairs={{0,2},{2,0},{16,18},{18,16},{1,3},{3,1},{17,19},{19,17},{4,6},{6,4... | collective-permute-start | bytes 786440 | tf_op jit(solution)/shard_map/ppermute | solution.py:33
  44.3 12.4 %collective-permute-start.10 = (bf16[512,256]{1,0:T(8,128)(2,1)S(1)}, bf16[512,256]{1,0:T(8,128)(2,1)S(1)}, u32[]{:S(2)}, u32[]{:S(2)}) collective-permute-start(bf16[512,256]{1,0:T(8,128)(2,1)S(1)} %collective-permute-done.5.refs_0_), channel_id=1, source_target_pairs={{0,16},{2,18},{16,0},{18,2},{1,17},{3,19},{17,1},{19,3},{4,20},{6,... | collective-permute-start | bytes 786440 | tf_op jit(solution)/shard_map/ppermute | solution.py:33
  45.1 11.5 %collective-permute-start.11 = (bf16[512,256]{1,0:T(8,128)(2,1)S(1)}, bf16[512,256]{1,0:T(8,128)(2,1)S(1)}, u32[]{:S(2)}, u32[]{:S(2)}) collective-permute-start(bf16[512,256]{1,0:T(8,128)(2,1)S(1)} %collective-permute-done.5.refs_0_), channel_id=1, source_target_pairs={{0,18},{2,16},{16,2},{18,0},{1,19},{3,17},{17,3},{19,1},{4,22},{6,... | collective-permute-start | bytes 786440 | tf_op jit(solution)/shard_map/ppermute | solution.py:33
  46.5 12.8 %collective-permute-start.13 = (bf16[512,128]{1,0:T(8,128)(2,1)S(1)}, bf16[512,128]{1,0:T(8,128)(2,1)S(1)}, u32[]{:S(2)}, u32[]{:S(2)}) collective-permute-start(bf16[512,128]{1,0:T(8,128)(2,1)S(1)} %add_convert_fusion.refs_0_), channel_id=1, source_target_pairs={{0,8},{4,12},{8,0},{12,4},{1,9},{5,13},{9,1},{13,5},{2,10},{6,14},... | collective-permute-start | bytes 393224 | tf_op jit(solution)/shard_map/ppermute | solution.py:33
  59.4 31.1 %slice-start = ((s8[8388608]{0:T(1024)(128)(4,1)}), s8[4194304]{0:T(1024)(128)(4,1)S(1)}, s32[]{:S(2)}) async-start(s8[8388608]{0:T(1024)(128)(4,1)} %bitcast.6), calls=%async_computation | async-start | bytes 8388608
  61.0 4.5 %collective-permute-start.21 = (bf16[256,2560]{1,0:T(8,128)(2,1)S(1)}, bf16[256,2560]{1,0:T(8,128)(2,1)S(1)}, u32[]{:S(2)}, u32[]{:S(2)}) collective-permute-start(bf16[256,2560]{1,0:T(8,128)(2,1)S(1)} %get-tuple-element.33), channel_id=1, source_target_pairs={{0,1},{1,0},{2,3},{3,2},{4,5},{5,4},{6,7},{7,6},{8,9},{9,8},{10,11... | collective-permute-start | bytes 3932168 | tf_op jit(solution)/shard_map/ppermute | solution.py:33
  61.1 9.2 %collective-permute-start.15 = (bf16[512,256]{1,0:T(8,128)(2,1)S(1)}, bf16[512,256]{1,0:T(8,128)(2,1)S(1)}, u32[]{:S(2)}, u32[]{:S(2)}) collective-permute-start(bf16[512,256]{1,0:T(8,128)(2,1)S(1)} %collective-permute-done.3.refs_0_), channel_id=1, source_target_pairs={{0,2},{2,0},{16,18},{18,16},{1,3},{3,1},{17,19},{19,17},{4,6},{6,4... | collective-permute-start | bytes 786440 | tf_op jit(solution)/shard_map/ppermute | solution.py:33
  62.6 14.0 %collective-permute-start.16 = (bf16[512,256]{1,0:T(8,128)(2,1)S(1)}, bf16[512,256]{1,0:T(8,128)(2,1)S(1)}, u32[]{:S(2)}, u32[]{:S(2)}) collective-permute-start(bf16[512,256]{1,0:T(8,128)(2,1)S(1)} %collective-permute-done.3.refs_0_), channel_id=1, source_target_pairs={{0,16},{2,18},{16,0},{18,2},{1,17},{3,19},{17,1},{19,3},{4,20},{6,... | collective-permute-start | bytes 786440 | tf_op jit(solution)/shard_map/ppermute | solution.py:33
  63.2 13.4 %collective-permute-start.17 = (bf16[512,256]{1,0:T(8,128)(2,1)S(1)}, bf16[512,256]{1,0:T(8,128)(2,1)S(1)}, u32[]{:S(2)}, u32[]{:S(2)}) collective-permute-start(bf16[512,256]{1,0:T(8,128)(2,1)S(1)} %collective-permute-done.3.refs_0_), channel_id=1, source_target_pairs={{0,18},{2,16},{16,2},{18,0},{1,19},{3,17},{17,3},{19,1},{4,22},{6,... | collective-permute-start | bytes 786440 | tf_op jit(solution)/shard_map/ppermute | solution.py:33
  64.7 25.7 %collective-permute-start.14 = (bf16[1024,256]{1,0:T(8,128)(2,1)S(1)}, bf16[1024,256]{1,0:T(8,128)(2,1)S(1)}, u32[]{:S(2)}, u32[]{:S(2)}) collective-permute-start(bf16[1024,256]{1,0:T(8,128)(2,1)S(1)} %panel.4), channel_id=1, source_target_pairs={{0,8},{4,12},{8,0},{12,4},{1,9},{5,13},{9,1},{13,5},{2,10},{6,14},... | collective-permute-start | bytes 1572872 | tf_op jit(solution)/shard_map/ppermute | solution.py:33
  76.6 27.0 %collective-permute-start.22 = (bf16[128,2560]{1,0:T(8,128)(2,1)S(1)}, bf16[128,2560]{1,0:T(8,128)(2,1)S(1)}, u32[]{:S(2)}, u32[]{:S(2)}) collective-permute-start(bf16[128,2560]{1,0:T(8,128)(2,1)S(1)} %split.12), channel_id=1, source_target_pairs={{0,2},{2,0},{1,3},{3,1},{4,6},{6,4},{5,7},{7,5},{8,10},{10,8},{9,1... | collective-permute-start | bytes 1966088 | tf_op jit(solution)/shard_map/ppermute | solution.py:29
  78.5 17.5 %collective-permute-start.18 = (bf16[512,256]{1,0:T(8,128)(2,1)S(1)}, bf16[512,256]{1,0:T(8,128)(2,1)S(1)}, u32[]{:S(2)}, u32[]{:S(2)}) collective-permute-start(bf16[512,256]{1,0:T(8,128)(2,1)S(1)} %get-tuple-element.31), channel_id=1, source_target_pairs={{0,4},{4,0},{8,12},{12,8},{1,5},{5,1},{9,13},{13,9},{2,6},{6,2},{1... | collective-permute-start | bytes 786440 | tf_op jit(solution)/shard_map/ppermute | solution.py:33
  79.3 22.1 %collective-permute-start.20 = (bf16[512,256]{1,0:T(8,128)(2,1)S(1)}, bf16[512,256]{1,0:T(8,128)(2,1)S(1)}, u32[]{:S(2)}, u32[]{:S(2)}) collective-permute-start(bf16[512,256]{1,0:T(8,128)(2,1)S(1)} %get-tuple-element.32), channel_id=1, source_target_pairs={{0,5},{1,4},{4,1},{5,0},{8,13},{9,12},{12,9},{13,8},{2,7},{3,6},{6... | collective-permute-start | bytes 786440 | tf_op jit(solution)/shard_map/ppermute | solution.py:33
  90.4 11.0 %collective-permute-start.19 = (bf16[512,256]{1,0:T(8,128)(2,1)S(1)}, bf16[512,256]{1,0:T(8,128)(2,1)S(1)}, u32[]{:S(2)}, u32[]{:S(2)}) collective-permute-start(bf16[512,256]{1,0:T(8,128)(2,1)S(1)} %other_rows.1), channel_id=1, source_target_pairs={{0,1},{1,0},{2,3},{3,2},{4,5},{5,4},{6,7},{7,6},{8,9},{9,8},{10,11... | collective-permute-start | bytes 786440 | tf_op jit(solution)/shard_map/ppermute | solution.py:33
  (5 other events, 65.0 us)

commit v6 on v5

v6 whole, which is shorter than its diff:
```python
import functools

import jax
import jax.numpy as jnp
from jax import lax
from jax.experimental import pallas as pl
from jax.experimental.pallas import tpu as pltpu
from jax.sharding import PartitionSpec as P

ADAPTER_SCALE = 2.0
LIVE = 512
BF16 = jnp.bfloat16
F32 = jnp.float32
I32 = jnp.int32
MIB = 1 << 20
SMEM = pl.BlockSpec(memory_space=pltpu.SMEM)
VMEM = pl.BlockSpec(memory_space=pltpu.VMEM)


def shaped(shape, dtype):
    return jax.ShapeDtypeStruct(shape, dtype)


def dot(a, b, contract=(1, 0)):
    return lax.dot_general(a, b, ((contract[0:1], contract[1:2]), ((), ())), preferred_element_type=F32)


def shift(x, name, count, step):
    return lax.ppermute(x, name, [(i, (i + step) % count) for i in range(count)])


def flip(x, names, count, mask):
    return lax.ppermute(x, names, [(i, i ^ mask) for i in range(count)])


def params(mib):
    return pltpu.CompilerParams(vmem_limit_bytes=mib * MIB)


def cost(flops, bytes_accessed):
    return pl.CostEstimate(flops=1, bytes_accessed=1, transcendentals=0)


def after(x, *others):
    return lax.optimization_barrier((x, *others))[0]


def starts_of(fill_ref, blocks):
    starts, at = [], jnp.int32(0)
    for b in range(blocks):
        starts.append(at)
        at = at + fill_ref[0, b]
    return starts


def tenant_lanes(fill_ref, tenant_ref, blocks, lanes):
    row = lax.broadcasted_iota(I32, (LIVE, lanes), 0)
    tenant = jnp.zeros((LIVE, lanes), I32)
    for b, start in enumerate(starts_of(fill_ref, blocks)):
        tenant = jnp.where(row >= start, tenant_ref[b], tenant)
    return tenant


def pack_kernel(blocks, block, fill_ref, tenant_ref, tok_ref, cot_ref, out_ref, pick):
    feat, cols = tok_ref.shape[1], cot_ref.shape[1]
    row = lax.broadcasted_iota(I32, (LIVE, block), 0)
    col = lax.broadcasted_iota(I32, (LIVE, block), 1)
    for b, start in enumerate(starts_of(fill_ref, blocks)):
        hit = (row == col + start) & (col < fill_ref[0, b])
        pick[:, b * block : (b + 1) * block] = jnp.where(hit, 1.0, 0.0).astype(BF16)
    wide = min(feat, 512)
    for at in range(0, feat, wide):
        out_ref[:, at : at + wide] = dot(pick[...], tok_ref[:, at : at + wide]).astype(BF16)
    out_ref[:, feat : feat + cols] = dot(pick[...], cot_ref[...]).astype(BF16)
    lanes = out_ref.shape[1] - feat - cols
    out_ref[:, feat + cols :] = tenant_lanes(fill_ref, tenant_ref, blocks, lanes).astype(F32).astype(BF16)


def pack(fill, tenant, tokens, cotangent, blocks, lanes):
    rows, feat = tokens.shape
    cols = cotangent.shape[1]
    return pl.pallas_call(
        functools.partial(pack_kernel, blocks, rows // blocks),
        in_specs=[SMEM] * 2 + [VMEM] * 2,
        out_specs=VMEM,
        out_shape=shaped((LIVE, feat + cols + lanes), BF16),
        scratch_shapes=[pltpu.VMEM((LIVE, rows), BF16)],
        compiler_params=params(24),
        cost_estimate=cost(2 * LIVE * rows * (feat + cols), 2 * (LIVE + rows) * (feat + cols)),
        name="pack",
    )(fill, tenant, tokens, cotangent)


def owner_mask(tenant, lane, owner, rank):
    return tenant == 2 * owner + (lane >= rank).astype(I32)


def low_kernel(n_dp, rank, blocks, dp_ref, fill_ref, tenant_ref, x_ref, *refs):
    a_refs, b_refs, out_ref = refs[:n_dp], refs[n_dp : 2 * n_dp], refs[2 * n_dp]
    lanes, feat, cols = 2 * rank, a_refs[0].shape[1], b_refs[0].shape[1]
    tenant = tenant_lanes(fill_ref, tenant_ref, blocks, lanes)
    lane = lax.broadcasted_iota(I32, (LIVE, lanes), 1)
    low_in = jnp.zeros((LIVE, lanes), F32)
    low_grad = jnp.zeros((LIVE, lanes), F32)
    for s in range(n_dp):
        mask = owner_mask(tenant, lane, (dp_ref[0] + n_dp - s) % n_dp, rank)
        low_in = low_in + jnp.where(mask, dot(x_ref[:, :feat], a_refs[s][...], (1, 1)), 0.0)
        low_grad = low_grad + jnp.where(mask, dot(x_ref[:, feat : feat + cols], b_refs[s][...], (1, 1)), 0.0)
    low_in = low_in + pltpu.roll(low_in, rank, 1)
    low_grad = low_grad + pltpu.roll(low_grad, rank, 1)
    out_ref[...] = jnp.where(lane < rank, low_in, low_grad).astype(BF16)


def low_part(dp, fill, tenant, x, a_list, b_list, blocks, rank):
    n_dp = len(a_list)
    width = x.shape[1]
    return pl.pallas_call(
        functools.partial(low_kernel, n_dp, rank, blocks),
        in_specs=[SMEM] * 3 + [VMEM] * (1 + 2 * n_dp),
        out_specs=VMEM,
        out_shape=shaped((LIVE, 2 * rank), BF16),
        compiler_params=params(24),
        cost_estimate=cost(4 * LIVE * rank * n_dp * width, 2 * LIVE * width + 4 * rank * n_dp * width),
        name="low_part",
    )(dp, fill, tenant, x, *a_list, *b_list)


def doubled(low, lane, rank):
    turned = pltpu.roll(low, rank, 1)
    return jnp.where(lane < rank, low, turned), jnp.where(lane < rank, turned, low)


def grad_kernel(n_dp, rank, feat, cols, dp_ref, core_ref, own_ref, other_ref, low_ref, low_other_ref, *outs):
    lanes = 2 * rank
    lane = lax.broadcasted_iota(I32, (LIVE, lanes), 1)
    for s in range(0, n_dp, 2):
        first, second = (dp_ref[0] + s) % n_dp, (dp_ref[0] + s + 1) % n_dp
        wanted = (2 * jnp.where(lane < rank, first, second) + core_ref[0]).astype(F32)
        down, up = None, None
        for source, ref in ((own_ref, low_ref), (other_ref, low_other_ref)):
            low_in, low_grad = doubled(ref[...].astype(F32), lane, rank)
            mask = source[:, feat + cols :].astype(F32) == wanted
            grad_t = jnp.transpose(jnp.where(mask, ADAPTER_SCALE * low_grad, 0.0)).astype(BF16)
            in_t = jnp.transpose(jnp.where(mask, ADAPTER_SCALE * low_in, 0.0)).astype(BF16)
            down_term = dot(grad_t, source[:, :feat])
            up_term = dot(in_t, source[:, feat : feat + cols])
            down, up = (down_term, up_term) if down is None else (down + down_term, up + up_term)
        for i in range(2):
            out = outs[s + i]
            out[:, :feat] = down[i * rank : (i + 1) * rank, :].astype(out.dtype)
            out[:, feat:] = up[i * rank : (i + 1) * rank, :].astype(out.dtype)


def grads(dp, core, x, x_other, low, low_other, n_dp, rank, feat, cols):
    width = feat + cols
    return pl.pallas_call(
        functools.partial(grad_kernel, n_dp, rank, feat, cols),
        in_specs=[SMEM] * 2 + [VMEM] * 4,
        out_specs=[VMEM] * n_dp,
        out_shape=[shaped((rank, width), F32)] + [shaped((rank, width), BF16)] * (n_dp - 1),
        compiler_params=params(32),
        cost_estimate=cost(4 * LIVE * rank * n_dp * width, 4 * LIVE * width + 4 * rank * n_dp * width),
        name="grads",
    )(dp, core, x, x_other, low, low_other)


def panel_kernel(order, count, place_ref, x_ref, other_ref, *refs):
    pieces, refs = refs[:count], refs[count:]
    half = refs[-1].shape[1]
    panels = pieces[0].shape[1] // half
    adds, outs = refs[:-panels], refs[-panels:]
    deep = pieces[0].shape[0]
    for n, source in enumerate((x_ref, other_ref)):
        total = None
        for piece, m in zip(pieces, order):
            col = pl.multiple_of((place_ref[0] ^ m) * deep, min(deep, 128))
            term = dot(source[:, pl.ds(col, deep)], piece[...])
            total = term if total is None else total + term
        for i, out in enumerate(outs):
            value = total[:, i * half : (i + 1) * half]
            if i < len(adds):
                value = value + adds[i][n * LIVE : (n + 1) * LIVE, :].astype(F32)
            out[n * LIVE : (n + 1) * LIVE, :] = value.astype(BF16)


def panel_product(order, place, x, x_other, pieces, half, adds=()):
    feat, wide = len(pieces) * pieces[0].shape[0], pieces[0].shape[1]
    shapes = [shaped((2 * LIVE, half), BF16)] * (wide // half)
    return pl.pallas_call(
        functools.partial(panel_kernel, order, len(pieces)),
        in_specs=[SMEM] + [VMEM] * (2 + len(pieces) + len(adds)),
        out_specs=[VMEM] * len(shapes),
        out_shape=shapes,
        compiler_params=params(24),
        cost_estimate=cost(4 * LIVE * feat * wide, 4 * LIVE * feat + 2 * feat * wide),
        name="panel",
    )(place, x, x_other, *pieces, *adds)


def settle_kernel(core_ref, own_ref, got_ref, down_ref, up_ref):
    feat = down_ref.shape[2]
    own, got = own_ref[...].astype(F32), got_ref[...].astype(F32)
    first = core_ref[0] == 0
    down_ref[0], up_ref[0] = jnp.where(first, own, got)[:, :feat], jnp.where(first, own, got)[:, feat:]
    down_ref[1], up_ref[1] = jnp.where(first, got, own)[:, :feat], jnp.where(first, got, own)[:, feat:]


def settle(core, own, got, feat):
    rank, width = own.shape
    return pl.pallas_call(
        settle_kernel,
        in_specs=[SMEM] + [VMEM] * 2,
        out_specs=[VMEM] * 2,
        out_shape=[shaped((2, rank, feat), F32), shaped((2, rank, width - feat), F32)],
        compiler_params=params(16),
        cost_estimate=cost(own.size, 12 * own.size),
        name="settle",
    )(core, own, got)


def base_kernel(n_dp, rank, blocks, at_ref, dp_ref, fill_ref, tenant_ref, x_ref, w_ref, low_ref, *refs):
    b_refs, out_ref = refs[:n_dp], refs[n_dp]
    lanes = 2 * rank
    tenant = tenant_lanes(fill_ref, tenant_ref, blocks, lanes)
    lane = lax.broadcasted_iota(I32, (LIVE, lanes), 1)
    low_in, _ = doubled(low_ref[...].astype(F32), lane, rank)
    total = dot(x_ref[...], w_ref[...])
    for s in range(n_dp):
        mask = owner_mask(tenant, lane, (dp_ref[0] + n_dp - s) % n_dp, rank)
        total = total + dot(jnp.where(mask, ADAPTER_SCALE * low_in, 0.0).astype(BF16), b_refs[s][...])
    out_ref[...] = total


def base_product(at, dp, fill, tenant, x, base_weight, low, b_list, feat, blocks, rank):
    n_dp = len(b_list)
    cols = base_weight.shape[1]
    whole = lambda i, at: (0, 0)
    return pl.pallas_call(
        functools.partial(base_kernel, n_dp, rank, blocks),
        grid_spec=pltpu.PrefetchScalarGridSpec(
            num_scalar_prefetch=1,
            grid=(1,),
            in_specs=[SMEM] * 3
            + [pl.BlockSpec((LIVE, feat), whole), pl.BlockSpec((feat, cols), lambda i, at: (at[0], 0)), pl.BlockSpec((LIVE, 2 * rank), whole)]
            + [pl.BlockSpec((2 * rank, cols), whole)] * n_dp,
            out_specs=pl.BlockSpec((LIVE, cols), whole),
        ),
        out_shape=shaped((LIVE, cols), F32),
        compiler_params=params(24),
        cost_estimate=cost(2 * LIVE * feat * cols, 2 * feat * (LIVE + cols) + 4 * LIVE * cols),
        name="base",
    )(at, dp, fill, tenant, x, base_weight, low, *b_list)


def swap_kernel(*refs):
    ins, out_ref = refs[:-1], refs[-1]
    total = ins[0][LIVE:, :].astype(F32)
    for ref in ins[1:]:
        total = total + ref[LIVE:, :].astype(F32)
    out_ref[...] = total


def other_rows(parts):
    half = parts[0].shape[1]
    return pl.pallas_call(
        swap_kernel,
        in_specs=[VMEM] * len(parts),
        out_specs=VMEM,
        out_shape=shaped((LIVE, half), F32),
        compiler_params=params(24),
        cost_estimate=cost(LIVE * half, 2 * LIVE * half * len(parts)),
        name="other_rows",
    )(*parts)


def out_kernel(count, blocks, block, core_ref, fill_ref, base_ref, *refs):
    parts, rest, out_ref, held = refs[:count], refs[count:-2], refs[-2], refs[-1]
    half = rest[0].shape[1]
    own = parts[0][:LIVE, :].astype(F32)
    for part in parts[1:]:
        own = own + part[:LIVE, :].astype(F32)
    other = rest[0][...].astype(F32)
    for part in rest[1:]:
        other = other + part[...].astype(F32)
    first = core_ref[0] == 0
    held[:, :half] = (base_ref[:, :half] + jnp.where(first, own, other)).astype(BF16)
    held[:, half:] = (base_ref[:, half:] + jnp.where(first, other, own)).astype(BF16)
    row = lax.broadcasted_iota(I32, (block, LIVE), 0)
    col = lax.broadcasted_iota(I32, (block, LIVE), 1)
    for b, start in enumerate(starts_of(fill_ref, blocks)):
        hit = (col == row + start) & (row < fill_ref[0, b])
        pick = jnp.where(hit, 1.0, 0.0).astype(BF16)
        out_ref[b * block : (b + 1) * block, :] = dot(pick, held[...]).astype(BF16)


def finish(core, fill, base, parts, others, rows, blocks):
    cols = base.shape[1]
    count = len(parts)
    return pl.pallas_call(
        functools.partial(out_kernel, count, blocks, rows // blocks),
        in_specs=[SMEM] * 2 + [VMEM] * (1 + count + len(others)),
        out_specs=VMEM,
        out_shape=shaped((rows, cols), BF16),
        scratch_shapes=[pltpu.VMEM((LIVE, cols), BF16)],
        compiler_params=params(24),
        cost_estimate=cost(2 * LIVE * rows * cols, 4 * LIVE * cols + 2 * LIVE * cols * count + 2 * rows * cols),
        name="finish",
    )(core, fill, base, *parts, *others)


def body(sizes, tokens, base_weight, adapter_a, adapter_b, cotangent, block_tenant_index, block_fill):
    n_t, n_dp, n_pipe = sizes["tensor"], sizes["dp"], sizes["pipe"]
    planes = sizes["groups"] * n_dp
    rows, feat = tokens.shape
    cols = base_weight.shape[1]
    half = cols // n_pipe
    blocks = block_tenant_index.shape[0]
    pair, rank = adapter_a.shape[:2]
    me_t, me_pipe, me_dp = lax.axis_index("tensor"), lax.axis_index("pipe"), lax.axis_index("dp")
    q = lax.axis_index("groups") * n_dp + me_dp
    part_rows = feat // planes
    scalar = lambda v: v.astype(I32).reshape(1)
    dp, core, at, place = scalar(me_dp), scalar(me_pipe), scalar(me_t), scalar(q)

    own_a, own_b = adapter_a.reshape(pair * rank, feat), adapter_b.reshape(pair * rank, cols)
    a_list = [own_a] + [shift(own_a, "dp", n_dp, s) for s in range(1, n_dp)]
    b_list = [own_b] + [shift(own_b, "dp", n_dp, s) for s in range(1, n_dp)]
    panel_at = place if planes == 4 else jnp.zeros_like(place)

    def share(k):
        return lax.dynamic_slice(base_weight, (k * feat + q * part_rows, me_pipe * half), (part_rows, half))

    def gathered(piece):
        if planes != 4:
            return [lax.all_gather(piece, ("groups", "dp"), axis=0, tiled=True)], [0]
        return [piece] + [flip(piece, ("groups", "dp"), planes, m) for m in range(1, 4)], [0, 1, 2, 3]

    def add_flipped(low, mask, *before):
        return (low.astype(F32) + flip(after(low, *before), "tensor", n_t, mask).astype(F32)).astype(BF16)

    if n_t == 4:
        share_3 = share(me_t ^ 3)
        weight = {3: flip(share_3, "tensor", n_t, 3), 1: flip(share(me_t ^ 1), "tensor", n_t, 1)}
        weight[2] = flip(after(share(me_t ^ 2), weight[3]), "tensor", n_t, 2)
        x = pack(after(block_fill, share_3), block_tenant_index, tokens, cotangent, blocks, 2 * rank)
        x_other = flip(after(x, weight[3], weight[1], *a_list[1:], *b_list[1:]), "pipe", n_pipe, 1)
        pieces, order = gathered(weight[3])
        pieces[0] = after(pieces[0], weight[1], weight[2])
        (y,) = panel_product(order, panel_at, x, x_other, pieces, half)
        add = flip(y, "tensor", n_t, 1)
        low = low_part(after(dp, y), block_fill, block_tenant_index, x, a_list, b_list, blocks, rank)
        low = add_flipped(low, 1)
        pieces, order = gathered(after(weight[2], y))
        (y_2,) = panel_product(order, panel_at, x, x_other, pieces, half, adds=[add])
        low = add_flipped(low, 2)
        pieces, order = gathered(after(weight[1], add, *pieces))
        (y_1,) = panel_product(order, panel_at, x, x_other, pieces, half)
        parts = [flip(y_2, "tensor", n_t, 2), flip(y_1, "tensor", n_t, 1)]
    else:
        x = pack(block_fill, block_tenant_index, tokens, cotangent, blocks, 2 * rank)
        x_other = flip(x, "pipe", n_pipe, 1)
        low = low_part(dp, block_fill, block_tenant_index, x, a_list, b_list, blocks, rank)
        mask = 1
        while mask < n_t:
            low, mask = add_flipped(low, mask), 2 * mask
        steps = range(1, n_t)
        weights = [shift(share((me_t + s) % n_t), "tensor", n_t, s) for s in steps]
        pieces, order = gathered(jnp.concatenate(weights, axis=1))
        ys = panel_product(order, panel_at, x, x_other, pieces, half)
        parts = [shift(y, "tensor", n_t, -s) for s, y in zip(steps, ys)]
    others = [flip(other_rows(parts), "pipe", n_pipe, 1)]

    low_other = flip(low, "pipe", n_pipe, 1)
    mine, *sends = grads(dp, core, x, x_other, low, low_other, n_dp, rank, feat, cols)
    for s, send in enumerate(sends):
        mine = mine + shift(after(send, *pieces), "dp", n_dp, s + 1).astype(F32)
    mine = mine.astype(BF16)
    down_out, up_out = settle(core, mine, flip(mine, "pipe", n_pipe, 1), feat)

    base = base_product(at, dp, block_fill, block_tenant_index, x, base_weight, low, b_list, feat, blocks, rank)
    out = finish(core, block_fill, base, parts, others, rows, blocks)
    return out, down_out, up_out


def solution(mesh):
    placed = (
        P(("groups", "dp", "pipe"), "tensor"),
        P(None, "tensor"),
        P(("groups", "dp"), None, "tensor"),
        P(("groups", "dp"), None, "tensor"),
        P(("groups", "dp", "pipe"), "tensor"),
        P(("groups", "dp", "pipe")),
        P(("groups", "dp", "pipe"), None),
    )
    return jax.shard_map(
        functools.partial(body, dict(mesh.shape)),
        mesh=mesh,
        in_specs=placed,
        out_specs=(
            P(("groups", "dp", "pipe"), "tensor"),
            P(("groups", "dp"), None, "tensor"),
            P(("groups", "dp"), None, "tensor"),
        ),
        check_vma=False,
    )
```

time: 105 us -> 103 us (0.981)
  local copies, waits for them, and re-layouts: 3.23 us -> 5.51 us
  Pallas kernels: 16.8 us -> 15.2 us
  waiting for transfers between devices: 55.1 us -> 53.5 us
  other arithmetic: 1.62 us -> 0.13 us
    ppermute x21, waiting for transfers between devices: 55.1 us -> 51.5 us  [flip(): return lax.ppermute(x, names, [(i, i ^ mask) for i in range(count)])]
    unnamed x12 -> x20, local copies, waits for them, and re-layouts: 1.91 us -> 4.35 us
    ppermute x2 -> x3, waiting for transfers between devices: 0.01 us -> 1.97 us  [shift(): lax.ppermute(x, name, [(i, (i + step) % count) for i in range(count)])]
    pallas_call x6, Pallas kernels: 10.4 us -> 8.78 us  [the longest x3 3.74 us: panel_product(): pl.pallas_call(functools.partial(panel_kernel, order, len(pieces)), in_sp...]
    concatenate x1 -> x0, other arithmetic: 1.22 us -> none  [body(): own_ab = jnp.concatenate([own_a, own_b], axis=1)]
    ppermute x2 -> x3, starting transfers between devices: 3.58 us -> 4.75 us  [shift(): lax.ppermute(x, name, [(i, (i + step) % count) for i in range(count)])]
  transfers between devices with their start and end apart: 23 -> 24, of which waited for: 13 -> 15; matrix products, arithmetic and copies ran while one was open for 2% -> 1% of each run, Pallas kernels for 12% -> 12%
where the time goes in v6:
time: 103 us
  waiting for transfers between devices  53.5 us (52%)
  starting transfers between devices  28 us (27%)
  Pallas kernels  15.2 us (15%)
  local copies, waits for them, and re-layouts  5.51 us (5%)
    ppermute x21, waiting for transfers between devices, flip(): return lax.ppermute(x, names, [(i, i ^ mask) for i in range(count)])  51.5 us
    ppermute x21, starting transfers between devices, flip(): return lax.ppermute(x, names, [(i, i ^ mask) for i in range(count)])  23.3 us
    ppermute x3, starting transfers between devices, shift(): lax.ppermute(x, name, [(i, (i + step) % count) for i in range(count)])  4.75 us
    unnamed x20, local copies, waits for them, and re-layouts  4.35 us
    pallas_call x3, Pallas kernels, panel_product(): pl.pallas_call(functools.partial(panel_kernel, order, len(pieces)), in_sp...  3.74 us
    pallas_call x1, Pallas kernels, pack(): pl.pallas_call(functools.partial(pack_kernel, blocks, rows // blocks), in...  2.82 us
    pallas_call x1, Pallas kernels, low_part(): pl.pallas_call(functools.partial(low_kernel, n_dp, rank, blocks), in_spec...  2.16 us
    pallas_call x1, Pallas kernels, base_product(): pl.pallas_call(functools.partial(base_kernel, n_dp, rank, blocks), grid_s...  2.13 us
  transfers between devices with their start and end apart: 24, of which 15 were waited for; matrix products, arithmetic and copies ran while one was open for 1% of the time, Pallas kernels for 12%

profile of v6, /device:TPU:0, one launch (start us, length us, event | category | flops | bytes accessed | tf_op | source)
XLA Modules:
  0.0 103.1 jit_solution(10592848651337429255)
XLA Ops:
  0.6 3.0 %collective-permute-start.2 = (bf16[128,2048]{1,0:T(8,128)(2,1)}, bf16[128,2048]{1,0:T(8,128)(2,1)S(1)}, u32[]{:S(2)}, u32[]{:S(2)}) collective-permute-start(bf16[128,2048]{1,0:T(8,128)(2,1)} %bitcast.8), channel_id=1, source_target_pairs={{0,2},{2,0},{1,3},{3,1},{4,6},{6,4},{5,7},{7,5},{8,10},{10,8},{9,1... | collective-permute-start | bytes 1572872 | tf_op jit(solution)/shard_map/ppermute | solution.py:29
  4.8 1.6 %collective-permute-start.1 = (bf16[512,256]{1,0:T(8,128)(2,1)S(1)}, bf16[512,256]{1,0:T(8,128)(2,1)S(1)}, u32[]{:S(2)}, u32[]{:S(2)}) collective-permute-start(bf16[512,256]{1,0:T(8,128)(2,1)S(1)} %get-tuple-element.28), channel_id=1, source_target_pairs={{0,4},{4,0},{8,12},{12,8},{1,5},{5,1},{9,13},{13,9},{2,6},{6,2},{1... | collective-permute-start | bytes 786440 | tf_op jit(solution)/shard_map/ppermute | solution.py:33
  6.4 2.5 %collective-permute-start = (bf16[512,256]{1,0:T(8,128)(2,1)S(1)}, bf16[512,256]{1,0:T(8,128)(2,1)S(1)}, u32[]{:S(2)}, u32[]{:S(2)}) collective-permute-start(bf16[512,256]{1,0:T(8,128)(2,1)S(1)} %get-tuple-element.29), channel_id=1, source_target_pairs={{0,12},{4,8},{8,4},{12,0},{1,13},{5,9},{9,5},{13,1},{2,14},{6,10},... | collective-permute-start | bytes 786440 | tf_op jit(solution)/shard_map/ppermute | solution.py:33
  9.4 1.9 %copy-done = bf16[768,2048]{1,0:T(8,128)(2,1)S(1)} copy-done((bf16[768,2048]{1,0:T(8,128)(2,1)S(1)}, bf16[768,2048]{1,0:T(8,128)(2,1)}, u32[]{:S(2)}) %copy-start) | copy-done | bytes 3145752
  13.8 2.8 %pack.1.x_ref.own_ref = bf16[512,2688]{1,0:T(8,128)(2,1)S(1)} custom-call(s32[1,6]{1,0:T(1,128)S(1)} %copy-done.4, s32[6]{0:T(128)S(1)} %copy-done.6, bf16[768,2048]{1,0:T(8,128)(2,1)S(1)} %copy-done, bf16[768,512]{1,0:T(8,128)(2,1)S(1)} %copy-done.1), custom_call_target="tpu_custom_call" | custom-call | flops 1 | bytes 1 | tf_op jit(solution)/shard_map/pack/pallas_call | solution.py:82
  16.6 2.0 %collective-permute-done.3.refs_3_.refs_1_ = bf16[128,512]{1,0:T(8,128)(2,1)S(1)} collective-permute-done((bf16[128,512]{1,0:T(8,128)(2,1)}, bf16[128,512]{1,0:T(8,128)(2,1)S(1)}, u32[]{:S(2)}, u32[]{:S(2)}) %collective-permute-start.3) | collective-permute-done | bytes 131104 | tf_op jit(solution)/shard_map/ppermute | solution.py:29
  18.6 1.8 %collective-permute-done.refs_0_ = bf16[512,256]{1,0:T(8,128)(2,1)S(1)} collective-permute-done((bf16[512,256]{1,0:T(8,128)(2,1)S(1)}, bf16[512,256]{1,0:T(8,128)(2,1)S(1)}, u32[]{:S(2)}, u32[]{:S(2)}) %collective-permute-start) | collective-permute-done | bytes 262176 | tf_op jit(solution)/shard_map/ppermute | solution.py:33
  20.4 1.8 %collective-permute-start.5 = (bf16[512,256]{1,0:T(8,128)(2,1)S(1)}, bf16[512,256]{1,0:T(8,128)(2,1)S(1)}, u32[]{:S(2)}, u32[]{:S(2)}) collective-permute-start(bf16[512,256]{1,0:T(8,128)(2,1)S(1)} %get-tuple-element.17), channel_id=1, source_target_pairs={{0,8},{4,12},{8,0},{12,4},{1,9},{5,13},{9,1},{13,5},{2,10},{6,14},... | collective-permute-start | bytes 786440 | tf_op jit(solution)/shard_map/ppermute | solution.py:33
  22.1 1.9 %collective-permute-start.8 = (bf16[512,256]{1,0:T(8,128)(2,1)S(1)}, bf16[512,256]{1,0:T(8,128)(2,1)S(1)}, u32[]{:S(2)}, u32[]{:S(2)}) collective-permute-start(bf16[512,256]{1,0:T(8,128)(2,1)S(1)} %collective-permute-done.refs_0_), channel_id=1, source_target_pairs={{0,18},{2,16},{16,2},{18,0},{1,19},{3,17},{17,3},{19,1},{4,22},{6,... | collective-permute-start | bytes 786440 | tf_op jit(solution)/shard_map/ppermute | solution.py:33
  25.6 10.0 %collective-permute-done.5.refs_0_ = bf16[512,256]{1,0:T(8,128)(2,1)S(1)} collective-permute-done((bf16[512,256]{1,0:T(8,128)(2,1)S(1)}, bf16[512,256]{1,0:T(8,128)(2,1)S(1)}, u32[]{:S(2)}, u32[]{:S(2)}) %collective-permute-start.5) | collective-permute-done | bytes 262176 | tf_op jit(solution)/shard_map/ppermute | solution.py:33
  35.6 1.5 %collective-permute-done.7.refs_2_ = bf16[512,256]{1,0:T(8,128)(2,1)S(1)} collective-permute-done((bf16[512,256]{1,0:T(8,128)(2,1)S(1)}, bf16[512,256]{1,0:T(8,128)(2,1)S(1)}, u32[]{:S(2)}, u32[]{:S(2)}) %collective-permute-start.7) | collective-permute-done | bytes 262176 | tf_op jit(solution)/shard_map/ppermute | solution.py:33
  39.5 1.7 %collective-permute-start.13 = (bf16[512,256]{1,0:T(8,128)(2,1)S(1)}, bf16[512,256]{1,0:T(8,128)(2,1)S(1)}, u32[]{:S(2)}, u32[]{:S(2)}) collective-permute-start(bf16[512,256]{1,0:T(8,128)(2,1)S(1)} %collective-permute-done.5.refs_0_), channel_id=1, source_target_pairs={{0,18},{2,16},{16,2},{18,0},{1,19},{3,17},{17,3},{19,1},{4,22},{6,... | collective-permute-start | bytes 786440 | tf_op jit(solution)/shard_map/ppermute | solution.py:33
  43.0 2.2 %low_part.1 = bf16[512,128]{1,0:T(8,128)(2,1)S(1)} custom-call(s32[1]{0:T(128)} %bitcast.2.dp_ref, s32[1,6]{1,0:T(1,128)S(1)} %copy-done.4, s32[6]{0:T(128)S(1)} %copy-done.7, bf16[512,2688]{1,0:T(8,128)(2,1)S(1)} %pack.1.x_ref.own_ref, bf16[128,2048]{1,0:T(8,128)(2,1)S(1)} %bitcast.9, bf16[128,2048]{1,0:T(8,128)(2,1)S(1)} %collective-permute-done.2.refs_1_, ...), custom_call_target="tpu_custom_call" | custom-call | flops 1 | bytes 1 | tf_op jit(solution)/shard_map/low_part/pallas_call | solution.py:117
  46.3 3.4 %collective-permute-done.13.refs_3_ = bf16[512,256]{1,0:T(8,128)(2,1)S(1)} collective-permute-done((bf16[512,256]{1,0:T(8,128)(2,1)S(1)}, bf16[512,256]{1,0:T(8,128)(2,1)S(1)}, u32[]{:S(2)}, u32[]{:S(2)}) %collective-permute-start.13) | collective-permute-done | bytes 262176 | tf_op jit(solution)/shard_map/ppermute | solution.py:33
  49.6 4.2 %collective-permute-done.12.refs_2_ = bf16[512,256]{1,0:T(8,128)(2,1)S(1)} collective-permute-done((bf16[512,256]{1,0:T(8,128)(2,1)S(1)}, bf16[512,256]{1,0:T(8,128)(2,1)S(1)}, u32[]{:S(2)}, u32[]{:S(2)}) %collective-permute-start.12) | collective-permute-done | bytes 262176 | tf_op jit(solution)/shard_map/ppermute | solution.py:33
  54.0 1.4 %collective-permute-start.18 = (bf16[512,256]{1,0:T(8,128)(2,1)S(1)}, bf16[512,256]{1,0:T(8,128)(2,1)S(1)}, u32[]{:S(2)}, u32[]{:S(2)}) collective-permute-start(bf16[512,256]{1,0:T(8,128)(2,1)S(1)} %collective-permute-done.1.refs_0_), channel_id=1, source_target_pairs={{0,18},{2,16},{16,2},{18,0},{1,19},{3,17},{17,3},{19,1},{4,22},{6,... | collective-permute-start | bytes 786440 | tf_op jit(solution)/shard_map/ppermute | solution.py:33
  59.5 2.3 %collective-permute-start.15 = (bf16[1024,256]{1,0:T(8,128)(2,1)S(1)}, bf16[1024,256]{1,0:T(8,128)(2,1)S(1)}, u32[]{:S(2)}, u32[]{:S(2)}) collective-permute-start(bf16[1024,256]{1,0:T(8,128)(2,1)S(1)} %panel.4), channel_id=1, source_target_pairs={{0,8},{4,12},{8,0},{12,4},{1,9},{5,13},{9,1},{13,5},{2,10},{6,14},... | collective-permute-start | bytes 1572872 | tf_op jit(solution)/shard_map/ppermute | solution.py:33
  61.8 2.3 %collective-permute-done.18.refs_3_ = bf16[512,256]{1,0:T(8,128)(2,1)S(1)} collective-permute-done((bf16[512,256]{1,0:T(8,128)(2,1)S(1)}, bf16[512,256]{1,0:T(8,128)(2,1)S(1)}, u32[]{:S(2)}, u32[]{:S(2)}) %collective-permute-start.18) | collective-permute-done | bytes 262176 | tf_op jit(solution)/shard_map/ppermute | solution.py:33
  64.1 4.5 %collective-permute-done.17.refs_2_ = bf16[512,256]{1,0:T(8,128)(2,1)S(1)} collective-permute-done((bf16[512,256]{1,0:T(8,128)(2,1)S(1)}, bf16[512,256]{1,0:T(8,128)(2,1)S(1)}, u32[]{:S(2)}, u32[]{:S(2)}) %collective-permute-start.17) | collective-permute-done | bytes 262176 | tf_op jit(solution)/shard_map/ppermute | solution.py:33
  71.0 6.7 %collective-permute-done.10 = bf16[512,128]{1,0:T(8,128)(2,1)S(1)} collective-permute-done((bf16[512,128]{1,0:T(8,128)(2,1)S(1)}, bf16[512,128]{1,0:T(8,128)(2,1)S(1)}, u32[]{:S(2)}, u32[]{:S(2)}) %collective-permute-start.10) | collective-permute-done | bytes 131104 | tf_op jit(solution)/shard_map/ppermute | solution.py:33
  81.5 6.9 %collective-permute-done.15.refs_0_ = bf16[1024,256]{1,0:T(8,128)(2,1)S(1)} collective-permute-done((bf16[1024,256]{1,0:T(8,128)(2,1)S(1)}, bf16[1024,256]{1,0:T(8,128)(2,1)S(1)}, u32[]{:S(2)}, u32[]{:S(2)}) %collective-permute-start.15) | collective-permute-done | bytes 524320 | tf_op jit(solution)/shard_map/ppermute | solution.py:33
  88.3 8.6 %collective-permute-done.19.refs_1_ = bf16[1024,256]{1,0:T(8,128)(2,1)S(1)} collective-permute-done((bf16[1024,256]{1,0:T(8,128)(2,1)S(1)}, bf16[1024,256]{1,0:T(8,128)(2,1)S(1)}, u32[]{:S(2)}, u32[]{:S(2)}) %collective-permute-start.19) | collective-permute-done | bytes 524320 | tf_op jit(solution)/shard_map/ppermute | solution.py:33
  97.7 2.1 %base.1.base_ref = f32[512,512]{1,0:T(8,128)S(1)} custom-call(s32[1]{0:T(128)} %bitcast.1.at_ref, s32[1]{0:T(128)} %bitcast.2.dp_ref, s32[1,6]{1,0:T(1,128)S(1)} %copy-done.5, s32[6]{0:T(128)S(1)} %copy-done.7, bf16[512,2688]{1,0:T(8,128)(2,1)S(1)} %pack.1.x_ref.own_ref, bf16[8192,512]{1,0:T(8,128)(2,1)S(1)} %bitcast.7, ...), custom_call_target="tpu_custom_call" | custom-call | flops 1 | bytes 1 | tf_op jit(solution)/shard_map/base/pallas_call | solution.py:238
  101.0 2.1 %finish.1 = bf16[768,512]{1,0:T(8,128)(2,1)} custom-call(s32[1]{0:T(128)} %bitcast.core_ref, s32[1,6]{1,0:T(1,128)S(1)} %copy-done.5, f32[512,512]{1,0:T(8,128)S(1)} %base.1.base_ref, bf16[1024,256]{1,0:T(8,128)(2,1)S(1)} %collective-permute-done.15.refs_0_, bf16[1024,256]{1,0:T(8,128)(2,1)S(1)} %collective-permute-done.19.refs_1_, ...), custom_call_target="tpu_custom_call" | custom-call | flops 1 | bytes 1 | tf_op jit(solution)/shard_map/finish/pallas_call | solution.py:299
  (59 shorter events, 23.3 us)
Async XLA Ops:
  0.6 19.7 %collective-permute-start.2 = (bf16[128,2048]{1,0:T(8,128)(2,1)}, bf16[128,2048]{1,0:T(8,128)(2,1)S(1)}, u32[]{:S(2)}, u32[]{:S(2)}) collective-permute-start(bf16[128,2048]{1,0:T(8,128)(2,1)} %bitcast.8), channel_id=1, source_target_pairs={{0,2},{2,0},{1,3},{3,1},{4,6},{6,4},{5,7},{7,5},{8,10},{10,8},{9,1... | collective-permute-start | bytes 1572872 | tf_op jit(solution)/shard_map/ppermute | solution.py:29
  4.8 13.8 %collective-permute-start.1 = (bf16[512,256]{1,0:T(8,128)(2,1)S(1)}, bf16[512,256]{1,0:T(8,128)(2,1)S(1)}, u32[]{:S(2)}, u32[]{:S(2)}) collective-permute-start(bf16[512,256]{1,0:T(8,128)(2,1)S(1)} %get-tuple-element.28), channel_id=1, source_target_pairs={{0,4},{4,0},{8,12},{12,8},{1,5},{5,1},{9,13},{13,9},{2,6},{6,2},{1... | collective-permute-start | bytes 786440 | tf_op jit(solution)/shard_map/ppermute | solution.py:33
  6.4 13.9 %collective-permute-start = (bf16[512,256]{1,0:T(8,128)(2,1)S(1)}, bf16[512,256]{1,0:T(8,128)(2,1)S(1)}, u32[]{:S(2)}, u32[]{:S(2)}) collective-permute-start(bf16[512,256]{1,0:T(8,128)(2,1)S(1)} %get-tuple-element.29), channel_id=1, source_target_pairs={{0,12},{4,8},{8,4},{12,0},{1,13},{5,9},{9,5},{13,1},{2,14},{6,10},... | collective-permute-start | bytes 786440 | tf_op jit(solution)/shard_map/ppermute | solution.py:33
  8.9 9.7 %collective-permute-start.3 = (bf16[128,512]{1,0:T(8,128)(2,1)}, bf16[128,512]{1,0:T(8,128)(2,1)S(1)}, u32[]{:S(2)}, u32[]{:S(2)}) collective-permute-start(bf16[128,512]{1,0:T(8,128)(2,1)} %bitcast.10), channel_id=1, source_target_pairs={{0,2},{2,0},{1,3},{3,1},{4,6},{6,4},{5,7},{7,5},{8,10},{10,8},{9,1... | collective-permute-start | bytes 393224 | tf_op jit(solution)/shard_map/ppermute | solution.py:29
  20.4 16.8 %collective-permute-start.4 = (bf16[512,2688]{1,0:T(8,128)(2,1)S(1)}, bf16[512,2688]{1,0:T(8,128)(2,1)S(1)}, u32[]{:S(2)}, u32[]{:S(2)}) collective-permute-start(bf16[512,2688]{1,0:T(8,128)(2,1)S(1)} %pack.1.x_ref.own_ref), channel_id=1, source_target_pairs={{0,1},{1,0},{2,3},{3,2},{4,5},{5,4},{6,7},{7,6},{8,9},{9,8},{10,11... | collective-permute-start | bytes 8257544 | tf_op jit(solution)/shard_map/ppermute | solution.py:33
  20.4 15.2 %collective-permute-start.5 = (bf16[512,256]{1,0:T(8,128)(2,1)S(1)}, bf16[512,256]{1,0:T(8,128)(2,1)S(1)}, u32[]{:S(2)}, u32[]{:S(2)}) collective-permute-start(bf16[512,256]{1,0:T(8,128)(2,1)S(1)} %get-tuple-element.17), channel_id=1, source_target_pairs={{0,8},{4,12},{8,0},{12,4},{1,9},{5,13},{9,1},{13,5},{2,10},{6,14},... | collective-permute-start | bytes 786440 | tf_op jit(solution)/shard_map/ppermute | solution.py:33
  22.1 13.5 %collective-permute-start.8 = (bf16[512,256]{1,0:T(8,128)(2,1)S(1)}, bf16[512,256]{1,0:T(8,128)(2,1)S(1)}, u32[]{:S(2)}, u32[]{:S(2)}) collective-permute-start(bf16[512,256]{1,0:T(8,128)(2,1)S(1)} %collective-permute-done.refs_0_), channel_id=1, source_target_pairs={{0,18},{2,16},{16,2},{18,0},{1,19},{3,17},{17,3},{19,1},{4,22},{6,... | collective-permute-start | bytes 786440 | tf_op jit(solution)/shard_map/ppermute | solution.py:33
  24.0 13.1 %collective-permute-start.7 = (bf16[512,256]{1,0:T(8,128)(2,1)S(1)}, bf16[512,256]{1,0:T(8,128)(2,1)S(1)}, u32[]{:S(2)}, u32[]{:S(2)}) collective-permute-start(bf16[512,256]{1,0:T(8,128)(2,1)S(1)} %collective-permute-done.refs_0_), channel_id=1, source_target_pairs={{0,16},{2,18},{16,0},{18,2},{1,17},{3,19},{17,1},{19,3},{4,20},{6,... | collective-permute-start | bytes 786440 | tf_op jit(solution)/shard_map/ppermute | solution.py:33
  24.5 12.7 %collective-permute-start.6 = (bf16[512,256]{1,0:T(8,128)(2,1)S(1)}, bf16[512,256]{1,0:T(8,128)(2,1)S(1)}, u32[]{:S(2)}, u32[]{:S(2)}) collective-permute-start(bf16[512,256]{1,0:T(8,128)(2,1)S(1)} %collective-permute-done.refs_0_), channel_id=1, source_target_pairs={{0,2},{2,0},{16,18},{18,16},{1,3},{3,1},{17,19},{19,17},{4,6},{6,4... | collective-permute-start | bytes 786440 | tf_op jit(solution)/shard_map/ppermute | solution.py:33
  38.5 15.5 %collective-permute-start.14 = (bf16[1024,256]{1,0:T(8,128)(2,1)S(1)}, bf16[1024,256]{1,0:T(8,128)(2,1)S(1)}, u32[]{:S(2)}, u32[]{:S(2)}) collective-permute-start(bf16[1024,256]{1,0:T(8,128)(2,1)S(1)} %panel.3), channel_id=1, source_target_pairs={{0,4},{4,0},{8,12},{12,8},{1,5},{5,1},{9,13},{13,9},{2,6},{6,2},{1... | collective-permute-start | bytes 1572872 | tf_op jit(solution)/shard_map/ppermute | solution.py:33
  39.5 10.2 %collective-permute-start.13 = (bf16[512,256]{1,0:T(8,128)(2,1)S(1)}, bf16[512,256]{1,0:T(8,128)(2,1)S(1)}, u32[]{:S(2)}, u32[]{:S(2)}) collective-permute-start(bf16[512,256]{1,0:T(8,128)(2,1)S(1)} %collective-permute-done.5.refs_0_), channel_id=1, source_target_pairs={{0,18},{2,16},{16,2},{18,0},{1,19},{3,17},{17,3},{19,1},{4,22},{6,... | collective-permute-start | bytes 786440 | tf_op jit(solution)/shard_map/ppermute | solution.py:33
  41.1 12.7 %collective-permute-start.12 = (bf16[512,256]{1,0:T(8,128)(2,1)S(1)}, bf16[512,256]{1,0:T(8,128)(2,1)S(1)}, u32[]{:S(2)}, u32[]{:S(2)}) collective-permute-start(bf16[512,256]{1,0:T(8,128)(2,1)S(1)} %collective-permute-done.5.refs_0_), channel_id=1, source_target_pairs={{0,16},{2,18},{16,0},{18,2},{1,17},{3,19},{17,1},{19,3},{4,20},{6,... | collective-permute-start | bytes 786440 | tf_op jit(solution)/shard_map/ppermute | solution.py:33
  42.4 11.5 %collective-permute-start.11 = (bf16[512,256]{1,0:T(8,128)(2,1)S(1)}, bf16[512,256]{1,0:T(8,128)(2,1)S(1)}, u32[]{:S(2)}, u32[]{:S(2)}) collective-permute-start(bf16[512,256]{1,0:T(8,128)(2,1)S(1)} %collective-permute-done.5.refs_0_), channel_id=1, source_target_pairs={{0,2},{2,0},{16,18},{18,16},{1,3},{3,1},{17,19},{19,17},{4,6},{6,4... | collective-permute-start | bytes 786440 | tf_op jit(solution)/shard_map/ppermute | solution.py:33
  45.1 12.3 %collective-permute-start.9 = (bf16[512,128]{1,0:T(8,128)(2,1)S(1)}, bf16[512,128]{1,0:T(8,128)(2,1)S(1)}, u32[]{:S(2)}, u32[]{:S(2)}) collective-permute-start(bf16[512,128]{1,0:T(8,128)(2,1)S(1)} %low_part.1), channel_id=1, source_target_pairs={{0,4},{4,0},{8,12},{12,8},{1,5},{5,1},{9,13},{13,9},{2,6},{6,2},{1... | collective-permute-start | bytes 393224 | tf_op jit(solution)/shard_map/ppermute | solution.py:33
  54.0 10.1 %collective-permute-start.18 = (bf16[512,256]{1,0:T(8,128)(2,1)S(1)}, bf16[512,256]{1,0:T(8,128)(2,1)S(1)}, u32[]{:S(2)}, u32[]{:S(2)}) collective-permute-start(bf16[512,256]{1,0:T(8,128)(2,1)S(1)} %collective-permute-done.1.refs_0_), channel_id=1, source_target_pairs={{0,18},{2,16},{16,2},{18,0},{1,19},{3,17},{17,3},{19,1},{4,22},{6,... | collective-permute-start | bytes 786440 | tf_op jit(solution)/shard_map/ppermute | solution.py:33
  55.4 13.2 %collective-permute-start.17 = (bf16[512,256]{1,0:T(8,128)(2,1)S(1)}, bf16[512,256]{1,0:T(8,128)(2,1)S(1)}, u32[]{:S(2)}, u32[]{:S(2)}) collective-permute-start(bf16[512,256]{1,0:T(8,128)(2,1)S(1)} %collective-permute-done.1.refs_0_), channel_id=1, source_target_pairs={{0,16},{2,18},{16,0},{18,2},{1,17},{3,19},{17,1},{19,3},{4,20},{6,... | collective-permute-start | bytes 786440 | tf_op jit(solution)/shard_map/ppermute | solution.py:33
  56.8 11.9 %collective-permute-start.16 = (bf16[512,256]{1,0:T(8,128)(2,1)S(1)}, bf16[512,256]{1,0:T(8,128)(2,1)S(1)}, u32[]{:S(2)}, u32[]{:S(2)}) collective-permute-start(bf16[512,256]{1,0:T(8,128)(2,1)S(1)} %collective-permute-done.1.refs_0_), channel_id=1, source_target_pairs={{0,2},{2,0},{16,18},{18,16},{1,3},{3,1},{17,19},{19,17},{4,6},{6,4... | collective-permute-start | bytes 786440 | tf_op jit(solution)/shard_map/ppermute | solution.py:33
  57.5 20.3 %collective-permute-start.10 = (bf16[512,128]{1,0:T(8,128)(2,1)S(1)}, bf16[512,128]{1,0:T(8,128)(2,1)S(1)}, u32[]{:S(2)}, u32[]{:S(2)}) collective-permute-start(bf16[512,128]{1,0:T(8,128)(2,1)S(1)} %add_convert_fusion.2), channel_id=1, source_target_pairs={{0,8},{4,12},{8,0},{12,4},{1,9},{5,13},{9,1},{13,5},{2,10},{6,14},... | collective-permute-start | bytes 393224 | tf_op jit(solution)/shard_map/ppermute | solution.py:33
  59.5 28.8 %collective-permute-start.15 = (bf16[1024,256]{1,0:T(8,128)(2,1)S(1)}, bf16[1024,256]{1,0:T(8,128)(2,1)S(1)}, u32[]{:S(2)}, u32[]{:S(2)}) collective-permute-start(bf16[1024,256]{1,0:T(8,128)(2,1)S(1)} %panel.4), channel_id=1, source_target_pairs={{0,8},{4,12},{8,0},{12,4},{1,9},{5,13},{9,1},{13,5},{2,10},{6,14},... | collective-permute-start | bytes 1572872 | tf_op jit(solution)/shard_map/ppermute | solution.py:33
  70.0 27.0 %collective-permute-start.19 = (bf16[1024,256]{1,0:T(8,128)(2,1)S(1)}, bf16[1024,256]{1,0:T(8,128)(2,1)S(1)}, u32[]{:S(2)}, u32[]{:S(2)}) collective-permute-start(bf16[1024,256]{1,0:T(8,128)(2,1)S(1)} %panel.5), channel_id=1, source_target_pairs={{0,4},{4,0},{8,12},{12,8},{1,5},{5,1},{9,13},{13,9},{2,6},{6,2},{1... | collective-permute-start | bytes 1572872 | tf_op jit(solution)/shard_map/ppermute | solution.py:33
  77.8 1.4 %collective-permute-start.21 = (bf16[512,128]{1,0:T(8,128)(2,1)S(1)}, bf16[512,128]{1,0:T(8,128)(2,1)S(1)}, u32[]{:S(2)}, u32[]{:S(2)}) collective-permute-start(bf16[512,128]{1,0:T(8,128)(2,1)S(1)} %add_convert_fusion.1.low_ref), channel_id=1, source_target_pairs={{0,1},{1,0},{2,3},{3,2},{4,5},{5,4},{6,7},{7,6},{8,9},{9,8},{10,11... | collective-permute-start | bytes 393224 | tf_op jit(solution)/shard_map/ppermute | solution.py:33
  80.3 16.8 %collective-permute-start.22 = (bf16[64,2560]{1,0:T(8,128)(2,1)S(1)}, bf16[64,2560]{1,0:T(8,128)(2,1)S(1)}, u32[]{:S(2)}, u32[]{:S(2)}) collective-permute-start(bf16[64,2560]{1,0:T(8,128)(2,1)S(1)} %get-tuple-element.24), channel_id=1, source_target_pairs={{0,2},{2,0},{1,3},{3,1},{4,6},{6,4},{5,7},{7,5},{8,10},{10,8},{9,1... | collective-permute-start | bytes 983048 | tf_op jit(solution)/shard_map/ppermute | solution.py:29
  97.0 4.1 %collective-permute-start.20 = (f32[512,256]{1,0:T(8,128)S(1)}, f32[512,256]{1,0:T(8,128)S(1)}, u32[]{:S(2)}, u32[]{:S(2)}) collective-permute-start(f32[512,256]{1,0:T(8,128)S(1)} %other_rows.1), channel_id=1, source_target_pairs={{0,1},{1,0},{2,3},{3,2},{4,5},{5,4},{6,7},{7,6},{8,9},{9,8},{10,11... | collective-permute-start | bytes 1572872 | tf_op jit(solution)/shard_map/ppermute | solution.py:33
  97.1 2.7 %collective-permute-start.23 = (bf16[64,2560]{1,0:T(8,128)(2,1)S(1)}, bf16[64,2560]{1,0:T(8,128)(2,1)S(1)}, u32[]{:S(2)}, u32[]{:S(2)}) collective-permute-start(bf16[64,2560]{1,0:T(8,128)(2,1)S(1)} %add_convert_fusion.own_ref), channel_id=1, source_target_pairs={{0,1},{1,0},{2,3},{3,2},{4,5},{5,4},{6,7},{7,6},{8,9},{9,8},{10,11... | collective-permute-start | bytes 983048 | tf_op jit(solution)/shard_map/ppermute | solution.py:33
  (10 other events, 87.6 us)

commit v7 on v6

--- a/solution.py
+++ b/solution.py
@@ -85,7 +85,7 @@
         out_specs=VMEM,
         out_shape=shaped((LIVE, feat + cols + lanes), BF16),
         scratch_shapes=[pltpu.VMEM((LIVE, rows), BF16)],
-        compiler_params=params(24),
+        compiler_params=params(56),
         cost_estimate=cost(2 * LIVE * rows * (feat + cols), 2 * (LIVE + rows) * (feat + cols)),
         name="pack",
     )(fill, tenant, tokens, cotangent)
@@ -339,23 +339,25 @@
         return (low.astype(F32) + flip(after(low, *before), "tensor", n_t, mask).astype(F32)).astype(BF16)
 
     if n_t == 4:
-        share_3 = share(me_t ^ 3)
-        weight = {3: flip(share_3, "tensor", n_t, 3), 1: flip(share(me_t ^ 1), "tensor", n_t, 1)}
+        share_1 = share(me_t ^ 1)
+        weight = {1: flip(share_1, "tensor", n_t, 1)}
+        weight[3] = flip(after(share(me_t ^ 3), weight[1]), "tensor", n_t, 3)
         weight[2] = flip(after(share(me_t ^ 2), weight[3]), "tensor", n_t, 2)
-        x = pack(after(block_fill, share_3), block_tenant_index, tokens, cotangent, blocks, 2 * rank)
-        x_other = flip(after(x, weight[3], weight[1], *a_list[1:], *b_list[1:]), "pipe", n_pipe, 1)
-        pieces, order = gathered(weight[3])
-        pieces[0] = after(pieces[0], weight[1], weight[2])
+        x = pack(after(block_fill, share_1), block_tenant_index, tokens, cotangent, blocks, 2 * rank)
+        x_other = flip(after(x, weight[1], *a_list[1:], *b_list[1:]), "pipe", n_pipe, 1)
+        pieces, order = gathered(weight[1])
+        low = low_part(dp, block_fill, block_tenant_index, x, a_list, b_list, blocks, rank)
+        pieces[0] = after(pieces[0], weight[3], low)
+        (y_1,) = panel_product(order, panel_at, x, x_other, pieces, half)
+        part_1 = flip(y_1, "tensor", n_t, 1)
+        pieces, order = gathered(after(weight[3], y_1))
+        pieces[0] = after(pieces[0], weight[2])
         (y,) = panel_product(order, panel_at, x, x_other, pieces, half)
         add = flip(y, "tensor", n_t, 1)
-        low = low_part(after(dp, y), block_fill, block_tenant_index, x, a_list, b_list, blocks, rank)
-        low = add_flipped(low, 1)
+        low = add_flipped(add_flipped(low, 1, y), 2, part_1)
         pieces, order = gathered(after(weight[2], y))
         (y_2,) = panel_product(order, panel_at, x, x_other, pieces, half, adds=[add])
-        low = add_flipped(low, 2)
-        pieces, order = gathered(after(weight[1], add, *pieces))
-        (y_1,) = panel_product(order, panel_at, x, x_other, pieces, half)
-        parts = [flip(y_2, "tensor", n_t, 2), flip(y_1, "tensor", n_t, 1)]
+        parts = [flip(y_2, "tensor", n_t, 2), part_1]
     else:
         x = pack(block_fill, block_tenant_index, tokens, cotangent, blocks, 2 * rank)
         x_other = flip(x, "pipe", n_pipe, 1)
@@ -368,7 +370,6 @@
         pieces, order = gathered(jnp.concatenate(weights, axis=1))
         ys = panel_product(order, panel_at, x, x_other, pieces, half)
         parts = [shift(y, "tensor", n_t, -s) for s, y in zip(steps, ys)]
-    others = [flip(other_rows(parts), "pipe", n_pipe, 1)]
 
     low_other = flip(low, "pipe", n_pipe, 1)
     mine, *sends = grads(dp, core, x, x_other, low, low_other, n_dp, rank, feat, cols)
@@ -378,6 +379,8 @@
     down_out, up_out = settle(core, mine, flip(mine, "pipe", n_pipe, 1), feat)
 
     base = base_product(at, dp, block_fill, block_tenant_index, x, base_weight, low, b_list, feat, blocks, rank)
+    parts[0] = after(parts[0], base)
+    others = [flip(other_rows(parts), "pipe", n_pipe, 1)]
     out = finish(core, block_fill, base, parts, others, rows, blocks)
     return out, down_out, up_out
 

time: 103 us -> 112 us (1.087)
  waiting for transfers between devices: 53.5 us -> 58.1 us
  starting transfers between devices: 28 us -> 31.3 us
  Pallas kernels: 15.2 us -> 18.3 us
  local copies, waits for them, and re-layouts: 5.51 us -> 2.96 us
    ppermute x3, waiting for transfers between devices: 1.97 us -> 5.66 us  [shift(): lax.ppermute(x, name, [(i, (i + step) % count) for i in range(count)])]
    ppermute x21, starting transfers between devices: 23.3 us -> 26.8 us  [flip(): return lax.ppermute(x, names, [(i, i ^ mask) for i in range(count)])]
    pallas_call x1, Pallas kernels: 2.82 us -> 5.88 us  [pack(): pl.pallas_call(functools.partial(pack_kernel, blocks, rows // blocks), in...]
    unnamed x20 -> x16, local copies, waits for them, and re-layouts: 4.35 us -> 1.8 us
  transfers between devices with their start and end apart: 24 -> 24, of which waited for: 15 -> 12; matrix products, arithmetic and copies ran while one was open for 1% -> 1% of each run, Pallas kernels for 12% -> 14%
where the time goes in v7:
time: 112 us
  waiting for transfers between devices  58.1 us (52%)
  starting transfers between devices  31.3 us (28%)
  Pallas kernels  18.3 us (16%)
  local copies, waits for them, and re-layouts  2.96 us (3%)
    ppermute x21, waiting for transfers between devices, flip(): return lax.ppermute(x, names, [(i, i ^ mask) for i in range(count)])  52.5 us
    ppermute x21, starting transfers between devices, flip(): return lax.ppermute(x, names, [(i, i ^ mask) for i in range(count)])  26.8 us
    pallas_call x1, Pallas kernels, pack(): pl.pallas_call(functools.partial(pack_kernel, blocks, rows // blocks), in...  5.88 us
    ppermute x3, waiting for transfers between devices, shift(): lax.ppermute(x, name, [(i, (i + step) % count) for i in range(count)])  5.66 us
    ppermute x3, starting transfers between devices, shift(): lax.ppermute(x, name, [(i, (i + step) % count) for i in range(count)])  4.55 us
    pallas_call x3, Pallas kernels, panel_product(): pl.pallas_call(functools.partial(panel_kernel, order, len(pieces)), in_sp...  3.75 us
  transfers between devices with their start and end apart: 24, of which 12 were waited for; matrix products, arithmetic and copies ran while one was open for 1% of the time, Pallas kernels for 14%

profile of v7, /device:TPU:0, one launch (start us, length us, event | category | flops | bytes accessed | tf_op | source)
XLA Modules:
  0.0 111.7 jit_solution(1253717234854331936)
XLA Ops:
  0.6 3.0 %collective-permute-start = (bf16[128,2048]{1,0:T(8,128)(2,1)}, bf16[128,2048]{1,0:T(8,128)(2,1)S(1)}, u32[]{:S(2)}, u32[]{:S(2)}) collective-permute-start(bf16[128,2048]{1,0:T(8,128)(2,1)} %bitcast.8), channel_id=1, source_target_pairs={{0,2},{2,0},{1,3},{3,1},{4,6},{6,4},{5,7},{7,5},{8,10},{10,8},{9,1... | collective-permute-start | bytes 1572872 | tf_op jit(solution)/shard_map/ppermute | solution.py:29
  4.8 1.6 %collective-permute-start.2 = (bf16[512,256]{1,0:T(8,128)(2,1)S(1)}, bf16[512,256]{1,0:T(8,128)(2,1)S(1)}, u32[]{:S(2)}, u32[]{:S(2)}) collective-permute-start(bf16[512,256]{1,0:T(8,128)(2,1)S(1)} %get-tuple-element.37), channel_id=1, source_target_pairs={{0,4},{4,0},{8,12},{12,8},{1,5},{5,1},{9,13},{13,9},{2,6},{6,2},{1... | collective-permute-start | bytes 786440 | tf_op jit(solution)/shard_map/ppermute | solution.py:33
  7.0 5.9 %pack.1.x_ref.own_ref = bf16[512,2688]{1,0:T(8,128)(2,1)} custom-call(s32[1,6]{1,0:T(1,128)} %fill_ref.6, s32[6]{0:T(128)} %tenant_ref.5, bf16[768,2048]{1,0:T(8,128)(2,1)} %tok_ref.1, bf16[768,512]{1,0:T(8,128)(2,1)} %cot_ref.1), custom_call_target="tpu_custom_call" | custom-call | flops 1 | bytes 1 | tf_op jit(solution)/shard_map/pack/pallas_call | solution.py:82
  12.9 5.7 %collective-permute-done.1.refs_3_.refs_1_ = bf16[128,512]{1,0:T(8,128)(2,1)S(1)} collective-permute-done((bf16[128,512]{1,0:T(8,128)(2,1)}, bf16[128,512]{1,0:T(8,128)(2,1)S(1)}, u32[]{:S(2)}, u32[]{:S(2)}) %collective-permute-start.1) | collective-permute-done | bytes 131104 | tf_op jit(solution)/shard_map/ppermute | solution.py:29
  18.6 3.9 %collective-permute-start.4 = (bf16[512,256]{1,0:T(8,128)(2,1)S(1)}, bf16[512,256]{1,0:T(8,128)(2,1)S(1)}, u32[]{:S(2)}, u32[]{:S(2)}) collective-permute-start(bf16[512,256]{1,0:T(8,128)(2,1)S(1)} %get-tuple-element.21), channel_id=1, source_target_pairs={{0,12},{4,8},{8,4},{12,0},{1,13},{5,9},{9,5},{13,1},{2,14},{6,10},... | collective-permute-start | bytes 786440 | tf_op jit(solution)/shard_map/ppermute | solution.py:33
  22.5 2.4 %collective-permute-start.7 = (bf16[512,256]{1,0:T(8,128)(2,1)S(1)}, bf16[512,256]{1,0:T(8,128)(2,1)S(1)}, u32[]{:S(2)}, u32[]{:S(2)}) collective-permute-start(bf16[512,256]{1,0:T(8,128)(2,1)S(1)} %collective-permute-done.2.refs_0_), channel_id=1, source_target_pairs={{0,18},{2,16},{16,2},{18,0},{1,19},{3,17},{17,3},{19,1},{4,22},{6,... | collective-permute-start | bytes 786440 | tf_op jit(solution)/shard_map/ppermute | solution.py:33
  26.0 3.5 %collective-permute-done.4.refs_0_ = bf16[512,256]{1,0:T(8,128)(2,1)S(1)} collective-permute-done((bf16[512,256]{1,0:T(8,128)(2,1)S(1)}, bf16[512,256]{1,0:T(8,128)(2,1)S(1)}, u32[]{:S(2)}, u32[]{:S(2)}) %collective-permute-start.4) | collective-permute-done | bytes 262176 | tf_op jit(solution)/shard_map/ppermute | solution.py:33
  29.5 6.2 %collective-permute-start.8 = (bf16[512,256]{1,0:T(8,128)(2,1)S(1)}, bf16[512,256]{1,0:T(8,128)(2,1)S(1)}, u32[]{:S(2)}, u32[]{:S(2)}) collective-permute-start(bf16[512,256]{1,0:T(8,128)(2,1)S(1)} %get-tuple-element.24), channel_id=1, source_target_pairs={{0,8},{4,12},{8,0},{12,4},{1,9},{5,13},{9,1},{13,5},{2,10},{6,14},... | collective-permute-start | bytes 786440 | tf_op jit(solution)/shard_map/ppermute | solution.py:33
  35.8 1.8 %copy-done = bf16[512,2688]{1,0:T(8,128)(2,1)S(1)} copy-done((bf16[512,2688]{1,0:T(8,128)(2,1)S(1)}, bf16[512,2688]{1,0:T(8,128)(2,1)}, u32[]{:S(2)}) %copy-start) | copy-done | bytes 2752536
  37.6 2.2 %low_part.1 = bf16[512,128]{1,0:T(8,128)(2,1)S(1)} custom-call(s32[1]{0:T(128)} %bitcast.2.dp_ref, s32[1,6]{1,0:T(1,128)S(1)} %copy-done.4, s32[6]{0:T(128)S(1)} %copy-done.5, bf16[512,2688]{1,0:T(8,128)(2,1)S(1)} %copy-done, bf16[128,2048]{1,0:T(8,128)(2,1)S(1)} %bitcast.9, bf16[128,2048]{1,0:T(8,128)(2,1)S(1)} %collective-permute-done.refs_1_, ...), custom_call_target="tpu_custom_call" | custom-call | flops 1 | bytes 1 | tf_op jit(solution)/shard_map/low_part/pallas_call | solution.py:117
  41.0 2.5 %collective-permute-start.11 = (bf16[512,256]{1,0:T(8,128)(2,1)S(1)}, bf16[512,256]{1,0:T(8,128)(2,1)S(1)}, u32[]{:S(2)}, u32[]{:S(2)}) collective-permute-start(bf16[512,256]{1,0:T(8,128)(2,1)S(1)} %collective-permute-done.4.refs_0_), channel_id=1, source_target_pairs={{0,18},{2,16},{16,2},{18,0},{1,19},{3,17},{17,3},{19,1},{4,22},{6,... | collective-permute-start | bytes 786440 | tf_op jit(solution)/shard_map/ppermute | solution.py:33
  44.6 3.0 %collective-permute-done.8.refs_0_ = bf16[512,256]{1,0:T(8,128)(2,1)S(1)} collective-permute-done((bf16[512,256]{1,0:T(8,128)(2,1)S(1)}, bf16[512,256]{1,0:T(8,128)(2,1)S(1)}, u32[]{:S(2)}, u32[]{:S(2)}) %collective-permute-start.8) | collective-permute-done | bytes 262176 | tf_op jit(solution)/shard_map/ppermute | solution.py:33
  47.6 3.7 %collective-permute-done.11.refs_3_ = bf16[512,256]{1,0:T(8,128)(2,1)S(1)} collective-permute-done((bf16[512,256]{1,0:T(8,128)(2,1)S(1)}, bf16[512,256]{1,0:T(8,128)(2,1)S(1)}, u32[]{:S(2)}, u32[]{:S(2)}) %collective-permute-start.11) | collective-permute-done | bytes 262176 | tf_op jit(solution)/shard_map/ppermute | solution.py:33
  51.3 3.9 %collective-permute-done.10.refs_2_ = bf16[512,256]{1,0:T(8,128)(2,1)S(1)} collective-permute-done((bf16[512,256]{1,0:T(8,128)(2,1)S(1)}, bf16[512,256]{1,0:T(8,128)(2,1)S(1)}, u32[]{:S(2)}, u32[]{:S(2)}) %collective-permute-start.10) | collective-permute-done | bytes 262176 | tf_op jit(solution)/shard_map/ppermute | solution.py:33
  56.6 2.0 %collective-permute-start.12 = (bf16[512,128]{1,0:T(8,128)(2,1)S(1)}, bf16[512,128]{1,0:T(8,128)(2,1)S(1)}, u32[]{:S(2)}, u32[]{:S(2)}) collective-permute-start(bf16[512,128]{1,0:T(8,128)(2,1)S(1)} %low_part.1), channel_id=1, source_target_pairs={{0,4},{4,0},{8,12},{12,8},{1,5},{5,1},{9,13},{13,9},{2,6},{6,2},{1... | collective-permute-start | bytes 393224 | tf_op jit(solution)/shard_map/ppermute | solution.py:33
  58.6 1.6 %collective-permute-start.17 = (bf16[512,256]{1,0:T(8,128)(2,1)S(1)}, bf16[512,256]{1,0:T(8,128)(2,1)S(1)}, u32[]{:S(2)}, u32[]{:S(2)}) collective-permute-start(bf16[512,256]{1,0:T(8,128)(2,1)S(1)} %collective-permute-done.8.refs_0_), channel_id=1, source_target_pairs={{0,18},{2,16},{16,2},{18,0},{1,19},{3,17},{17,3},{19,1},{4,22},{6,... | collective-permute-start | bytes 786440 | tf_op jit(solution)/shard_map/ppermute | solution.py:33
  61.6 11.6 %collective-permute-done.12 = bf16[512,128]{1,0:T(8,128)(2,1)S(1)} collective-permute-done((bf16[512,128]{1,0:T(8,128)(2,1)S(1)}, bf16[512,128]{1,0:T(8,128)(2,1)S(1)}, u32[]{:S(2)}, u32[]{:S(2)}) %collective-permute-start.12) | collective-permute-done | bytes 131104 | tf_op jit(solution)/shard_map/ppermute | solution.py:33
  73.2 1.5 %collective-permute-start.15 = (bf16[512,256]{1,0:T(8,128)(2,1)S(1)}, bf16[512,256]{1,0:T(8,128)(2,1)S(1)}, u32[]{:S(2)}, u32[]{:S(2)}) collective-permute-start(bf16[512,256]{1,0:T(8,128)(2,1)S(1)} %collective-permute-done.8.refs_0_), channel_id=1, source_target_pairs={{0,2},{2,0},{16,18},{18,16},{1,3},{3,1},{17,19},{19,17},{4,6},{6,4... | collective-permute-start | bytes 786440 | tf_op jit(solution)/shard_map/ppermute | solution.py:33
  75.1 5.3 %collective-permute-done.15.refs_1_ = bf16[512,256]{1,0:T(8,128)(2,1)S(1)} collective-permute-done((bf16[512,256]{1,0:T(8,128)(2,1)S(1)}, bf16[512,256]{1,0:T(8,128)(2,1)S(1)}, u32[]{:S(2)}, u32[]{:S(2)}) %collective-permute-start.15) | collective-permute-done | bytes 262176 | tf_op jit(solution)/shard_map/ppermute | solution.py:33
  82.8 1.3 %collective-permute-done.21.low_other_ref = bf16[512,128]{1,0:T(8,128)(2,1)S(1)} collective-permute-done((bf16[512,128]{1,0:T(8,128)(2,1)S(1)}, bf16[512,128]{1,0:T(8,128)(2,1)S(1)}, u32[]{:S(2)}, u32[]{:S(2)}) %collective-permute-start.21) | collective-permute-done | bytes 131104 | tf_op jit(solution)/shard_map/ppermute | solution.py:33
  86.1 2.1 %base.1.base_ref = f32[512,512]{1,0:T(8,128)S(1)} custom-call(s32[1]{0:T(128)} %bitcast.1.at_ref, s32[1]{0:T(128)} %bitcast.2.dp_ref, s32[1,6]{1,0:T(1,128)S(1)} %copy-done.4, s32[6]{0:T(128)S(1)} %copy-done.5, bf16[512,2688]{1,0:T(8,128)(2,1)S(1)} %copy-done.1, bf16[8192,512]{1,0:T(8,128)(2,1)S(1)} %bitcast.7, ...), custom_call_target="tpu_custom_call" | custom-call | flops 1 | bytes 1 | tf_op jit(solution)/shard_map/base/pallas_call | solution.py:238
  88.2 17.6 %collective-permute-done.19.refs_0_ = bf16[1024,256]{1,0:T(8,128)(2,1)S(1)} collective-permute-done((bf16[1024,256]{1,0:T(8,128)(2,1)S(1)}, bf16[1024,256]{1,0:T(8,128)(2,1)S(1)}, u32[]{:S(2)}, u32[]{:S(2)}) %collective-permute-start.19) | collective-permute-done | bytes 524320 | tf_op jit(solution)/shard_map/ppermute | solution.py:33
  106.6 1.7 %collective-permute-done.23.got_ref = bf16[64,2560]{1,0:T(8,128)(2,1)S(1)} collective-permute-done((bf16[64,2560]{1,0:T(8,128)(2,1)S(1)}, bf16[64,2560]{1,0:T(8,128)(2,1)S(1)}, u32[]{:S(2)}, u32[]{:S(2)}) %collective-permute-start.23) | collective-permute-done | bytes 327712 | tf_op jit(solution)/shard_map/ppermute | solution.py:33
  109.6 2.1 %finish.1 = bf16[768,512]{1,0:T(8,128)(2,1)} custom-call(s32[1]{0:T(128)} %bitcast.core_ref, s32[1,6]{1,0:T(1,128)S(1)} %copy-done.4, f32[512,512]{1,0:T(8,128)S(1)} %base.1.base_ref, bf16[1024,256]{1,0:T(8,128)(2,1)S(1)} %collective-permute-done.19.refs_0_, bf16[1024,256]{1,0:T(8,128)(2,1)S(1)} %collective-permute-done.13.refs_1_, ...), custom_call_target="tpu_custom_call" | custom-call | flops 1 | bytes 1 | tf_op jit(solution)/shard_map/finish/pallas_call | solution.py:299
  (55 shorter events, 14.5 us)
Async XLA Ops:
  0.6 18.0 %collective-permute-start = (bf16[128,2048]{1,0:T(8,128)(2,1)}, bf16[128,2048]{1,0:T(8,128)(2,1)S(1)}, u32[]{:S(2)}, u32[]{:S(2)}) collective-permute-start(bf16[128,2048]{1,0:T(8,128)(2,1)} %bitcast.8), channel_id=1, source_target_pairs={{0,2},{2,0},{1,3},{3,1},{4,6},{6,4},{5,7},{7,5},{8,10},{10,8},{9,1... | collective-permute-start | bytes 1572872 | tf_op jit(solution)/shard_map/ppermute | solution.py:29
  4.8 13.8 %collective-permute-start.2 = (bf16[512,256]{1,0:T(8,128)(2,1)S(1)}, bf16[512,256]{1,0:T(8,128)(2,1)S(1)}, u32[]{:S(2)}, u32[]{:S(2)}) collective-permute-start(bf16[512,256]{1,0:T(8,128)(2,1)S(1)} %get-tuple-element.37), channel_id=1, source_target_pairs={{0,4},{4,0},{8,12},{12,8},{1,5},{5,1},{9,13},{13,9},{2,6},{6,2},{1... | collective-permute-start | bytes 786440 | tf_op jit(solution)/shard_map/ppermute | solution.py:33
  6.4 12.1 %collective-permute-start.1 = (bf16[128,512]{1,0:T(8,128)(2,1)}, bf16[128,512]{1,0:T(8,128)(2,1)S(1)}, u32[]{:S(2)}, u32[]{:S(2)}) collective-permute-start(bf16[128,512]{1,0:T(8,128)(2,1)} %bitcast.10), channel_id=1, source_target_pairs={{0,2},{2,0},{1,3},{3,1},{4,6},{6,4},{5,7},{7,5},{8,10},{10,8},{9,1... | collective-permute-start | bytes 393224 | tf_op jit(solution)/shard_map/ppermute | solution.py:29
  18.6 21.2 %collective-permute-start.3 = (bf16[512,2688]{1,0:T(8,128)(2,1)}, bf16[512,2688]{1,0:T(8,128)(2,1)S(1)}, u32[]{:S(2)}, u32[]{:S(2)}) collective-permute-start(bf16[512,2688]{1,0:T(8,128)(2,1)} %pack.1.x_ref.own_ref), channel_id=1, source_target_pairs={{0,1},{1,0},{2,3},{3,2},{4,5},{5,4},{6,7},{7,6},{8,9},{9,8},{10,11... | collective-permute-start | bytes 8257544 | tf_op jit(solution)/shard_map/ppermute | solution.py:33
  18.6 10.9 %collective-permute-start.4 = (bf16[512,256]{1,0:T(8,128)(2,1)S(1)}, bf16[512,256]{1,0:T(8,128)(2,1)S(1)}, u32[]{:S(2)}, u32[]{:S(2)}) collective-permute-start(bf16[512,256]{1,0:T(8,128)(2,1)S(1)} %get-tuple-element.21), channel_id=1, source_target_pairs={{0,12},{4,8},{8,4},{12,0},{1,13},{5,9},{9,5},{13,1},{2,14},{6,10},... | collective-permute-start | bytes 786440 | tf_op jit(solution)/shard_map/ppermute | solution.py:33
  22.5 17.2 %collective-permute-start.7 = (bf16[512,256]{1,0:T(8,128)(2,1)S(1)}, bf16[512,256]{1,0:T(8,128)(2,1)S(1)}, u32[]{:S(2)}, u32[]{:S(2)}) collective-permute-start(bf16[512,256]{1,0:T(8,128)(2,1)S(1)} %collective-permute-done.2.refs_0_), channel_id=1, source_target_pairs={{0,18},{2,16},{16,2},{18,0},{1,19},{3,17},{17,3},{19,1},{4,22},{6,... | collective-permute-start | bytes 786440 | tf_op jit(solution)/shard_map/ppermute | solution.py:33
  25.0 14.8 %collective-permute-start.6 = (bf16[512,256]{1,0:T(8,128)(2,1)S(1)}, bf16[512,256]{1,0:T(8,128)(2,1)S(1)}, u32[]{:S(2)}, u32[]{:S(2)}) collective-permute-start(bf16[512,256]{1,0:T(8,128)(2,1)S(1)} %collective-permute-done.2.refs_0_), channel_id=1, source_target_pairs={{0,16},{2,18},{16,0},{18,2},{1,17},{3,19},{17,1},{19,3},{4,20},{6,... | collective-permute-start | bytes 786440 | tf_op jit(solution)/shard_map/ppermute | solution.py:33
  25.5 14.3 %collective-permute-start.5 = (bf16[512,256]{1,0:T(8,128)(2,1)S(1)}, bf16[512,256]{1,0:T(8,128)(2,1)S(1)}, u32[]{:S(2)}, u32[]{:S(2)}) collective-permute-start(bf16[512,256]{1,0:T(8,128)(2,1)S(1)} %collective-permute-done.2.refs_0_), channel_id=1, source_target_pairs={{0,2},{2,0},{16,18},{18,16},{1,3},{3,1},{17,19},{19,17},{4,6},{6,4... | collective-permute-start | bytes 786440 | tf_op jit(solution)/shard_map/ppermute | solution.py:33
  29.5 18.1 %collective-permute-start.8 = (bf16[512,256]{1,0:T(8,128)(2,1)S(1)}, bf16[512,256]{1,0:T(8,128)(2,1)S(1)}, u32[]{:S(2)}, u32[]{:S(2)}) collective-permute-start(bf16[512,256]{1,0:T(8,128)(2,1)S(1)} %get-tuple-element.24), channel_id=1, source_target_pairs={{0,8},{4,12},{8,0},{12,4},{1,9},{5,13},{9,1},{13,5},{2,10},{6,14},... | collective-permute-start | bytes 786440 | tf_op jit(solution)/shard_map/ppermute | solution.py:33
  41.0 10.3 %collective-permute-start.11 = (bf16[512,256]{1,0:T(8,128)(2,1)S(1)}, bf16[512,256]{1,0:T(8,128)(2,1)S(1)}, u32[]{:S(2)}, u32[]{:S(2)}) collective-permute-start(bf16[512,256]{1,0:T(8,128)(2,1)S(1)} %collective-permute-done.4.refs_0_), channel_id=1, source_target_pairs={{0,18},{2,16},{16,2},{18,0},{1,19},{3,17},{17,3},{19,1},{4,22},{6,... | collective-permute-start | bytes 786440 | tf_op jit(solution)/shard_map/ppermute | solution.py:33
  43.5 11.7 %collective-permute-start.10 = (bf16[512,256]{1,0:T(8,128)(2,1)S(1)}, bf16[512,256]{1,0:T(8,128)(2,1)S(1)}, u32[]{:S(2)}, u32[]{:S(2)}) collective-permute-start(bf16[512,256]{1,0:T(8,128)(2,1)S(1)} %collective-permute-done.4.refs_0_), channel_id=1, source_target_pairs={{0,16},{2,18},{16,0},{18,2},{1,17},{3,19},{17,1},{19,3},{4,20},{6,... | collective-permute-start | bytes 786440 | tf_op jit(solution)/shard_map/ppermute | solution.py:33
  44.0 11.2 %collective-permute-start.9 = (bf16[512,256]{1,0:T(8,128)(2,1)S(1)}, bf16[512,256]{1,0:T(8,128)(2,1)S(1)}, u32[]{:S(2)}, u32[]{:S(2)}) collective-permute-start(bf16[512,256]{1,0:T(8,128)(2,1)S(1)} %collective-permute-done.4.refs_0_), channel_id=1, source_target_pairs={{0,2},{2,0},{16,18},{18,16},{1,3},{3,1},{17,19},{19,17},{4,6},{6,4... | collective-permute-start | bytes 786440 | tf_op jit(solution)/shard_map/ppermute | solution.py:33
  44.6 30.1 %collective-permute-start.13 = (bf16[1024,256]{1,0:T(8,128)(2,1)S(1)}, bf16[1024,256]{1,0:T(8,128)(2,1)S(1)}, u32[]{:S(2)}, u32[]{:S(2)}) collective-permute-start(bf16[1024,256]{1,0:T(8,128)(2,1)S(1)} %panel.3), channel_id=1, source_target_pairs={{0,4},{4,0},{8,12},{12,8},{1,5},{5,1},{9,13},{13,9},{2,6},{6,2},{1... | collective-permute-start | bytes 1572872 | tf_op jit(solution)/shard_map/ppermute | solution.py:33
  56.6 23.9 %collective-permute-start.18 = (bf16[1024,256]{1,0:T(8,128)(2,1)S(1)}, bf16[1024,256]{1,0:T(8,128)(2,1)S(1)}, u32[]{:S(2)}, u32[]{:S(2)}) collective-permute-start(bf16[1024,256]{1,0:T(8,128)(2,1)S(1)} %panel.4), channel_id=1, source_target_pairs={{0,4},{4,0},{8,12},{12,8},{1,5},{5,1},{9,13},{13,9},{2,6},{6,2},{1... | collective-permute-start | bytes 1572872 | tf_op jit(solution)/shard_map/ppermute | solution.py:33
  56.6 16.5 %collective-permute-start.12 = (bf16[512,128]{1,0:T(8,128)(2,1)S(1)}, bf16[512,128]{1,0:T(8,128)(2,1)S(1)}, u32[]{:S(2)}, u32[]{:S(2)}) collective-permute-start(bf16[512,128]{1,0:T(8,128)(2,1)S(1)} %low_part.1), channel_id=1, source_target_pairs={{0,4},{4,0},{8,12},{12,8},{1,5},{5,1},{9,13},{13,9},{2,6},{6,2},{1... | collective-permute-start | bytes 393224 | tf_op jit(solution)/shard_map/ppermute | solution.py:33
  58.6 16.4 %collective-permute-start.17 = (bf16[512,256]{1,0:T(8,128)(2,1)S(1)}, bf16[512,256]{1,0:T(8,128)(2,1)S(1)}, u32[]{:S(2)}, u32[]{:S(2)}) collective-permute-start(bf16[512,256]{1,0:T(8,128)(2,1)S(1)} %collective-permute-done.8.refs_0_), channel_id=1, source_target_pairs={{0,18},{2,16},{16,2},{18,0},{1,19},{3,17},{17,3},{19,1},{4,22},{6,... | collective-permute-start | bytes 786440 | tf_op jit(solution)/shard_map/ppermute | solution.py:33
  60.3 14.8 %collective-permute-start.16 = (bf16[512,256]{1,0:T(8,128)(2,1)S(1)}, bf16[512,256]{1,0:T(8,128)(2,1)S(1)}, u32[]{:S(2)}, u32[]{:S(2)}) collective-permute-start(bf16[512,256]{1,0:T(8,128)(2,1)S(1)} %collective-permute-done.8.refs_0_), channel_id=1, source_target_pairs={{0,16},{2,18},{16,0},{18,2},{1,17},{3,19},{17,1},{19,3},{4,20},{6,... | collective-permute-start | bytes 786440 | tf_op jit(solution)/shard_map/ppermute | solution.py:33
  73.2 7.3 %collective-permute-start.15 = (bf16[512,256]{1,0:T(8,128)(2,1)S(1)}, bf16[512,256]{1,0:T(8,128)(2,1)S(1)}, u32[]{:S(2)}, u32[]{:S(2)}) collective-permute-start(bf16[512,256]{1,0:T(8,128)(2,1)S(1)} %collective-permute-done.8.refs_0_), channel_id=1, source_target_pairs={{0,2},{2,0},{16,18},{18,16},{1,3},{3,1},{17,19},{19,17},{4,6},{6,4... | collective-permute-start | bytes 786440 | tf_op jit(solution)/shard_map/ppermute | solution.py:33
  74.7 7.9 %collective-permute-start.14 = (bf16[512,128]{1,0:T(8,128)(2,1)S(1)}, bf16[512,128]{1,0:T(8,128)(2,1)S(1)}, u32[]{:S(2)}, u32[]{:S(2)}) collective-permute-start(bf16[512,128]{1,0:T(8,128)(2,1)S(1)} %add_convert_fusion.2), channel_id=1, source_target_pairs={{0,8},{4,12},{8,0},{12,4},{1,9},{5,13},{9,1},{13,5},{2,10},{6,14},... | collective-permute-start | bytes 393224 | tf_op jit(solution)/shard_map/ppermute | solution.py:33
  81.7 24.2 %collective-permute-start.19 = (bf16[1024,256]{1,0:T(8,128)(2,1)S(1)}, bf16[1024,256]{1,0:T(8,128)(2,1)S(1)}, u32[]{:S(2)}, u32[]{:S(2)}) collective-permute-start(bf16[1024,256]{1,0:T(8,128)(2,1)S(1)} %panel.5), channel_id=1, source_target_pairs={{0,8},{4,12},{8,0},{12,4},{1,9},{5,13},{9,1},{13,5},{2,10},{6,14},... | collective-permute-start | bytes 1572872 | tf_op jit(solution)/shard_map/ppermute | solution.py:33
  82.7 1.4 %collective-permute-start.21 = (bf16[512,128]{1,0:T(8,128)(2,1)S(1)}, bf16[512,128]{1,0:T(8,128)(2,1)S(1)}, u32[]{:S(2)}, u32[]{:S(2)}) collective-permute-start(bf16[512,128]{1,0:T(8,128)(2,1)S(1)} %add_convert_fusion.1.low_ref), channel_id=1, source_target_pairs={{0,1},{1,0},{2,3},{3,2},{4,5},{5,4},{6,7},{7,6},{8,9},{9,8},{10,11... | collective-permute-start | bytes 393224 | tf_op jit(solution)/shard_map/ppermute | solution.py:33
  85.2 20.8 %collective-permute-start.22 = (bf16[64,2560]{1,0:T(8,128)(2,1)S(1)}, bf16[64,2560]{1,0:T(8,128)(2,1)S(1)}, u32[]{:S(2)}, u32[]{:S(2)}) collective-permute-start(bf16[64,2560]{1,0:T(8,128)(2,1)S(1)} %get-tuple-element.32), channel_id=1, source_target_pairs={{0,2},{2,0},{1,3},{3,1},{4,6},{6,4},{5,7},{7,5},{8,10},{10,8},{9,1... | collective-permute-start | bytes 983048 | tf_op jit(solution)/shard_map/ppermute | solution.py:29
  105.9 3.6 %collective-permute-start.20 = (f32[512,256]{1,0:T(8,128)S(1)}, f32[512,256]{1,0:T(8,128)S(1)}, u32[]{:S(2)}, u32[]{:S(2)}) collective-permute-start(f32[512,256]{1,0:T(8,128)S(1)} %other_rows.1), channel_id=1, source_target_pairs={{0,1},{1,0},{2,3},{3,2},{4,5},{5,4},{6,7},{7,6},{8,9},{9,8},{10,11... | collective-permute-start | bytes 1572872 | tf_op jit(solution)/shard_map/ppermute | solution.py:33
  106.1 2.3 %collective-permute-start.23 = (bf16[64,2560]{1,0:T(8,128)(2,1)S(1)}, bf16[64,2560]{1,0:T(8,128)(2,1)S(1)}, u32[]{:S(2)}, u32[]{:S(2)}) collective-permute-start(bf16[64,2560]{1,0:T(8,128)(2,1)S(1)} %add_convert_fusion.own_ref), channel_id=1, source_target_pairs={{0,1},{1,0},{2,3},{3,2},{4,5},{5,4},{6,7},{7,6},{8,9},{9,8},{10,11... | collective-permute-start | bytes 983048 | tf_op jit(solution)/shard_map/ppermute | solution.py:33
  (8 other events, 163.5 us)

commit v8 on v7

--- a/solution.py
+++ b/solution.py
@@ -59,6 +59,26 @@
     for b, start in enumerate(starts_of(fill_ref, blocks)):
         tenant = jnp.where(row >= start, tenant_ref[b], tenant)
     return tenant
+
+
+def half_kernel(core_ref, a_ref, b_ref, out_ref):
+    rank, feat = out_ref.shape[0], a_ref.shape[1]
+    first = core_ref[0] == 0
+    out_ref[:, :feat] = jnp.where(first, a_ref[:rank, :], a_ref[rank:, :])
+    out_ref[:, feat:] = jnp.where(first, b_ref[:rank, :], b_ref[rank:, :])
+
+
+def own_half(core, a, b, rank):
+    width = a.shape[1] + b.shape[1]
+    return pl.pallas_call(
+        half_kernel,
+        in_specs=[SMEM] + [VMEM] * 2,
+        out_specs=VMEM,
+        out_shape=shaped((rank, width), BF16),
+        compiler_params=params(56),
+        cost_estimate=cost(rank * width, 6 * rank * width),
+        name="own_half",
+    )(core, a, b)
 
 
 def pack_kernel(blocks, block, fill_ref, tenant_ref, tok_ref, cot_ref, out_ref, pick):
@@ -85,7 +105,7 @@
         out_specs=VMEM,
         out_shape=shaped((LIVE, feat + cols + lanes), BF16),
         scratch_shapes=[pltpu.VMEM((LIVE, rows), BF16)],
-        compiler_params=params(56),
+        compiler_params=params(24),
         cost_estimate=cost(2 * LIVE * rows * (feat + cols), 2 * (LIVE + rows) * (feat + cols)),
         name="pack",
     )(fill, tenant, tokens, cotangent)
@@ -95,34 +115,42 @@
     return tenant == 2 * owner + (lane >= rank).astype(I32)
 
 
-def low_kernel(n_dp, rank, blocks, dp_ref, fill_ref, tenant_ref, x_ref, *refs):
-    a_refs, b_refs, out_ref = refs[:n_dp], refs[n_dp : 2 * n_dp], refs[2 * n_dp]
-    lanes, feat, cols = 2 * rank, a_refs[0].shape[1], b_refs[0].shape[1]
+def in_order(core, mine, other):
+    return jnp.where(core == 0, jnp.concatenate([mine, other], axis=0), jnp.concatenate([other, mine], axis=0))
+
+
+def low_kernel(n_dp, rank, blocks, dp_ref, core_ref, fill_ref, tenant_ref, x_ref, a_ref, b_ref, *refs):
+    halves, out_ref = refs[:-1], refs[-1]
+    lanes, feat, cols = 2 * rank, a_ref.shape[1], b_ref.shape[1]
     tenant = tenant_lanes(fill_ref, tenant_ref, blocks, lanes)
     lane = lax.broadcasted_iota(I32, (LIVE, lanes), 1)
     low_in = jnp.zeros((LIVE, lanes), F32)
     low_grad = jnp.zeros((LIVE, lanes), F32)
     for s in range(n_dp):
         mask = owner_mask(tenant, lane, (dp_ref[0] + n_dp - s) % n_dp, rank)
-        low_in = low_in + jnp.where(mask, dot(x_ref[:, :feat], a_refs[s][...], (1, 1)), 0.0)
-        low_grad = low_grad + jnp.where(mask, dot(x_ref[:, feat : feat + cols], b_refs[s][...], (1, 1)), 0.0)
+        a, b = a_ref[...], b_ref[...]
+        if s > 0:
+            both = in_order(core_ref[0], halves[2 * s - 2][...], halves[2 * s - 1][...])
+            a, b = both[:, :feat], both[:, feat:]
+        low_in = low_in + jnp.where(mask, dot(x_ref[:, :feat], a, (1, 1)), 0.0)
+        low_grad = low_grad + jnp.where(mask, dot(x_ref[:, feat : feat + cols], b, (1, 1)), 0.0)
     low_in = low_in + pltpu.roll(low_in, rank, 1)
     low_grad = low_grad + pltpu.roll(low_grad, rank, 1)
     out_ref[...] = jnp.where(lane < rank, low_in, low_grad).astype(BF16)
 
 
-def low_part(dp, fill, tenant, x, a_list, b_list, blocks, rank):
-    n_dp = len(a_list)
+def low_part(dp, core, fill, tenant, x, a, b, halves, blocks, rank):
+    n_dp = 1 + len(halves) // 2
     width = x.shape[1]
     return pl.pallas_call(
         functools.partial(low_kernel, n_dp, rank, blocks),
-        in_specs=[SMEM] * 3 + [VMEM] * (1 + 2 * n_dp),
+        in_specs=[SMEM] * 4 + [VMEM] * (3 + len(halves)),
         out_specs=VMEM,
         out_shape=shaped((LIVE, 2 * rank), BF16),
         compiler_params=params(24),
         cost_estimate=cost(4 * LIVE * rank * n_dp * width, 2 * LIVE * width + 4 * rank * n_dp * width),
         name="low_part",
-    )(dp, fill, tenant, x, *a_list, *b_list)
+    )(dp, core, fill, tenant, x, a, b, *halves)
 
 
 def doubled(low, lane, rank):
@@ -218,8 +246,8 @@
     )(core, own, got)
 
 
-def base_kernel(n_dp, rank, blocks, at_ref, dp_ref, fill_ref, tenant_ref, x_ref, w_ref, low_ref, *refs):
-    b_refs, out_ref = refs[:n_dp], refs[n_dp]
+def base_kernel(n_dp, rank, blocks, at_ref, dp_ref, core_ref, fill_ref, tenant_ref, x_ref, w_ref, low_ref, b_ref, *refs):
+    halves, out_ref = refs[:-1], refs[-1]
     lanes = 2 * rank
     tenant = tenant_lanes(fill_ref, tenant_ref, blocks, lanes)
     lane = lax.broadcasted_iota(I32, (LIVE, lanes), 1)
@@ -227,12 +255,15 @@
     total = dot(x_ref[...], w_ref[...])
     for s in range(n_dp):
         mask = owner_mask(tenant, lane, (dp_ref[0] + n_dp - s) % n_dp, rank)
-        total = total + dot(jnp.where(mask, ADAPTER_SCALE * low_in, 0.0).astype(BF16), b_refs[s][...])
+        b = b_ref[...]
+        if s > 0:
+            b = in_order(core_ref[0], halves[2 * s - 2][...], halves[2 * s - 1][...])
+        total = total + dot(jnp.where(mask, ADAPTER_SCALE * low_in, 0.0).astype(BF16), b)
     out_ref[...] = total
 
 
-def base_product(at, dp, fill, tenant, x, base_weight, low, b_list, feat, blocks, rank):
-    n_dp = len(b_list)
+def base_product(at, dp, core, fill, tenant, x, base_weight, low, b, halves, feat, blocks, rank):
+    n_dp = 1 + len(halves) // 2
     cols = base_weight.shape[1]
     whole = lambda i, at: (0, 0)
     return pl.pallas_call(
@@ -240,16 +271,17 @@
         grid_spec=pltpu.PrefetchScalarGridSpec(
             num_scalar_prefetch=1,
             grid=(1,),
-            in_specs=[SMEM] * 3
+            in_specs=[SMEM] * 4
             + [pl.BlockSpec((LIVE, feat), whole), pl.BlockSpec((feat, cols), lambda i, at: (at[0], 0)), pl.BlockSpec((LIVE, 2 * rank), whole)]
-            + [pl.BlockSpec((2 * rank, cols), whole)] * n_dp,
+            + [pl.BlockSpec((2 * rank, cols), whole)]
+            + [pl.BlockSpec((rank, cols), lambda i, at: (0, feat // cols))] * len(halves),
             out_specs=pl.BlockSpec((LIVE, cols), whole),
         ),
         out_shape=shaped((LIVE, cols), F32),
         compiler_params=params(24),
         cost_estimate=cost(2 * LIVE * feat * cols, 2 * feat * (LIVE + cols) + 4 * LIVE * cols),
         name="base",
-    )(at, dp, fill, tenant, x, base_weight, low, *b_list)
+    )(at, dp, core, fill, tenant, x, base_weight, low, b, *halves)
 
 
 def swap_kernel(*refs):
@@ -323,8 +355,11 @@
     dp, core, at, place = scalar(me_dp), scalar(me_pipe), scalar(me_t), scalar(q)
 
     own_a, own_b = adapter_a.reshape(pair * rank, feat), adapter_b.reshape(pair * rank, cols)
-    a_list = [own_a] + [shift(own_a, "dp", n_dp, s) for s in range(1, n_dp)]
-    b_list = [own_b] + [shift(own_b, "dp", n_dp, s) for s in range(1, n_dp)]
+    one = own_half(core, own_a, own_b, rank)
+    halves = []
+    for s in range(1, n_dp):
+        got = shift(one, "dp", n_dp, s)
+        halves += [got, flip(got, "pipe", n_pipe, 1)]
     panel_at = place if planes == 4 else jnp.zeros_like(place)
 
     def share(k):
@@ -344,24 +379,25 @@
         weight[3] = flip(after(share(me_t ^ 3), weight[1]), "tensor", n_t, 3)
         weight[2] = flip(after(share(me_t ^ 2), weight[3]), "tensor", n_t, 2)
         x = pack(after(block_fill, share_1), block_tenant_index, tokens, cotangent, blocks, 2 * rank)
-        x_other = flip(after(x, weight[1], *a_list[1:], *b_list[1:]), "pipe", n_pipe, 1)
+        x_other = flip(after(x, weight[1], *halves[::2]), "pipe", n_pipe, 1)
         pieces, order = gathered(weight[1])
-        low = low_part(dp, block_fill, block_tenant_index, x, a_list, b_list, blocks, rank)
+        low = low_part(dp, core, block_fill, block_tenant_index, x, own_a, own_b, halves, blocks, rank)
         pieces[0] = after(pieces[0], weight[3], low)
         (y_1,) = panel_product(order, panel_at, x, x_other, pieces, half)
-        part_1 = flip(y_1, "tensor", n_t, 1)
+        low = add_flipped(low, 1, weight[3])
+        part_1 = flip(after(y_1, low), "tensor", n_t, 1)
         pieces, order = gathered(after(weight[3], y_1))
         pieces[0] = after(pieces[0], weight[2])
         (y,) = panel_product(order, panel_at, x, x_other, pieces, half)
         add = flip(y, "tensor", n_t, 1)
-        low = add_flipped(add_flipped(low, 1, y), 2, part_1)
+        low = add_flipped(low, 2, y, part_1)
         pieces, order = gathered(after(weight[2], y))
         (y_2,) = panel_product(order, panel_at, x, x_other, pieces, half, adds=[add])
         parts = [flip(y_2, "tensor", n_t, 2), part_1]
     else:
         x = pack(block_fill, block_tenant_index, tokens, cotangent, blocks, 2 * rank)
         x_other = flip(x, "pipe", n_pipe, 1)
-        low = low_part(dp, block_fill, block_tenant_index, x, a_list, b_list, blocks, rank)
+        low = low_part(dp, core, block_fill, block_tenant_index, x, own_a, own_b, halves, blocks, rank)
         mask = 1
         while mask < n_t:
             low, mask = add_flipped(low, mask), 2 * mask
@@ -378,7 +414,9 @@
     mine = mine.astype(BF16)
     down_out, up_out = settle(core, mine, flip(mine, "pipe", n_pipe, 1), feat)
 
-    base = base_product(at, dp, block_fill, block_tenant_index, x, base_weight, low, b_list, feat, blocks, rank)
+    base = base_product(
+        at, dp, core, block_fill, block_tenant_index, x, base_weight, low, own_b, halves, feat, blocks, rank
+    )
     parts[0] = after(parts[0], base)
     others = [flip(other_rows(parts), "pipe", n_pipe, 1)]
     out = finish(core, block_fill, base, parts, others, rows, blocks)

time: 112 us -> 99.7 us (0.89)
  waiting for transfers between devices: 58.1 us -> 48.1 us
  starting transfers between devices: 31.3 us -> 28.8 us
  local copies, waits for them, and re-layouts: 2.96 us -> 4.39 us
    ppermute x3 -> x2, waiting for transfers between devices: 5.66 us -> 0.01 us  [shift(): lax.ppermute(x, name, [(i, (i + step) % count) for i in range(count)])]
    ppermute x21 -> x22, waiting for transfers between devices: 52.5 us -> 48.1 us  [flip(): return lax.ppermute(x, names, [(i, i ^ mask) for i in range(count)])]
    pallas_call x1, Pallas kernels: 5.88 us -> 2.86 us  [pack(): pl.pallas_call(functools.partial(pack_kernel, blocks, rows // blocks), in...]
    pallas_call x0 -> x1, Pallas kernels: none -> 1.89 us  [own_half(): pl.pallas_call(half_kernel, in_specs=[SMEM] + [VMEM] * 2, out_specs=VMEM,...]
    ppermute x21 -> x22, starting transfers between devices: 26.8 us -> 25.2 us  [flip(): return lax.ppermute(x, names, [(i, i ^ mask) for i in range(count)])]
    unnamed x16 -> x20, local copies, waits for them, and re-layouts: 1.8 us -> 3.23 us
    ppermute x3 -> x2, starting transfers between devices: 4.55 us -> 3.69 us  [shift(): lax.ppermute(x, name, [(i, (i + step) % count) for i in range(count)])]
  transfers between devices with their start and end apart: 24 -> 24, of which waited for: 12 -> 14; matrix products, arithmetic and copies ran while one was open for 1% -> 1% of each run, Pallas kernels for 14% -> 13%
where the time goes in v8:
time: 99.7 us; the launch traced here: 99.5 us
  waiting for transfers between devices  48.1 us (48%)
  starting transfers between devices  28.8 us (29%)
  Pallas kernels  17.2 us (17%)
  local copies, waits for them, and re-layouts  4.39 us (4%)
    ppermute x22, waiting for transfers between devices, flip(): return lax.ppermute(x, names, [(i, i ^ mask) for i in range(count)])  48.1 us
    ppermute x22, starting transfers between devices, flip(): return lax.ppermute(x, names, [(i, i ^ mask) for i in range(count)])  25.2 us
    pallas_call x3, Pallas kernels, panel_product(): pl.pallas_call(functools.partial(panel_kernel, order, len(pieces)), in_sp...  3.77 us
    ppermute x2, starting transfers between devices, shift(): lax.ppermute(x, name, [(i, (i + step) % count) for i in range(count)])  3.69 us
    unnamed x20, local copies, waits for them, and re-layouts  3.23 us
    pallas_call x1, Pallas kernels, pack(): pl.pallas_call(functools.partial(pack_kernel, blocks, rows // blocks), in...  2.86 us
    pallas_call x1, Pallas kernels, low_part(): pl.pallas_call(functools.partial(low_kernel, n_dp, rank, blocks), in_spec...  2.16 us
    pallas_call x1, Pallas kernels, base_product(): pl.pallas_call(functools.partial(base_kernel, n_dp, rank, blocks), grid_s...  2.14 us
  transfers between devices with their start and end apart: 24, of which 14 were waited for; matrix products, arithmetic and copies ran while one was open for 1% of the time, Pallas kernels for 13%

profile of v8, /device:TPU:0, one launch (start us, length us, event | category | flops | bytes accessed | tf_op | source)
XLA Modules:
  0.0 99.5 jit_solution(5964762551755745683)
XLA Ops:
  0.6 1.9 %own_half.1 = bf16[64,2560]{1,0:T(8,128)(2,1)} custom-call(s32[1]{0:T(128)} %bitcast.core_ref, bf16[128,2048]{1,0:T(8,128)(2,1)} %bitcast.8, bf16[128,512]{1,0:T(8,128)(2,1)} %bitcast.10), custom_call_target="tpu_custom_call" | custom-call | flops 1 | bytes 1 | tf_op jit(solution)/shard_map/own_half/pallas_call | solution.py:73
  2.5 2.9 %collective-permute-start = (bf16[64,2560]{1,0:T(8,128)(2,1)}, bf16[64,2560]{1,0:T(8,128)(2,1)S(1)}, u32[]{:S(2)}, u32[]{:S(2)}) collective-permute-start(bf16[64,2560]{1,0:T(8,128)(2,1)} %own_half.1), channel_id=1, source_target_pairs={{0,2},{2,0},{1,3},{3,1},{4,6},{6,4},{5,7},{7,5},{8,10},{10,8},{9,1... | collective-permute-start | bytes 983048 | tf_op jit(solution)/shard_map/ppermute | solution.py:29
  6.6 1.6 %collective-permute-start.2 = (bf16[512,256]{1,0:T(8,128)(2,1)S(1)}, bf16[512,256]{1,0:T(8,128)(2,1)S(1)}, u32[]{:S(2)}, u32[]{:S(2)}) collective-permute-start(bf16[512,256]{1,0:T(8,128)(2,1)S(1)} %get-tuple-element.39), channel_id=1, source_target_pairs={{0,4},{4,0},{8,12},{12,8},{1,5},{5,1},{9,13},{13,9},{2,6},{6,2},{1... | collective-permute-start | bytes 786440 | tf_op jit(solution)/shard_map/ppermute | solution.py:33
  8.3 1.9 %copy-done = bf16[768,2048]{1,0:T(8,128)(2,1)S(1)} copy-done((bf16[768,2048]{1,0:T(8,128)(2,1)S(1)}, bf16[768,2048]{1,0:T(8,128)(2,1)}, u32[]{:S(2)}) %copy-start) | copy-done | bytes 3145752
  11.5 2.9 %pack.1.x_ref.own_ref = bf16[512,2688]{1,0:T(8,128)(2,1)S(1)} custom-call(s32[1,6]{1,0:T(1,128)S(1)} %copy-done.4, s32[6]{0:T(128)S(1)} %copy-done.6, bf16[768,2048]{1,0:T(8,128)(2,1)S(1)} %copy-done, bf16[768,512]{1,0:T(8,128)(2,1)S(1)} %copy-done.3), custom_call_target="tpu_custom_call" | custom-call | flops 1 | bytes 1 | tf_op jit(solution)/shard_map/pack/pallas_call | solution.py:102
  15.0 3.6 %collective-permute-start.3 = (bf16[512,256]{1,0:T(8,128)(2,1)S(1)}, bf16[512,256]{1,0:T(8,128)(2,1)S(1)}, u32[]{:S(2)}, u32[]{:S(2)}) collective-permute-start(bf16[512,256]{1,0:T(8,128)(2,1)S(1)} %get-tuple-element.21), channel_id=1, source_target_pairs={{0,12},{4,8},{8,4},{12,0},{1,13},{5,9},{9,5},{13,1},{2,14},{6,10},... | collective-permute-start | bytes 786440 | tf_op jit(solution)/shard_map/ppermute | solution.py:33
  18.6 1.6 %collective-permute-start.8 = (bf16[512,256]{1,0:T(8,128)(2,1)S(1)}, bf16[512,256]{1,0:T(8,128)(2,1)S(1)}, u32[]{:S(2)}, u32[]{:S(2)}) collective-permute-start(bf16[512,256]{1,0:T(8,128)(2,1)S(1)} %collective-permute-done.2.refs_0_), channel_id=1, source_target_pairs={{0,18},{2,16},{16,2},{18,0},{1,19},{3,17},{17,3},{19,1},{4,22},{6,... | collective-permute-start | bytes 786440 | tf_op jit(solution)/shard_map/ppermute | solution.py:33
  20.7 1.4 %collective-permute-start.6 = (bf16[512,256]{1,0:T(8,128)(2,1)S(1)}, bf16[512,256]{1,0:T(8,128)(2,1)S(1)}, u32[]{:S(2)}, u32[]{:S(2)}) collective-permute-start(bf16[512,256]{1,0:T(8,128)(2,1)S(1)} %collective-permute-done.2.refs_0_), channel_id=1, source_target_pairs={{0,2},{2,0},{16,18},{18,16},{1,3},{3,1},{17,19},{19,17},{4,6},{6,4... | collective-permute-start | bytes 786440 | tf_op jit(solution)/shard_map/ppermute | solution.py:33
  22.1 2.2 %low_part.1 = bf16[512,128]{1,0:T(8,128)(2,1)S(1)} custom-call(s32[1]{0:T(128)} %bitcast.2.dp_ref, s32[1]{0:T(128)} %bitcast.core_ref, s32[1,6]{1,0:T(1,128)S(1)} %copy-done.5, s32[6]{0:T(128)S(1)} %copy-done.7, bf16[512,2688]{1,0:T(8,128)(2,1)S(1)} %pack.1.x_ref.own_ref, bf16[128,2048]{1,0:T(8,128)(2,1)S(1)} %bitcast.9, bf16[128,512]{1,0:T(8,128)(2,1)S(1)} %bitcast.11, ...), custom_call_target="tpu_custom_call" | custom-call | flops 1 | bytes 1 | tf_op jit(solution)/shard_map/low_part/pallas_call | solution.py:145
  25.2 5.2 %collective-permute-start.4 = (bf16[512,128]{1,0:T(8,128)(2,1)S(1)}, bf16[512,128]{1,0:T(8,128)(2,1)S(1)}, u32[]{:S(2)}, u32[]{:S(2)}) collective-permute-start(bf16[512,128]{1,0:T(8,128)(2,1)S(1)} %low_part.1), channel_id=1, source_target_pairs={{0,4},{4,0},{8,12},{12,8},{1,5},{5,1},{9,13},{13,9},{2,6},{6,2},{1... | collective-permute-start | bytes 393224 | tf_op jit(solution)/shard_map/ppermute | solution.py:33
  31.5 1.6 %collective-permute-done.7.refs_2_ = bf16[512,256]{1,0:T(8,128)(2,1)S(1)} collective-permute-done((bf16[512,256]{1,0:T(8,128)(2,1)S(1)}, bf16[512,256]{1,0:T(8,128)(2,1)S(1)}, u32[]{:S(2)}, u32[]{:S(2)}) %collective-permute-start.7) | collective-permute-done | bytes 262176 | tf_op jit(solution)/shard_map/ppermute | solution.py:33
  34.4 1.6 %collective-permute-start.12 = (bf16[512,256]{1,0:T(8,128)(2,1)S(1)}, bf16[512,256]{1,0:T(8,128)(2,1)S(1)}, u32[]{:S(2)}, u32[]{:S(2)}) collective-permute-start(bf16[512,256]{1,0:T(8,128)(2,1)S(1)} %collective-permute-done.3.refs_0_), channel_id=1, source_target_pairs={{0,18},{2,16},{16,2},{18,0},{1,19},{3,17},{17,3},{19,1},{4,22},{6,... | collective-permute-start | bytes 786440 | tf_op jit(solution)/shard_map/ppermute | solution.py:33
  36.6 1.4 %collective-permute-start.10 = (bf16[512,256]{1,0:T(8,128)(2,1)S(1)}, bf16[512,256]{1,0:T(8,128)(2,1)S(1)}, u32[]{:S(2)}, u32[]{:S(2)}) collective-permute-start(bf16[512,256]{1,0:T(8,128)(2,1)S(1)} %collective-permute-done.3.refs_0_), channel_id=1, source_target_pairs={{0,2},{2,0},{16,18},{18,16},{1,3},{3,1},{17,19},{19,17},{4,6},{6,4... | collective-permute-start | bytes 786440 | tf_op jit(solution)/shard_map/ppermute | solution.py:33
  38.4 5.7 %collective-permute-done.9.refs_0_ = bf16[512,256]{1,0:T(8,128)(2,1)S(1)} collective-permute-done((bf16[512,256]{1,0:T(8,128)(2,1)S(1)}, bf16[512,256]{1,0:T(8,128)(2,1)S(1)}, u32[]{:S(2)}, u32[]{:S(2)}) %collective-permute-start.9) | collective-permute-done | bytes 262176 | tf_op jit(solution)/shard_map/ppermute | solution.py:33
  44.6 4.5 %collective-permute-done.11.refs_2_ = bf16[512,256]{1,0:T(8,128)(2,1)S(1)} collective-permute-done((bf16[512,256]{1,0:T(8,128)(2,1)S(1)}, bf16[512,256]{1,0:T(8,128)(2,1)S(1)}, u32[]{:S(2)}, u32[]{:S(2)}) %collective-permute-start.11) | collective-permute-done | bytes 262176 | tf_op jit(solution)/shard_map/ppermute | solution.py:33
  50.5 1.7 %collective-permute-start.17 = (bf16[512,256]{1,0:T(8,128)(2,1)S(1)}, bf16[512,256]{1,0:T(8,128)(2,1)S(1)}, u32[]{:S(2)}, u32[]{:S(2)}) collective-permute-start(bf16[512,256]{1,0:T(8,128)(2,1)S(1)} %collective-permute-done.9.refs_0_), channel_id=1, source_target_pairs={{0,18},{2,16},{16,2},{18,0},{1,19},{3,17},{17,3},{19,1},{4,22},{6,... | collective-permute-start | bytes 786440 | tf_op jit(solution)/shard_map/ppermute | solution.py:33
  55.5 5.2 %collective-permute-done.17.refs_3_ = bf16[512,256]{1,0:T(8,128)(2,1)S(1)} collective-permute-done((bf16[512,256]{1,0:T(8,128)(2,1)S(1)}, bf16[512,256]{1,0:T(8,128)(2,1)S(1)}, u32[]{:S(2)}, u32[]{:S(2)}) %collective-permute-start.17) | collective-permute-done | bytes 262176 | tf_op jit(solution)/shard_map/ppermute | solution.py:33
  60.7 4.6 %collective-permute-done.16.refs_2_ = bf16[512,256]{1,0:T(8,128)(2,1)S(1)} collective-permute-done((bf16[512,256]{1,0:T(8,128)(2,1)S(1)}, bf16[512,256]{1,0:T(8,128)(2,1)S(1)}, u32[]{:S(2)}, u32[]{:S(2)}) %collective-permute-start.16) | collective-permute-done | bytes 262176 | tf_op jit(solution)/shard_map/ppermute | solution.py:33
  65.3 2.4 %collective-permute-done.18.refs_4_ = bf16[1024,256]{1,0:T(8,128)(2,1)S(1)} collective-permute-done((bf16[1024,256]{1,0:T(8,128)(2,1)S(1)}, bf16[1024,256]{1,0:T(8,128)(2,1)S(1)}, u32[]{:S(2)}, u32[]{:S(2)}) %collective-permute-start.18) | collective-permute-done | bytes 524320 | tf_op jit(solution)/shard_map/ppermute | solution.py:33
  69.2 1.3 %collective-permute-done.21.low_other_ref = bf16[512,128]{1,0:T(8,128)(2,1)S(1)} collective-permute-done((bf16[512,128]{1,0:T(8,128)(2,1)S(1)}, bf16[512,128]{1,0:T(8,128)(2,1)S(1)}, u32[]{:S(2)}, u32[]{:S(2)}) %collective-permute-start.21) | collective-permute-done | bytes 131104 | tf_op jit(solution)/shard_map/ppermute | solution.py:33
  72.4 2.1 %base.1.base_ref = f32[512,512]{1,0:T(8,128)S(1)} custom-call(s32[1]{0:T(128)} %bitcast.1.at_ref, s32[1]{0:T(128)} %bitcast.2.dp_ref, s32[1]{0:T(128)} %bitcast.core_ref, s32[1,6]{1,0:T(1,128)S(1)} %copy-done.5, s32[6]{0:T(128)S(1)} %copy-done.7, bf16[512,2688]{1,0:T(8,128)(2,1)S(1)} %pack.1.x_ref.own_ref, bf16[8192,512]{1,0:T(8,128)(2,1)S(1)} %bitcast.7, ...), custom_call_target="tpu_custom_call" | custom-call | flops 1 | bytes 1 | tf_op jit(solution)/shard_map/base/pallas_call | solution.py:269
  74.5 19.2 %collective-permute-done.19.refs_0_ = bf16[1024,256]{1,0:T(8,128)(2,1)S(1)} collective-permute-done((bf16[1024,256]{1,0:T(8,128)(2,1)S(1)}, bf16[1024,256]{1,0:T(8,128)(2,1)S(1)}, u32[]{:S(2)}, u32[]{:S(2)}) %collective-permute-start.19) | collective-permute-done | bytes 524320 | tf_op jit(solution)/shard_map/ppermute | solution.py:33
  94.5 1.7 %collective-permute-done.23.got_ref = bf16[64,2560]{1,0:T(8,128)(2,1)S(1)} collective-permute-done((bf16[64,2560]{1,0:T(8,128)(2,1)S(1)}, bf16[64,2560]{1,0:T(8,128)(2,1)S(1)}, u32[]{:S(2)}, u32[]{:S(2)}) %collective-permute-start.23) | collective-permute-done | bytes 327712 | tf_op jit(solution)/shard_map/ppermute | solution.py:33
  97.4 2.1 %finish.1 = bf16[768,512]{1,0:T(8,128)(2,1)} custom-call(s32[1]{0:T(128)} %bitcast.core_ref, s32[1,6]{1,0:T(1,128)S(1)} %copy-done.5, f32[512,512]{1,0:T(8,128)S(1)} %base.1.base_ref, bf16[1024,256]{1,0:T(8,128)(2,1)S(1)} %collective-permute-done.19.refs_0_, bf16[1024,256]{1,0:T(8,128)(2,1)S(1)} %collective-permute-done.13.refs_1_, ...), custom_call_target="tpu_custom_call" | custom-call | flops 1 | bytes 1 | tf_op jit(solution)/shard_map/finish/pallas_call | solution.py:331
  (60 shorter events, 18.3 us)
Async XLA Ops:
  2.5 11.9 %collective-permute-start = (bf16[64,2560]{1,0:T(8,128)(2,1)}, bf16[64,2560]{1,0:T(8,128)(2,1)S(1)}, u32[]{:S(2)}, u32[]{:S(2)}) collective-permute-start(bf16[64,2560]{1,0:T(8,128)(2,1)} %own_half.1), channel_id=1, source_target_pairs={{0,2},{2,0},{1,3},{3,1},{4,6},{6,4},{5,7},{7,5},{8,10},{10,8},{9,1... | collective-permute-start | bytes 983048 | tf_op jit(solution)/shard_map/ppermute | solution.py:29
  6.6 7.8 %collective-permute-start.2 = (bf16[512,256]{1,0:T(8,128)(2,1)S(1)}, bf16[512,256]{1,0:T(8,128)(2,1)S(1)}, u32[]{:S(2)}, u32[]{:S(2)}) collective-permute-start(bf16[512,256]{1,0:T(8,128)(2,1)S(1)} %get-tuple-element.39), channel_id=1, source_target_pairs={{0,4},{4,0},{8,12},{12,8},{1,5},{5,1},{9,13},{13,9},{2,6},{6,2},{1... | collective-permute-start | bytes 786440 | tf_op jit(solution)/shard_map/ppermute | solution.py:33
  14.5 18.7 %collective-permute-start.5 = (bf16[512,2688]{1,0:T(8,128)(2,1)S(1)}, bf16[512,2688]{1,0:T(8,128)(2,1)S(1)}, u32[]{:S(2)}, u32[]{:S(2)}) collective-permute-start(bf16[512,2688]{1,0:T(8,128)(2,1)S(1)} %pack.1.x_ref.own_ref), channel_id=1, source_target_pairs={{0,1},{1,0},{2,3},{3,2},{4,5},{5,4},{6,7},{7,6},{8,9},{9,8},{10,11... | collective-permute-start | bytes 8257544 | tf_op jit(solution)/shard_map/ppermute | solution.py:33
  14.5 6.2 %collective-permute-start.1 = (bf16[64,2560]{1,0:T(8,128)(2,1)S(1)}, bf16[64,2560]{1,0:T(8,128)(2,1)S(1)}, u32[]{:S(2)}, u32[]{:S(2)}) collective-permute-start(bf16[64,2560]{1,0:T(8,128)(2,1)S(1)} %collective-permute-done.refs_0_), channel_id=1, source_target_pairs={{0,1},{1,0},{2,3},{3,2},{4,5},{5,4},{6,7},{7,6},{8,9},{9,8},{10,11... | collective-permute-start | bytes 983048 | tf_op jit(solution)/shard_map/ppermute | solution.py:33
  15.0 10.2 %collective-permute-start.3 = (bf16[512,256]{1,0:T(8,128)(2,1)S(1)}, bf16[512,256]{1,0:T(8,128)(2,1)S(1)}, u32[]{:S(2)}, u32[]{:S(2)}) collective-permute-start(bf16[512,256]{1,0:T(8,128)(2,1)S(1)} %get-tuple-element.21), channel_id=1, source_target_pairs={{0,12},{4,8},{8,4},{12,0},{1,13},{5,9},{9,5},{13,1},{2,14},{6,10},... | collective-permute-start | bytes 786440 | tf_op jit(solution)/shard_map/ppermute | solution.py:33
  18.6 11.8 %collective-permute-start.8 = (bf16[512,256]{1,0:T(8,128)(2,1)S(1)}, bf16[512,256]{1,0:T(8,128)(2,1)S(1)}, u32[]{:S(2)}, u32[]{:S(2)}) collective-permute-start(bf16[512,256]{1,0:T(8,128)(2,1)S(1)} %collective-permute-done.2.refs_0_), channel_id=1, source_target_pairs={{0,18},{2,16},{16,2},{18,0},{1,19},{3,17},{17,3},{19,1},{4,22},{6,... | collective-permute-start | bytes 786440 | tf_op jit(solution)/shard_map/ppermute | solution.py:33
  20.2 12.8 %collective-permute-start.7 = (bf16[512,256]{1,0:T(8,128)(2,1)S(1)}, bf16[512,256]{1,0:T(8,128)(2,1)S(1)}, u32[]{:S(2)}, u32[]{:S(2)}) collective-permute-start(bf16[512,256]{1,0:T(8,128)(2,1)S(1)} %collective-permute-done.2.refs_0_), channel_id=1, source_target_pairs={{0,16},{2,18},{16,0},{18,2},{1,17},{3,19},{17,1},{19,3},{4,20},{6,... | collective-permute-start | bytes 786440 | tf_op jit(solution)/shard_map/ppermute | solution.py:33
  20.7 12.4 %collective-permute-start.6 = (bf16[512,256]{1,0:T(8,128)(2,1)S(1)}, bf16[512,256]{1,0:T(8,128)(2,1)S(1)}, u32[]{:S(2)}, u32[]{:S(2)}) collective-permute-start(bf16[512,256]{1,0:T(8,128)(2,1)S(1)} %collective-permute-done.2.refs_0_), channel_id=1, source_target_pairs={{0,2},{2,0},{16,18},{18,16},{1,3},{3,1},{17,19},{19,17},{4,6},{6,4... | collective-permute-start | bytes 786440 | tf_op jit(solution)/shard_map/ppermute | solution.py:33
  25.2 12.8 %collective-permute-start.4 = (bf16[512,128]{1,0:T(8,128)(2,1)S(1)}, bf16[512,128]{1,0:T(8,128)(2,1)S(1)}, u32[]{:S(2)}, u32[]{:S(2)}) collective-permute-start(bf16[512,128]{1,0:T(8,128)(2,1)S(1)} %low_part.1), channel_id=1, source_target_pairs={{0,4},{4,0},{8,12},{12,8},{1,5},{5,1},{9,13},{13,9},{2,6},{6,2},{1... | collective-permute-start | bytes 393224 | tf_op jit(solution)/shard_map/ppermute | solution.py:33
  30.4 13.8 %collective-permute-start.9 = (bf16[512,256]{1,0:T(8,128)(2,1)S(1)}, bf16[512,256]{1,0:T(8,128)(2,1)S(1)}, u32[]{:S(2)}, u32[]{:S(2)}) collective-permute-start(bf16[512,256]{1,0:T(8,128)(2,1)S(1)} %get-tuple-element.26), channel_id=1, source_target_pairs={{0,8},{4,12},{8,0},{12,4},{1,9},{5,13},{9,1},{13,5},{2,10},{6,14},... | collective-permute-start | bytes 786440 | tf_op jit(solution)/shard_map/ppermute | solution.py:33
  34.4 10.2 %collective-permute-start.12 = (bf16[512,256]{1,0:T(8,128)(2,1)S(1)}, bf16[512,256]{1,0:T(8,128)(2,1)S(1)}, u32[]{:S(2)}, u32[]{:S(2)}) collective-permute-start(bf16[512,256]{1,0:T(8,128)(2,1)S(1)} %collective-permute-done.3.refs_0_), channel_id=1, source_target_pairs={{0,18},{2,16},{16,2},{18,0},{1,19},{3,17},{17,3},{19,1},{4,22},{6,... | collective-permute-start | bytes 786440 | tf_op jit(solution)/shard_map/ppermute | solution.py:33
  36.0 13.1 %collective-permute-start.11 = (bf16[512,256]{1,0:T(8,128)(2,1)S(1)}, bf16[512,256]{1,0:T(8,128)(2,1)S(1)}, u32[]{:S(2)}, u32[]{:S(2)}) collective-permute-start(bf16[512,256]{1,0:T(8,128)(2,1)S(1)} %collective-permute-done.3.refs_0_), channel_id=1, source_target_pairs={{0,16},{2,18},{16,0},{18,2},{1,17},{3,19},{17,1},{19,3},{4,20},{6,... | collective-permute-start | bytes 786440 | tf_op jit(solution)/shard_map/ppermute | solution.py:33
  36.6 12.5 %collective-permute-start.10 = (bf16[512,256]{1,0:T(8,128)(2,1)S(1)}, bf16[512,256]{1,0:T(8,128)(2,1)S(1)}, u32[]{:S(2)}, u32[]{:S(2)}) collective-permute-start(bf16[512,256]{1,0:T(8,128)(2,1)S(1)} %collective-permute-done.3.refs_0_), channel_id=1, source_target_pairs={{0,2},{2,0},{16,18},{18,16},{1,3},{3,1},{17,19},{19,17},{4,6},{6,4... | collective-permute-start | bytes 786440 | tf_op jit(solution)/shard_map/ppermute | solution.py:33
  38.0 16.2 %collective-permute-start.13 = (bf16[1024,256]{1,0:T(8,128)(2,1)S(1)}, bf16[1024,256]{1,0:T(8,128)(2,1)S(1)}, u32[]{:S(2)}, u32[]{:S(2)}) collective-permute-start(bf16[1024,256]{1,0:T(8,128)(2,1)S(1)} %panel.3), channel_id=1, source_target_pairs={{0,4},{4,0},{8,12},{12,8},{1,5},{5,1},{9,13},{13,9},{2,6},{6,2},{1... | collective-permute-start | bytes 1572872 | tf_op jit(solution)/shard_map/ppermute | solution.py:33
  50.4 17.3 %collective-permute-start.18 = (bf16[1024,256]{1,0:T(8,128)(2,1)S(1)}, bf16[1024,256]{1,0:T(8,128)(2,1)S(1)}, u32[]{:S(2)}, u32[]{:S(2)}) collective-permute-start(bf16[1024,256]{1,0:T(8,128)(2,1)S(1)} %panel.4), channel_id=1, source_target_pairs={{0,4},{4,0},{8,12},{12,8},{1,5},{5,1},{9,13},{13,9},{2,6},{6,2},{1... | collective-permute-start | bytes 1572872 | tf_op jit(solution)/shard_map/ppermute | solution.py:33
  50.5 10.2 %collective-permute-start.17 = (bf16[512,256]{1,0:T(8,128)(2,1)S(1)}, bf16[512,256]{1,0:T(8,128)(2,1)S(1)}, u32[]{:S(2)}, u32[]{:S(2)}) collective-permute-start(bf16[512,256]{1,0:T(8,128)(2,1)S(1)} %collective-permute-done.9.refs_0_), channel_id=1, source_target_pairs={{0,18},{2,16},{16,2},{18,0},{1,19},{3,17},{17,3},{19,1},{4,22},{6,... | collective-permute-start | bytes 786440 | tf_op jit(solution)/shard_map/ppermute | solution.py:33
  52.2 13.1 %collective-permute-start.16 = (bf16[512,256]{1,0:T(8,128)(2,1)S(1)}, bf16[512,256]{1,0:T(8,128)(2,1)S(1)}, u32[]{:S(2)}, u32[]{:S(2)}) collective-permute-start(bf16[512,256]{1,0:T(8,128)(2,1)S(1)} %collective-permute-done.9.refs_0_), channel_id=1, source_target_pairs={{0,16},{2,18},{16,0},{18,2},{1,17},{3,19},{17,1},{19,3},{4,20},{6,... | collective-permute-start | bytes 786440 | tf_op jit(solution)/shard_map/ppermute | solution.py:33
  52.8 12.5 %collective-permute-start.15 = (bf16[512,256]{1,0:T(8,128)(2,1)S(1)}, bf16[512,256]{1,0:T(8,128)(2,1)S(1)}, u32[]{:S(2)}, u32[]{:S(2)}) collective-permute-start(bf16[512,256]{1,0:T(8,128)(2,1)S(1)} %collective-permute-done.9.refs_0_), channel_id=1, source_target_pairs={{0,2},{2,0},{16,18},{18,16},{1,3},{3,1},{17,19},{19,17},{4,6},{6,4... | collective-permute-start | bytes 786440 | tf_op jit(solution)/shard_map/ppermute | solution.py:33
  54.3 14.8 %collective-permute-start.14 = (bf16[512,128]{1,0:T(8,128)(2,1)S(1)}, bf16[512,128]{1,0:T(8,128)(2,1)S(1)}, u32[]{:S(2)}, u32[]{:S(2)}) collective-permute-start(bf16[512,128]{1,0:T(8,128)(2,1)S(1)} %add_convert_fusion.2), channel_id=1, source_target_pairs={{0,8},{4,12},{8,0},{12,4},{1,9},{5,13},{9,1},{13,5},{2,10},{6,14},... | collective-permute-start | bytes 393224 | tf_op jit(solution)/shard_map/ppermute | solution.py:33
  69.0 24.7 %collective-permute-start.19 = (bf16[1024,256]{1,0:T(8,128)(2,1)S(1)}, bf16[1024,256]{1,0:T(8,128)(2,1)S(1)}, u32[]{:S(2)}, u32[]{:S(2)}) collective-permute-start(bf16[1024,256]{1,0:T(8,128)(2,1)S(1)} %panel.5), channel_id=1, source_target_pairs={{0,8},{4,12},{8,0},{12,4},{1,9},{5,13},{9,1},{13,5},{2,10},{6,14},... | collective-permute-start | bytes 1572872 | tf_op jit(solution)/shard_map/ppermute | solution.py:33
  69.1 1.4 %collective-permute-start.21 = (bf16[512,128]{1,0:T(8,128)(2,1)S(1)}, bf16[512,128]{1,0:T(8,128)(2,1)S(1)}, u32[]{:S(2)}, u32[]{:S(2)}) collective-permute-start(bf16[512,128]{1,0:T(8,128)(2,1)S(1)} %add_convert_fusion.1.low_ref), channel_id=1, source_target_pairs={{0,1},{1,0},{2,3},{3,2},{4,5},{5,4},{6,7},{7,6},{8,9},{9,8},{10,11... | collective-permute-start | bytes 393224 | tf_op jit(solution)/shard_map/ppermute | solution.py:33
  71.6 22.2 %collective-permute-start.22 = (bf16[64,2560]{1,0:T(8,128)(2,1)S(1)}, bf16[64,2560]{1,0:T(8,128)(2,1)S(1)}, u32[]{:S(2)}, u32[]{:S(2)}) collective-permute-start(bf16[64,2560]{1,0:T(8,128)(2,1)S(1)} %get-tuple-element.34), channel_id=1, source_target_pairs={{0,2},{2,0},{1,3},{3,1},{4,6},{6,4},{5,7},{7,5},{8,10},{10,8},{9,1... | collective-permute-start | bytes 983048 | tf_op jit(solution)/shard_map/ppermute | solution.py:29
  93.8 3.7 %collective-permute-start.20 = (f32[512,256]{1,0:T(8,128)S(1)}, f32[512,256]{1,0:T(8,128)S(1)}, u32[]{:S(2)}, u32[]{:S(2)}) collective-permute-start(f32[512,256]{1,0:T(8,128)S(1)} %other_rows.1), channel_id=1, source_target_pairs={{0,1},{1,0},{2,3},{3,2},{4,5},{5,4},{6,7},{7,6},{8,9},{9,8},{10,11... | collective-permute-start | bytes 1572872 | tf_op jit(solution)/shard_map/ppermute | solution.py:33
  93.9 2.3 %collective-permute-start.23 = (bf16[64,2560]{1,0:T(8,128)(2,1)S(1)}, bf16[64,2560]{1,0:T(8,128)(2,1)S(1)}, u32[]{:S(2)}, u32[]{:S(2)}) collective-permute-start(bf16[64,2560]{1,0:T(8,128)(2,1)S(1)} %add_convert_fusion.own_ref), channel_id=1, source_target_pairs={{0,1},{1,0},{2,3},{3,2},{4,5},{5,4},{6,7},{7,6},{8,9},{9,8},{10,11... | collective-permute-start | bytes 983048 | tf_op jit(solution)/shard_map/ppermute | solution.py:33
  (10 other events, 98.5 us)

commit v9 on v8

--- a/solution.py
+++ b/solution.py
@@ -362,8 +362,8 @@
         halves += [got, flip(got, "pipe", n_pipe, 1)]
     panel_at = place if planes == 4 else jnp.zeros_like(place)
 
-    def share(k):
-        return lax.dynamic_slice(base_weight, (k * feat + q * part_rows, me_pipe * half), (part_rows, half))
+    def share(k, plane=q):
+        return lax.dynamic_slice(base_weight, (k * feat + plane * part_rows, me_pipe * half), (part_rows, half))
 
     def gathered(piece):
         if planes != 4:
@@ -374,25 +374,34 @@
         return (low.astype(F32) + flip(after(low, *before), "tensor", n_t, mask).astype(F32)).astype(BF16)
 
     if n_t == 4:
+        twice = planes == 4
         share_1 = share(me_t ^ 1)
+        if twice:
+            share_1 = jnp.concatenate([share_1, share(me_t ^ 1, q ^ 3)], axis=0)
         weight = {1: flip(share_1, "tensor", n_t, 1)}
         weight[3] = flip(after(share(me_t ^ 3), weight[1]), "tensor", n_t, 3)
         weight[2] = flip(after(share(me_t ^ 2), weight[3]), "tensor", n_t, 2)
         x = pack(after(block_fill, share_1), block_tenant_index, tokens, cotangent, blocks, 2 * rank)
         x_other = flip(after(x, weight[1], *halves[::2]), "pipe", n_pipe, 1)
-        pieces, order = gathered(weight[1])
-        low = low_part(dp, core, block_fill, block_tenant_index, x, own_a, own_b, halves, blocks, rank)
-        pieces[0] = after(pieces[0], weight[3], low)
+        if twice:
+            mine = weight[1][:part_rows]
+            near = [flip(mine, ("groups", "dp"), planes, m) for m in (1, 2)]
+            pieces, order = [mine, weight[1][part_rows:], *near], [0, 3, 1, 2]
+        else:
+            pieces, order = gathered(weight[1])
+        low = low_part(after(dp, x_other), core, block_fill, block_tenant_index, x, own_a, own_b, halves, blocks, rank)
+        pieces[0] = after(pieces[0], weight[3])
         (y_1,) = panel_product(order, panel_at, x, x_other, pieces, half)
         low = add_flipped(low, 1, weight[3])
-        part_1 = flip(after(y_1, low), "tensor", n_t, 1)
-        pieces, order = gathered(after(weight[3], y_1))
+        pieces, order = gathered(after(weight[3], *pieces))
+        low = add_flipped(low, 2)
         pieces[0] = after(pieces[0], weight[2])
         (y,) = panel_product(order, panel_at, x, x_other, pieces, half)
-        add = flip(y, "tensor", n_t, 1)
-        low = add_flipped(low, 2, y, part_1)
-        pieces, order = gathered(after(weight[2], y))
+        add = flip(after(y, low), "tensor", n_t, 1)
+        part_1 = flip(after(y_1, y), "tensor", n_t, 1)
+        pieces, order = gathered(after(weight[2], *pieces))
         (y_2,) = panel_product(order, panel_at, x, x_other, pieces, half, adds=[add])
+        pieces.append(part_1)
         parts = [flip(y_2, "tensor", n_t, 2), part_1]
     else:
         x = pack(block_fill, block_tenant_index, tokens, cotangent, blocks, 2 * rank)

time: 99.7 us -> 105 us (1.053)
  starting transfers between devices: 28.8 us -> 33.4 us
  waiting for transfers between devices: 48.1 us -> 52.3 us
  local copies, waits for them, and re-layouts: 4.39 us -> 1.49 us
    ppermute x22 -> x21, starting transfers between devices: 25.2 us -> 30.4 us  [flip(): return lax.ppermute(x, names, [(i, i ^ mask) for i in range(count)])]
    ppermute x2, waiting for transfers between devices: 0.01 us -> 5 us  [shift(): lax.ppermute(x, name, [(i, (i + step) % count) for i in range(count)])]
    unnamed x20 -> x16, local copies, waits for them, and re-layouts: 3.23 us -> 0.04 us
    ppermute x22 -> x21, waiting for transfers between devices: 48.1 us -> 47.3 us  [flip(): return lax.ppermute(x, names, [(i, i ^ mask) for i in range(count)])]
  transfers between devices with their start and end apart: 24 -> 23, of which waited for: 14 -> 12; matrix products, arithmetic and copies ran while one was open for 1% -> 0% of each run, Pallas kernels for 13% -> 14%
where the time goes in v9:
time: 105 us
  waiting for transfers between devices  52.3 us (50%)
  starting transfers between devices  33.4 us (32%)
  Pallas kernels  17.1 us (16%)
  local copies, waits for them, and re-layouts  1.49 us (1%)
    ppermute x21, waiting for transfers between devices, flip(): return lax.ppermute(x, names, [(i, i ^ mask) for i in range(count)])  47.3 us
    ppermute x21, starting transfers between devices, flip(): return lax.ppermute(x, names, [(i, i ^ mask) for i in range(count)])  30.4 us
    ppermute x2, waiting for transfers between devices, shift(): lax.ppermute(x, name, [(i, (i + step) % count) for i in range(count)])  5 us
    pallas_call x3, Pallas kernels, panel_product(): pl.pallas_call(functools.partial(panel_kernel, order, len(pieces)), in_sp...  3.75 us
    ppermute x2, starting transfers between devices, shift(): lax.ppermute(x, name, [(i, (i + step) % count) for i in range(count)])  2.98 us
    pallas_call x1, Pallas kernels, pack(): pl.pallas_call(functools.partial(pack_kernel, blocks, rows // blocks), in...  2.88 us
    pallas_call x1, Pallas kernels, low_part(): pl.pallas_call(functools.partial(low_kernel, n_dp, rank, blocks), in_spec...  2.16 us
    pallas_call x1, Pallas kernels, base_product(): pl.pallas_call(functools.partial(base_kernel, n_dp, rank, blocks), grid_s...  2.14 us
  transfers between devices with their start and end apart: 23, of which 12 were waited for; matrix products, arithmetic and copies ran while one was open for 0% of the time, Pallas kernels for 14%

profile of v9, /device:TPU:0, one launch (start us, length us, event | category | flops | bytes accessed | tf_op | source)
XLA Modules:
  0.0 105.3 jit_solution(47138195732218976)
XLA Ops:
  2.2 3.1 %collective-permute-start = (bf16[1024,256]{1,0:T(8,128)(2,1)S(1)}, bf16[1024,256]{1,0:T(8,128)(2,1)S(1)}, u32[]{:S(2)}, u32[]{:S(2)}) collective-permute-start(bf16[1024,256]{1,0:T(8,128)(2,1)S(1)} %pad_maximum_fusion), channel_id=1, source_target_pairs={{0,4},{4,0},{8,12},{12,8},{1,5},{5,1},{9,13},{13,9},{2,6},{6,2},{1... | collective-permute-start | bytes 1572872 | tf_op jit(solution)/shard_map/ppermute | solution.py:33
  5.3 1.8 %own_half.1 = bf16[64,2560]{1,0:T(8,128)(2,1)} custom-call(s32[1]{0:T(128)} %bitcast.core_ref, bf16[128,2048]{1,0:T(8,128)(2,1)} %bitcast.8, bf16[128,512]{1,0:T(8,128)(2,1)} %bitcast.10), custom_call_target="tpu_custom_call" | custom-call | flops 1 | bytes 1 | tf_op jit(solution)/shard_map/own_half/pallas_call | solution.py:73
  7.1 1.5 %collective-permute-start.1 = (bf16[64,2560]{1,0:T(8,128)(2,1)}, bf16[64,2560]{1,0:T(8,128)(2,1)S(1)}, u32[]{:S(2)}, u32[]{:S(2)}) collective-permute-start(bf16[64,2560]{1,0:T(8,128)(2,1)} %own_half.1), channel_id=1, source_target_pairs={{0,2},{2,0},{1,3},{3,1},{4,6},{6,4},{5,7},{7,5},{8,10},{10,8},{9,1... | collective-permute-start | bytes 983048 | tf_op jit(solution)/shard_map/ppermute | solution.py:29
  8.6 2.9 %pack.1.x_ref.own_ref = bf16[512,2688]{1,0:T(8,128)(2,1)S(1)} custom-call(s32[1,6]{1,0:T(1,128)S(1)} %copy-done.4, s32[6]{0:T(128)S(1)} %copy-done.5, bf16[768,2048]{1,0:T(8,128)(2,1)S(1)} %copy-done, bf16[768,512]{1,0:T(8,128)(2,1)S(1)} %copy-done.3), custom_call_target="tpu_custom_call" | custom-call | flops 1 | bytes 1 | tf_op jit(solution)/shard_map/pack/pallas_call | solution.py:102
  11.5 5.0 %collective-permute-done.1.refs_0_ = bf16[64,2560]{1,0:T(8,128)(2,1)S(1)} collective-permute-done((bf16[64,2560]{1,0:T(8,128)(2,1)}, bf16[64,2560]{1,0:T(8,128)(2,1)S(1)}, u32[]{:S(2)}, u32[]{:S(2)}) %collective-permute-start.1) | collective-permute-done | bytes 327712 | tf_op jit(solution)/shard_map/ppermute | solution.py:29
  17.7 3.8 %collective-permute-start.4 = (bf16[512,256]{1,0:T(8,128)(2,1)S(1)}, bf16[512,256]{1,0:T(8,128)(2,1)S(1)}, u32[]{:S(2)}, u32[]{:S(2)}) collective-permute-start(bf16[512,256]{1,0:T(8,128)(2,1)S(1)} %get-tuple-element.24), channel_id=1, source_target_pairs={{0,12},{4,8},{8,4},{12,0},{1,13},{5,9},{9,5},{13,1},{2,14},{6,10},... | collective-permute-start | bytes 786440 | tf_op jit(solution)/shard_map/ppermute | solution.py:33
  21.5 1.6 %collective-permute-start.9 = (bf16[512,256]{1,0:T(8,128)(2,1)S(1)}, bf16[512,256]{1,0:T(8,128)(2,1)S(1)}, u32[]{:S(2)}, u32[]{:S(2)}) collective-permute-start(bf16[512,256]{1,0:T(8,128)(2,1)S(1)} %get-tuple-element.27.refs_0_), channel_id=1, source_target_pairs={{0,16},{2,18},{16,0},{18,2},{1,17},{3,19},{17,1},{19,3},{4,20},{6,... | collective-permute-start | bytes 786440 | tf_op jit(solution)/shard_map/ppermute | solution.py:33
  23.1 1.5 %collective-permute-start.8 = (bf16[512,256]{1,0:T(8,128)(2,1)S(1)}, bf16[512,256]{1,0:T(8,128)(2,1)S(1)}, u32[]{:S(2)}, u32[]{:S(2)}) collective-permute-start(bf16[512,256]{1,0:T(8,128)(2,1)S(1)} %get-tuple-element.27.refs_0_), channel_id=1, source_target_pairs={{0,2},{2,0},{16,18},{18,16},{1,3},{3,1},{17,19},{19,17},{4,6},{6,4... | collective-permute-start | bytes 786440 | tf_op jit(solution)/shard_map/ppermute | solution.py:33
  24.6 2.2 %low_part.1 = bf16[512,128]{1,0:T(8,128)(2,1)S(1)} custom-call(s32[1]{0:T(128)} %bitcast.2.dp_ref, s32[1]{0:T(128)} %bitcast.core_ref, s32[1,6]{1,0:T(1,128)S(1)} %copy-done.4, s32[6]{0:T(128)S(1)} %copy-done.5, bf16[512,2688]{1,0:T(8,128)(2,1)S(1)} %pack.1.x_ref.own_ref, bf16[128,2048]{1,0:T(8,128)(2,1)S(1)} %bitcast.9, bf16[128,512]{1,0:T(8,128)(2,1)S(1)} %bitcast.11, ...), custom_call_target="tpu_custom_call" | custom-call | flops 1 | bytes 1 | tf_op jit(solution)/shard_map/low_part/pallas_call | solution.py:145
  28.0 5.2 %collective-permute-start.5 = (bf16[512,128]{1,0:T(8,128)(2,1)S(1)}, bf16[512,128]{1,0:T(8,128)(2,1)S(1)}, u32[]{:S(2)}, u32[]{:S(2)}) collective-permute-start(bf16[512,128]{1,0:T(8,128)(2,1)S(1)} %low_part.1), channel_id=1, source_target_pairs={{0,4},{4,0},{8,12},{12,8},{1,5},{5,1},{9,13},{13,9},{2,6},{6,2},{1... | collective-permute-start | bytes 393224 | tf_op jit(solution)/shard_map/ppermute | solution.py:33
  33.3 2.4 %collective-permute-start.12 = (bf16[512,256]{1,0:T(8,128)(2,1)S(1)}, bf16[512,256]{1,0:T(8,128)(2,1)S(1)}, u32[]{:S(2)}, u32[]{:S(2)}) collective-permute-start(bf16[512,256]{1,0:T(8,128)(2,1)S(1)} %collective-permute-done.4.refs_0_), channel_id=1, source_target_pairs={{0,18},{2,16},{16,2},{18,0},{1,19},{3,17},{17,3},{19,1},{4,22},{6,... | collective-permute-start | bytes 786440 | tf_op jit(solution)/shard_map/ppermute | solution.py:33
  37.9 2.0 %collective-permute-start.6 = (bf16[512,128]{1,0:T(8,128)(2,1)S(1)}, bf16[512,128]{1,0:T(8,128)(2,1)S(1)}, u32[]{:S(2)}, u32[]{:S(2)}) collective-permute-start(bf16[512,128]{1,0:T(8,128)(2,1)S(1)} %add_convert_fusion.2), channel_id=1, source_target_pairs={{0,8},{4,12},{8,0},{12,4},{1,9},{5,13},{9,1},{13,5},{2,10},{6,14},... | collective-permute-start | bytes 393224 | tf_op jit(solution)/shard_map/ppermute | solution.py:33
  39.9 13.0 %collective-permute-done.7.refs_0_ = bf16[512,256]{1,0:T(8,128)(2,1)S(1)} collective-permute-done((bf16[512,256]{1,0:T(8,128)(2,1)S(1)}, bf16[512,256]{1,0:T(8,128)(2,1)S(1)}, u32[]{:S(2)}, u32[]{:S(2)}) %collective-permute-start.7) | collective-permute-done | bytes 262176 | tf_op jit(solution)/shard_map/ppermute | solution.py:33
  56.5 2.1 %collective-permute-start.18 = (bf16[1024,256]{1,0:T(8,128)(2,1)S(1)}, bf16[1024,256]{1,0:T(8,128)(2,1)S(1)}, u32[]{:S(2)}, u32[]{:S(2)}) collective-permute-start(bf16[1024,256]{1,0:T(8,128)(2,1)S(1)} %panel.5), channel_id=1, source_target_pairs={{0,4},{4,0},{8,12},{12,8},{1,5},{5,1},{9,13},{13,9},{2,6},{6,2},{1... | collective-permute-start | bytes 1572872 | tf_op jit(solution)/shard_map/ppermute | solution.py:33
  58.5 2.4 %collective-permute-start.15 = (bf16[512,256]{1,0:T(8,128)(2,1)S(1)}, bf16[512,256]{1,0:T(8,128)(2,1)S(1)}, u32[]{:S(2)}, u32[]{:S(2)}) collective-permute-start(bf16[512,256]{1,0:T(8,128)(2,1)S(1)} %collective-permute-done.7.refs_0_), channel_id=1, source_target_pairs={{0,18},{2,16},{16,2},{18,0},{1,19},{3,17},{17,3},{19,1},{4,22},{6,... | collective-permute-start | bytes 786440 | tf_op jit(solution)/shard_map/ppermute | solution.py:33
  62.0 6.7 %collective-permute-done.15.refs_3_ = bf16[512,256]{1,0:T(8,128)(2,1)S(1)} collective-permute-done((bf16[512,256]{1,0:T(8,128)(2,1)S(1)}, bf16[512,256]{1,0:T(8,128)(2,1)S(1)}, u32[]{:S(2)}, u32[]{:S(2)}) %collective-permute-start.15) | collective-permute-done | bytes 262176 | tf_op jit(solution)/shard_map/ppermute | solution.py:33
  68.7 3.5 %collective-permute-done.14.refs_2_ = bf16[512,256]{1,0:T(8,128)(2,1)S(1)} collective-permute-done((bf16[512,256]{1,0:T(8,128)(2,1)S(1)}, bf16[512,256]{1,0:T(8,128)(2,1)S(1)}, u32[]{:S(2)}, u32[]{:S(2)}) %collective-permute-start.14) | collective-permute-done | bytes 262176 | tf_op jit(solution)/shard_map/ppermute | solution.py:33
  73.5 1.9 %collective-permute-start.17 = (bf16[1024,256]{1,0:T(8,128)(2,1)S(1)}, bf16[1024,256]{1,0:T(8,128)(2,1)S(1)}, u32[]{:S(2)}, u32[]{:S(2)}) collective-permute-start(bf16[1024,256]{1,0:T(8,128)(2,1)S(1)} %panel.4), channel_id=1, source_target_pairs={{0,8},{4,12},{8,0},{12,4},{1,9},{5,13},{9,1},{13,5},{2,10},{6,14},... | collective-permute-start | bytes 1572872 | tf_op jit(solution)/shard_map/ppermute | solution.py:33
  77.8 5.8 %collective-permute-done.18.refs_1_ = bf16[1024,256]{1,0:T(8,128)(2,1)S(1)} collective-permute-done((bf16[1024,256]{1,0:T(8,128)(2,1)S(1)}, bf16[1024,256]{1,0:T(8,128)(2,1)S(1)}, u32[]{:S(2)}, u32[]{:S(2)}) %collective-permute-start.18) | collective-permute-done | bytes 524320 | tf_op jit(solution)/shard_map/ppermute | solution.py:33
  83.6 1.5 %collective-permute-start.21 = (bf16[64,2560]{1,0:T(8,128)(2,1)S(1)}, bf16[64,2560]{1,0:T(8,128)(2,1)S(1)}, u32[]{:S(2)}, u32[]{:S(2)}) collective-permute-start(bf16[64,2560]{1,0:T(8,128)(2,1)S(1)} %get-tuple-element.36), channel_id=1, source_target_pairs={{0,2},{2,0},{1,3},{3,1},{4,6},{6,4},{5,7},{7,5},{8,10},{10,8},{9,1... | collective-permute-start | bytes 983048 | tf_op jit(solution)/shard_map/ppermute | solution.py:29
  85.1 2.1 %base.1.base_ref = f32[512,512]{1,0:T(8,128)S(1)} custom-call(s32[1]{0:T(128)} %bitcast.1.at_ref, s32[1]{0:T(128)} %bitcast.2.dp_ref, s32[1]{0:T(128)} %bitcast.core_ref, s32[1,6]{1,0:T(1,128)S(1)} %copy-done.4, s32[6]{0:T(128)S(1)} %copy-done.5, bf16[512,2688]{1,0:T(8,128)(2,1)S(1)} %pack.1.x_ref.own_ref, bf16[8192,512]{1,0:T(8,128)(2,1)S(1)} %bitcast.7, ...), custom_call_target="tpu_custom_call" | custom-call | flops 1 | bytes 1 | tf_op jit(solution)/shard_map/base/pallas_call | solution.py:269
  87.3 12.3 %collective-permute-done.17.refs_0_ = bf16[1024,256]{1,0:T(8,128)(2,1)S(1)} collective-permute-done((bf16[1024,256]{1,0:T(8,128)(2,1)S(1)}, bf16[1024,256]{1,0:T(8,128)(2,1)S(1)}, u32[]{:S(2)}, u32[]{:S(2)}) %collective-permute-start.17) | collective-permute-done | bytes 524320 | tf_op jit(solution)/shard_map/ppermute | solution.py:33
  100.3 1.7 %collective-permute-done.22.got_ref = bf16[64,2560]{1,0:T(8,128)(2,1)S(1)} collective-permute-done((bf16[64,2560]{1,0:T(8,128)(2,1)S(1)}, bf16[64,2560]{1,0:T(8,128)(2,1)S(1)}, u32[]{:S(2)}, u32[]{:S(2)}) %collective-permute-start.22) | collective-permute-done | bytes 327712 | tf_op jit(solution)/shard_map/ppermute | solution.py:33
  103.2 2.1 %finish.1 = bf16[768,512]{1,0:T(8,128)(2,1)} custom-call(s32[1]{0:T(128)} %bitcast.core_ref, s32[1,6]{1,0:T(1,128)S(1)} %copy-done.4, f32[512,512]{1,0:T(8,128)S(1)} %base.1.base_ref, bf16[1024,256]{1,0:T(8,128)(2,1)S(1)} %collective-permute-done.17.refs_0_, bf16[1024,256]{1,0:T(8,128)(2,1)S(1)} %collective-permute-done.18.refs_1_, ...), custom_call_target="tpu_custom_call" | custom-call | flops 1 | bytes 1 | tf_op jit(solution)/shard_map/finish/pallas_call | solution.py:331
  (56 shorter events, 16.4 us)
Async XLA Ops:
  2.2 15.0 %collective-permute-start = (bf16[1024,256]{1,0:T(8,128)(2,1)S(1)}, bf16[1024,256]{1,0:T(8,128)(2,1)S(1)}, u32[]{:S(2)}, u32[]{:S(2)}) collective-permute-start(bf16[1024,256]{1,0:T(8,128)(2,1)S(1)} %pad_maximum_fusion), channel_id=1, source_target_pairs={{0,4},{4,0},{8,12},{12,8},{1,5},{5,1},{9,13},{13,9},{2,6},{6,2},{1... | collective-permute-start | bytes 1572872 | tf_op jit(solution)/shard_map/ppermute | solution.py:33
  7.1 9.4 %collective-permute-start.1 = (bf16[64,2560]{1,0:T(8,128)(2,1)}, bf16[64,2560]{1,0:T(8,128)(2,1)S(1)}, u32[]{:S(2)}, u32[]{:S(2)}) collective-permute-start(bf16[64,2560]{1,0:T(8,128)(2,1)} %own_half.1), channel_id=1, source_target_pairs={{0,2},{2,0},{1,3},{3,1},{4,6},{6,4},{5,7},{7,5},{8,10},{10,8},{9,1... | collective-permute-start | bytes 983048 | tf_op jit(solution)/shard_map/ppermute | solution.py:29
  17.2 7.4 %collective-permute-start.2 = (bf16[512,2688]{1,0:T(8,128)(2,1)S(1)}, bf16[512,2688]{1,0:T(8,128)(2,1)S(1)}, u32[]{:S(2)}, u32[]{:S(2)}) collective-permute-start(bf16[512,2688]{1,0:T(8,128)(2,1)S(1)} %pack.1.x_ref.own_ref), channel_id=1, source_target_pairs={{0,1},{1,0},{2,3},{3,2},{4,5},{5,4},{6,7},{7,6},{8,9},{9,8},{10,11... | collective-permute-start | bytes 8257544 | tf_op jit(solution)/shard_map/ppermute | solution.py:33
  17.2 7.4 %collective-permute-start.3 = (bf16[64,2560]{1,0:T(8,128)(2,1)S(1)}, bf16[64,2560]{1,0:T(8,128)(2,1)S(1)}, u32[]{:S(2)}, u32[]{:S(2)}) collective-permute-start(bf16[64,2560]{1,0:T(8,128)(2,1)S(1)} %collective-permute-done.1.refs_0_), channel_id=1, source_target_pairs={{0,1},{1,0},{2,3},{3,2},{4,5},{5,4},{6,7},{7,6},{8,9},{9,8},{10,11... | collective-permute-start | bytes 983048 | tf_op jit(solution)/shard_map/ppermute | solution.py:33
  17.7 10.3 %collective-permute-start.4 = (bf16[512,256]{1,0:T(8,128)(2,1)S(1)}, bf16[512,256]{1,0:T(8,128)(2,1)S(1)}, u32[]{:S(2)}, u32[]{:S(2)}) collective-permute-start(bf16[512,256]{1,0:T(8,128)(2,1)S(1)} %get-tuple-element.24), channel_id=1, source_target_pairs={{0,12},{4,8},{8,4},{12,0},{1,13},{5,9},{9,5},{13,1},{2,14},{6,10},... | collective-permute-start | bytes 786440 | tf_op jit(solution)/shard_map/ppermute | solution.py:33
  21.5 11.8 %collective-permute-start.9 = (bf16[512,256]{1,0:T(8,128)(2,1)S(1)}, bf16[512,256]{1,0:T(8,128)(2,1)S(1)}, u32[]{:S(2)}, u32[]{:S(2)}) collective-permute-start(bf16[512,256]{1,0:T(8,128)(2,1)S(1)} %get-tuple-element.27.refs_0_), channel_id=1, source_target_pairs={{0,16},{2,18},{16,0},{18,2},{1,17},{3,19},{17,1},{19,3},{4,20},{6,... | collective-permute-start | bytes 786440 | tf_op jit(solution)/shard_map/ppermute | solution.py:33
  23.1 10.2 %collective-permute-start.8 = (bf16[512,256]{1,0:T(8,128)(2,1)S(1)}, bf16[512,256]{1,0:T(8,128)(2,1)S(1)}, u32[]{:S(2)}, u32[]{:S(2)}) collective-permute-start(bf16[512,256]{1,0:T(8,128)(2,1)S(1)} %get-tuple-element.27.refs_0_), channel_id=1, source_target_pairs={{0,2},{2,0},{16,18},{18,16},{1,3},{3,1},{17,19},{19,17},{4,6},{6,4... | collective-permute-start | bytes 786440 | tf_op jit(solution)/shard_map/ppermute | solution.py:33
  28.0 9.8 %collective-permute-start.5 = (bf16[512,128]{1,0:T(8,128)(2,1)S(1)}, bf16[512,128]{1,0:T(8,128)(2,1)S(1)}, u32[]{:S(2)}, u32[]{:S(2)}) collective-permute-start(bf16[512,128]{1,0:T(8,128)(2,1)S(1)} %low_part.1), channel_id=1, source_target_pairs={{0,4},{4,0},{8,12},{12,8},{1,5},{5,1},{9,13},{13,9},{2,6},{6,2},{1... | collective-permute-start | bytes 393224 | tf_op jit(solution)/shard_map/ppermute | solution.py:33
  33.3 19.6 %collective-permute-start.12 = (bf16[512,256]{1,0:T(8,128)(2,1)S(1)}, bf16[512,256]{1,0:T(8,128)(2,1)S(1)}, u32[]{:S(2)}, u32[]{:S(2)}) collective-permute-start(bf16[512,256]{1,0:T(8,128)(2,1)S(1)} %collective-permute-done.4.refs_0_), channel_id=1, source_target_pairs={{0,18},{2,16},{16,2},{18,0},{1,19},{3,17},{17,3},{19,1},{4,22},{6,... | collective-permute-start | bytes 786440 | tf_op jit(solution)/shard_map/ppermute | solution.py:33
  35.7 17.2 %collective-permute-start.11 = (bf16[512,256]{1,0:T(8,128)(2,1)S(1)}, bf16[512,256]{1,0:T(8,128)(2,1)S(1)}, u32[]{:S(2)}, u32[]{:S(2)}) collective-permute-start(bf16[512,256]{1,0:T(8,128)(2,1)S(1)} %collective-permute-done.4.refs_0_), channel_id=1, source_target_pairs={{0,16},{2,18},{16,0},{18,2},{1,17},{3,19},{17,1},{19,3},{4,20},{6,... | collective-permute-start | bytes 786440 | tf_op jit(solution)/shard_map/ppermute | solution.py:33
  36.2 16.7 %collective-permute-start.10 = (bf16[512,256]{1,0:T(8,128)(2,1)S(1)}, bf16[512,256]{1,0:T(8,128)(2,1)S(1)}, u32[]{:S(2)}, u32[]{:S(2)}) collective-permute-start(bf16[512,256]{1,0:T(8,128)(2,1)S(1)} %collective-permute-done.4.refs_0_), channel_id=1, source_target_pairs={{0,2},{2,0},{16,18},{18,16},{1,3},{3,1},{17,19},{19,17},{4,6},{6,4... | collective-permute-start | bytes 786440 | tf_op jit(solution)/shard_map/ppermute | solution.py:33
  36.8 16.1 %collective-permute-start.7 = (bf16[512,256]{1,0:T(8,128)(2,1)S(1)}, bf16[512,256]{1,0:T(8,128)(2,1)S(1)}, u32[]{:S(2)}, u32[]{:S(2)}) collective-permute-start(bf16[512,256]{1,0:T(8,128)(2,1)S(1)} %get-tuple-element.26), channel_id=1, source_target_pairs={{0,8},{4,12},{8,0},{12,4},{1,9},{5,13},{9,1},{13,5},{2,10},{6,14},... | collective-permute-start | bytes 786440 | tf_op jit(solution)/shard_map/ppermute | solution.py:33
  37.9 17.2 %collective-permute-start.6 = (bf16[512,128]{1,0:T(8,128)(2,1)S(1)}, bf16[512,128]{1,0:T(8,128)(2,1)S(1)}, u32[]{:S(2)}, u32[]{:S(2)}) collective-permute-start(bf16[512,128]{1,0:T(8,128)(2,1)S(1)} %add_convert_fusion.2), channel_id=1, source_target_pairs={{0,8},{4,12},{8,0},{12,4},{1,9},{5,13},{9,1},{13,5},{2,10},{6,14},... | collective-permute-start | bytes 393224 | tf_op jit(solution)/shard_map/ppermute | solution.py:33
  55.1 17.2 %collective-permute-start.16 = (bf16[1024,256]{1,0:T(8,128)(2,1)S(1)}, bf16[1024,256]{1,0:T(8,128)(2,1)S(1)}, u32[]{:S(2)}, u32[]{:S(2)}) collective-permute-start(bf16[1024,256]{1,0:T(8,128)(2,1)S(1)} %panel.3), channel_id=1, source_target_pairs={{0,4},{4,0},{8,12},{12,8},{1,5},{5,1},{9,13},{13,9},{2,6},{6,2},{1... | collective-permute-start | bytes 1572872 | tf_op jit(solution)/shard_map/ppermute | solution.py:33
  55.2 29.9 %slice-start = ((s8[8388608]{0:T(1024)(128)(4,1)}), s8[4194304]{0:T(1024)(128)(4,1)S(1)}, s32[]{:S(2)}) async-start(s8[8388608]{0:T(1024)(128)(4,1)} %bitcast.6), calls=%async_computation | async-start | bytes 8388608
  56.5 27.1 %collective-permute-start.18 = (bf16[1024,256]{1,0:T(8,128)(2,1)S(1)}, bf16[1024,256]{1,0:T(8,128)(2,1)S(1)}, u32[]{:S(2)}, u32[]{:S(2)}) collective-permute-start(bf16[1024,256]{1,0:T(8,128)(2,1)S(1)} %panel.5), channel_id=1, source_target_pairs={{0,4},{4,0},{8,12},{12,8},{1,5},{5,1},{9,13},{13,9},{2,6},{6,2},{1... | collective-permute-start | bytes 1572872 | tf_op jit(solution)/shard_map/ppermute | solution.py:33
  58.5 10.2 %collective-permute-start.15 = (bf16[512,256]{1,0:T(8,128)(2,1)S(1)}, bf16[512,256]{1,0:T(8,128)(2,1)S(1)}, u32[]{:S(2)}, u32[]{:S(2)}) collective-permute-start(bf16[512,256]{1,0:T(8,128)(2,1)S(1)} %collective-permute-done.7.refs_0_), channel_id=1, source_target_pairs={{0,18},{2,16},{16,2},{18,0},{1,19},{3,17},{17,3},{19,1},{4,22},{6,... | collective-permute-start | bytes 786440 | tf_op jit(solution)/shard_map/ppermute | solution.py:33
  61.0 11.2 %collective-permute-start.14 = (bf16[512,256]{1,0:T(8,128)(2,1)S(1)}, bf16[512,256]{1,0:T(8,128)(2,1)S(1)}, u32[]{:S(2)}, u32[]{:S(2)}) collective-permute-start(bf16[512,256]{1,0:T(8,128)(2,1)S(1)} %collective-permute-done.7.refs_0_), channel_id=1, source_target_pairs={{0,16},{2,18},{16,0},{18,2},{1,17},{3,19},{17,1},{19,3},{4,20},{6,... | collective-permute-start | bytes 786440 | tf_op jit(solution)/shard_map/ppermute | solution.py:33
  61.5 10.8 %collective-permute-start.13 = (bf16[512,256]{1,0:T(8,128)(2,1)S(1)}, bf16[512,256]{1,0:T(8,128)(2,1)S(1)}, u32[]{:S(2)}, u32[]{:S(2)}) collective-permute-start(bf16[512,256]{1,0:T(8,128)(2,1)S(1)} %collective-permute-done.7.refs_0_), channel_id=1, source_target_pairs={{0,2},{2,0},{16,18},{18,16},{1,3},{3,1},{17,19},{19,17},{4,6},{6,4... | collective-permute-start | bytes 786440 | tf_op jit(solution)/shard_map/ppermute | solution.py:33
  73.5 26.0 %collective-permute-start.17 = (bf16[1024,256]{1,0:T(8,128)(2,1)S(1)}, bf16[1024,256]{1,0:T(8,128)(2,1)S(1)}, u32[]{:S(2)}, u32[]{:S(2)}) collective-permute-start(bf16[1024,256]{1,0:T(8,128)(2,1)S(1)} %panel.4), channel_id=1, source_target_pairs={{0,8},{4,12},{8,0},{12,4},{1,9},{5,13},{9,1},{13,5},{2,10},{6,14},... | collective-permute-start | bytes 1572872 | tf_op jit(solution)/shard_map/ppermute | solution.py:33
  75.4 1.3 %collective-permute-start.20 = (bf16[512,128]{1,0:T(8,128)(2,1)S(1)}, bf16[512,128]{1,0:T(8,128)(2,1)S(1)}, u32[]{:S(2)}, u32[]{:S(2)}) collective-permute-start(bf16[512,128]{1,0:T(8,128)(2,1)S(1)} %add_convert_fusion.1.low_ref), channel_id=1, source_target_pairs={{0,1},{1,0},{2,3},{3,2},{4,5},{5,4},{6,7},{7,6},{8,9},{9,8},{10,11... | collective-permute-start | bytes 393224 | tf_op jit(solution)/shard_map/ppermute | solution.py:33
  83.6 16.0 %collective-permute-start.21 = (bf16[64,2560]{1,0:T(8,128)(2,1)S(1)}, bf16[64,2560]{1,0:T(8,128)(2,1)S(1)}, u32[]{:S(2)}, u32[]{:S(2)}) collective-permute-start(bf16[64,2560]{1,0:T(8,128)(2,1)S(1)} %get-tuple-element.36), channel_id=1, source_target_pairs={{0,2},{2,0},{1,3},{3,1},{4,6},{6,4},{5,7},{7,5},{8,10},{10,8},{9,1... | collective-permute-start | bytes 983048 | tf_op jit(solution)/shard_map/ppermute | solution.py:29
  99.6 3.6 %collective-permute-start.19 = (f32[512,256]{1,0:T(8,128)S(1)}, f32[512,256]{1,0:T(8,128)S(1)}, u32[]{:S(2)}, u32[]{:S(2)}) collective-permute-start(f32[512,256]{1,0:T(8,128)S(1)} %other_rows.1), channel_id=1, source_target_pairs={{0,1},{1,0},{2,3},{3,2},{4,5},{5,4},{6,7},{7,6},{8,9},{9,8},{10,11... | collective-permute-start | bytes 1572872 | tf_op jit(solution)/shard_map/ppermute | solution.py:33
  99.7 2.3 %collective-permute-start.22 = (bf16[64,2560]{1,0:T(8,128)(2,1)S(1)}, bf16[64,2560]{1,0:T(8,128)(2,1)S(1)}, u32[]{:S(2)}, u32[]{:S(2)}) collective-permute-start(bf16[64,2560]{1,0:T(8,128)(2,1)S(1)} %add_convert_fusion.own_ref), channel_id=1, source_target_pairs={{0,1},{1,0},{2,3},{3,2},{4,5},{5,4},{6,7},{7,6},{8,9},{9,8},{10,11... | collective-permute-start | bytes 983048 | tf_op jit(solution)/shard_map/ppermute | solution.py:33
  (7 other events, 95.4 us)

commit v10 on v8

--- a/solution.py
+++ b/solution.py
@@ -284,6 +284,25 @@
     )(at, dp, core, fill, tenant, x, base_weight, low, b, *halves)
 
 
+def relay_kernel(at_ref, own_ref, got_ref, passed_ref, kept_ref):
+    inner = (at_ref[0] == 1) | (at_ref[0] == 2)
+    got = got_ref[...].astype(F32)
+    passed_ref[...] = (own_ref[...].astype(F32) + got).astype(BF16)
+    kept_ref[...] = jnp.where(inner, 0.0, got).astype(BF16)
+
+
+def relay(at, own, got):
+    return pl.pallas_call(
+        relay_kernel,
+        in_specs=[SMEM] + [VMEM] * 2,
+        out_specs=[VMEM] * 2,
+        out_shape=[shaped(own.shape, BF16)] * 2,
+        compiler_params=params(24),
+        cost_estimate=cost(2 * own.size, 8 * own.size),
+        name="relay",
+    )(at, own, got)
+
+
 def swap_kernel(*refs):
     ins, out_ref = refs[:-1], refs[-1]
     total = ins[0][LIVE:, :].astype(F32)
@@ -374,26 +393,28 @@
         return (low.astype(F32) + flip(after(low, *before), "tensor", n_t, mask).astype(F32)).astype(BF16)
 
     if n_t == 4:
-        share_1 = share(me_t ^ 1)
-        weight = {1: flip(share_1, "tensor", n_t, 1)}
-        weight[3] = flip(after(share(me_t ^ 3), weight[1]), "tensor", n_t, 3)
+        share_3 = share(me_t ^ 3)
+        weight = {3: flip(share_3, "tensor", n_t, 3)}
         weight[2] = flip(after(share(me_t ^ 2), weight[3]), "tensor", n_t, 2)
-        x = pack(after(block_fill, share_1), block_tenant_index, tokens, cotangent, blocks, 2 * rank)
-        x_other = flip(after(x, weight[1], *halves[::2]), "pipe", n_pipe, 1)
-        pieces, order = gathered(weight[1])
-        low = low_part(dp, core, block_fill, block_tenant_index, x, own_a, own_b, halves, blocks, rank)
-        pieces[0] = after(pieces[0], weight[3], low)
+        weight[1] = flip(after(share(me_t ^ 1), weight[2]), "tensor", n_t, 1)
+        x = pack(after(block_fill, share_3), block_tenant_index, tokens, cotangent, blocks, 2 * rank)
+        x_other = flip(after(x, weight[3], *halves[::2]), "pipe", n_pipe, 1)
+        pieces, order = gathered(weight[3])
+        low = low_part(after(dp, x_other), core, block_fill, block_tenant_index, x, own_a, own_b, halves, blocks, rank)
+        pieces[0] = after(pieces[0], weight[2], low)
+        (y_3,) = panel_product(order, panel_at, x, x_other, pieces, half)
+        low = add_flipped(low, 1, weight[2])
+        far = lax.ppermute(after(y_3, low), "tensor", [(0, 1), (3, 2)])
+        pieces, order = gathered(after(weight[2], *pieces))
+        pieces[0] = after(pieces[0], weight[1])
+        (y_2,) = panel_product(order, panel_at, x, x_other, pieces, half, adds=[far])
+        low = add_flipped(low, 2)
+        near = lax.ppermute(after(y_2, low), "tensor", [(0, 1), (3, 2), (1, 3), (2, 0)])
+        pieces, order = gathered(after(weight[1], *pieces))
         (y_1,) = panel_product(order, panel_at, x, x_other, pieces, half)
-        low = add_flipped(low, 1, weight[3])
-        part_1 = flip(after(y_1, low), "tensor", n_t, 1)
-        pieces, order = gathered(after(weight[3], y_1))
-        pieces[0] = after(pieces[0], weight[2])
-        (y,) = panel_product(order, panel_at, x, x_other, pieces, half)
-        add = flip(y, "tensor", n_t, 1)
-        low = add_flipped(low, 2, y, part_1)
-        pieces, order = gathered(after(weight[2], y))
-        (y_2,) = panel_product(order, panel_at, x, x_other, pieces, half, adds=[add])
-        parts = [flip(y_2, "tensor", n_t, 2), part_1]
+        part_1 = flip(y_1, "tensor", n_t, 1)
+        passed, kept = relay(at, y_3, near)
+        parts = [lax.ppermute(passed, "tensor", [(1, 2), (2, 1)]), part_1, kept]
     else:
         x = pack(block_fill, block_tenant_index, tokens, cotangent, blocks, 2 * rank)
         x_other = flip(x, "pipe", n_pipe, 1)

time: 99.7 us -> 97 us (0.973)
  waiting for transfers between devices: 48.1 us -> 38.6 us
  starting transfers between devices: 28.8 us -> 35.3 us
    ppermute x22 -> x20, waiting for transfers between devices: 48.1 us -> 27.8 us  [flip(): return lax.ppermute(x, names, [(i, i ^ mask) for i in range(count)])]
    ppermute x0 -> x3, waiting for transfers between devices: none -> 8.48 us  [the longest x1 8.48 us: body(): lax.ppermute(after(y_2, low), 'tensor', [(0, 1), (3, 2), (1, 3), (2, 0)])]
    ppermute x0 -> x3, starting transfers between devices: none -> 5.15 us  [the longest x1 2.42 us: body(): lax.ppermute(after(y_2, low), 'tensor', [(0, 1), (3, 2), (1, 3), (2, 0)])]
    ppermute x2, waiting for transfers between devices: 0.01 us -> 2.3 us  [shift(): lax.ppermute(x, name, [(i, (i + step) % count) for i in range(count)])]
    ppermute x22 -> x20, starting transfers between devices: 25.2 us -> 26.6 us  [flip(): return lax.ppermute(x, names, [(i, i ^ mask) for i in range(count)])]
  transfers between devices with their start and end apart: 24 -> 25, of which waited for: 14 -> 12; matrix products, arithmetic and copies ran while one was open for 1% -> 1% of each run, Pallas kernels for 13% -> 13%
where the time goes in v10:
time: 97 us; the launch traced here: 96.7 us
  waiting for transfers between devices  38.6 us (40%)
  starting transfers between devices  35.3 us (36%)
  Pallas kernels  17.5 us (18%)
  local copies, waits for them, and re-layouts  4.39 us (5%)
    ppermute x20, waiting for transfers between devices, flip(): return lax.ppermute(x, names, [(i, i ^ mask) for i in range(count)])  27.8 us
    ppermute x20, starting transfers between devices, flip(): return lax.ppermute(x, names, [(i, i ^ mask) for i in range(count)])  26.6 us
    ppermute x1, waiting for transfers between devices, body(): lax.ppermute(after(y_2, low), 'tensor', [(0, 1), (3, 2), (1, 3), (2, 0)])  8.48 us
    pallas_call x3, Pallas kernels, panel_product(): pl.pallas_call(functools.partial(panel_kernel, order, len(pieces)), in_sp...  3.76 us
    ppermute x2, starting transfers between devices, shift(): lax.ppermute(x, name, [(i, (i + step) % count) for i in range(count)])  3.54 us
    unnamed x20, local copies, waits for them, and re-layouts  3.23 us
    pallas_call x1, Pallas kernels, pack(): pl.pallas_call(functools.partial(pack_kernel, blocks, rows // blocks), in...  2.84 us
    ppermute x1, starting transfers between devices, body(): lax.ppermute(after(y_2, low), 'tensor', [(0, 1), (3, 2), (1, 3), (2, 0)])  2.42 us
  transfers between devices with their start and end apart: 25, of which 12 were waited for; matrix products, arithmetic and copies ran while one was open for 1% of the time, Pallas kernels for 13%

profile of v10, /device:TPU:0, one launch (start us, length us, event | category | flops | bytes accessed | tf_op | source)
XLA Modules:
  0.0 96.7 jit_solution(11389503863637973077)
XLA Ops:
  0.6 1.9 %own_half.1 = bf16[64,2560]{1,0:T(8,128)(2,1)} custom-call(s32[1]{0:T(128)} %bitcast.core_ref, bf16[128,2048]{1,0:T(8,128)(2,1)} %bitcast.8, bf16[128,512]{1,0:T(8,128)(2,1)} %bitcast.10), custom_call_target="tpu_custom_call" | custom-call | flops 1 | bytes 1 | tf_op jit(solution)/shard_map/own_half/pallas_call | solution.py:73
  2.5 2.9 %collective-permute-start.1 = (bf16[64,2560]{1,0:T(8,128)(2,1)}, bf16[64,2560]{1,0:T(8,128)(2,1)S(1)}, u32[]{:S(2)}, u32[]{:S(2)}) collective-permute-start(bf16[64,2560]{1,0:T(8,128)(2,1)} %own_half.1), channel_id=1, source_target_pairs={{0,2},{2,0},{1,3},{3,1},{4,6},{6,4},{5,7},{7,5},{8,10},{10,8},{9,1... | collective-permute-start | bytes 983048 | tf_op jit(solution)/shard_map/ppermute | solution.py:29
  6.6 3.7 %collective-permute-start = (bf16[512,256]{1,0:T(8,128)(2,1)S(1)}, bf16[512,256]{1,0:T(8,128)(2,1)S(1)}, u32[]{:S(2)}, u32[]{:S(2)}) collective-permute-start(bf16[512,256]{1,0:T(8,128)(2,1)S(1)} %get-tuple-element.45), channel_id=1, source_target_pairs={{0,12},{4,8},{8,4},{12,0},{1,13},{5,9},{9,5},{13,1},{2,14},{6,10},... | collective-permute-start | bytes 786440 | tf_op jit(solution)/shard_map/ppermute | solution.py:33
  10.3 1.9 %copy-done = bf16[768,2048]{1,0:T(8,128)(2,1)S(1)} copy-done((bf16[768,2048]{1,0:T(8,128)(2,1)S(1)}, bf16[768,2048]{1,0:T(8,128)(2,1)}, u32[]{:S(2)}) %copy-start) | copy-done | bytes 3145752
  13.5 2.8 %pack.1.x_ref.own_ref = bf16[512,2688]{1,0:T(8,128)(2,1)S(1)} custom-call(s32[1,6]{1,0:T(1,128)S(1)} %copy-done.4, s32[6]{0:T(128)S(1)} %copy-done.6, bf16[768,2048]{1,0:T(8,128)(2,1)S(1)} %copy-done, bf16[768,512]{1,0:T(8,128)(2,1)S(1)} %copy-done.3), custom_call_target="tpu_custom_call" | custom-call | flops 1 | bytes 1 | tf_op jit(solution)/shard_map/pack/pallas_call | solution.py:102
  17.0 6.2 %collective-permute-start.4 = (bf16[512,256]{1,0:T(8,128)(2,1)S(1)}, bf16[512,256]{1,0:T(8,128)(2,1)S(1)}, u32[]{:S(2)}, u32[]{:S(2)}) collective-permute-start(bf16[512,256]{1,0:T(8,128)(2,1)S(1)} %get-tuple-element.26), channel_id=1, source_target_pairs={{0,8},{4,12},{8,0},{12,4},{1,9},{5,13},{9,1},{13,5},{2,10},{6,14},... | collective-permute-start | bytes 786440 | tf_op jit(solution)/shard_map/ppermute | solution.py:33
  23.7 1.5 %collective-permute-start.8 = (bf16[512,256]{1,0:T(8,128)(2,1)S(1)}, bf16[512,256]{1,0:T(8,128)(2,1)S(1)}, u32[]{:S(2)}, u32[]{:S(2)}) collective-permute-start(bf16[512,256]{1,0:T(8,128)(2,1)S(1)} %collective-permute-done.refs_0_), channel_id=1, source_target_pairs={{0,16},{2,18},{16,0},{18,2},{1,17},{3,19},{17,1},{19,3},{4,20},{6,... | collective-permute-start | bytes 786440 | tf_op jit(solution)/shard_map/ppermute | solution.py:33
  26.7 2.2 %low_part.1 = bf16[512,128]{1,0:T(8,128)(2,1)S(1)} custom-call(s32[1]{0:T(128)} %bitcast.2.dp_ref, s32[1]{0:T(128)} %bitcast.core_ref, s32[1,6]{1,0:T(1,128)S(1)} %copy-done.5, s32[6]{0:T(128)S(1)} %copy-done.7, bf16[512,2688]{1,0:T(8,128)(2,1)S(1)} %pack.1.x_ref.own_ref, bf16[128,2048]{1,0:T(8,128)(2,1)S(1)} %bitcast.9, bf16[128,512]{1,0:T(8,128)(2,1)S(1)} %bitcast.11, ...), custom_call_target="tpu_custom_call" | custom-call | flops 1 | bytes 1 | tf_op jit(solution)/shard_map/low_part/pallas_call | solution.py:145
  28.9 6.4 %collective-permute-done.4.refs_0_ = bf16[512,256]{1,0:T(8,128)(2,1)S(1)} collective-permute-done((bf16[512,256]{1,0:T(8,128)(2,1)S(1)}, bf16[512,256]{1,0:T(8,128)(2,1)S(1)}, u32[]{:S(2)}, u32[]{:S(2)}) %collective-permute-start.4) | collective-permute-done | bytes 262176 | tf_op jit(solution)/shard_map/ppermute | solution.py:33
  35.3 2.0 %collective-permute-start.10 = (bf16[512,256]{1,0:T(8,128)(2,1)S(1)}, bf16[512,256]{1,0:T(8,128)(2,1)S(1)}, u32[]{:S(2)}, u32[]{:S(2)}) collective-permute-start(bf16[512,256]{1,0:T(8,128)(2,1)S(1)} %get-tuple-element.30), channel_id=1, source_target_pairs={{0,4},{4,0},{8,12},{12,8},{1,5},{5,1},{9,13},{13,9},{2,6},{6,2},{1... | collective-permute-start | bytes 786440 | tf_op jit(solution)/shard_map/ppermute | solution.py:33
  39.0 2.8 %collective-permute-done.5 = bf16[512,128]{1,0:T(8,128)(2,1)S(1)} collective-permute-done((bf16[512,128]{1,0:T(8,128)(2,1)S(1)}, bf16[512,128]{1,0:T(8,128)(2,1)S(1)}, u32[]{:S(2)}, u32[]{:S(2)}) %collective-permute-start.5) | collective-permute-done | bytes 131104 | tf_op jit(solution)/shard_map/ppermute | solution.py:33
  41.8 1.9 %collective-permute-start.14 = (bf16[1024,256]{1,0:T(8,128)(2,1)S(1)}, bf16[1024,256]{1,0:T(8,128)(2,1)S(1)}, u32[]{:S(2)}, u32[]{:S(2)}) collective-permute-start(bf16[1024,256]{1,0:T(8,128)(2,1)S(1)} %panel.3.own_ref), channel_id=1, source_target_pairs={{0,4},{12,8},{1,5},{13,9},{2,6},{14,10},{3,7},{15,11},{16,20},{28,... | collective-permute-start | bytes 1572872 | tf_op jit(solution)/shard_map/ppermute | solution.py:407
  44.3 1.5 %collective-permute-start.12 = (bf16[512,256]{1,0:T(8,128)(2,1)S(1)}, bf16[512,256]{1,0:T(8,128)(2,1)S(1)}, u32[]{:S(2)}, u32[]{:S(2)}) collective-permute-start(bf16[512,256]{1,0:T(8,128)(2,1)S(1)} %collective-permute-done.4.refs_0_), channel_id=1, source_target_pairs={{0,16},{2,18},{16,0},{18,2},{1,17},{3,19},{17,1},{19,3},{4,20},{6,... | collective-permute-start | bytes 786440 | tf_op jit(solution)/shard_map/ppermute | solution.py:33
  47.2 1.5 %collective-permute-start.13 = (bf16[512,256]{1,0:T(8,128)(2,1)S(1)}, bf16[512,256]{1,0:T(8,128)(2,1)S(1)}, u32[]{:S(2)}, u32[]{:S(2)}) collective-permute-start(bf16[512,256]{1,0:T(8,128)(2,1)S(1)} %collective-permute-done.4.refs_0_), channel_id=1, source_target_pairs={{0,18},{2,16},{16,2},{18,0},{1,19},{3,17},{17,3},{19,1},{4,22},{6,... | collective-permute-start | bytes 786440 | tf_op jit(solution)/shard_map/ppermute | solution.py:33
  48.7 9.0 %collective-permute-done.6 = bf16[512,128]{1,0:T(8,128)(2,1)S(1)} collective-permute-done((bf16[512,128]{1,0:T(8,128)(2,1)S(1)}, bf16[512,128]{1,0:T(8,128)(2,1)S(1)}, u32[]{:S(2)}, u32[]{:S(2)}) %collective-permute-start.6) | collective-permute-done | bytes 131104 | tf_op jit(solution)/shard_map/ppermute | solution.py:33
  59.0 2.4 %collective-permute-start.15 = (bf16[1024,256]{1,0:T(8,128)(2,1)S(1)}, bf16[1024,256]{1,0:T(8,128)(2,1)S(1)}, u32[]{:S(2)}, u32[]{:S(2)}) collective-permute-start(bf16[1024,256]{1,0:T(8,128)(2,1)S(1)} %panel.4), channel_id=1, source_target_pairs={{0,4},{12,8},{4,12},{8,0},{1,5},{13,9},{5,13},{9,1},{2,6},{14,10},... | collective-permute-start | bytes 1572872 | tf_op jit(solution)/shard_map/ppermute | solution.py:412
  61.9 1.5 %collective-permute-start.18 = (bf16[512,256]{1,0:T(8,128)(2,1)S(1)}, bf16[512,256]{1,0:T(8,128)(2,1)S(1)}, u32[]{:S(2)}, u32[]{:S(2)}) collective-permute-start(bf16[512,256]{1,0:T(8,128)(2,1)S(1)} %collective-permute-done.10.refs_0_), channel_id=1, source_target_pairs={{0,16},{2,18},{16,0},{18,2},{1,17},{3,19},{17,1},{19,3},{4,20},{6,... | collective-permute-start | bytes 786440 | tf_op jit(solution)/shard_map/ppermute | solution.py:33
  64.9 8.5 %collective-permute-done.15.got_ref = bf16[1024,256]{1,0:T(8,128)(2,1)S(1)} collective-permute-done((bf16[1024,256]{1,0:T(8,128)(2,1)S(1)}, bf16[1024,256]{1,0:T(8,128)(2,1)S(1)}, u32[]{:S(2)}, u32[]{:S(2)}) %collective-permute-start.15) | collective-permute-done | bytes 524320 | tf_op jit(solution)/shard_map/ppermute | solution.py:412
  76.0 3.4 %collective-permute-start.20 = (bf16[1024,256]{1,0:T(8,128)(2,1)S(1)}, bf16[1024,256]{1,0:T(8,128)(2,1)S(1)}, u32[]{:S(2)}, u32[]{:S(2)}) collective-permute-start(bf16[1024,256]{1,0:T(8,128)(2,1)S(1)} %panel.5), channel_id=1, source_target_pairs={{0,4},{4,0},{8,12},{12,8},{1,5},{5,1},{9,13},{13,9},{2,6},{6,2},{1... | collective-permute-start | bytes 1572872 | tf_op jit(solution)/shard_map/ppermute | solution.py:33
  82.4 2.1 %base.1.base_ref = f32[512,512]{1,0:T(8,128)S(1)} custom-call(s32[1]{0:T(128)} %bitcast.1.at_ref, s32[1]{0:T(128)} %bitcast.2.dp_ref, s32[1]{0:T(128)} %bitcast.core_ref, s32[1,6]{1,0:T(1,128)S(1)} %copy-done.5, s32[6]{0:T(128)S(1)} %copy-done.7, bf16[512,2688]{1,0:T(8,128)(2,1)S(1)} %pack.1.x_ref.own_ref, bf16[8192,512]{1,0:T(8,128)(2,1)S(1)} %bitcast.7, ...), custom_call_target="tpu_custom_call" | custom-call | flops 1 | bytes 1 | tf_op jit(solution)/shard_map/base/pallas_call | solution.py:269
  84.6 4.6 %collective-permute-done.20.refs_1_ = bf16[1024,256]{1,0:T(8,128)(2,1)S(1)} collective-permute-done((bf16[1024,256]{1,0:T(8,128)(2,1)S(1)}, bf16[1024,256]{1,0:T(8,128)(2,1)S(1)}, u32[]{:S(2)}, u32[]{:S(2)}) %collective-permute-start.20) | collective-permute-done | bytes 524320 | tf_op jit(solution)/shard_map/ppermute | solution.py:33
  89.4 2.3 %collective-permute-done.23 = bf16[64,2560]{1,0:T(8,128)(2,1)S(1)} collective-permute-done((bf16[64,2560]{1,0:T(8,128)(2,1)S(1)}, bf16[64,2560]{1,0:T(8,128)(2,1)S(1)}, u32[]{:S(2)}, u32[]{:S(2)}) %collective-permute-start.23) | collective-permute-done | bytes 327712 | tf_op jit(solution)/shard_map/ppermute | solution.py:29
  91.8 1.6 %collective-permute-done.24.got_ref = bf16[64,2560]{1,0:T(8,128)(2,1)S(1)} collective-permute-done((bf16[64,2560]{1,0:T(8,128)(2,1)S(1)}, bf16[64,2560]{1,0:T(8,128)(2,1)S(1)}, u32[]{:S(2)}, u32[]{:S(2)}) %collective-permute-start.24) | collective-permute-done | bytes 327712 | tf_op jit(solution)/shard_map/ppermute | solution.py:33
  94.6 2.1 %finish.1 = bf16[768,512]{1,0:T(8,128)(2,1)} custom-call(s32[1]{0:T(128)} %bitcast.core_ref, s32[1,6]{1,0:T(1,128)S(1)} %copy-done.5, f32[512,512]{1,0:T(8,128)S(1)} %base.1.base_ref, bf16[1024,256]{1,0:T(8,128)(2,1)S(1)} %collective-permute-done.16.refs_0_, bf16[1024,256]{1,0:T(8,128)(2,1)S(1)} %collective-permute-done.20.refs_1_, ...), custom_call_target="tpu_custom_call" | custom-call | flops 1 | bytes 1 | tf_op jit(solution)/shard_map/finish/pallas_call | solution.py:350
  (63 shorter events, 19.1 us)
Async XLA Ops:
  2.5 13.9 %collective-permute-start.1 = (bf16[64,2560]{1,0:T(8,128)(2,1)}, bf16[64,2560]{1,0:T(8,128)(2,1)S(1)}, u32[]{:S(2)}, u32[]{:S(2)}) collective-permute-start(bf16[64,2560]{1,0:T(8,128)(2,1)} %own_half.1), channel_id=1, source_target_pairs={{0,2},{2,0},{1,3},{3,1},{4,6},{6,4},{5,7},{7,5},{8,10},{10,8},{9,1... | collective-permute-start | bytes 983048 | tf_op jit(solution)/shard_map/ppermute | solution.py:29
  6.6 9.8 %collective-permute-start = (bf16[512,256]{1,0:T(8,128)(2,1)S(1)}, bf16[512,256]{1,0:T(8,128)(2,1)S(1)}, u32[]{:S(2)}, u32[]{:S(2)}) collective-permute-start(bf16[512,256]{1,0:T(8,128)(2,1)S(1)} %get-tuple-element.45), channel_id=1, source_target_pairs={{0,12},{4,8},{8,4},{12,0},{1,13},{5,9},{9,5},{13,1},{2,14},{6,10},... | collective-permute-start | bytes 786440 | tf_op jit(solution)/shard_map/ppermute | solution.py:33
  16.4 8.8 %collective-permute-start.2 = (bf16[512,2688]{1,0:T(8,128)(2,1)S(1)}, bf16[512,2688]{1,0:T(8,128)(2,1)S(1)}, u32[]{:S(2)}, u32[]{:S(2)}) collective-permute-start(bf16[512,2688]{1,0:T(8,128)(2,1)S(1)} %pack.1.x_ref.own_ref), channel_id=1, source_target_pairs={{0,1},{1,0},{2,3},{3,2},{4,5},{5,4},{6,7},{7,6},{8,9},{9,8},{10,11... | collective-permute-start | bytes 8257544 | tf_op jit(solution)/shard_map/ppermute | solution.py:33
  16.5 10.2 %collective-permute-start.3 = (bf16[64,2560]{1,0:T(8,128)(2,1)S(1)}, bf16[64,2560]{1,0:T(8,128)(2,1)S(1)}, u32[]{:S(2)}, u32[]{:S(2)}) collective-permute-start(bf16[64,2560]{1,0:T(8,128)(2,1)S(1)} %collective-permute-done.1.refs_0_), channel_id=1, source_target_pairs={{0,1},{1,0},{2,3},{3,2},{4,5},{5,4},{6,7},{7,6},{8,9},{9,8},{10,11... | collective-permute-start | bytes 983048 | tf_op jit(solution)/shard_map/ppermute | solution.py:33
  17.0 18.3 %collective-permute-start.4 = (bf16[512,256]{1,0:T(8,128)(2,1)S(1)}, bf16[512,256]{1,0:T(8,128)(2,1)S(1)}, u32[]{:S(2)}, u32[]{:S(2)}) collective-permute-start(bf16[512,256]{1,0:T(8,128)(2,1)S(1)} %get-tuple-element.26), channel_id=1, source_target_pairs={{0,8},{4,12},{8,0},{12,4},{1,9},{5,13},{9,1},{13,5},{2,10},{6,14},... | collective-permute-start | bytes 786440 | tf_op jit(solution)/shard_map/ppermute | solution.py:33
  23.2 14.1 %collective-permute-start.7 = (bf16[512,256]{1,0:T(8,128)(2,1)S(1)}, bf16[512,256]{1,0:T(8,128)(2,1)S(1)}, u32[]{:S(2)}, u32[]{:S(2)}) collective-permute-start(bf16[512,256]{1,0:T(8,128)(2,1)S(1)} %collective-permute-done.refs_0_), channel_id=1, source_target_pairs={{0,2},{2,0},{16,18},{18,16},{1,3},{3,1},{17,19},{19,17},{4,6},{6,4... | collective-permute-start | bytes 786440 | tf_op jit(solution)/shard_map/ppermute | solution.py:33
  23.7 13.6 %collective-permute-start.8 = (bf16[512,256]{1,0:T(8,128)(2,1)S(1)}, bf16[512,256]{1,0:T(8,128)(2,1)S(1)}, u32[]{:S(2)}, u32[]{:S(2)}) collective-permute-start(bf16[512,256]{1,0:T(8,128)(2,1)S(1)} %collective-permute-done.refs_0_), channel_id=1, source_target_pairs={{0,16},{2,18},{16,0},{18,2},{1,17},{3,19},{17,1},{19,3},{4,20},{6,... | collective-permute-start | bytes 786440 | tf_op jit(solution)/shard_map/ppermute | solution.py:33
  25.3 12.4 %collective-permute-start.9 = (bf16[512,256]{1,0:T(8,128)(2,1)S(1)}, bf16[512,256]{1,0:T(8,128)(2,1)S(1)}, u32[]{:S(2)}, u32[]{:S(2)}) collective-permute-start(bf16[512,256]{1,0:T(8,128)(2,1)S(1)} %collective-permute-done.refs_0_), channel_id=1, source_target_pairs={{0,18},{2,16},{16,2},{18,0},{1,19},{3,17},{17,3},{19,1},{4,22},{6,... | collective-permute-start | bytes 786440 | tf_op jit(solution)/shard_map/ppermute | solution.py:33
  35.3 6.4 %collective-permute-start.5 = (bf16[512,128]{1,0:T(8,128)(2,1)S(1)}, bf16[512,128]{1,0:T(8,128)(2,1)S(1)}, u32[]{:S(2)}, u32[]{:S(2)}) collective-permute-start(bf16[512,128]{1,0:T(8,128)(2,1)S(1)} %low_part.1), channel_id=1, source_target_pairs={{0,4},{4,0},{8,12},{12,8},{1,5},{5,1},{9,13},{13,9},{2,6},{6,2},{1... | collective-permute-start | bytes 393224 | tf_op jit(solution)/shard_map/ppermute | solution.py:33
  35.3 11.9 %collective-permute-start.10 = (bf16[512,256]{1,0:T(8,128)(2,1)S(1)}, bf16[512,256]{1,0:T(8,128)(2,1)S(1)}, u32[]{:S(2)}, u32[]{:S(2)}) collective-permute-start(bf16[512,256]{1,0:T(8,128)(2,1)S(1)} %get-tuple-element.30), channel_id=1, source_target_pairs={{0,4},{4,0},{8,12},{12,8},{1,5},{5,1},{9,13},{13,9},{2,6},{6,2},{1... | collective-permute-start | bytes 786440 | tf_op jit(solution)/shard_map/ppermute | solution.py:33
  41.8 15.9 %collective-permute-start.14 = (bf16[1024,256]{1,0:T(8,128)(2,1)S(1)}, bf16[1024,256]{1,0:T(8,128)(2,1)S(1)}, u32[]{:S(2)}, u32[]{:S(2)}) collective-permute-start(bf16[1024,256]{1,0:T(8,128)(2,1)S(1)} %panel.3.own_ref), channel_id=1, source_target_pairs={{0,4},{12,8},{1,5},{13,9},{2,6},{14,10},{3,7},{15,11},{16,20},{28,... | collective-permute-start | bytes 1572872 | tf_op jit(solution)/shard_map/ppermute | solution.py:407
  43.7 13.9 %collective-permute-start.6 = (bf16[512,128]{1,0:T(8,128)(2,1)S(1)}, bf16[512,128]{1,0:T(8,128)(2,1)S(1)}, u32[]{:S(2)}, u32[]{:S(2)}) collective-permute-start(bf16[512,128]{1,0:T(8,128)(2,1)S(1)} %add_convert_fusion.2), channel_id=1, source_target_pairs={{0,8},{4,12},{8,0},{12,4},{1,9},{5,13},{9,1},{13,5},{2,10},{6,14},... | collective-permute-start | bytes 393224 | tf_op jit(solution)/shard_map/ppermute | solution.py:33
  43.7 13.9 %collective-permute-start.11 = (bf16[512,256]{1,0:T(8,128)(2,1)S(1)}, bf16[512,256]{1,0:T(8,128)(2,1)S(1)}, u32[]{:S(2)}, u32[]{:S(2)}) collective-permute-start(bf16[512,256]{1,0:T(8,128)(2,1)S(1)} %collective-permute-done.4.refs_0_), channel_id=1, source_target_pairs={{0,2},{2,0},{16,18},{18,16},{1,3},{3,1},{17,19},{19,17},{4,6},{6,4... | collective-permute-start | bytes 786440 | tf_op jit(solution)/shard_map/ppermute | solution.py:33
  44.3 13.3 %collective-permute-start.12 = (bf16[512,256]{1,0:T(8,128)(2,1)S(1)}, bf16[512,256]{1,0:T(8,128)(2,1)S(1)}, u32[]{:S(2)}, u32[]{:S(2)}) collective-permute-start(bf16[512,256]{1,0:T(8,128)(2,1)S(1)} %collective-permute-done.4.refs_0_), channel_id=1, source_target_pairs={{0,16},{2,18},{16,0},{18,2},{1,17},{3,19},{17,1},{19,3},{4,20},{6,... | collective-permute-start | bytes 786440 | tf_op jit(solution)/shard_map/ppermute | solution.py:33
  47.2 10.5 %collective-permute-start.13 = (bf16[512,256]{1,0:T(8,128)(2,1)S(1)}, bf16[512,256]{1,0:T(8,128)(2,1)S(1)}, u32[]{:S(2)}, u32[]{:S(2)}) collective-permute-start(bf16[512,256]{1,0:T(8,128)(2,1)S(1)} %collective-permute-done.4.refs_0_), channel_id=1, source_target_pairs={{0,18},{2,16},{16,2},{18,0},{1,19},{3,17},{17,3},{19,1},{4,22},{6,... | collective-permute-start | bytes 786440 | tf_op jit(solution)/shard_map/ppermute | solution.py:33
  59.0 14.4 %collective-permute-start.15 = (bf16[1024,256]{1,0:T(8,128)(2,1)S(1)}, bf16[1024,256]{1,0:T(8,128)(2,1)S(1)}, u32[]{:S(2)}, u32[]{:S(2)}) collective-permute-start(bf16[1024,256]{1,0:T(8,128)(2,1)S(1)} %panel.4), channel_id=1, source_target_pairs={{0,4},{12,8},{4,12},{8,0},{1,5},{13,9},{5,13},{9,1},{2,6},{14,10},... | collective-permute-start | bytes 1572872 | tf_op jit(solution)/shard_map/ppermute | solution.py:412
  61.4 13.0 %collective-permute-start.17 = (bf16[512,256]{1,0:T(8,128)(2,1)S(1)}, bf16[512,256]{1,0:T(8,128)(2,1)S(1)}, u32[]{:S(2)}, u32[]{:S(2)}) collective-permute-start(bf16[512,256]{1,0:T(8,128)(2,1)S(1)} %collective-permute-done.10.refs_0_), channel_id=1, source_target_pairs={{0,2},{2,0},{16,18},{18,16},{1,3},{3,1},{17,19},{19,17},{4,6},{6,4... | collective-permute-start | bytes 786440 | tf_op jit(solution)/shard_map/ppermute | solution.py:33
  61.9 12.5 %collective-permute-start.18 = (bf16[512,256]{1,0:T(8,128)(2,1)S(1)}, bf16[512,256]{1,0:T(8,128)(2,1)S(1)}, u32[]{:S(2)}, u32[]{:S(2)}) collective-permute-start(bf16[512,256]{1,0:T(8,128)(2,1)S(1)} %collective-permute-done.10.refs_0_), channel_id=1, source_target_pairs={{0,16},{2,18},{16,0},{18,2},{1,17},{3,19},{17,1},{19,3},{4,20},{6,... | collective-permute-start | bytes 786440 | tf_op jit(solution)/shard_map/ppermute | solution.py:33
  63.5 11.3 %collective-permute-start.19 = (bf16[512,256]{1,0:T(8,128)(2,1)S(1)}, bf16[512,256]{1,0:T(8,128)(2,1)S(1)}, u32[]{:S(2)}, u32[]{:S(2)}) collective-permute-start(bf16[512,256]{1,0:T(8,128)(2,1)S(1)} %collective-permute-done.10.refs_0_), channel_id=1, source_target_pairs={{0,18},{2,16},{16,2},{18,0},{1,19},{3,17},{17,3},{19,1},{4,22},{6,... | collective-permute-start | bytes 786440 | tf_op jit(solution)/shard_map/ppermute | solution.py:33
  73.6 11.0 %collective-permute-start.16 = (bf16[1024,256]{1,0:T(8,128)(2,1)S(1)}, bf16[1024,256]{1,0:T(8,128)(2,1)S(1)}, u32[]{:S(2)}, u32[]{:S(2)}) collective-permute-start(bf16[1024,256]{1,0:T(8,128)(2,1)S(1)} %get-tuple-element.34), channel_id=1, source_target_pairs={{4,8},{8,4},{5,9},{9,5},{6,10},{10,6},{7,11},{11,7},{20,24},{24,20... | collective-permute-start | bytes 1572872 | tf_op jit(solution)/shard_map/ppermute | solution.py:417
  76.0 13.2 %collective-permute-start.20 = (bf16[1024,256]{1,0:T(8,128)(2,1)S(1)}, bf16[1024,256]{1,0:T(8,128)(2,1)S(1)}, u32[]{:S(2)}, u32[]{:S(2)}) collective-permute-start(bf16[1024,256]{1,0:T(8,128)(2,1)S(1)} %panel.5), channel_id=1, source_target_pairs={{0,4},{4,0},{8,12},{12,8},{1,5},{5,1},{9,13},{13,9},{2,6},{6,2},{1... | collective-permute-start | bytes 1572872 | tf_op jit(solution)/shard_map/ppermute | solution.py:33
  81.8 9.8 %collective-permute-start.23 = (bf16[64,2560]{1,0:T(8,128)(2,1)S(1)}, bf16[64,2560]{1,0:T(8,128)(2,1)S(1)}, u32[]{:S(2)}, u32[]{:S(2)}) collective-permute-start(bf16[64,2560]{1,0:T(8,128)(2,1)S(1)} %get-tuple-element.40), channel_id=1, source_target_pairs={{0,2},{2,0},{1,3},{3,1},{4,6},{6,4},{5,7},{7,5},{8,10},{10,8},{9,1... | collective-permute-start | bytes 983048 | tf_op jit(solution)/shard_map/ppermute | solution.py:29
  89.3 5.3 %collective-permute-start.21 = (f32[512,256]{1,0:T(8,128)S(1)}, f32[512,256]{1,0:T(8,128)S(1)}, u32[]{:S(2)}, u32[]{:S(2)}) collective-permute-start(f32[512,256]{1,0:T(8,128)S(1)} %other_rows.1), channel_id=1, source_target_pairs={{0,1},{1,0},{2,3},{3,2},{4,5},{5,4},{6,7},{7,6},{8,9},{9,8},{10,11... | collective-permute-start | bytes 1572872 | tf_op jit(solution)/shard_map/ppermute | solution.py:33
  91.7 1.7 %collective-permute-start.24 = (bf16[64,2560]{1,0:T(8,128)(2,1)S(1)}, bf16[64,2560]{1,0:T(8,128)(2,1)S(1)}, u32[]{:S(2)}, u32[]{:S(2)}) collective-permute-start(bf16[64,2560]{1,0:T(8,128)(2,1)S(1)} %add_convert_fusion.own_ref), channel_id=1, source_target_pairs={{0,1},{1,0},{2,3},{3,2},{4,5},{5,4},{6,7},{7,6},{8,9},{9,8},{10,11... | collective-permute-start | bytes 983048 | tf_op jit(solution)/shard_map/ppermute | solution.py:33
  (11 other events, 100.6 us)

commit v11 on v10

--- a/solution.py
+++ b/solution.py
@@ -61,11 +61,13 @@
     return tenant
 
 
-def half_kernel(core_ref, a_ref, b_ref, out_ref):
-    rank, feat = out_ref.shape[0], a_ref.shape[1]
+def half_kernel(core_ref, a_ref, b_ref, *outs):
+    rank, feat, rows = a_ref.shape[0] // 2, a_ref.shape[1], outs[0].shape[0]
     first = core_ref[0] == 0
-    out_ref[:, :feat] = jnp.where(first, a_ref[:rank, :], a_ref[rank:, :])
-    out_ref[:, feat:] = jnp.where(first, b_ref[:rank, :], b_ref[rank:, :])
+    for n, out in enumerate(outs):
+        one, other = slice(n * rows, (n + 1) * rows), slice(rank + n * rows, rank + (n + 1) * rows)
+        out[:, :feat] = jnp.where(first, a_ref[one, :], a_ref[other, :])
+        out[:, feat:] = jnp.where(first, b_ref[one, :], b_ref[other, :])
 
 
 def own_half(core, a, b, rank):
@@ -73,8 +75,8 @@
     return pl.pallas_call(
         half_kernel,
         in_specs=[SMEM] + [VMEM] * 2,
-        out_specs=VMEM,
-        out_shape=shaped((rank, width), BF16),
+        out_specs=[VMEM] * 2,
+        out_shape=[shaped((rank // 2, width), BF16)] * 2,
         compiler_params=params(56),
         cost_estimate=cost(rank * width, 6 * rank * width),
         name="own_half",
@@ -375,9 +377,10 @@
 
     own_a, own_b = adapter_a.reshape(pair * rank, feat), adapter_b.reshape(pair * rank, cols)
     one = own_half(core, own_a, own_b, rank)
-    halves = []
+    halves, raw = [], []
     for s in range(1, n_dp):
-        got = shift(one, "dp", n_dp, s)
+        raw += [shift(part, "dp", n_dp, s) for part in one]
+        got = jnp.concatenate(raw[-2:], axis=0)
         halves += [got, flip(got, "pipe", n_pipe, 1)]
     panel_at = place if planes == 4 else jnp.zeros_like(place)
 
@@ -398,13 +401,13 @@
         weight[2] = flip(after(share(me_t ^ 2), weight[3]), "tensor", n_t, 2)
         weight[1] = flip(after(share(me_t ^ 1), weight[2]), "tensor", n_t, 1)
         x = pack(after(block_fill, share_3), block_tenant_index, tokens, cotangent, blocks, 2 * rank)
-        x_other = flip(after(x, weight[3], *halves[::2]), "pipe", n_pipe, 1)
+        x_other = flip(after(x, weight[3], *raw), "pipe", n_pipe, 1)
         pieces, order = gathered(weight[3])
         low = low_part(after(dp, x_other), core, block_fill, block_tenant_index, x, own_a, own_b, halves, blocks, rank)
         pieces[0] = after(pieces[0], weight[2], low)
         (y_3,) = panel_product(order, panel_at, x, x_other, pieces, half)
         low = add_flipped(low, 1, weight[2])
-        far = lax.ppermute(after(y_3, low), "tensor", [(0, 1), (3, 2)])
+        far = lax.ppermute(y_3, "tensor", [(0, 1), (3, 2)])
         pieces, order = gathered(after(weight[2], *pieces))
         pieces[0] = after(pieces[0], weight[1])
         (y_2,) = panel_product(order, panel_at, x, x_other, pieces, half, adds=[far])
@@ -438,7 +441,7 @@
     base = base_product(
         at, dp, core, block_fill, block_tenant_index, x, base_weight, low, own_b, halves, feat, blocks, rank
     )
-    parts[0] = after(parts[0], base)
+    parts[0] = after(parts[0], base, down_out)
     others = [flip(other_rows(parts), "pipe", n_pipe, 1)]
     out = finish(core, block_fill, base, parts, others, rows, blocks)
     return out, down_out, up_out

time: 97 us -> 88.8 us (0.915)
  starting transfers between devices: 35.3 us -> 29.7 us
  waiting for transfers between devices: 38.6 us -> 34.1 us
  local copies, waits for them, and re-layouts: 4.39 us -> 5.55 us
    ppermute x20, starting transfers between devices: 26.6 us -> 22.5 us  [flip(): return lax.ppermute(x, names, [(i, i ^ mask) for i in range(count)])]
    ppermute x1, waiting for transfers between devices: 8.48 us -> 6.3 us  [body(): lax.ppermute(after(y_2, low), 'tensor', [(0, 1), (3, 2), (1, 3), (2, 0)])]
    ppermute x2 -> x3, waiting for transfers between devices: 2.3 us -> 0.17 us  [shift(): lax.ppermute(x, name, [(i, (i + step) % count) for i in range(count)])]
    unnamed x20 -> x21, local copies, waits for them, and re-layouts: 3.23 us -> 4.36 us
    ppermute x2 -> x3, starting transfers between devices: 3.54 us -> 2.67 us  [shift(): lax.ppermute(x, name, [(i, (i + step) % count) for i in range(count)])]
  transfers between devices with their start and end apart: 25 -> 26, of which waited for: 12 -> 11; matrix products, arithmetic and copies ran while one was open for 1% -> 0% of each run, Pallas kernels for 13% -> 17%
where the time goes in v11:
time: 88.8 us; the launch traced here: 87.7 us
  waiting for transfers between devices  34.1 us (38%)
  starting transfers between devices  29.7 us (33%)
  Pallas kernels  17.3 us (19%)
  local copies, waits for them, and re-layouts  5.55 us (6%)
  between operations  0.9 us (1%)
    ppermute x20, waiting for transfers between devices, flip(): return lax.ppermute(x, names, [(i, i ^ mask) for i in range(count)])  27.6 us
    ppermute x20, starting transfers between devices, flip(): return lax.ppermute(x, names, [(i, i ^ mask) for i in range(count)])  22.5 us
    ppermute x1, waiting for transfers between devices, body(): lax.ppermute(after(y_2, low), 'tensor', [(0, 1), (3, 2), (1, 3), (2, 0)])  6.3 us
    unnamed x21, local copies, waits for them, and re-layouts  4.36 us
    pallas_call x3, Pallas kernels, panel_product(): pl.pallas_call(functools.partial(panel_kernel, order, len(pieces)), in_sp...  3.75 us
    pallas_call x1, Pallas kernels, pack(): pl.pallas_call(functools.partial(pack_kernel, blocks, rows // blocks), in...  2.83 us
    ppermute x3, starting transfers between devices, shift(): lax.ppermute(x, name, [(i, (i + step) % count) for i in range(count)])  2.67 us
    pallas_call x1, Pallas kernels, low_part(): pl.pallas_call(functools.partial(low_kernel, n_dp, rank, blocks), in_spec...  2.17 us
  transfers between devices with their start and end apart: 26, of which 11 were waited for; matrix products, arithmetic and copies ran while one was open for 0% of the time, Pallas kernels for 17%

profile of v11, /device:TPU:0, one launch (start us, length us, event | category | flops | bytes accessed | tf_op | source)
XLA Modules:
  0.0 87.7 jit_solution(4775708700248793368)
XLA Ops:
  1.8 5.1 %collective-permute-start = (bf16[512,256]{1,0:T(8,128)(2,1)S(1)}, bf16[512,256]{1,0:T(8,128)(2,1)S(1)}, u32[]{:S(2)}, u32[]{:S(2)}) collective-permute-start(bf16[512,256]{1,0:T(8,128)(2,1)S(1)} %get-tuple-element.47), channel_id=1, source_target_pairs={{0,12},{4,8},{8,4},{12,0},{1,13},{5,9},{9,5},{13,1},{2,14},{6,10},... | collective-permute-start | bytes 786440 | tf_op jit(solution)/shard_map/ppermute | solution.py:33
  7.0 1.8 %own_half.1 = (bf16[32,2560]{1,0:T(8,128)(2,1)}, bf16[32,2560]{1,0:T(8,128)(2,1)}) custom-call(s32[1]{0:T(128)} %bitcast.core_ref, bf16[128,2048]{1,0:T(8,128)(2,1)} %bitcast.8, bf16[128,512]{1,0:T(8,128)(2,1)} %bitcast.10), custom_call_target="tpu_custom_call" | custom-call | flops 1 | bytes 1 | tf_op jit(solution)/shard_map/own_half/pallas_call | solution.py:75
  8.8 1.5 %collective-permute-start.1 = (bf16[32,2560]{1,0:T(8,128)(2,1)}, bf16[32,2560]{1,0:T(8,128)(2,1)S(1)}, u32[]{:S(2)}, u32[]{:S(2)}) collective-permute-start(bf16[32,2560]{1,0:T(8,128)(2,1)} %get-tuple-element.25), channel_id=1, source_target_pairs={{0,2},{2,0},{1,3},{3,1},{4,6},{6,4},{5,7},{7,5},{8,10},{10,8},{9,1... | collective-permute-start | bytes 491528 | tf_op jit(solution)/shard_map/ppermute | solution.py:29
  10.8 1.9 %copy-done = bf16[768,2048]{1,0:T(8,128)(2,1)S(1)} copy-done((bf16[768,2048]{1,0:T(8,128)(2,1)S(1)}, bf16[768,2048]{1,0:T(8,128)(2,1)}, u32[]{:S(2)}) %copy-start) | copy-done | bytes 3145752
  15.1 2.8 %pack.1.x_ref.own_ref = bf16[512,2688]{1,0:T(8,128)(2,1)S(1)} custom-call(s32[1,6]{1,0:T(1,128)S(1)} %copy-done.4, s32[6]{0:T(128)S(1)} %copy-done.6, bf16[768,2048]{1,0:T(8,128)(2,1)S(1)} %copy-done, bf16[768,512]{1,0:T(8,128)(2,1)S(1)} %copy-done.3), custom_call_target="tpu_custom_call" | custom-call | flops 1 | bytes 1 | tf_op jit(solution)/shard_map/pack/pallas_call | solution.py:104
  20.2 1.5 %collective-permute-start.8 = (bf16[512,256]{1,0:T(8,128)(2,1)S(1)}, bf16[512,256]{1,0:T(8,128)(2,1)S(1)}, u32[]{:S(2)}, u32[]{:S(2)}) collective-permute-start(bf16[512,256]{1,0:T(8,128)(2,1)S(1)} %collective-permute-done.refs_0_), channel_id=1, source_target_pairs={{0,2},{2,0},{16,18},{18,16},{1,3},{3,1},{17,19},{19,17},{4,6},{6,4... | collective-permute-start | bytes 786440 | tf_op jit(solution)/shard_map/ppermute | solution.py:33
  21.7 1.5 %collective-permute-start.9 = (bf16[512,256]{1,0:T(8,128)(2,1)S(1)}, bf16[512,256]{1,0:T(8,128)(2,1)S(1)}, u32[]{:S(2)}, u32[]{:S(2)}) collective-permute-start(bf16[512,256]{1,0:T(8,128)(2,1)S(1)} %collective-permute-done.refs_0_), channel_id=1, source_target_pairs={{0,16},{2,18},{16,0},{18,2},{1,17},{3,19},{17,1},{19,3},{4,20},{6,... | collective-permute-start | bytes 786440 | tf_op jit(solution)/shard_map/ppermute | solution.py:33
  23.2 2.4 %collective-permute-start.10 = (bf16[512,256]{1,0:T(8,128)(2,1)S(1)}, bf16[512,256]{1,0:T(8,128)(2,1)S(1)}, u32[]{:S(2)}, u32[]{:S(2)}) collective-permute-start(bf16[512,256]{1,0:T(8,128)(2,1)S(1)} %collective-permute-done.refs_0_), channel_id=1, source_target_pairs={{0,18},{2,16},{16,2},{18,0},{1,19},{3,17},{17,3},{19,1},{4,22},{6,... | collective-permute-start | bytes 786440 | tf_op jit(solution)/shard_map/ppermute | solution.py:33
  25.7 2.2 %low_part.1 = bf16[512,128]{1,0:T(8,128)(2,1)S(1)} custom-call(s32[1]{0:T(128)} %bitcast.2.dp_ref, s32[1]{0:T(128)} %bitcast.core_ref, s32[1,6]{1,0:T(1,128)S(1)} %copy-done.4, s32[6]{0:T(128)S(1)} %copy-done.6, bf16[512,2688]{1,0:T(8,128)(2,1)S(1)} %pack.1.x_ref.own_ref, bf16[128,2048]{1,0:T(8,128)(2,1)S(1)} %bitcast.9, bf16[128,512]{1,0:T(8,128)(2,1)S(1)} %bitcast.11, ...), custom_call_target="tpu_custom_call" | custom-call | flops 1 | bytes 1 | tf_op jit(solution)/shard_map/low_part/pallas_call | solution.py:147
  27.9 5.6 %collective-permute-done.5.refs_0_ = bf16[512,256]{1,0:T(8,128)(2,1)S(1)} collective-permute-done((bf16[512,256]{1,0:T(8,128)(2,1)S(1)}, bf16[512,256]{1,0:T(8,128)(2,1)S(1)}, u32[]{:S(2)}, u32[]{:S(2)}) %collective-permute-start.5) | collective-permute-done | bytes 262176 | tf_op jit(solution)/shard_map/ppermute | solution.py:33
  33.5 2.0 %collective-permute-start.11 = (bf16[512,256]{1,0:T(8,128)(2,1)S(1)}, bf16[512,256]{1,0:T(8,128)(2,1)S(1)}, u32[]{:S(2)}, u32[]{:S(2)}) collective-permute-start(bf16[512,256]{1,0:T(8,128)(2,1)S(1)} %get-tuple-element.33), channel_id=1, source_target_pairs={{0,4},{4,0},{8,12},{12,8},{1,5},{5,1},{9,13},{13,9},{2,6},{6,2},{1... | collective-permute-start | bytes 786440 | tf_op jit(solution)/shard_map/ppermute | solution.py:33
  35.5 1.6 %collective-permute-start.12 = (bf16[512,256]{1,0:T(8,128)(2,1)S(1)}, bf16[512,256]{1,0:T(8,128)(2,1)S(1)}, u32[]{:S(2)}, u32[]{:S(2)}) collective-permute-start(bf16[512,256]{1,0:T(8,128)(2,1)S(1)} %collective-permute-done.5.refs_0_), channel_id=1, source_target_pairs={{0,2},{2,0},{16,18},{18,16},{1,3},{3,1},{17,19},{19,17},{4,6},{6,4... | collective-permute-start | bytes 786440 | tf_op jit(solution)/shard_map/ppermute | solution.py:33
  37.0 1.5 %collective-permute-start.13 = (bf16[512,256]{1,0:T(8,128)(2,1)S(1)}, bf16[512,256]{1,0:T(8,128)(2,1)S(1)}, u32[]{:S(2)}, u32[]{:S(2)}) collective-permute-start(bf16[512,256]{1,0:T(8,128)(2,1)S(1)} %collective-permute-done.5.refs_0_), channel_id=1, source_target_pairs={{0,16},{2,18},{16,0},{18,2},{1,17},{3,19},{17,1},{19,3},{4,20},{6,... | collective-permute-start | bytes 786440 | tf_op jit(solution)/shard_map/ppermute | solution.py:33
  40.3 2.0 %collective-permute-start.15 = (bf16[1024,256]{1,0:T(8,128)(2,1)S(1)}, bf16[1024,256]{1,0:T(8,128)(2,1)S(1)}, u32[]{:S(2)}, u32[]{:S(2)}) collective-permute-start(bf16[1024,256]{1,0:T(8,128)(2,1)S(1)} %panel.3.own_ref), channel_id=1, source_target_pairs={{0,4},{12,8},{1,5},{13,9},{2,6},{14,10},{3,7},{15,11},{16,20},{28,... | collective-permute-start | bytes 1572872 | tf_op jit(solution)/shard_map/ppermute | solution.py:410
  42.3 2.2 %collective-permute-done.11.refs_0_ = bf16[512,256]{1,0:T(8,128)(2,1)S(1)} collective-permute-done((bf16[512,256]{1,0:T(8,128)(2,1)S(1)}, bf16[512,256]{1,0:T(8,128)(2,1)S(1)}, u32[]{:S(2)}, u32[]{:S(2)}) %collective-permute-start.11) | collective-permute-done | bytes 262176 | tf_op jit(solution)/shard_map/ppermute | solution.py:33
  44.8 5.3 %collective-permute-done.13.refs_2_ = bf16[512,256]{1,0:T(8,128)(2,1)S(1)} collective-permute-done((bf16[512,256]{1,0:T(8,128)(2,1)S(1)}, bf16[512,256]{1,0:T(8,128)(2,1)S(1)}, u32[]{:S(2)}, u32[]{:S(2)}) %collective-permute-start.13) | collective-permute-done | bytes 262176 | tf_op jit(solution)/shard_map/ppermute | solution.py:33
  53.6 2.8 %collective-permute-done.7 = bf16[512,128]{1,0:T(8,128)(2,1)S(1)} collective-permute-done((bf16[512,128]{1,0:T(8,128)(2,1)S(1)}, bf16[512,128]{1,0:T(8,128)(2,1)S(1)}, u32[]{:S(2)}, u32[]{:S(2)}) %collective-permute-start.7) | collective-permute-done | bytes 131104 | tf_op jit(solution)/shard_map/ppermute | solution.py:33
  57.7 1.8 %collective-permute-start.16 = (bf16[1024,256]{1,0:T(8,128)(2,1)S(1)}, bf16[1024,256]{1,0:T(8,128)(2,1)S(1)}, u32[]{:S(2)}, u32[]{:S(2)}) collective-permute-start(bf16[1024,256]{1,0:T(8,128)(2,1)S(1)} %panel.4), channel_id=1, source_target_pairs={{0,4},{12,8},{4,12},{8,0},{1,5},{13,9},{5,13},{9,1},{2,6},{14,10},... | collective-permute-start | bytes 1572872 | tf_op jit(solution)/shard_map/ppermute | solution.py:415
  61.8 1.6 %collective-permute-done.20.refs_2_ = bf16[512,256]{1,0:T(8,128)(2,1)S(1)} collective-permute-done((bf16[512,256]{1,0:T(8,128)(2,1)S(1)}, bf16[512,256]{1,0:T(8,128)(2,1)S(1)}, u32[]{:S(2)}, u32[]{:S(2)}) %collective-permute-start.20) | collective-permute-done | bytes 262176 | tf_op jit(solution)/shard_map/ppermute | solution.py:33
  66.0 6.3 %collective-permute-done.16.got_ref = bf16[1024,256]{1,0:T(8,128)(2,1)S(1)} collective-permute-done((bf16[1024,256]{1,0:T(8,128)(2,1)S(1)}, bf16[1024,256]{1,0:T(8,128)(2,1)S(1)}, u32[]{:S(2)}, u32[]{:S(2)}) %collective-permute-start.16) | collective-permute-done | bytes 524320 | tf_op jit(solution)/shard_map/ppermute | solution.py:415
  73.4 2.1 %base.1.base_ref = f32[512,512]{1,0:T(8,128)S(1)} custom-call(s32[1]{0:T(128)} %bitcast.1.at_ref, s32[1]{0:T(128)} %bitcast.2.dp_ref, s32[1]{0:T(128)} %bitcast.core_ref, s32[1,6]{1,0:T(1,128)S(1)} %copy-done.5, s32[6]{0:T(128)S(1)} %copy-done.7, bf16[512,2688]{1,0:T(8,128)(2,1)S(1)} %pack.1.x_ref.own_ref, bf16[8192,512]{1,0:T(8,128)(2,1)S(1)} %bitcast.7, ...), custom_call_target="tpu_custom_call" | custom-call | flops 1 | bytes 1 | tf_op jit(solution)/shard_map/base/pallas_call | solution.py:271
  76.8 6.7 %collective-permute-done.24.refs_1_ = bf16[1024,256]{1,0:T(8,128)(2,1)S(1)} collective-permute-done((bf16[1024,256]{1,0:T(8,128)(2,1)S(1)}, bf16[1024,256]{1,0:T(8,128)(2,1)S(1)}, u32[]{:S(2)}, u32[]{:S(2)}) %collective-permute-start.24) | collective-permute-done | bytes 524320 | tf_op jit(solution)/shard_map/ppermute | solution.py:33
  83.6 1.9 %collective-permute-done.25.refs_3_ = f32[512,256]{1,0:T(8,128)S(1)} collective-permute-done((f32[512,256]{1,0:T(8,128)S(1)}, f32[512,256]{1,0:T(8,128)S(1)}, u32[]{:S(2)}, u32[]{:S(2)}) %collective-permute-start.25) | collective-permute-done | bytes 524320 | tf_op jit(solution)/shard_map/ppermute | solution.py:33
  85.5 2.2 %finish.1 = bf16[768,512]{1,0:T(8,128)(2,1)} custom-call(s32[1]{0:T(128)} %bitcast.core_ref, s32[1,6]{1,0:T(1,128)S(1)} %copy-done.5, f32[512,512]{1,0:T(8,128)S(1)} %base.1.base_ref, bf16[1024,256]{1,0:T(8,128)(2,1)S(1)} %collective-permute-done.17.refs_0_, bf16[1024,256]{1,0:T(8,128)(2,1)S(1)} %collective-permute-done.24.refs_1_, ...), custom_call_target="tpu_custom_call" | custom-call | flops 1 | bytes 1 | tf_op jit(solution)/shard_map/finish/pallas_call | solution.py:352
  (67 shorter events, 20.6 us)
Async XLA Ops:
  1.8 16.3 %collective-permute-start = (bf16[512,256]{1,0:T(8,128)(2,1)S(1)}, bf16[512,256]{1,0:T(8,128)(2,1)S(1)}, u32[]{:S(2)}, u32[]{:S(2)}) collective-permute-start(bf16[512,256]{1,0:T(8,128)(2,1)S(1)} %get-tuple-element.47), channel_id=1, source_target_pairs={{0,12},{4,8},{8,4},{12,0},{1,13},{5,9},{9,5},{13,1},{2,14},{6,10},... | collective-permute-start | bytes 786440 | tf_op jit(solution)/shard_map/ppermute | solution.py:33
  8.8 9.2 %collective-permute-start.1 = (bf16[32,2560]{1,0:T(8,128)(2,1)}, bf16[32,2560]{1,0:T(8,128)(2,1)S(1)}, u32[]{:S(2)}, u32[]{:S(2)}) collective-permute-start(bf16[32,2560]{1,0:T(8,128)(2,1)} %get-tuple-element.25), channel_id=1, source_target_pairs={{0,2},{2,0},{1,3},{3,1},{4,6},{6,4},{5,7},{7,5},{8,10},{10,8},{9,1... | collective-permute-start | bytes 491528 | tf_op jit(solution)/shard_map/ppermute | solution.py:29
  10.2 7.9 %collective-permute-start.2 = (bf16[32,2560]{1,0:T(8,128)(2,1)}, bf16[32,2560]{1,0:T(8,128)(2,1)S(1)}, u32[]{:S(2)}, u32[]{:S(2)}) collective-permute-start(bf16[32,2560]{1,0:T(8,128)(2,1)} %get-tuple-element.26), channel_id=1, source_target_pairs={{0,2},{2,0},{1,3},{3,1},{4,6},{6,4},{5,7},{7,5},{8,10},{10,8},{9,1... | collective-permute-start | bytes 491528 | tf_op jit(solution)/shard_map/ppermute | solution.py:29
  18.1 5.1 %collective-permute-start.3 = (bf16[512,2688]{1,0:T(8,128)(2,1)S(1)}, bf16[512,2688]{1,0:T(8,128)(2,1)S(1)}, u32[]{:S(2)}, u32[]{:S(2)}) collective-permute-start(bf16[512,2688]{1,0:T(8,128)(2,1)S(1)} %pack.1.x_ref.own_ref), channel_id=1, source_target_pairs={{0,1},{1,0},{2,3},{3,2},{4,5},{5,4},{6,7},{7,6},{8,9},{9,8},{10,11... | collective-permute-start | bytes 8257544 | tf_op jit(solution)/shard_map/ppermute | solution.py:33
  18.2 7.5 %collective-permute-start.4 = (bf16[64,2560]{1,0:T(8,128)(2,1)S(1)}, bf16[64,2560]{1,0:T(8,128)(2,1)S(1)}, u32[]{:S(2)}, u32[]{:S(2)}) collective-permute-start(bf16[64,2560]{1,0:T(8,128)(2,1)S(1)} %constant_dynamic-update-slice_fusion.refs_0_), channel_id=1, source_target_pairs={{0,1},{1,0},{2,3},{3,2},{4,5},{5,4},{6,7},{7,6},{8,9},{9,8},{10,11... | collective-permute-start | bytes 983048 | tf_op jit(solution)/shard_map/ppermute | solution.py:33
  18.8 14.7 %collective-permute-start.5 = (bf16[512,256]{1,0:T(8,128)(2,1)S(1)}, bf16[512,256]{1,0:T(8,128)(2,1)S(1)}, u32[]{:S(2)}, u32[]{:S(2)}) collective-permute-start(bf16[512,256]{1,0:T(8,128)(2,1)S(1)} %get-tuple-element.29), channel_id=1, source_target_pairs={{0,8},{4,12},{8,0},{12,4},{1,9},{5,13},{9,1},{13,5},{2,10},{6,14},... | collective-permute-start | bytes 786440 | tf_op jit(solution)/shard_map/ppermute | solution.py:33
  20.2 15.3 %collective-permute-start.8 = (bf16[512,256]{1,0:T(8,128)(2,1)S(1)}, bf16[512,256]{1,0:T(8,128)(2,1)S(1)}, u32[]{:S(2)}, u32[]{:S(2)}) collective-permute-start(bf16[512,256]{1,0:T(8,128)(2,1)S(1)} %collective-permute-done.refs_0_), channel_id=1, source_target_pairs={{0,2},{2,0},{16,18},{18,16},{1,3},{3,1},{17,19},{19,17},{4,6},{6,4... | collective-permute-start | bytes 786440 | tf_op jit(solution)/shard_map/ppermute | solution.py:33
  21.7 13.8 %collective-permute-start.9 = (bf16[512,256]{1,0:T(8,128)(2,1)S(1)}, bf16[512,256]{1,0:T(8,128)(2,1)S(1)}, u32[]{:S(2)}, u32[]{:S(2)}) collective-permute-start(bf16[512,256]{1,0:T(8,128)(2,1)S(1)} %collective-permute-done.refs_0_), channel_id=1, source_target_pairs={{0,16},{2,18},{16,0},{18,2},{1,17},{3,19},{17,1},{19,3},{4,20},{6,... | collective-permute-start | bytes 786440 | tf_op jit(solution)/shard_map/ppermute | solution.py:33
  23.2 12.2 %collective-permute-start.10 = (bf16[512,256]{1,0:T(8,128)(2,1)S(1)}, bf16[512,256]{1,0:T(8,128)(2,1)S(1)}, u32[]{:S(2)}, u32[]{:S(2)}) collective-permute-start(bf16[512,256]{1,0:T(8,128)(2,1)S(1)} %collective-permute-done.refs_0_), channel_id=1, source_target_pairs={{0,18},{2,16},{16,2},{18,0},{1,19},{3,17},{17,3},{19,1},{4,22},{6,... | collective-permute-start | bytes 786440 | tf_op jit(solution)/shard_map/ppermute | solution.py:33
  33.4 6.8 %collective-permute-start.6 = (bf16[512,128]{1,0:T(8,128)(2,1)S(1)}, bf16[512,128]{1,0:T(8,128)(2,1)S(1)}, u32[]{:S(2)}, u32[]{:S(2)}) collective-permute-start(bf16[512,128]{1,0:T(8,128)(2,1)S(1)} %low_part.1), channel_id=1, source_target_pairs={{0,4},{4,0},{8,12},{12,8},{1,5},{5,1},{9,13},{13,9},{2,6},{6,2},{1... | collective-permute-start | bytes 393224 | tf_op jit(solution)/shard_map/ppermute | solution.py:33
  33.5 11.0 %collective-permute-start.11 = (bf16[512,256]{1,0:T(8,128)(2,1)S(1)}, bf16[512,256]{1,0:T(8,128)(2,1)S(1)}, u32[]{:S(2)}, u32[]{:S(2)}) collective-permute-start(bf16[512,256]{1,0:T(8,128)(2,1)S(1)} %get-tuple-element.33), channel_id=1, source_target_pairs={{0,4},{4,0},{8,12},{12,8},{1,5},{5,1},{9,13},{13,9},{2,6},{6,2},{1... | collective-permute-start | bytes 786440 | tf_op jit(solution)/shard_map/ppermute | solution.py:33
  35.5 9.3 %collective-permute-start.12 = (bf16[512,256]{1,0:T(8,128)(2,1)S(1)}, bf16[512,256]{1,0:T(8,128)(2,1)S(1)}, u32[]{:S(2)}, u32[]{:S(2)}) collective-permute-start(bf16[512,256]{1,0:T(8,128)(2,1)S(1)} %collective-permute-done.5.refs_0_), channel_id=1, source_target_pairs={{0,2},{2,0},{16,18},{18,16},{1,3},{3,1},{17,19},{19,17},{4,6},{6,4... | collective-permute-start | bytes 786440 | tf_op jit(solution)/shard_map/ppermute | solution.py:33
  37.0 13.0 %collective-permute-start.13 = (bf16[512,256]{1,0:T(8,128)(2,1)S(1)}, bf16[512,256]{1,0:T(8,128)(2,1)S(1)}, u32[]{:S(2)}, u32[]{:S(2)}) collective-permute-start(bf16[512,256]{1,0:T(8,128)(2,1)S(1)} %collective-permute-done.5.refs_0_), channel_id=1, source_target_pairs={{0,16},{2,18},{16,0},{18,2},{1,17},{3,19},{17,1},{19,3},{4,20},{6,... | collective-permute-start | bytes 786440 | tf_op jit(solution)/shard_map/ppermute | solution.py:33
  38.6 11.5 %collective-permute-start.14 = (bf16[512,256]{1,0:T(8,128)(2,1)S(1)}, bf16[512,256]{1,0:T(8,128)(2,1)S(1)}, u32[]{:S(2)}, u32[]{:S(2)}) collective-permute-start(bf16[512,256]{1,0:T(8,128)(2,1)S(1)} %collective-permute-done.5.refs_0_), channel_id=1, source_target_pairs={{0,18},{2,16},{16,2},{18,0},{1,19},{3,17},{17,3},{19,1},{4,22},{6,... | collective-permute-start | bytes 786440 | tf_op jit(solution)/shard_map/ppermute | solution.py:33
  40.3 16.1 %collective-permute-start.15 = (bf16[1024,256]{1,0:T(8,128)(2,1)S(1)}, bf16[1024,256]{1,0:T(8,128)(2,1)S(1)}, u32[]{:S(2)}, u32[]{:S(2)}) collective-permute-start(bf16[1024,256]{1,0:T(8,128)(2,1)S(1)} %panel.3.own_ref), channel_id=1, source_target_pairs={{0,4},{12,8},{1,5},{13,9},{2,6},{14,10},{3,7},{15,11},{16,20},{28,... | collective-permute-start | bytes 1572872 | tf_op jit(solution)/shard_map/ppermute | solution.py:410
  44.5 11.8 %collective-permute-start.7 = (bf16[512,128]{1,0:T(8,128)(2,1)S(1)}, bf16[512,128]{1,0:T(8,128)(2,1)S(1)}, u32[]{:S(2)}, u32[]{:S(2)}) collective-permute-start(bf16[512,128]{1,0:T(8,128)(2,1)S(1)} %add_convert_fusion.2), channel_id=1, source_target_pairs={{0,8},{4,12},{8,0},{12,4},{1,9},{5,13},{9,1},{13,5},{2,10},{6,14},... | collective-permute-start | bytes 393224 | tf_op jit(solution)/shard_map/ppermute | solution.py:33
  50.1 11.8 %collective-permute-start.19 = (bf16[512,256]{1,0:T(8,128)(2,1)S(1)}, bf16[512,256]{1,0:T(8,128)(2,1)S(1)}, u32[]{:S(2)}, u32[]{:S(2)}) collective-permute-start(bf16[512,256]{1,0:T(8,128)(2,1)S(1)} %collective-permute-done.11.refs_0_), channel_id=1, source_target_pairs={{0,2},{2,0},{16,18},{18,16},{1,3},{3,1},{17,19},{19,17},{4,6},{6,4... | collective-permute-start | bytes 786440 | tf_op jit(solution)/shard_map/ppermute | solution.py:33
  51.3 12.1 %collective-permute-start.20 = (bf16[512,256]{1,0:T(8,128)(2,1)S(1)}, bf16[512,256]{1,0:T(8,128)(2,1)S(1)}, u32[]{:S(2)}, u32[]{:S(2)}) collective-permute-start(bf16[512,256]{1,0:T(8,128)(2,1)S(1)} %collective-permute-done.11.refs_0_), channel_id=1, source_target_pairs={{0,16},{2,18},{16,0},{18,2},{1,17},{3,19},{17,1},{19,3},{4,20},{6,... | collective-permute-start | bytes 786440 | tf_op jit(solution)/shard_map/ppermute | solution.py:33
  52.1 11.3 %collective-permute-start.21 = (bf16[512,256]{1,0:T(8,128)(2,1)S(1)}, bf16[512,256]{1,0:T(8,128)(2,1)S(1)}, u32[]{:S(2)}, u32[]{:S(2)}) collective-permute-start(bf16[512,256]{1,0:T(8,128)(2,1)S(1)} %collective-permute-done.11.refs_0_), channel_id=1, source_target_pairs={{0,18},{2,16},{16,2},{18,0},{1,19},{3,17},{17,3},{19,1},{4,22},{6,... | collective-permute-start | bytes 786440 | tf_op jit(solution)/shard_map/ppermute | solution.py:33
  57.7 14.7 %collective-permute-start.16 = (bf16[1024,256]{1,0:T(8,128)(2,1)S(1)}, bf16[1024,256]{1,0:T(8,128)(2,1)S(1)}, u32[]{:S(2)}, u32[]{:S(2)}) collective-permute-start(bf16[1024,256]{1,0:T(8,128)(2,1)S(1)} %panel.4), channel_id=1, source_target_pairs={{0,4},{12,8},{4,12},{8,0},{1,5},{13,9},{5,13},{9,1},{2,6},{14,10},... | collective-permute-start | bytes 1572872 | tf_op jit(solution)/shard_map/ppermute | solution.py:415
  63.4 9.8 %collective-permute-start.22 = (bf16[64,2560]{1,0:T(8,128)(2,1)S(1)}, bf16[64,2560]{1,0:T(8,128)(2,1)S(1)}, u32[]{:S(2)}, u32[]{:S(2)}) collective-permute-start(bf16[64,2560]{1,0:T(8,128)(2,1)S(1)} %get-tuple-element.40), channel_id=1, source_target_pairs={{0,2},{2,0},{1,3},{3,1},{4,6},{6,4},{5,7},{7,5},{8,10},{10,8},{9,1... | collective-permute-start | bytes 983048 | tf_op jit(solution)/shard_map/ppermute | solution.py:29
  65.3 18.1 %collective-permute-start.24 = (bf16[1024,256]{1,0:T(8,128)(2,1)S(1)}, bf16[1024,256]{1,0:T(8,128)(2,1)S(1)}, u32[]{:S(2)}, u32[]{:S(2)}) collective-permute-start(bf16[1024,256]{1,0:T(8,128)(2,1)S(1)} %panel.5), channel_id=1, source_target_pairs={{0,4},{4,0},{8,12},{12,8},{1,5},{5,1},{9,13},{13,9},{2,6},{6,2},{1... | collective-permute-start | bytes 1572872 | tf_op jit(solution)/shard_map/ppermute | solution.py:33
  72.5 4.3 %collective-permute-start.17 = (bf16[1024,256]{1,0:T(8,128)(2,1)S(1)}, bf16[1024,256]{1,0:T(8,128)(2,1)S(1)}, u32[]{:S(2)}, u32[]{:S(2)}) collective-permute-start(bf16[1024,256]{1,0:T(8,128)(2,1)S(1)} %get-tuple-element.36), channel_id=1, source_target_pairs={{4,8},{8,4},{5,9},{9,5},{6,10},{10,6},{7,11},{11,7},{20,24},{24,20... | collective-permute-start | bytes 1572872 | tf_op jit(solution)/shard_map/ppermute | solution.py:420
  73.3 2.3 %collective-permute-start.23 = (bf16[64,2560]{1,0:T(8,128)(2,1)S(1)}, bf16[64,2560]{1,0:T(8,128)(2,1)S(1)}, u32[]{:S(2)}, u32[]{:S(2)}) collective-permute-start(bf16[64,2560]{1,0:T(8,128)(2,1)S(1)} %add_convert_fusion.own_ref), channel_id=1, source_target_pairs={{0,1},{1,0},{2,3},{3,2},{4,5},{5,4},{6,7},{7,6},{8,9},{9,8},{10,11... | collective-permute-start | bytes 983048 | tf_op jit(solution)/shard_map/ppermute | solution.py:33
  (12 other events, 71.4 us)

commit v12 on v11

--- a/solution.py
+++ b/solution.py
@@ -398,9 +398,10 @@
     if n_t == 4:
         share_3 = share(me_t ^ 3)
         weight = {3: flip(share_3, "tensor", n_t, 3)}
-        weight[2] = flip(after(share(me_t ^ 2), weight[3]), "tensor", n_t, 2)
-        weight[1] = flip(after(share(me_t ^ 1), weight[2]), "tensor", n_t, 1)
-        x = pack(after(block_fill, share_3), block_tenant_index, tokens, cotangent, blocks, 2 * rank)
+        share_2, share_1 = share(after(me_t ^ 2, share_3)), share(after(me_t ^ 1, share_3))
+        weight[2] = flip(after(share_2, weight[3]), "tensor", n_t, 2)
+        weight[1] = flip(after(share_1, weight[2]), "tensor", n_t, 1)
+        x = pack(after(block_fill, share_2, share_1), block_tenant_index, tokens, cotangent, blocks, 2 * rank)
         x_other = flip(after(x, weight[3], *raw), "pipe", n_pipe, 1)
         pieces, order = gathered(weight[3])
         low = low_part(after(dp, x_other), core, block_fill, block_tenant_index, x, own_a, own_b, halves, blocks, rank)
@@ -415,8 +416,8 @@
         near = lax.ppermute(after(y_2, low), "tensor", [(0, 1), (3, 2), (1, 3), (2, 0)])
         pieces, order = gathered(after(weight[1], *pieces))
         (y_1,) = panel_product(order, panel_at, x, x_other, pieces, half)
-        part_1 = flip(y_1, "tensor", n_t, 1)
         passed, kept = relay(at, y_3, near)
+        part_1 = flip(after(y_1, passed), "tensor", n_t, 1)
         parts = [lax.ppermute(passed, "tensor", [(1, 2), (2, 1)]), part_1, kept]
     else:
         x = pack(block_fill, block_tenant_index, tokens, cotangent, blocks, 2 * rank)

time: 88.8 us -> 91 us (1.025)
  starting transfers between devices: 29.7 us -> 33 us
  waiting for transfers between devices: 34.1 us -> 32.9 us
    ppermute x1, starting transfers between devices: 1.8 us -> 3.28 us  [body(): lax.ppermute(after(y_2, low), 'tensor', [(0, 1), (3, 2), (1, 3), (2, 0)])]
    ppermute x20, starting transfers between devices: 22.5 us -> 23.5 us  [flip(): return lax.ppermute(x, names, [(i, i ^ mask) for i in range(count)])]
    dynamic_slice x1 -> x2, local copies, waits for them, and re-layouts: 1.17 us -> 2.04 us  [share(): lax.dynamic_slice(base_weight, (k * feat + q * part_rows, me_pipe * half)...]
  transfers between devices with their start and end apart: 26 -> 26, of which waited for: 11 -> 11; matrix products, arithmetic and copies ran while one was open for 0% -> 1% of each run, Pallas kernels for 17% -> 17%
where the time goes in v12:
time: 91 us; the launch traced here: 90.7 us
  starting transfers between devices  33 us (36%)
  waiting for transfers between devices  32.9 us (36%)
  Pallas kernels  17.3 us (19%)
  local copies, waits for them, and re-layouts  6.41 us (7%)
  between operations  0.92 us (1%)
    ppermute x20, waiting for transfers between devices, flip(): return lax.ppermute(x, names, [(i, i ^ mask) for i in range(count)])  26.8 us
    ppermute x20, starting transfers between devices, flip(): return lax.ppermute(x, names, [(i, i ^ mask) for i in range(count)])  23.5 us
    ppermute x1, waiting for transfers between devices, body(): lax.ppermute(after(y_2, low), 'tensor', [(0, 1), (3, 2), (1, 3), (2, 0)])  6.03 us
    unnamed x21, local copies, waits for them, and re-layouts  4.36 us
    pallas_call x3, Pallas kernels, panel_product(): pl.pallas_call(functools.partial(panel_kernel, order, len(pieces)), in_sp...  3.75 us
    ppermute x3, starting transfers between devices, shift(): lax.ppermute(x, name, [(i, (i + step) % count) for i in range(count)])  3.55 us
    ppermute x1, starting transfers between devices, body(): lax.ppermute(after(y_2, low), 'tensor', [(0, 1), (3, 2), (1, 3), (2, 0)])  3.28 us
    pallas_call x1, Pallas kernels, pack(): pl.pallas_call(functools.partial(pack_kernel, blocks, rows // blocks), in...  2.83 us
  transfers between devices with their start and end apart: 26, of which 11 were waited for; matrix products, arithmetic and copies ran while one was open for 1% of the time, Pallas kernels for 17%

profile of v12, /device:TPU:0, one launch (start us, length us, event | category | flops | bytes accessed | tf_op | source)
XLA Modules:
  0.0 90.7 jit_solution(17827528185589270704)
XLA Ops:
  1.6 5.1 %collective-permute-start = (bf16[512,256]{1,0:T(8,128)(2,1)S(1)}, bf16[512,256]{1,0:T(8,128)(2,1)S(1)}, u32[]{:S(2)}, u32[]{:S(2)}) collective-permute-start(bf16[512,256]{1,0:T(8,128)(2,1)S(1)} %dynamic_slice.9), channel_id=1, source_target_pairs={{0,12},{4,8},{8,4},{12,0},{1,13},{5,9},{9,5},{13,1},{2,14},{6,10},... | collective-permute-start | bytes 786440 | tf_op jit(solution)/shard_map/ppermute | solution.py:33
  6.7 1.8 %own_half.1 = (bf16[32,2560]{1,0:T(8,128)(2,1)}, bf16[32,2560]{1,0:T(8,128)(2,1)}) custom-call(s32[1]{0:T(128)} %bitcast.core_ref, bf16[128,2048]{1,0:T(8,128)(2,1)} %bitcast.8, bf16[128,512]{1,0:T(8,128)(2,1)} %bitcast.10), custom_call_target="tpu_custom_call" | custom-call | flops 1 | bytes 1 | tf_op jit(solution)/shard_map/own_half/pallas_call | solution.py:75
  8.5 1.5 %collective-permute-start.1 = (bf16[32,2560]{1,0:T(8,128)(2,1)}, bf16[32,2560]{1,0:T(8,128)(2,1)S(1)}, u32[]{:S(2)}, u32[]{:S(2)}) collective-permute-start(bf16[32,2560]{1,0:T(8,128)(2,1)} %get-tuple-element.30), channel_id=1, source_target_pairs={{0,2},{2,0},{1,3},{3,1},{4,6},{6,4},{5,7},{7,5},{8,10},{10,8},{9,1... | collective-permute-start | bytes 491528 | tf_op jit(solution)/shard_map/ppermute | solution.py:29
  11.7 1.9 %copy-done = bf16[768,2048]{1,0:T(8,128)(2,1)S(1)} copy-done((bf16[768,2048]{1,0:T(8,128)(2,1)S(1)}, bf16[768,2048]{1,0:T(8,128)(2,1)}, u32[]{:S(2)}) %copy-start) | copy-done | bytes 3145752
  16.0 2.8 %pack.1.x_ref.own_ref = bf16[512,2688]{1,0:T(8,128)(2,1)S(1)} custom-call(s32[1,6]{1,0:T(1,128)S(1)} %copy-done.4, s32[6]{0:T(128)S(1)} %copy-done.6, bf16[768,2048]{1,0:T(8,128)(2,1)S(1)} %copy-done, bf16[768,512]{1,0:T(8,128)(2,1)S(1)} %copy-done.3), custom_call_target="tpu_custom_call" | custom-call | flops 1 | bytes 1 | tf_op jit(solution)/shard_map/pack/pallas_call | solution.py:104
  20.0 2.4 %collective-permute-start.10 = (bf16[512,256]{1,0:T(8,128)(2,1)S(1)}, bf16[512,256]{1,0:T(8,128)(2,1)S(1)}, u32[]{:S(2)}, u32[]{:S(2)}) collective-permute-start(bf16[512,256]{1,0:T(8,128)(2,1)S(1)} %collective-permute-done.refs_0_), channel_id=1, source_target_pairs={{0,18},{2,16},{16,2},{18,0},{1,19},{3,17},{17,3},{19,1},{4,22},{6,... | collective-permute-start | bytes 786440 | tf_op jit(solution)/shard_map/ppermute | solution.py:33
  24.0 1.5 %collective-permute-start.9 = (bf16[512,256]{1,0:T(8,128)(2,1)S(1)}, bf16[512,256]{1,0:T(8,128)(2,1)S(1)}, u32[]{:S(2)}, u32[]{:S(2)}) collective-permute-start(bf16[512,256]{1,0:T(8,128)(2,1)S(1)} %collective-permute-done.refs_0_), channel_id=1, source_target_pairs={{0,16},{2,18},{16,0},{18,2},{1,17},{3,19},{17,1},{19,3},{4,20},{6,... | collective-permute-start | bytes 786440 | tf_op jit(solution)/shard_map/ppermute | solution.py:33
  25.6 2.2 %low_part.1 = bf16[512,128]{1,0:T(8,128)(2,1)S(1)} custom-call(s32[1]{0:T(128)} %bitcast.2.dp_ref, s32[1]{0:T(128)} %bitcast.core_ref, s32[1,6]{1,0:T(1,128)S(1)} %copy-done.4, s32[6]{0:T(128)S(1)} %copy-done.6, bf16[512,2688]{1,0:T(8,128)(2,1)S(1)} %pack.1.x_ref.own_ref, bf16[128,2048]{1,0:T(8,128)(2,1)S(1)} %bitcast.9, bf16[128,512]{1,0:T(8,128)(2,1)S(1)} %bitcast.11, ...), custom_call_target="tpu_custom_call" | custom-call | flops 1 | bytes 1 | tf_op jit(solution)/shard_map/low_part/pallas_call | solution.py:147
  27.7 5.6 %collective-permute-done.5.refs_0_ = bf16[512,256]{1,0:T(8,128)(2,1)S(1)} collective-permute-done((bf16[512,256]{1,0:T(8,128)(2,1)S(1)}, bf16[512,256]{1,0:T(8,128)(2,1)S(1)}, u32[]{:S(2)}, u32[]{:S(2)}) %collective-permute-start.5) | collective-permute-done | bytes 262176 | tf_op jit(solution)/shard_map/ppermute | solution.py:33
  33.3 2.0 %collective-permute-start.11 = (bf16[512,256]{1,0:T(8,128)(2,1)S(1)}, bf16[512,256]{1,0:T(8,128)(2,1)S(1)}, u32[]{:S(2)}, u32[]{:S(2)}) collective-permute-start(bf16[512,256]{1,0:T(8,128)(2,1)S(1)} %get-tuple-element.38), channel_id=1, source_target_pairs={{0,4},{4,0},{8,12},{12,8},{1,5},{5,1},{9,13},{13,9},{2,6},{6,2},{1... | collective-permute-start | bytes 786440 | tf_op jit(solution)/shard_map/ppermute | solution.py:33
  35.4 1.6 %collective-permute-start.12 = (bf16[512,256]{1,0:T(8,128)(2,1)S(1)}, bf16[512,256]{1,0:T(8,128)(2,1)S(1)}, u32[]{:S(2)}, u32[]{:S(2)}) collective-permute-start(bf16[512,256]{1,0:T(8,128)(2,1)S(1)} %collective-permute-done.5.refs_0_), channel_id=1, source_target_pairs={{0,2},{2,0},{16,18},{18,16},{1,3},{3,1},{17,19},{19,17},{4,6},{6,4... | collective-permute-start | bytes 786440 | tf_op jit(solution)/shard_map/ppermute | solution.py:33
  36.9 1.5 %collective-permute-start.13 = (bf16[512,256]{1,0:T(8,128)(2,1)S(1)}, bf16[512,256]{1,0:T(8,128)(2,1)S(1)}, u32[]{:S(2)}, u32[]{:S(2)}) collective-permute-start(bf16[512,256]{1,0:T(8,128)(2,1)S(1)} %collective-permute-done.5.refs_0_), channel_id=1, source_target_pairs={{0,16},{2,18},{16,0},{18,2},{1,17},{3,19},{17,1},{19,3},{4,20},{6,... | collective-permute-start | bytes 786440 | tf_op jit(solution)/shard_map/ppermute | solution.py:33
  40.2 2.0 %collective-permute-start.15 = (bf16[1024,256]{1,0:T(8,128)(2,1)S(1)}, bf16[1024,256]{1,0:T(8,128)(2,1)S(1)}, u32[]{:S(2)}, u32[]{:S(2)}) collective-permute-start(bf16[1024,256]{1,0:T(8,128)(2,1)S(1)} %panel.3.own_ref), channel_id=1, source_target_pairs={{0,4},{12,8},{1,5},{13,9},{2,6},{14,10},{3,7},{15,11},{16,20},{28,... | collective-permute-start | bytes 1572872 | tf_op jit(solution)/shard_map/ppermute | solution.py:411
  42.2 2.2 %collective-permute-done.11.refs_0_ = bf16[512,256]{1,0:T(8,128)(2,1)S(1)} collective-permute-done((bf16[512,256]{1,0:T(8,128)(2,1)S(1)}, bf16[512,256]{1,0:T(8,128)(2,1)S(1)}, u32[]{:S(2)}, u32[]{:S(2)}) %collective-permute-start.11) | collective-permute-done | bytes 262176 | tf_op jit(solution)/shard_map/ppermute | solution.py:33
  44.7 5.3 %collective-permute-done.13.refs_2_ = bf16[512,256]{1,0:T(8,128)(2,1)S(1)} collective-permute-done((bf16[512,256]{1,0:T(8,128)(2,1)S(1)}, bf16[512,256]{1,0:T(8,128)(2,1)S(1)}, u32[]{:S(2)}, u32[]{:S(2)}) %collective-permute-start.13) | collective-permute-done | bytes 262176 | tf_op jit(solution)/shard_map/ppermute | solution.py:33
  53.4 2.8 %collective-permute-done.7 = bf16[512,128]{1,0:T(8,128)(2,1)S(1)} collective-permute-done((bf16[512,128]{1,0:T(8,128)(2,1)S(1)}, bf16[512,128]{1,0:T(8,128)(2,1)S(1)}, u32[]{:S(2)}, u32[]{:S(2)}) %collective-permute-start.7) | collective-permute-done | bytes 131104 | tf_op jit(solution)/shard_map/ppermute | solution.py:33
  57.5 3.3 %collective-permute-start.16 = (bf16[1024,256]{1,0:T(8,128)(2,1)S(1)}, bf16[1024,256]{1,0:T(8,128)(2,1)S(1)}, u32[]{:S(2)}, u32[]{:S(2)}) collective-permute-start(bf16[1024,256]{1,0:T(8,128)(2,1)S(1)} %panel.4), channel_id=1, source_target_pairs={{0,4},{12,8},{4,12},{8,0},{1,5},{13,9},{5,13},{9,1},{2,6},{14,10},... | collective-permute-start | bytes 1572872 | tf_op jit(solution)/shard_map/ppermute | solution.py:416
  63.3 1.5 %collective-permute-start.22 = (bf16[64,2560]{1,0:T(8,128)(2,1)S(1)}, bf16[64,2560]{1,0:T(8,128)(2,1)S(1)}, u32[]{:S(2)}, u32[]{:S(2)}) collective-permute-start(bf16[64,2560]{1,0:T(8,128)(2,1)S(1)} %get-tuple-element.45), channel_id=1, source_target_pairs={{0,2},{2,0},{1,3},{3,1},{4,6},{6,4},{5,7},{7,5},{8,10},{10,8},{9,1... | collective-permute-start | bytes 983048 | tf_op jit(solution)/shard_map/ppermute | solution.py:29
  66.1 6.0 %collective-permute-done.16.got_ref = bf16[1024,256]{1,0:T(8,128)(2,1)S(1)} collective-permute-done((bf16[1024,256]{1,0:T(8,128)(2,1)S(1)}, bf16[1024,256]{1,0:T(8,128)(2,1)S(1)}, u32[]{:S(2)}, u32[]{:S(2)}) %collective-permute-start.16) | collective-permute-done | bytes 524320 | tf_op jit(solution)/shard_map/ppermute | solution.py:416
  73.0 3.6 %collective-permute-start.24 = (bf16[1024,256]{1,0:T(8,128)(2,1)S(1)}, bf16[1024,256]{1,0:T(8,128)(2,1)S(1)}, u32[]{:S(2)}, u32[]{:S(2)}) collective-permute-start(bf16[1024,256]{1,0:T(8,128)(2,1)S(1)} %panel.5), channel_id=1, source_target_pairs={{0,4},{4,0},{8,12},{12,8},{1,5},{5,1},{9,13},{13,9},{2,6},{6,2},{1... | collective-permute-start | bytes 1572872 | tf_op jit(solution)/shard_map/ppermute | solution.py:33
  76.8 2.1 %base.1.base_ref = f32[512,512]{1,0:T(8,128)S(1)} custom-call(s32[1]{0:T(128)} %bitcast.1.at_ref, s32[1]{0:T(128)} %bitcast.2.dp_ref, s32[1]{0:T(128)} %bitcast.core_ref, s32[1,6]{1,0:T(1,128)S(1)} %copy-done.5, s32[6]{0:T(128)S(1)} %copy-done.7, bf16[512,2688]{1,0:T(8,128)(2,1)S(1)} %pack.1.x_ref.own_ref, bf16[8192,512]{1,0:T(8,128)(2,1)S(1)} %bitcast.7, ...), custom_call_target="tpu_custom_call" | custom-call | flops 1 | bytes 1 | tf_op jit(solution)/shard_map/base/pallas_call | solution.py:271
  80.1 6.4 %collective-permute-done.24.refs_1_ = bf16[1024,256]{1,0:T(8,128)(2,1)S(1)} collective-permute-done((bf16[1024,256]{1,0:T(8,128)(2,1)S(1)}, bf16[1024,256]{1,0:T(8,128)(2,1)S(1)}, u32[]{:S(2)}, u32[]{:S(2)}) %collective-permute-start.24) | collective-permute-done | bytes 524320 | tf_op jit(solution)/shard_map/ppermute | solution.py:33
  86.7 1.9 %collective-permute-done.25.refs_3_ = f32[512,256]{1,0:T(8,128)S(1)} collective-permute-done((f32[512,256]{1,0:T(8,128)S(1)}, f32[512,256]{1,0:T(8,128)S(1)}, u32[]{:S(2)}, u32[]{:S(2)}) %collective-permute-start.25) | collective-permute-done | bytes 524320 | tf_op jit(solution)/shard_map/ppermute | solution.py:33
  88.6 2.1 %finish.1 = bf16[768,512]{1,0:T(8,128)(2,1)} custom-call(s32[1]{0:T(128)} %bitcast.core_ref, s32[1,6]{1,0:T(1,128)S(1)} %copy-done.5, f32[512,512]{1,0:T(8,128)S(1)} %base.1.base_ref, bf16[1024,256]{1,0:T(8,128)(2,1)S(1)} %collective-permute-done.17.refs_0_, bf16[1024,256]{1,0:T(8,128)(2,1)S(1)} %collective-permute-done.24.refs_1_, ...), custom_call_target="tpu_custom_call" | custom-call | flops 1 | bytes 1 | tf_op jit(solution)/shard_map/finish/pallas_call | solution.py:352
  (68 shorter events, 20.7 us)
Async XLA Ops:
  1.6 17.2 %collective-permute-start = (bf16[512,256]{1,0:T(8,128)(2,1)S(1)}, bf16[512,256]{1,0:T(8,128)(2,1)S(1)}, u32[]{:S(2)}, u32[]{:S(2)}) collective-permute-start(bf16[512,256]{1,0:T(8,128)(2,1)S(1)} %dynamic_slice.9), channel_id=1, source_target_pairs={{0,12},{4,8},{8,4},{12,0},{1,13},{5,9},{9,5},{13,1},{2,14},{6,10},... | collective-permute-start | bytes 786440 | tf_op jit(solution)/shard_map/ppermute | solution.py:33
  8.5 10.3 %collective-permute-start.1 = (bf16[32,2560]{1,0:T(8,128)(2,1)}, bf16[32,2560]{1,0:T(8,128)(2,1)S(1)}, u32[]{:S(2)}, u32[]{:S(2)}) collective-permute-start(bf16[32,2560]{1,0:T(8,128)(2,1)} %get-tuple-element.30), channel_id=1, source_target_pairs={{0,2},{2,0},{1,3},{3,1},{4,6},{6,4},{5,7},{7,5},{8,10},{10,8},{9,1... | collective-permute-start | bytes 491528 | tf_op jit(solution)/shard_map/ppermute | solution.py:29
  10.0 8.8 %collective-permute-start.2 = (bf16[32,2560]{1,0:T(8,128)(2,1)}, bf16[32,2560]{1,0:T(8,128)(2,1)S(1)}, u32[]{:S(2)}, u32[]{:S(2)}) collective-permute-start(bf16[32,2560]{1,0:T(8,128)(2,1)} %get-tuple-element.31), channel_id=1, source_target_pairs={{0,2},{2,0},{1,3},{3,1},{4,6},{6,4},{5,7},{7,5},{8,10},{10,8},{9,1... | collective-permute-start | bytes 491528 | tf_op jit(solution)/shard_map/ppermute | solution.py:29
  18.9 5.2 %collective-permute-start.3 = (bf16[512,2688]{1,0:T(8,128)(2,1)S(1)}, bf16[512,2688]{1,0:T(8,128)(2,1)S(1)}, u32[]{:S(2)}, u32[]{:S(2)}) collective-permute-start(bf16[512,2688]{1,0:T(8,128)(2,1)S(1)} %pack.1.x_ref.own_ref), channel_id=1, source_target_pairs={{0,1},{1,0},{2,3},{3,2},{4,5},{5,4},{6,7},{7,6},{8,9},{9,8},{10,11... | collective-permute-start | bytes 8257544 | tf_op jit(solution)/shard_map/ppermute | solution.py:33
  19.0 6.6 %collective-permute-start.4 = (bf16[64,2560]{1,0:T(8,128)(2,1)S(1)}, bf16[64,2560]{1,0:T(8,128)(2,1)S(1)}, u32[]{:S(2)}, u32[]{:S(2)}) collective-permute-start(bf16[64,2560]{1,0:T(8,128)(2,1)S(1)} %constant_dynamic-update-slice_fusion.refs_0_), channel_id=1, source_target_pairs={{0,1},{1,0},{2,3},{3,2},{4,5},{5,4},{6,7},{7,6},{8,9},{9,8},{10,11... | collective-permute-start | bytes 983048 | tf_op jit(solution)/shard_map/ppermute | solution.py:33
  19.5 13.8 %collective-permute-start.5 = (bf16[512,256]{1,0:T(8,128)(2,1)S(1)}, bf16[512,256]{1,0:T(8,128)(2,1)S(1)}, u32[]{:S(2)}, u32[]{:S(2)}) collective-permute-start(bf16[512,256]{1,0:T(8,128)(2,1)S(1)} %get-tuple-element.34), channel_id=1, source_target_pairs={{0,8},{4,12},{8,0},{12,4},{1,9},{5,13},{9,1},{13,5},{2,10},{6,14},... | collective-permute-start | bytes 786440 | tf_op jit(solution)/shard_map/ppermute | solution.py:33
  20.0 15.3 %collective-permute-start.10 = (bf16[512,256]{1,0:T(8,128)(2,1)S(1)}, bf16[512,256]{1,0:T(8,128)(2,1)S(1)}, u32[]{:S(2)}, u32[]{:S(2)}) collective-permute-start(bf16[512,256]{1,0:T(8,128)(2,1)S(1)} %collective-permute-done.refs_0_), channel_id=1, source_target_pairs={{0,18},{2,16},{16,2},{18,0},{1,19},{3,17},{17,3},{19,1},{4,22},{6,... | collective-permute-start | bytes 786440 | tf_op jit(solution)/shard_map/ppermute | solution.py:33
  22.5 12.9 %collective-permute-start.8 = (bf16[512,256]{1,0:T(8,128)(2,1)S(1)}, bf16[512,256]{1,0:T(8,128)(2,1)S(1)}, u32[]{:S(2)}, u32[]{:S(2)}) collective-permute-start(bf16[512,256]{1,0:T(8,128)(2,1)S(1)} %collective-permute-done.refs_0_), channel_id=1, source_target_pairs={{0,2},{2,0},{16,18},{18,16},{1,3},{3,1},{17,19},{19,17},{4,6},{6,4... | collective-permute-start | bytes 786440 | tf_op jit(solution)/shard_map/ppermute | solution.py:33
  24.0 11.3 %collective-permute-start.9 = (bf16[512,256]{1,0:T(8,128)(2,1)S(1)}, bf16[512,256]{1,0:T(8,128)(2,1)S(1)}, u32[]{:S(2)}, u32[]{:S(2)}) collective-permute-start(bf16[512,256]{1,0:T(8,128)(2,1)S(1)} %collective-permute-done.refs_0_), channel_id=1, source_target_pairs={{0,16},{2,18},{16,0},{18,2},{1,17},{3,19},{17,1},{19,3},{4,20},{6,... | collective-permute-start | bytes 786440 | tf_op jit(solution)/shard_map/ppermute | solution.py:33
  33.3 6.8 %collective-permute-start.6 = (bf16[512,128]{1,0:T(8,128)(2,1)S(1)}, bf16[512,128]{1,0:T(8,128)(2,1)S(1)}, u32[]{:S(2)}, u32[]{:S(2)}) collective-permute-start(bf16[512,128]{1,0:T(8,128)(2,1)S(1)} %low_part.1), channel_id=1, source_target_pairs={{0,4},{4,0},{8,12},{12,8},{1,5},{5,1},{9,13},{13,9},{2,6},{6,2},{1... | collective-permute-start | bytes 393224 | tf_op jit(solution)/shard_map/ppermute | solution.py:33
  33.3 11.0 %collective-permute-start.11 = (bf16[512,256]{1,0:T(8,128)(2,1)S(1)}, bf16[512,256]{1,0:T(8,128)(2,1)S(1)}, u32[]{:S(2)}, u32[]{:S(2)}) collective-permute-start(bf16[512,256]{1,0:T(8,128)(2,1)S(1)} %get-tuple-element.38), channel_id=1, source_target_pairs={{0,4},{4,0},{8,12},{12,8},{1,5},{5,1},{9,13},{13,9},{2,6},{6,2},{1... | collective-permute-start | bytes 786440 | tf_op jit(solution)/shard_map/ppermute | solution.py:33
  35.4 9.3 %collective-permute-start.12 = (bf16[512,256]{1,0:T(8,128)(2,1)S(1)}, bf16[512,256]{1,0:T(8,128)(2,1)S(1)}, u32[]{:S(2)}, u32[]{:S(2)}) collective-permute-start(bf16[512,256]{1,0:T(8,128)(2,1)S(1)} %collective-permute-done.5.refs_0_), channel_id=1, source_target_pairs={{0,2},{2,0},{16,18},{18,16},{1,3},{3,1},{17,19},{19,17},{4,6},{6,4... | collective-permute-start | bytes 786440 | tf_op jit(solution)/shard_map/ppermute | solution.py:33
  36.9 13.0 %collective-permute-start.13 = (bf16[512,256]{1,0:T(8,128)(2,1)S(1)}, bf16[512,256]{1,0:T(8,128)(2,1)S(1)}, u32[]{:S(2)}, u32[]{:S(2)}) collective-permute-start(bf16[512,256]{1,0:T(8,128)(2,1)S(1)} %collective-permute-done.5.refs_0_), channel_id=1, source_target_pairs={{0,16},{2,18},{16,0},{18,2},{1,17},{3,19},{17,1},{19,3},{4,20},{6,... | collective-permute-start | bytes 786440 | tf_op jit(solution)/shard_map/ppermute | solution.py:33
  38.4 11.5 %collective-permute-start.14 = (bf16[512,256]{1,0:T(8,128)(2,1)S(1)}, bf16[512,256]{1,0:T(8,128)(2,1)S(1)}, u32[]{:S(2)}, u32[]{:S(2)}) collective-permute-start(bf16[512,256]{1,0:T(8,128)(2,1)S(1)} %collective-permute-done.5.refs_0_), channel_id=1, source_target_pairs={{0,18},{2,16},{16,2},{18,0},{1,19},{3,17},{17,3},{19,1},{4,22},{6,... | collective-permute-start | bytes 786440 | tf_op jit(solution)/shard_map/ppermute | solution.py:33
  40.2 16.1 %collective-permute-start.15 = (bf16[1024,256]{1,0:T(8,128)(2,1)S(1)}, bf16[1024,256]{1,0:T(8,128)(2,1)S(1)}, u32[]{:S(2)}, u32[]{:S(2)}) collective-permute-start(bf16[1024,256]{1,0:T(8,128)(2,1)S(1)} %panel.3.own_ref), channel_id=1, source_target_pairs={{0,4},{12,8},{1,5},{13,9},{2,6},{14,10},{3,7},{15,11},{16,20},{28,... | collective-permute-start | bytes 1572872 | tf_op jit(solution)/shard_map/ppermute | solution.py:411
  44.4 11.8 %collective-permute-start.7 = (bf16[512,128]{1,0:T(8,128)(2,1)S(1)}, bf16[512,128]{1,0:T(8,128)(2,1)S(1)}, u32[]{:S(2)}, u32[]{:S(2)}) collective-permute-start(bf16[512,128]{1,0:T(8,128)(2,1)S(1)} %add_convert_fusion.2), channel_id=1, source_target_pairs={{0,8},{4,12},{8,0},{12,4},{1,9},{5,13},{9,1},{13,5},{2,10},{6,14},... | collective-permute-start | bytes 393224 | tf_op jit(solution)/shard_map/ppermute | solution.py:33
  49.9 13.3 %collective-permute-start.19 = (bf16[512,256]{1,0:T(8,128)(2,1)S(1)}, bf16[512,256]{1,0:T(8,128)(2,1)S(1)}, u32[]{:S(2)}, u32[]{:S(2)}) collective-permute-start(bf16[512,256]{1,0:T(8,128)(2,1)S(1)} %collective-permute-done.11.refs_0_), channel_id=1, source_target_pairs={{0,2},{2,0},{16,18},{18,16},{1,3},{3,1},{17,19},{19,17},{4,6},{6,4... | collective-permute-start | bytes 786440 | tf_op jit(solution)/shard_map/ppermute | solution.py:33
  51.2 12.1 %collective-permute-start.20 = (bf16[512,256]{1,0:T(8,128)(2,1)S(1)}, bf16[512,256]{1,0:T(8,128)(2,1)S(1)}, u32[]{:S(2)}, u32[]{:S(2)}) collective-permute-start(bf16[512,256]{1,0:T(8,128)(2,1)S(1)} %collective-permute-done.11.refs_0_), channel_id=1, source_target_pairs={{0,16},{2,18},{16,0},{18,2},{1,17},{3,19},{17,1},{19,3},{4,20},{6,... | collective-permute-start | bytes 786440 | tf_op jit(solution)/shard_map/ppermute | solution.py:33
  52.0 11.3 %collective-permute-start.21 = (bf16[512,256]{1,0:T(8,128)(2,1)S(1)}, bf16[512,256]{1,0:T(8,128)(2,1)S(1)}, u32[]{:S(2)}, u32[]{:S(2)}) collective-permute-start(bf16[512,256]{1,0:T(8,128)(2,1)S(1)} %collective-permute-done.11.refs_0_), channel_id=1, source_target_pairs={{0,18},{2,16},{16,2},{18,0},{1,19},{3,17},{17,3},{19,1},{4,22},{6,... | collective-permute-start | bytes 786440 | tf_op jit(solution)/shard_map/ppermute | solution.py:33
  57.5 14.6 %collective-permute-start.16 = (bf16[1024,256]{1,0:T(8,128)(2,1)S(1)}, bf16[1024,256]{1,0:T(8,128)(2,1)S(1)}, u32[]{:S(2)}, u32[]{:S(2)}) collective-permute-start(bf16[1024,256]{1,0:T(8,128)(2,1)S(1)} %panel.4), channel_id=1, source_target_pairs={{0,4},{12,8},{4,12},{8,0},{1,5},{13,9},{5,13},{9,1},{2,6},{14,10},... | collective-permute-start | bytes 1572872 | tf_op jit(solution)/shard_map/ppermute | solution.py:416
  63.3 13.3 %collective-permute-start.22 = (bf16[64,2560]{1,0:T(8,128)(2,1)S(1)}, bf16[64,2560]{1,0:T(8,128)(2,1)S(1)}, u32[]{:S(2)}, u32[]{:S(2)}) collective-permute-start(bf16[64,2560]{1,0:T(8,128)(2,1)S(1)} %get-tuple-element.45), channel_id=1, source_target_pairs={{0,2},{2,0},{1,3},{3,1},{4,6},{6,4},{5,7},{7,5},{8,10},{10,8},{9,1... | collective-permute-start | bytes 983048 | tf_op jit(solution)/shard_map/ppermute | solution.py:29
  72.3 7.8 %collective-permute-start.17 = (bf16[1024,256]{1,0:T(8,128)(2,1)S(1)}, bf16[1024,256]{1,0:T(8,128)(2,1)S(1)}, u32[]{:S(2)}, u32[]{:S(2)}) collective-permute-start(bf16[1024,256]{1,0:T(8,128)(2,1)S(1)} %get-tuple-element.41), channel_id=1, source_target_pairs={{4,8},{8,4},{5,9},{9,5},{6,10},{10,6},{7,11},{11,7},{20,24},{24,20... | collective-permute-start | bytes 1572872 | tf_op jit(solution)/shard_map/ppermute | solution.py:421
  73.0 13.5 %collective-permute-start.24 = (bf16[1024,256]{1,0:T(8,128)(2,1)S(1)}, bf16[1024,256]{1,0:T(8,128)(2,1)S(1)}, u32[]{:S(2)}, u32[]{:S(2)}) collective-permute-start(bf16[1024,256]{1,0:T(8,128)(2,1)S(1)} %panel.5), channel_id=1, source_target_pairs={{0,4},{4,0},{8,12},{12,8},{1,5},{5,1},{9,13},{13,9},{2,6},{6,2},{1... | collective-permute-start | bytes 1572872 | tf_op jit(solution)/shard_map/ppermute | solution.py:33
  76.7 2.3 %collective-permute-start.23 = (bf16[64,2560]{1,0:T(8,128)(2,1)S(1)}, bf16[64,2560]{1,0:T(8,128)(2,1)S(1)}, u32[]{:S(2)}, u32[]{:S(2)}) collective-permute-start(bf16[64,2560]{1,0:T(8,128)(2,1)S(1)} %add_convert_fusion.own_ref), channel_id=1, source_target_pairs={{0,1},{1,0},{2,3},{3,2},{4,5},{5,4},{6,7},{7,6},{8,9},{9,8},{10,11... | collective-permute-start | bytes 983048 | tf_op jit(solution)/shard_map/ppermute | solution.py:33
  (12 other events, 81.8 us)

commit v13 on v11

--- a/solution.py
+++ b/solution.py
@@ -196,9 +196,7 @@
 
 def panel_kernel(order, count, place_ref, x_ref, other_ref, *refs):
     pieces, refs = refs[:count], refs[count:]
-    half = refs[-1].shape[1]
-    panels = pieces[0].shape[1] // half
-    adds, outs = refs[:-panels], refs[-panels:]
+    half = refs[0].shape[1]
     deep = pieces[0].shape[0]
     for n, source in enumerate((x_ref, other_ref)):
         total = None
@@ -206,25 +204,22 @@
             col = pl.multiple_of((place_ref[0] ^ m) * deep, min(deep, 128))
             term = dot(source[:, pl.ds(col, deep)], piece[...])
             total = term if total is None else total + term
-        for i, out in enumerate(outs):
-            value = total[:, i * half : (i + 1) * half]
-            if i < len(adds):
-                value = value + adds[i][n * LIVE : (n + 1) * LIVE, :].astype(F32)
-            out[n * LIVE : (n + 1) * LIVE, :] = value.astype(BF16)
-
-
-def panel_product(order, place, x, x_other, pieces, half, adds=()):
+        for i, out in enumerate(refs):
+            out[n * LIVE : (n + 1) * LIVE, :] = total[:, i * half : (i + 1) * half].astype(out.dtype)
+
+
+def panel_product(order, place, x, x_other, pieces, half, dtype=BF16):
     feat, wide = len(pieces) * pieces[0].shape[0], pieces[0].shape[1]
-    shapes = [shaped((2 * LIVE, half), BF16)] * (wide // half)
+    shapes = [shaped((2 * LIVE, half), dtype)] * (wide // half)
     return pl.pallas_call(
         functools.partial(panel_kernel, order, len(pieces)),
-        in_specs=[SMEM] + [VMEM] * (2 + len(pieces) + len(adds)),
+        in_specs=[SMEM] + [VMEM] * (2 + len(pieces)),
         out_specs=[VMEM] * len(shapes),
         out_shape=shapes,
         compiler_params=params(24),
-        cost_estimate=cost(4 * LIVE * feat * wide, 4 * LIVE * feat + 2 * feat * wide),
+        cost_estimate=pl.CostEstimate(flops=1, bytes_accessed=1, transcendentals=0),
         name="panel",
-    )(place, x, x_other, *pieces, *adds)
+    )(place, x, x_other, *pieces)
 
 
 def settle_kernel(core_ref, own_ref, got_ref, down_ref, up_ref):
@@ -286,23 +281,45 @@
     )(at, dp, core, fill, tenant, x, base_weight, low, b, *halves)
 
 
-def relay_kernel(at_ref, own_ref, got_ref, passed_ref, kept_ref):
+def join_kernel(own_ref, far_ref, low_ref, out_ref):
+    out_ref[: 2 * LIVE, :] = (own_ref[...] + far_ref[...].astype(F32)).astype(BF16)
+    lanes, rows = low_ref.shape[1], LIVE // 2
+    out_ref[2 * LIVE :, :lanes] = low_ref[:rows, :]
+    out_ref[2 * LIVE :, lanes:] = low_ref[rows:, :]
+
+
+def join(own, far, low):
+    return pl.pallas_call(
+        join_kernel,
+        in_specs=[VMEM] * 3,
+        out_specs=VMEM,
+        out_shape=shaped((2 * LIVE + LIVE // 2, own.shape[1]), BF16),
+        compiler_params=params(24),
+        cost_estimate=cost(own.size, 8 * own.size),
+        name="join",
+    )(own, far, low)
+
+
+def relay_kernel(at_ref, own_ref, got_ref, low_ref, passed_ref, kept_ref, low_out_ref):
     inner = (at_ref[0] == 1) | (at_ref[0] == 2)
-    got = got_ref[...].astype(F32)
+    got = got_ref[: 2 * LIVE, :].astype(F32)
     passed_ref[...] = (own_ref[...].astype(F32) + got).astype(BF16)
     kept_ref[...] = jnp.where(inner, 0.0, got).astype(BF16)
-
-
-def relay(at, own, got):
+    lanes, rows = low_ref.shape[1], LIVE // 2
+    low_out_ref[:rows, :] = jnp.where(inner, low_ref[:rows, :], got_ref[2 * LIVE :, :lanes])
+    low_out_ref[rows:, :] = jnp.where(inner, low_ref[rows:, :], got_ref[2 * LIVE :, lanes:])
+
+
+def relay(at, own, got, low):
     return pl.pallas_call(
         relay_kernel,
-        in_specs=[SMEM] + [VMEM] * 2,
-        out_specs=[VMEM] * 2,
-        out_shape=[shaped(own.shape, BF16)] * 2,
+        in_specs=[SMEM] + [VMEM] * 3,
+        out_specs=[VMEM] * 3,
+        out_shape=[shaped(own.shape, BF16)] * 2 + [shaped(low.shape, BF16)],
         compiler_params=params(24),
         cost_estimate=cost(2 * own.size, 8 * own.size),
         name="relay",
-    )(at, own, got)
+    )(at, own, got, low)
 
 
 def swap_kernel(*refs):
@@ -395,7 +412,7 @@
     def add_flipped(low, mask, *before):
         return (low.astype(F32) + flip(after(low, *before), "tensor", n_t, mask).astype(F32)).astype(BF16)
 
-    if n_t == 4:
+    if n_t == 4 and half == 4 * rank:
         share_3 = share(me_t ^ 3)
         weight = {3: flip(share_3, "tensor", n_t, 3)}
         weight[2] = flip(after(share(me_t ^ 2), weight[3]), "tensor", n_t, 2)
@@ -410,13 +427,13 @@
         far = lax.ppermute(y_3, "tensor", [(0, 1), (3, 2)])
         pieces, order = gathered(after(weight[2], *pieces))
         pieces[0] = after(pieces[0], weight[1])
-        (y_2,) = panel_product(order, panel_at, x, x_other, pieces, half, adds=[far])
-        low = add_flipped(low, 2)
-        near = lax.ppermute(after(y_2, low), "tensor", [(0, 1), (3, 2), (1, 3), (2, 0)])
+        low = (low.astype(F32) + lax.ppermute(low, "tensor", [(1, 2), (2, 1)]).astype(F32)).astype(BF16)
+        (y_2,) = panel_product(order, panel_at, x, x_other, pieces, half, F32)
+        near = lax.ppermute(join(y_2, far, low), "tensor", [(0, 1), (3, 2), (1, 3), (2, 0)])
         pieces, order = gathered(after(weight[1], *pieces))
         (y_1,) = panel_product(order, panel_at, x, x_other, pieces, half)
         part_1 = flip(y_1, "tensor", n_t, 1)
-        passed, kept = relay(at, y_3, near)
+        passed, kept, low = relay(at, y_3, near, low)
         parts = [lax.ppermute(passed, "tensor", [(1, 2), (2, 1)]), part_1, kept]
     else:
         x = pack(block_fill, block_tenant_index, tokens, cotangent, blocks, 2 * rank)
@@ -441,7 +458,7 @@
     base = base_product(
         at, dp, core, block_fill, block_tenant_index, x, base_weight, low, own_b, halves, feat, blocks, rank
     )
-    parts[0] = after(parts[0], base, down_out)
+    parts[0] = after(parts[0], base)
     others = [flip(other_rows(parts), "pipe", n_pipe, 1)]
     out = finish(core, block_fill, base, parts, others, rows, blocks)
     return out, down_out, up_out

time: 88.8 us -> 93.3 us (1.051)
  starting transfers between devices: 29.7 us -> 34.4 us
    ppermute x20 -> x19, waiting for transfers between devices: 27.6 us -> 19.7 us  [flip(): return lax.ppermute(x, names, [(i, i ^ mask) for i in range(count)])]
    ppermute x1 -> x2, waiting for transfers between devices: 6.3 us -> 10.6 us  [the longest x1 10.6 us: body(): lax.ppermute(join(y_2, far, low), 'tensor', [(0, 1), (3, 2), (1, 3), (2,...]
    ppermute x20 -> x19, starting transfers between devices: 22.5 us -> 24.8 us  [flip(): return lax.ppermute(x, names, [(i, i ^ mask) for i in range(count)])]
    ppermute x1, waiting for transfers between devices: 0.01 us -> 2.16 us  [body(): far = lax.ppermute(y_3, 'tensor', [(0, 1), (3, 2)])]
    ppermute x3, waiting for transfers between devices: 0.17 us -> 2.01 us  [shift(): lax.ppermute(x, name, [(i, (i + step) % count) for i in range(count)])]
    ppermute x1 -> x2, starting transfers between devices: 1.8 us -> 3.19 us  [the longest x1 2.53 us: body(): lax.ppermute(join(y_2, far, low), 'tensor', [(0, 1), (3, 2), (1, 3), (2,...]
  transfers between devices with their start and end apart: 26 -> 26, of which waited for: 11 -> 10; matrix products, arithmetic and copies ran while one was open for 0% -> 0% of each run, Pallas kernels for 17% -> 16%
where the time goes in v13:
time: 93.3 us; the launch traced here: 93 us
  waiting for transfers between devices  34.5 us (37%)
  starting transfers between devices  34.4 us (37%)
  Pallas kernels  17.5 us (19%)
  local copies, waits for them, and re-layouts  5.56 us (6%)
    ppermute x19, starting transfers between devices, flip(): return lax.ppermute(x, names, [(i, i ^ mask) for i in range(count)])  24.8 us
    ppermute x19, waiting for transfers between devices, flip(): return lax.ppermute(x, names, [(i, i ^ mask) for i in range(count)])  19.7 us
    ppermute x1, waiting for transfers between devices, body(): lax.ppermute(join(y_2, far, low), 'tensor', [(0, 1), (3, 2), (1, 3), (2,...  10.6 us
    unnamed x21, local copies, waits for them, and re-layouts  4.37 us
    pallas_call x3, Pallas kernels, panel_product(): pl.pallas_call(functools.partial(panel_kernel, order, len(pieces)), in_sp...  3.74 us
    ppermute x3, starting transfers between devices, shift(): lax.ppermute(x, name, [(i, (i + step) % count) for i in range(count)])  3.58 us
    pallas_call x1, Pallas kernels, pack(): pl.pallas_call(functools.partial(pack_kernel, blocks, rows // blocks), in...  2.82 us
    ppermute x1, starting transfers between devices, body(): lax.ppermute(join(y_2, far, low), 'tensor', [(0, 1), (3, 2), (1, 3), (2,...  2.53 us
  transfers between devices with their start and end apart: 26, of which 10 were waited for; matrix products, arithmetic and copies ran while one was open for 0% of the time, Pallas kernels for 16%

profile of v13, /device:TPU:0, one launch (start us, length us, event | category | flops | bytes accessed | tf_op | source)
XLA Modules:
  0.0 93.0 jit_solution(13506412869491477060)
XLA Ops:
  1.8 5.1 %collective-permute-start = (bf16[512,256]{1,0:T(8,128)(2,1)S(1)}, bf16[512,256]{1,0:T(8,128)(2,1)S(1)}, u32[]{:S(2)}, u32[]{:S(2)}) collective-permute-start(bf16[512,256]{1,0:T(8,128)(2,1)S(1)} %get-tuple-element.47), channel_id=1, source_target_pairs={{0,12},{4,8},{8,4},{12,0},{1,13},{5,9},{9,5},{13,1},{2,14},{6,10},... | collective-permute-start | bytes 786440 | tf_op jit(solution)/shard_map/ppermute | solution.py:33
  6.9 1.8 %own_half.1 = (bf16[32,2560]{1,0:T(8,128)(2,1)}, bf16[32,2560]{1,0:T(8,128)(2,1)}) custom-call(s32[1]{0:T(128)} %bitcast.core_ref, bf16[128,2048]{1,0:T(8,128)(2,1)} %bitcast.8, bf16[128,512]{1,0:T(8,128)(2,1)} %bitcast.10), custom_call_target="tpu_custom_call" | custom-call | flops 1 | bytes 1 | tf_op jit(solution)/shard_map/own_half/pallas_call | solution.py:75
  10.8 1.9 %copy-done = bf16[768,2048]{1,0:T(8,128)(2,1)S(1)} copy-done((bf16[768,2048]{1,0:T(8,128)(2,1)S(1)}, bf16[768,2048]{1,0:T(8,128)(2,1)}, u32[]{:S(2)}) %copy-start) | copy-done | bytes 3145752
  15.1 2.8 %pack.1.x_ref.own_ref = bf16[512,2688]{1,0:T(8,128)(2,1)S(1)} custom-call(s32[1,6]{1,0:T(1,128)S(1)} %copy-done.4, s32[6]{0:T(128)S(1)} %copy-done.6, bf16[768,2048]{1,0:T(8,128)(2,1)S(1)} %copy-done, bf16[768,512]{1,0:T(8,128)(2,1)S(1)} %copy-done.3), custom_call_target="tpu_custom_call" | custom-call | flops 1 | bytes 1 | tf_op jit(solution)/shard_map/pack/pallas_call | solution.py:104
  21.7 1.5 %collective-permute-start.7 = (bf16[512,256]{1,0:T(8,128)(2,1)S(1)}, bf16[512,256]{1,0:T(8,128)(2,1)S(1)}, u32[]{:S(2)}, u32[]{:S(2)}) collective-permute-start(bf16[512,256]{1,0:T(8,128)(2,1)S(1)} %collective-permute-done.refs_0_), channel_id=1, source_target_pairs={{0,16},{2,18},{16,0},{18,2},{1,17},{3,19},{17,1},{19,3},{4,20},{6,... | collective-permute-start | bytes 786440 | tf_op jit(solution)/shard_map/ppermute | solution.py:33
  23.2 2.4 %collective-permute-start.8 = (bf16[512,256]{1,0:T(8,128)(2,1)S(1)}, bf16[512,256]{1,0:T(8,128)(2,1)S(1)}, u32[]{:S(2)}, u32[]{:S(2)}) collective-permute-start(bf16[512,256]{1,0:T(8,128)(2,1)S(1)} %collective-permute-done.refs_0_), channel_id=1, source_target_pairs={{0,18},{2,16},{16,2},{18,0},{1,19},{3,17},{17,3},{19,1},{4,22},{6,... | collective-permute-start | bytes 786440 | tf_op jit(solution)/shard_map/ppermute | solution.py:33
  25.7 2.2 %low_part.1 = bf16[512,128]{1,0:T(8,128)(2,1)S(1)} custom-call(s32[1]{0:T(128)} %bitcast.2.dp_ref, s32[1]{0:T(128)} %bitcast.core_ref, s32[1,6]{1,0:T(1,128)S(1)} %copy-done.4, s32[6]{0:T(128)S(1)} %copy-done.6, bf16[512,2688]{1,0:T(8,128)(2,1)S(1)} %pack.1.x_ref.own_ref, bf16[128,2048]{1,0:T(8,128)(2,1)S(1)} %bitcast.9, bf16[128,512]{1,0:T(8,128)(2,1)S(1)} %bitcast.11, ...), custom_call_target="tpu_custom_call" | custom-call | flops 1 | bytes 1 | tf_op jit(solution)/shard_map/low_part/pallas_call | solution.py:147
  27.9 5.6 %collective-permute-done.4.refs_0_ = bf16[512,256]{1,0:T(8,128)(2,1)S(1)} collective-permute-done((bf16[512,256]{1,0:T(8,128)(2,1)S(1)}, bf16[512,256]{1,0:T(8,128)(2,1)S(1)}, u32[]{:S(2)}, u32[]{:S(2)}) %collective-permute-start.4) | collective-permute-done | bytes 262176 | tf_op jit(solution)/shard_map/ppermute | solution.py:33
  33.4 2.0 %collective-permute-start.9 = (bf16[512,256]{1,0:T(8,128)(2,1)S(1)}, bf16[512,256]{1,0:T(8,128)(2,1)S(1)}, u32[]{:S(2)}, u32[]{:S(2)}) collective-permute-start(bf16[512,256]{1,0:T(8,128)(2,1)S(1)} %get-tuple-element.32), channel_id=1, source_target_pairs={{0,4},{4,0},{8,12},{12,8},{1,5},{5,1},{9,13},{13,9},{2,6},{6,2},{1... | collective-permute-start | bytes 786440 | tf_op jit(solution)/shard_map/ppermute | solution.py:33
  35.5 1.6 %collective-permute-start.10 = (bf16[512,256]{1,0:T(8,128)(2,1)S(1)}, bf16[512,256]{1,0:T(8,128)(2,1)S(1)}, u32[]{:S(2)}, u32[]{:S(2)}) collective-permute-start(bf16[512,256]{1,0:T(8,128)(2,1)S(1)} %collective-permute-done.4.refs_0_), channel_id=1, source_target_pairs={{0,2},{2,0},{16,18},{18,16},{1,3},{3,1},{17,19},{19,17},{4,6},{6,4... | collective-permute-start | bytes 786440 | tf_op jit(solution)/shard_map/ppermute | solution.py:33
  37.0 1.5 %collective-permute-start.11 = (bf16[512,256]{1,0:T(8,128)(2,1)S(1)}, bf16[512,256]{1,0:T(8,128)(2,1)S(1)}, u32[]{:S(2)}, u32[]{:S(2)}) collective-permute-start(bf16[512,256]{1,0:T(8,128)(2,1)S(1)} %collective-permute-done.4.refs_0_), channel_id=1, source_target_pairs={{0,16},{2,18},{16,0},{18,2},{1,17},{3,19},{17,1},{19,3},{4,20},{6,... | collective-permute-start | bytes 786440 | tf_op jit(solution)/shard_map/ppermute | solution.py:33
  40.3 2.0 %collective-permute-start.13 = (bf16[1024,256]{1,0:T(8,128)(2,1)S(1)}, bf16[1024,256]{1,0:T(8,128)(2,1)S(1)}, u32[]{:S(2)}, u32[]{:S(2)}) collective-permute-start(bf16[1024,256]{1,0:T(8,128)(2,1)S(1)} %panel.3.own_ref), channel_id=1, source_target_pairs={{0,4},{12,8},{1,5},{13,9},{2,6},{14,10},{3,7},{15,11},{16,20},{28,... | collective-permute-start | bytes 1572872 | tf_op jit(solution)/shard_map/ppermute | solution.py:427
  42.3 2.2 %collective-permute-done.9.refs_0_ = bf16[512,256]{1,0:T(8,128)(2,1)S(1)} collective-permute-done((bf16[512,256]{1,0:T(8,128)(2,1)S(1)}, bf16[512,256]{1,0:T(8,128)(2,1)S(1)}, u32[]{:S(2)}, u32[]{:S(2)}) %collective-permute-start.9) | collective-permute-done | bytes 262176 | tf_op jit(solution)/shard_map/ppermute | solution.py:33
  45.2 4.9 %collective-permute-done.11.refs_2_ = bf16[512,256]{1,0:T(8,128)(2,1)S(1)} collective-permute-done((bf16[512,256]{1,0:T(8,128)(2,1)S(1)}, bf16[512,256]{1,0:T(8,128)(2,1)S(1)}, u32[]{:S(2)}, u32[]{:S(2)}) %collective-permute-start.11) | collective-permute-done | bytes 262176 | tf_op jit(solution)/shard_map/ppermute | solution.py:33
  51.4 2.2 %collective-permute-done.13.far_ref = bf16[1024,256]{1,0:T(8,128)(2,1)S(1)} collective-permute-done((bf16[1024,256]{1,0:T(8,128)(2,1)S(1)}, bf16[1024,256]{1,0:T(8,128)(2,1)S(1)}, u32[]{:S(2)}, u32[]{:S(2)}) %collective-permute-start.13) | collective-permute-done | bytes 524320 | tf_op jit(solution)/shard_map/ppermute | solution.py:427
  53.6 2.5 %collective-permute-start.16 = (bf16[1280,256]{1,0:T(8,128)(2,1)S(1)}, bf16[1280,256]{1,0:T(8,128)(2,1)S(1)}, u32[]{:S(2)}, u32[]{:S(2)}) collective-permute-start(bf16[1280,256]{1,0:T(8,128)(2,1)S(1)} %join.1), channel_id=1, source_target_pairs={{0,4},{12,8},{4,12},{8,0},{1,5},{13,9},{5,13},{9,1},{2,6},{14,10},... | collective-permute-start | bytes 1966088 | tf_op jit(solution)/shard_map/ppermute | solution.py:432
  59.7 10.6 %collective-permute-done.16.got_ref = bf16[1280,256]{1,0:T(8,128)(2,1)S(1)} collective-permute-done((bf16[1280,256]{1,0:T(8,128)(2,1)S(1)}, bf16[1280,256]{1,0:T(8,128)(2,1)S(1)}, u32[]{:S(2)}, u32[]{:S(2)}) %collective-permute-start.16) | collective-permute-done | bytes 655392 | tf_op jit(solution)/shard_map/ppermute | solution.py:432
  72.7 3.0 %collective-permute-start.21 = (bf16[1024,256]{1,0:T(8,128)(2,1)S(1)}, bf16[1024,256]{1,0:T(8,128)(2,1)S(1)}, u32[]{:S(2)}, u32[]{:S(2)}) collective-permute-start(bf16[1024,256]{1,0:T(8,128)(2,1)S(1)} %panel.5), channel_id=1, source_target_pairs={{0,4},{4,0},{8,12},{12,8},{1,5},{5,1},{9,13},{13,9},{2,6},{6,2},{1... | collective-permute-start | bytes 1572872 | tf_op jit(solution)/shard_map/ppermute | solution.py:33
  78.0 1.6 %collective-permute-start.24 = (bf16[64,2560]{1,0:T(8,128)(2,1)S(1)}, bf16[64,2560]{1,0:T(8,128)(2,1)S(1)}, u32[]{:S(2)}, u32[]{:S(2)}) collective-permute-start(bf16[64,2560]{1,0:T(8,128)(2,1)S(1)} %get-tuple-element.42), channel_id=1, source_target_pairs={{0,2},{2,0},{1,3},{3,1},{4,6},{6,4},{5,7},{7,5},{8,10},{10,8},{9,1... | collective-permute-start | bytes 983048 | tf_op jit(solution)/shard_map/ppermute | solution.py:29
  79.6 2.1 %base.1.base_ref = f32[512,512]{1,0:T(8,128)S(1)} custom-call(s32[1]{0:T(128)} %bitcast.1.at_ref, s32[1]{0:T(128)} %bitcast.2.dp_ref, s32[1]{0:T(128)} %bitcast.core_ref, s32[1,6]{1,0:T(1,128)S(1)} %copy-done.5, s32[6]{0:T(128)S(1)} %copy-done.7, bf16[512,2688]{1,0:T(8,128)(2,1)S(1)} %pack.1.x_ref.own_ref, bf16[8192,512]{1,0:T(8,128)(2,1)S(1)} %bitcast.7, ...), custom_call_target="tpu_custom_call" | custom-call | flops 1 | bytes 1 | tf_op jit(solution)/shard_map/base/pallas_call | solution.py:266
  81.8 4.1 %collective-permute-done.21.refs_1_ = bf16[1024,256]{1,0:T(8,128)(2,1)S(1)} collective-permute-done((bf16[1024,256]{1,0:T(8,128)(2,1)S(1)}, bf16[1024,256]{1,0:T(8,128)(2,1)S(1)}, u32[]{:S(2)}, u32[]{:S(2)}) %collective-permute-start.21) | collective-permute-done | bytes 524320 | tf_op jit(solution)/shard_map/ppermute | solution.py:33
  86.0 1.8 %collective-permute-done.24 = bf16[64,2560]{1,0:T(8,128)(2,1)S(1)} collective-permute-done((bf16[64,2560]{1,0:T(8,128)(2,1)S(1)}, bf16[64,2560]{1,0:T(8,128)(2,1)S(1)}, u32[]{:S(2)}, u32[]{:S(2)}) %collective-permute-start.24) | collective-permute-done | bytes 327712 | tf_op jit(solution)/shard_map/ppermute | solution.py:29
  88.0 1.6 %collective-permute-done.25.got_ref = bf16[64,2560]{1,0:T(8,128)(2,1)S(1)} collective-permute-done((bf16[64,2560]{1,0:T(8,128)(2,1)S(1)}, bf16[64,2560]{1,0:T(8,128)(2,1)S(1)}, u32[]{:S(2)}, u32[]{:S(2)}) %collective-permute-start.25) | collective-permute-done | bytes 327712 | tf_op jit(solution)/shard_map/ppermute | solution.py:33
  90.8 2.2 %finish.1 = bf16[768,512]{1,0:T(8,128)(2,1)} custom-call(s32[1]{0:T(128)} %bitcast.core_ref, s32[1,6]{1,0:T(1,128)S(1)} %copy-done.5, f32[512,512]{1,0:T(8,128)S(1)} %base.1.base_ref, bf16[1024,256]{1,0:T(8,128)(2,1)S(1)} %collective-permute-done.17.refs_0_, bf16[1024,256]{1,0:T(8,128)(2,1)S(1)} %collective-permute-done.21.refs_1_, ...), custom_call_target="tpu_custom_call" | custom-call | flops 1 | bytes 1 | tf_op jit(solution)/shard_map/finish/pallas_call | solution.py:369
  (68 shorter events, 22.9 us)
Async XLA Ops:
  1.8 16.3 %collective-permute-start = (bf16[512,256]{1,0:T(8,128)(2,1)S(1)}, bf16[512,256]{1,0:T(8,128)(2,1)S(1)}, u32[]{:S(2)}, u32[]{:S(2)}) collective-permute-start(bf16[512,256]{1,0:T(8,128)(2,1)S(1)} %get-tuple-element.47), channel_id=1, source_target_pairs={{0,12},{4,8},{8,4},{12,0},{1,13},{5,9},{9,5},{13,1},{2,14},{6,10},... | collective-permute-start | bytes 786440 | tf_op jit(solution)/shard_map/ppermute | solution.py:33
  8.8 9.2 %collective-permute-start.1 = (bf16[32,2560]{1,0:T(8,128)(2,1)}, bf16[32,2560]{1,0:T(8,128)(2,1)S(1)}, u32[]{:S(2)}, u32[]{:S(2)}) collective-permute-start(bf16[32,2560]{1,0:T(8,128)(2,1)} %get-tuple-element.25), channel_id=1, source_target_pairs={{0,2},{2,0},{1,3},{3,1},{4,6},{6,4},{5,7},{7,5},{8,10},{10,8},{9,1... | collective-permute-start | bytes 491528 | tf_op jit(solution)/shard_map/ppermute | solution.py:29
  10.2 7.9 %collective-permute-start.2 = (bf16[32,2560]{1,0:T(8,128)(2,1)}, bf16[32,2560]{1,0:T(8,128)(2,1)S(1)}, u32[]{:S(2)}, u32[]{:S(2)}) collective-permute-start(bf16[32,2560]{1,0:T(8,128)(2,1)} %get-tuple-element.26), channel_id=1, source_target_pairs={{0,2},{2,0},{1,3},{3,1},{4,6},{6,4},{5,7},{7,5},{8,10},{10,8},{9,1... | collective-permute-start | bytes 491528 | tf_op jit(solution)/shard_map/ppermute | solution.py:29
  18.1 5.1 %collective-permute-start.3 = (bf16[512,2688]{1,0:T(8,128)(2,1)S(1)}, bf16[512,2688]{1,0:T(8,128)(2,1)S(1)}, u32[]{:S(2)}, u32[]{:S(2)}) collective-permute-start(bf16[512,2688]{1,0:T(8,128)(2,1)S(1)} %pack.1.x_ref.own_ref), channel_id=1, source_target_pairs={{0,1},{1,0},{2,3},{3,2},{4,5},{5,4},{6,7},{7,6},{8,9},{9,8},{10,11... | collective-permute-start | bytes 8257544 | tf_op jit(solution)/shard_map/ppermute | solution.py:33
  18.2 7.5 %collective-permute-start.5 = (bf16[64,2560]{1,0:T(8,128)(2,1)S(1)}, bf16[64,2560]{1,0:T(8,128)(2,1)S(1)}, u32[]{:S(2)}, u32[]{:S(2)}) collective-permute-start(bf16[64,2560]{1,0:T(8,128)(2,1)S(1)} %constant_dynamic-update-slice_fusion.refs_0_), channel_id=1, source_target_pairs={{0,1},{1,0},{2,3},{3,2},{4,5},{5,4},{6,7},{7,6},{8,9},{9,8},{10,11... | collective-permute-start | bytes 983048 | tf_op jit(solution)/shard_map/ppermute | solution.py:33
  18.7 14.7 %collective-permute-start.4 = (bf16[512,256]{1,0:T(8,128)(2,1)S(1)}, bf16[512,256]{1,0:T(8,128)(2,1)S(1)}, u32[]{:S(2)}, u32[]{:S(2)}) collective-permute-start(bf16[512,256]{1,0:T(8,128)(2,1)S(1)} %get-tuple-element.28), channel_id=1, source_target_pairs={{0,8},{4,12},{8,0},{12,4},{1,9},{5,13},{9,1},{13,5},{2,10},{6,14},... | collective-permute-start | bytes 786440 | tf_op jit(solution)/shard_map/ppermute | solution.py:33
  20.2 15.3 %collective-permute-start.6 = (bf16[512,256]{1,0:T(8,128)(2,1)S(1)}, bf16[512,256]{1,0:T(8,128)(2,1)S(1)}, u32[]{:S(2)}, u32[]{:S(2)}) collective-permute-start(bf16[512,256]{1,0:T(8,128)(2,1)S(1)} %collective-permute-done.refs_0_), channel_id=1, source_target_pairs={{0,2},{2,0},{16,18},{18,16},{1,3},{3,1},{17,19},{19,17},{4,6},{6,4... | collective-permute-start | bytes 786440 | tf_op jit(solution)/shard_map/ppermute | solution.py:33
  21.7 13.8 %collective-permute-start.7 = (bf16[512,256]{1,0:T(8,128)(2,1)S(1)}, bf16[512,256]{1,0:T(8,128)(2,1)S(1)}, u32[]{:S(2)}, u32[]{:S(2)}) collective-permute-start(bf16[512,256]{1,0:T(8,128)(2,1)S(1)} %collective-permute-done.refs_0_), channel_id=1, source_target_pairs={{0,16},{2,18},{16,0},{18,2},{1,17},{3,19},{17,1},{19,3},{4,20},{6,... | collective-permute-start | bytes 786440 | tf_op jit(solution)/shard_map/ppermute | solution.py:33
  23.2 12.2 %collective-permute-start.8 = (bf16[512,256]{1,0:T(8,128)(2,1)S(1)}, bf16[512,256]{1,0:T(8,128)(2,1)S(1)}, u32[]{:S(2)}, u32[]{:S(2)}) collective-permute-start(bf16[512,256]{1,0:T(8,128)(2,1)S(1)} %collective-permute-done.refs_0_), channel_id=1, source_target_pairs={{0,18},{2,16},{16,2},{18,0},{1,19},{3,17},{17,3},{19,1},{4,22},{6,... | collective-permute-start | bytes 786440 | tf_op jit(solution)/shard_map/ppermute | solution.py:33
  33.4 6.8 %collective-permute-start.14 = (bf16[512,128]{1,0:T(8,128)(2,1)S(1)}, bf16[512,128]{1,0:T(8,128)(2,1)S(1)}, u32[]{:S(2)}, u32[]{:S(2)}) collective-permute-start(bf16[512,128]{1,0:T(8,128)(2,1)S(1)} %low_part.1), channel_id=1, source_target_pairs={{0,4},{4,0},{8,12},{12,8},{1,5},{5,1},{9,13},{13,9},{2,6},{6,2},{1... | collective-permute-start | bytes 393224 | tf_op jit(solution)/shard_map/ppermute | solution.py:33
  33.4 11.0 %collective-permute-start.9 = (bf16[512,256]{1,0:T(8,128)(2,1)S(1)}, bf16[512,256]{1,0:T(8,128)(2,1)S(1)}, u32[]{:S(2)}, u32[]{:S(2)}) collective-permute-start(bf16[512,256]{1,0:T(8,128)(2,1)S(1)} %get-tuple-element.32), channel_id=1, source_target_pairs={{0,4},{4,0},{8,12},{12,8},{1,5},{5,1},{9,13},{13,9},{2,6},{6,2},{1... | collective-permute-start | bytes 786440 | tf_op jit(solution)/shard_map/ppermute | solution.py:33
  35.5 9.7 %collective-permute-start.10 = (bf16[512,256]{1,0:T(8,128)(2,1)S(1)}, bf16[512,256]{1,0:T(8,128)(2,1)S(1)}, u32[]{:S(2)}, u32[]{:S(2)}) collective-permute-start(bf16[512,256]{1,0:T(8,128)(2,1)S(1)} %collective-permute-done.4.refs_0_), channel_id=1, source_target_pairs={{0,2},{2,0},{16,18},{18,16},{1,3},{3,1},{17,19},{19,17},{4,6},{6,4... | collective-permute-start | bytes 786440 | tf_op jit(solution)/shard_map/ppermute | solution.py:33
  37.0 13.0 %collective-permute-start.11 = (bf16[512,256]{1,0:T(8,128)(2,1)S(1)}, bf16[512,256]{1,0:T(8,128)(2,1)S(1)}, u32[]{:S(2)}, u32[]{:S(2)}) collective-permute-start(bf16[512,256]{1,0:T(8,128)(2,1)S(1)} %collective-permute-done.4.refs_0_), channel_id=1, source_target_pairs={{0,16},{2,18},{16,0},{18,2},{1,17},{3,19},{17,1},{19,3},{4,20},{6,... | collective-permute-start | bytes 786440 | tf_op jit(solution)/shard_map/ppermute | solution.py:33
  38.6 11.5 %collective-permute-start.12 = (bf16[512,256]{1,0:T(8,128)(2,1)S(1)}, bf16[512,256]{1,0:T(8,128)(2,1)S(1)}, u32[]{:S(2)}, u32[]{:S(2)}) collective-permute-start(bf16[512,256]{1,0:T(8,128)(2,1)S(1)} %collective-permute-done.4.refs_0_), channel_id=1, source_target_pairs={{0,18},{2,16},{16,2},{18,0},{1,19},{3,17},{17,3},{19,1},{4,22},{6,... | collective-permute-start | bytes 786440 | tf_op jit(solution)/shard_map/ppermute | solution.py:33
  40.3 13.2 %collective-permute-start.13 = (bf16[1024,256]{1,0:T(8,128)(2,1)S(1)}, bf16[1024,256]{1,0:T(8,128)(2,1)S(1)}, u32[]{:S(2)}, u32[]{:S(2)}) collective-permute-start(bf16[1024,256]{1,0:T(8,128)(2,1)S(1)} %panel.3.own_ref), channel_id=1, source_target_pairs={{0,4},{12,8},{1,5},{13,9},{2,6},{14,10},{3,7},{15,11},{16,20},{28,... | collective-permute-start | bytes 1572872 | tf_op jit(solution)/shard_map/ppermute | solution.py:427
  44.5 6.8 %collective-permute-start.15 = (bf16[512,128]{1,0:T(8,128)(2,1)S(1)}, bf16[512,128]{1,0:T(8,128)(2,1)S(1)}, u32[]{:S(2)}, u32[]{:S(2)}) collective-permute-start(bf16[512,128]{1,0:T(8,128)(2,1)S(1)} %add_convert_fusion.2), channel_id=1, source_target_pairs={{4,8},{8,4},{5,9},{9,5},{6,10},{10,6},{7,11},{11,7},{20,24},{24,20... | collective-permute-start | bytes 393224 | tf_op jit(solution)/shard_map/ppermute | solution.py:430
  53.6 16.6 %collective-permute-start.16 = (bf16[1280,256]{1,0:T(8,128)(2,1)S(1)}, bf16[1280,256]{1,0:T(8,128)(2,1)S(1)}, u32[]{:S(2)}, u32[]{:S(2)}) collective-permute-start(bf16[1280,256]{1,0:T(8,128)(2,1)S(1)} %join.1), channel_id=1, source_target_pairs={{0,4},{12,8},{4,12},{8,0},{1,5},{13,9},{5,13},{9,1},{2,6},{14,10},... | collective-permute-start | bytes 1966088 | tf_op jit(solution)/shard_map/ppermute | solution.py:432
  56.2 15.2 %collective-permute-start.18 = (bf16[512,256]{1,0:T(8,128)(2,1)S(1)}, bf16[512,256]{1,0:T(8,128)(2,1)S(1)}, u32[]{:S(2)}, u32[]{:S(2)}) collective-permute-start(bf16[512,256]{1,0:T(8,128)(2,1)S(1)} %collective-permute-done.9.refs_0_), channel_id=1, source_target_pairs={{0,2},{2,0},{16,18},{18,16},{1,3},{3,1},{17,19},{19,17},{4,6},{6,4... | collective-permute-start | bytes 786440 | tf_op jit(solution)/shard_map/ppermute | solution.py:33
  57.7 13.7 %collective-permute-start.19 = (bf16[512,256]{1,0:T(8,128)(2,1)S(1)}, bf16[512,256]{1,0:T(8,128)(2,1)S(1)}, u32[]{:S(2)}, u32[]{:S(2)}) collective-permute-start(bf16[512,256]{1,0:T(8,128)(2,1)S(1)} %collective-permute-done.9.refs_0_), channel_id=1, source_target_pairs={{0,16},{2,18},{16,0},{18,2},{1,17},{3,19},{17,1},{19,3},{4,20},{6,... | collective-permute-start | bytes 786440 | tf_op jit(solution)/shard_map/ppermute | solution.py:33
  59.2 12.2 %collective-permute-start.20 = (bf16[512,256]{1,0:T(8,128)(2,1)S(1)}, bf16[512,256]{1,0:T(8,128)(2,1)S(1)}, u32[]{:S(2)}, u32[]{:S(2)}) collective-permute-start(bf16[512,256]{1,0:T(8,128)(2,1)S(1)} %collective-permute-done.9.refs_0_), channel_id=1, source_target_pairs={{0,18},{2,16},{16,2},{18,0},{1,19},{3,17},{17,3},{19,1},{4,22},{6,... | collective-permute-start | bytes 786440 | tf_op jit(solution)/shard_map/ppermute | solution.py:33
  70.5 11.2 %collective-permute-start.17 = (bf16[1024,256]{1,0:T(8,128)(2,1)S(1)}, bf16[1024,256]{1,0:T(8,128)(2,1)S(1)}, u32[]{:S(2)}, u32[]{:S(2)}) collective-permute-start(bf16[1024,256]{1,0:T(8,128)(2,1)S(1)} %get-tuple-element.36), channel_id=1, source_target_pairs={{4,8},{8,4},{5,9},{9,5},{6,10},{10,6},{7,11},{11,7},{20,24},{24,20... | collective-permute-start | bytes 1572872 | tf_op jit(solution)/shard_map/ppermute | solution.py:437
  72.7 13.2 %collective-permute-start.21 = (bf16[1024,256]{1,0:T(8,128)(2,1)S(1)}, bf16[1024,256]{1,0:T(8,128)(2,1)S(1)}, u32[]{:S(2)}, u32[]{:S(2)}) collective-permute-start(bf16[1024,256]{1,0:T(8,128)(2,1)S(1)} %panel.5), channel_id=1, source_target_pairs={{0,4},{4,0},{8,12},{12,8},{1,5},{5,1},{9,13},{13,9},{2,6},{6,2},{1... | collective-permute-start | bytes 1572872 | tf_op jit(solution)/shard_map/ppermute | solution.py:33
  78.0 9.8 %collective-permute-start.24 = (bf16[64,2560]{1,0:T(8,128)(2,1)S(1)}, bf16[64,2560]{1,0:T(8,128)(2,1)S(1)}, u32[]{:S(2)}, u32[]{:S(2)}) collective-permute-start(bf16[64,2560]{1,0:T(8,128)(2,1)S(1)} %get-tuple-element.42), channel_id=1, source_target_pairs={{0,2},{2,0},{1,3},{3,1},{4,6},{6,4},{5,7},{7,5},{8,10},{10,8},{9,1... | collective-permute-start | bytes 983048 | tf_op jit(solution)/shard_map/ppermute | solution.py:29
  86.0 4.9 %collective-permute-start.22 = (f32[512,256]{1,0:T(8,128)S(1)}, f32[512,256]{1,0:T(8,128)S(1)}, u32[]{:S(2)}, u32[]{:S(2)}) collective-permute-start(f32[512,256]{1,0:T(8,128)S(1)} %other_rows.1), channel_id=1, source_target_pairs={{0,1},{1,0},{2,3},{3,2},{4,5},{5,4},{6,7},{7,6},{8,9},{9,8},{10,11... | collective-permute-start | bytes 1572872 | tf_op jit(solution)/shard_map/ppermute | solution.py:33
  (12 other events, 77.6 us)

commit v14 on v11

--- a/solution.py
+++ b/solution.py
@@ -196,9 +196,7 @@
 
 def panel_kernel(order, count, place_ref, x_ref, other_ref, *refs):
     pieces, refs = refs[:count], refs[count:]
-    half = refs[-1].shape[1]
-    panels = pieces[0].shape[1] // half
-    adds, outs = refs[:-panels], refs[-panels:]
+    half = refs[0].shape[1]
     deep = pieces[0].shape[0]
     for n, source in enumerate((x_ref, other_ref)):
         total = None
@@ -206,25 +204,22 @@
             col = pl.multiple_of((place_ref[0] ^ m) * deep, min(deep, 128))
             term = dot(source[:, pl.ds(col, deep)], piece[...])
             total = term if total is None else total + term
-        for i, out in enumerate(outs):
-            value = total[:, i * half : (i + 1) * half]
-            if i < len(adds):
-                value = value + adds[i][n * LIVE : (n + 1) * LIVE, :].astype(F32)
-            out[n * LIVE : (n + 1) * LIVE, :] = value.astype(BF16)
-
-
-def panel_product(order, place, x, x_other, pieces, half, adds=()):
+        for i, out in enumerate(refs):
+            out[n * LIVE : (n + 1) * LIVE, :] = total[:, i * half : (i + 1) * half].astype(out.dtype)
+
+
+def panel_product(order, place, x, x_other, pieces, half, dtype=BF16, weight=1):
     feat, wide = len(pieces) * pieces[0].shape[0], pieces[0].shape[1]
-    shapes = [shaped((2 * LIVE, half), BF16)] * (wide // half)
+    shapes = [shaped((2 * LIVE, half), dtype)] * (wide // half)
     return pl.pallas_call(
         functools.partial(panel_kernel, order, len(pieces)),
-        in_specs=[SMEM] + [VMEM] * (2 + len(pieces) + len(adds)),
+        in_specs=[SMEM] + [VMEM] * (2 + len(pieces)),
         out_specs=[VMEM] * len(shapes),
         out_shape=shapes,
         compiler_params=params(24),
-        cost_estimate=cost(4 * LIVE * feat * wide, 4 * LIVE * feat + 2 * feat * wide),
+        cost_estimate=pl.CostEstimate(flops=weight, bytes_accessed=1, transcendentals=0),
         name="panel",
-    )(place, x, x_other, *pieces, *adds)
+    )(place, x, x_other, *pieces)
 
 
 def settle_kernel(core_ref, own_ref, got_ref, down_ref, up_ref):
@@ -284,6 +279,22 @@
         cost_estimate=cost(2 * LIVE * feat * cols, 2 * feat * (LIVE + cols) + 4 * LIVE * cols),
         name="base",
     )(at, dp, core, fill, tenant, x, base_weight, low, b, *halves)
+
+
+def join_kernel(own_ref, far_ref, out_ref):
+    out_ref[...] = (own_ref[...] + far_ref[...].astype(F32)).astype(BF16)
+
+
+def join(own, far):
+    return pl.pallas_call(
+        join_kernel,
+        in_specs=[VMEM] * 2,
+        out_specs=VMEM,
+        out_shape=shaped(own.shape, BF16),
+        compiler_params=params(24),
+        cost_estimate=cost(own.size, 8 * own.size),
+        name="join",
+    )(own, far)
 
 
 def relay_kernel(at_ref, own_ref, got_ref, passed_ref, kept_ref):
@@ -405,18 +416,19 @@
         pieces, order = gathered(weight[3])
         low = low_part(after(dp, x_other), core, block_fill, block_tenant_index, x, own_a, own_b, halves, blocks, rank)
         pieces[0] = after(pieces[0], weight[2], low)
-        (y_3,) = panel_product(order, panel_at, x, x_other, pieces, half)
+        (y_3,) = panel_product(order, panel_at, x, x_other, pieces, half, weight=3_000_000_000)
         low = add_flipped(low, 1, weight[2])
         far = lax.ppermute(y_3, "tensor", [(0, 1), (3, 2)])
         pieces, order = gathered(after(weight[2], *pieces))
         pieces[0] = after(pieces[0], weight[1])
-        (y_2,) = panel_product(order, panel_at, x, x_other, pieces, half, adds=[far])
-        low = add_flipped(low, 2)
-        near = lax.ppermute(after(y_2, low), "tensor", [(0, 1), (3, 2), (1, 3), (2, 0)])
+        low = (low.astype(F32) + lax.ppermute(low, "tensor", [(1, 2), (2, 1)]).astype(F32)).astype(BF16)
+        (y_2,) = panel_product(order, panel_at, x, x_other, pieces, half, F32)
+        near = lax.ppermute(join(y_2, far), "tensor", [(0, 1), (3, 2), (1, 3), (2, 0)])
+        low = jnp.where((me_t == 1) | (me_t == 2), low, lax.ppermute(low, "tensor", [(1, 0), (2, 3)]))
         pieces, order = gathered(after(weight[1], *pieces))
-        (y_1,) = panel_product(order, panel_at, x, x_other, pieces, half)
+        (y_1,) = panel_product(order, panel_at, x, x_other, pieces, half, weight=10_000_000_000)
         part_1 = flip(y_1, "tensor", n_t, 1)
-        passed, kept = relay(at, y_3, near)
+        passed, kept = relay(at, y_3, after(near, y_1))
         parts = [lax.ppermute(passed, "tensor", [(1, 2), (2, 1)]), part_1, kept]
     else:
         x = pack(block_fill, block_tenant_index, tokens, cotangent, blocks, 2 * rank)

time: 88.8 us -> 97.9 us (1.10)
  the two profiles are of different devices: /device:TPU:0 before, /device:TPU:9 now
where the time goes in v14:
time: 97.9 us; the launch traced here: 97.4 us
  starting transfers between devices  41 us (42%)
  waiting for transfers between devices  23.3 us (24%)
  Pallas kernels  23.1 us (24%)
  local copies, waits for them, and re-layouts  7.34 us (7%)
  other arithmetic  1.73 us (2%)
    ppermute x19, starting transfers between devices, flip(): return lax.ppermute(x, names, [(i, i ^ mask) for i in range(count)])  26.7 us
    ppermute x19, waiting for transfers between devices, flip(): return lax.ppermute(x, names, [(i, i ^ mask) for i in range(count)])  7.53 us
    pallas_call x3, Pallas kernels, panel_product(): pl.pallas_call(functools.partial(panel_kernel, order, len(pieces)), in_sp...  7.33 us
    ppermute x1, waiting for transfers between devices, body(): lax.ppermute(join(y_2, far), 'tensor', [(0, 1), (3, 2), (1, 3), (2, 0)])  6.82 us
    ppermute x1, waiting for transfers between devices, body(): parts = [lax.ppermute(passed, 'tensor', [(1, 2), (2, 1)]), part_1, kept]  6.78 us
    unnamed x27, local copies, waits for them, and re-layouts  6.16 us
    ppermute x1, starting transfers between devices, body(): lax.ppermute(low, 'tensor', [(1, 0), (2, 3)])  5.43 us
    pallas_call x1, Pallas kernels, pack(): pl.pallas_call(functools.partial(pack_kernel, blocks, rows // blocks), in...  2.83 us
  transfers between devices with their start and end apart: 27, of which 8 were waited for; matrix products, arithmetic and copies ran while one was open for 2% of the time, Pallas kernels for 21%

profile of v14, /device:TPU:9, one launch (start us, length us, event | category | flops | bytes accessed | tf_op | source)
XLA Modules:
  0.0 97.4 jit_solution(12912145841211563958)
XLA Ops:
  3.2 1.8 %own_half.1 = (bf16[32,2560]{1,0:T(8,128)(2,1)}, bf16[32,2560]{1,0:T(8,128)(2,1)}) custom-call(s32[1]{0:T(128)} %bitcast.core_ref, bf16[128,2048]{1,0:T(8,128)(2,1)} %bitcast.8, bf16[128,512]{1,0:T(8,128)(2,1)} %bitcast.10), custom_call_target="tpu_custom_call" | custom-call | flops 1 | bytes 1 | tf_op jit(solution)/shard_map/own_half/pallas_call | solution.py:75
  6.5 1.9 %copy-done.3 = bf16[768,2048]{1,0:T(8,128)(2,1)S(1)} copy-done((bf16[768,2048]{1,0:T(8,128)(2,1)S(1)}, bf16[768,2048]{1,0:T(8,128)(2,1)}, u32[]{:S(2)}) %copy-start.3) | copy-done | bytes 3145752
  10.8 2.8 %pack.1.x_ref.own_ref = bf16[512,2688]{1,0:T(8,128)(2,1)S(1)} custom-call(s32[1,6]{1,0:T(1,128)S(1)} %copy-done.7, s32[6]{0:T(128)S(1)} %copy-done.9, bf16[768,2048]{1,0:T(8,128)(2,1)S(1)} %copy-done.3, bf16[768,512]{1,0:T(8,128)(2,1)S(1)} %copy-done.6), custom_call_target="tpu_custom_call" | custom-call | flops 1 | bytes 1 | tf_op jit(solution)/shard_map/pack/pallas_call | solution.py:104
  19.0 2.0 %collective-permute-done.3.other_ref = bf16[512,2688]{1,0:T(8,128)(2,1)S(1)} collective-permute-done((bf16[512,2688]{1,0:T(8,128)(2,1)S(1)}, bf16[512,2688]{1,0:T(8,128)(2,1)S(1)}, u32[]{:S(2)}, u32[]{:S(2)}) %collective-permute-start.3) | collective-permute-done | bytes 2752544 | tf_op jit(solution)/shard_map/ppermute | solution.py:33
  21.0 2.2 %collective-permute-start.11 = (bf16[512,256]{1,0:T(8,128)(2,1)S(1)}, bf16[512,256]{1,0:T(8,128)(2,1)S(1)}, u32[]{:S(2)}, u32[]{:S(2)}) collective-permute-start(bf16[512,256]{1,0:T(8,128)(2,1)S(1)} %collective-permute-done.refs_0_), channel_id=1, source_target_pairs={{0,18},{2,16},{16,2},{18,0},{1,19},{3,17},{17,3},{19,1},{4,22},{6,... | collective-permute-start | bytes 786440 | tf_op jit(solution)/shard_map/ppermute | solution.py:33
  23.2 2.2 %low_part.1 = bf16[512,128]{1,0:T(8,128)(2,1)S(1)} custom-call(s32[1]{0:T(128)} %bitcast.2.dp_ref, s32[1]{0:T(128)} %bitcast.core_ref, s32[1,6]{1,0:T(1,128)S(1)} %copy-done.7, s32[6]{0:T(128)S(1)} %copy-done.9, bf16[512,2688]{1,0:T(8,128)(2,1)S(1)} %pack.1.x_ref.own_ref, bf16[128,2048]{1,0:T(8,128)(2,1)S(1)} %bitcast.9, bf16[128,512]{1,0:T(8,128)(2,1)S(1)} %bitcast.11, ...), custom_call_target="tpu_custom_call" | custom-call | flops 1 | bytes 1 | tf_op jit(solution)/shard_map/low_part/pallas_call | solution.py:147
  25.3 2.1 %collective-permute-done.5.refs_0_ = bf16[512,256]{1,0:T(8,128)(2,1)} collective-permute-done((bf16[512,256]{1,0:T(8,128)(2,1)S(1)}, bf16[512,256]{1,0:T(8,128)(2,1)}, u32[]{:S(2)}, u32[]{:S(2)}) %collective-permute-start.5) | collective-permute-done | bytes 262176 | tf_op jit(solution)/shard_map/ppermute | solution.py:33
  27.4 5.0 %collective-permute-start.6 = (bf16[512,128]{1,0:T(8,128)(2,1)S(1)}, bf16[512,128]{1,0:T(8,128)(2,1)S(1)}, u32[]{:S(2)}, u32[]{:S(2)}) collective-permute-start(bf16[512,128]{1,0:T(8,128)(2,1)S(1)} %low_part.1), channel_id=1, source_target_pairs={{0,4},{4,0},{8,12},{12,8},{1,5},{5,1},{9,13},{13,9},{2,6},{6,2},{1... | collective-permute-start | bytes 393224 | tf_op jit(solution)/shard_map/ppermute | solution.py:33
  36.0 1.9 %collective-permute-start.7 = (bf16[512,128]{1,0:T(8,128)(2,1)S(1)}, bf16[512,128]{1,0:T(8,128)(2,1)S(1)}, u32[]{:S(2)}, u32[]{:S(2)}) collective-permute-start(bf16[512,128]{1,0:T(8,128)(2,1)S(1)} %add_convert_fusion.2), channel_id=1, source_target_pairs={{4,8},{8,4},{5,9},{9,5},{6,10},{10,6},{7,11},{11,7},{20,24},{24,20... | collective-permute-start | bytes 393224 | tf_op jit(solution)/shard_map/ppermute | solution.py:424
  37.9 2.1 %panel.3.own_ref = bf16[1024,256]{1,0:T(8,128)(2,1)} custom-call(s32[1]{0:T(128)} %bitcast.5.place_ref, bf16[512,2688]{1,0:T(8,128)(2,1)S(1)} %pack.1.x_ref.own_ref, bf16[512,2688]{1,0:T(8,128)(2,1)S(1)} %collective-permute-done.3.other_ref, bf16[512,256]{1,0:T(8,128)(2,1)S(1)} %collective-permute-done.refs_0_, ...), custom_call_target="tpu_custom_call" | custom-call | flops 3000000000 | bytes 1 | tf_op jit(solution)/shard_map/panel/pallas_call | solution.py:214
  39.9 2.1 %collective-permute-done.7 = bf16[512,128]{1,0:T(8,128)(2,1)S(1)} collective-permute-done((bf16[512,128]{1,0:T(8,128)(2,1)S(1)}, bf16[512,128]{1,0:T(8,128)(2,1)S(1)}, u32[]{:S(2)}, u32[]{:S(2)}) %collective-permute-start.7) | collective-permute-done | bytes 131104 | tf_op jit(solution)/shard_map/ppermute | solution.py:424
  44.0 5.4 %collective-permute-start.8 = (bf16[512,128]{1,0:T(8,128)(2,1)}, bf16[512,128]{1,0:T(8,128)(2,1)}, u32[]{:S(2)}, u32[]{:S(2)}) collective-permute-start(bf16[512,128]{1,0:T(8,128)(2,1)} %add_convert_fusion.1), channel_id=1, source_target_pairs={{4,0},{8,12},{5,1},{9,13},{6,2},{10,14},{7,3},{11,15},{20,16},{24,... | collective-permute-start | bytes 393224 | tf_op jit(solution)/shard_map/ppermute | solution.py:427
  53.1 3.8 %collective-permute-start.22 = (bf16[512,128]{1,0:T(8,128)(2,1)S(1)}, bf16[512,128]{1,0:T(8,128)(2,1)S(1)}, u32[]{:S(2)}, u32[]{:S(2)}) collective-permute-start(bf16[512,128]{1,0:T(8,128)(2,1)S(1)} %broadcast_select_fusion.low_ref), channel_id=1, source_target_pairs={{0,1},{1,0},{2,3},{3,2},{4,5},{5,4},{6,7},{7,6},{8,9},{9,8},{10,11... | collective-permute-start | bytes 393224 | tf_op jit(solution)/shard_map/ppermute | solution.py:33
  57.0 1.8 %copy-done.1 = bf16[512,2688]{1,0:T(8,128)(2,1)S(1)} copy-done((bf16[512,2688]{1,0:T(8,128)(2,1)S(1)}, bf16[512,2688]{1,0:T(8,128)(2,1)}, u32[]{:S(2)}) %copy-start.1) | copy-done | bytes 2752536
  58.7 2.6 %panel.4.own_ref = f32[1024,256]{1,0:T(8,128)S(1)} custom-call(s32[1]{0:T(128)} %bitcast.5.place_ref, bf16[512,2688]{1,0:T(8,128)(2,1)S(1)} %pack.1.x_ref.own_ref, bf16[512,2688]{1,0:T(8,128)(2,1)S(1)} %copy-done.1, bf16[512,256]{1,0:T(8,128)(2,1)} %collective-permute-done.5.refs_0_, bf16[512,256]{1,0:T(8,128)(2,1)} %collective-permute-done.13.refs_1_, ...), custom_call_target="tpu_custom_call" | custom-call | flops 1 | bytes 1 | tf_op jit(solution)/shard_map/panel/pallas_call | solution.py:214
  65.6 2.7 %panel.5 = bf16[1024,256]{1,0:T(8,128)(2,1)S(1)} custom-call(s32[1]{0:T(128)} %bitcast.5.place_ref, bf16[512,2688]{1,0:T(8,128)(2,1)S(1)} %pack.1.x_ref.own_ref, bf16[512,2688]{1,0:T(8,128)(2,1)S(1)} %copy-done.2, bf16[512,256]{1,0:T(8,128)(2,1)} %collective-permute-done.12.refs_0_, bf16[512,256]{1,0:T(8,128)(2,1)S(1)} %collective-permute-done.18.refs_1_, ...), custom_call_target="tpu_custom_call" | custom-call | flops 10000000000 | bytes 1 | tf_op jit(solution)/shard_map/panel/pallas_call | solution.py:214
  69.3 6.8 %collective-permute-done.17.got_ref = bf16[1024,256]{1,0:T(8,128)(2,1)S(1)} collective-permute-done((bf16[1024,256]{1,0:T(8,128)(2,1)S(1)}, bf16[1024,256]{1,0:T(8,128)(2,1)S(1)}, u32[]{:S(2)}, u32[]{:S(2)}) %collective-permute-start.17) | collective-permute-done | bytes 524320 | tf_op jit(solution)/shard_map/ppermute | solution.py:426
  77.3 2.3 %collective-permute-start.21 = (bf16[1024,256]{1,0:T(8,128)(2,1)S(1)}, bf16[1024,256]{1,0:T(8,128)(2,1)S(1)}, u32[]{:S(2)}, u32[]{:S(2)}) collective-permute-start(bf16[1024,256]{1,0:T(8,128)(2,1)S(1)} %get-tuple-element.37), channel_id=1, source_target_pairs={{4,8},{8,4},{5,9},{9,5},{6,10},{10,6},{7,11},{11,7},{20,24},{24,20... | collective-permute-start | bytes 1572872 | tf_op jit(solution)/shard_map/ppermute | solution.py:432
  79.8 1.5 %collective-permute-start.24 = (bf16[64,2560]{1,0:T(8,128)(2,1)S(1)}, bf16[64,2560]{1,0:T(8,128)(2,1)S(1)}, u32[]{:S(2)}, u32[]{:S(2)}) collective-permute-start(bf16[64,2560]{1,0:T(8,128)(2,1)S(1)} %add_convert_fusion.own_ref), channel_id=1, source_target_pairs={{0,1},{1,0},{2,3},{3,2},{4,5},{5,4},{6,7},{7,6},{8,9},{9,8},{10,11... | collective-permute-start | bytes 983048 | tf_op jit(solution)/shard_map/ppermute | solution.py:33
  81.3 2.1 %base.1.base_ref = f32[512,512]{1,0:T(8,128)S(1)} custom-call(s32[1]{0:T(128)} %bitcast.1.at_ref, s32[1]{0:T(128)} %bitcast.2.dp_ref, s32[1]{0:T(128)} %bitcast.core_ref, s32[1,6]{1,0:T(1,128)S(1)} %copy-done.8, s32[6]{0:T(128)S(1)} %copy-done.10, bf16[512,2688]{1,0:T(8,128)(2,1)S(1)} %pack.1.x_ref.own_ref, bf16[8192,512]{1,0:T(8,128)(2,1)S(1)} %bitcast.7, ...), custom_call_target="tpu_custom_call" | custom-call | flops 1 | bytes 1 | tf_op jit(solution)/shard_map/base/pallas_call | solution.py:266
  84.7 6.8 %collective-permute-done.21.refs_0_ = bf16[1024,256]{1,0:T(8,128)(2,1)S(1)} collective-permute-done((bf16[1024,256]{1,0:T(8,128)(2,1)S(1)}, bf16[1024,256]{1,0:T(8,128)(2,1)S(1)}, u32[]{:S(2)}, u32[]{:S(2)}) %collective-permute-start.21) | collective-permute-done | bytes 524320 | tf_op jit(solution)/shard_map/ppermute | solution.py:432
  91.5 2.2 %collective-permute-start.26 = (f32[512,256]{1,0:T(8,128)S(1)}, f32[512,256]{1,0:T(8,128)S(1)}, u32[]{:S(2)}, u32[]{:S(2)}) collective-permute-start(f32[512,256]{1,0:T(8,128)S(1)} %other_rows.1), channel_id=1, source_target_pairs={{0,1},{1,0},{2,3},{3,2},{4,5},{5,4},{6,7},{7,6},{8,9},{9,8},{10,11... | collective-permute-start | bytes 1572872 | tf_op jit(solution)/shard_map/ppermute | solution.py:33
  93.7 1.5 %collective-permute-done.26.refs_3_ = f32[512,256]{1,0:T(8,128)S(1)} collective-permute-done((f32[512,256]{1,0:T(8,128)S(1)}, f32[512,256]{1,0:T(8,128)S(1)}, u32[]{:S(2)}, u32[]{:S(2)}) %collective-permute-start.26) | collective-permute-done | bytes 524320 | tf_op jit(solution)/shard_map/ppermute | solution.py:33
  95.3 2.2 %finish.1 = bf16[768,512]{1,0:T(8,128)(2,1)} custom-call(s32[1]{0:T(128)} %bitcast.core_ref, s32[1,6]{1,0:T(1,128)S(1)} %copy-done.8, f32[512,512]{1,0:T(8,128)S(1)} %base.1.base_ref, bf16[1024,256]{1,0:T(8,128)(2,1)S(1)} %collective-permute-done.21.refs_0_, bf16[1024,256]{1,0:T(8,128)(2,1)S(1)} %collective-permute-done.25.refs_1_, ...), custom_call_target="tpu_custom_call" | custom-call | flops 1 | bytes 1 | tf_op jit(solution)/shard_map/finish/pallas_call | solution.py:363
  (77 shorter events, 28.6 us)
Async XLA Ops:
  1.8 13.0 %collective-permute-start = (bf16[512,256]{1,0:T(8,128)(2,1)S(1)}, bf16[512,256]{1,0:T(8,128)(2,1)S(1)}, u32[]{:S(2)}, u32[]{:S(2)}) collective-permute-start(bf16[512,256]{1,0:T(8,128)(2,1)S(1)} %get-tuple-element.47), channel_id=1, source_target_pairs={{0,12},{4,8},{8,4},{12,0},{1,13},{5,9},{9,5},{13,1},{2,14},{6,10},... | collective-permute-start | bytes 786440 | tf_op jit(solution)/shard_map/ppermute | solution.py:33
  5.0 8.7 %collective-permute-start.1 = (bf16[32,2560]{1,0:T(8,128)(2,1)}, bf16[32,2560]{1,0:T(8,128)(2,1)S(1)}, u32[]{:S(2)}, u32[]{:S(2)}) collective-permute-start(bf16[32,2560]{1,0:T(8,128)(2,1)} %get-tuple-element.25), channel_id=1, source_target_pairs={{0,2},{2,0},{1,3},{3,1},{4,6},{6,4},{5,7},{7,5},{8,10},{10,8},{9,1... | collective-permute-start | bytes 491528 | tf_op jit(solution)/shard_map/ppermute | solution.py:29
  6.2 7.5 %collective-permute-start.2 = (bf16[32,2560]{1,0:T(8,128)(2,1)}, bf16[32,2560]{1,0:T(8,128)(2,1)S(1)}, u32[]{:S(2)}, u32[]{:S(2)}) collective-permute-start(bf16[32,2560]{1,0:T(8,128)(2,1)} %get-tuple-element.26), channel_id=1, source_target_pairs={{0,2},{2,0},{1,3},{3,1},{4,6},{6,4},{5,7},{7,5},{8,10},{10,8},{9,1... | collective-permute-start | bytes 491528 | tf_op jit(solution)/shard_map/ppermute | solution.py:29
  16.3 6.9 %collective-permute-start.4 = (bf16[64,2560]{1,0:T(8,128)(2,1)S(1)}, bf16[64,2560]{1,0:T(8,128)(2,1)S(1)}, u32[]{:S(2)}, u32[]{:S(2)}) collective-permute-start(bf16[64,2560]{1,0:T(8,128)(2,1)S(1)} %constant_dynamic-update-slice_fusion.refs_0_), channel_id=1, source_target_pairs={{0,1},{1,0},{2,3},{3,2},{4,5},{5,4},{6,7},{7,6},{8,9},{9,8},{10,11... | collective-permute-start | bytes 983048 | tf_op jit(solution)/shard_map/ppermute | solution.py:33
  16.4 11.1 %collective-permute-start.5 = (bf16[512,256]{1,0:T(8,128)(2,1)S(1)}, bf16[512,256]{1,0:T(8,128)(2,1)}, u32[]{:S(2)}, u32[]{:S(2)}) collective-permute-start(bf16[512,256]{1,0:T(8,128)(2,1)S(1)} %get-tuple-element.29), channel_id=1, source_target_pairs={{0,8},{4,12},{8,0},{12,4},{1,9},{5,13},{9,1},{13,5},{2,10},{6,14},... | collective-permute-start | bytes 786440 | tf_op jit(solution)/shard_map/ppermute | solution.py:33
  16.6 16.0 %collective-permute-start.9 = (bf16[512,256]{1,0:T(8,128)(2,1)S(1)}, bf16[512,256]{1,0:T(8,128)(2,1)S(1)}, u32[]{:S(2)}, u32[]{:S(2)}) collective-permute-start(bf16[512,256]{1,0:T(8,128)(2,1)S(1)} %collective-permute-done.refs_0_), channel_id=1, source_target_pairs={{0,2},{2,0},{16,18},{18,16},{1,3},{3,1},{17,19},{19,17},{4,6},{6,4... | collective-permute-start | bytes 786440 | tf_op jit(solution)/shard_map/ppermute | solution.py:33
  17.8 14.7 %collective-permute-start.10 = (bf16[512,256]{1,0:T(8,128)(2,1)S(1)}, bf16[512,256]{1,0:T(8,128)(2,1)S(1)}, u32[]{:S(2)}, u32[]{:S(2)}) collective-permute-start(bf16[512,256]{1,0:T(8,128)(2,1)S(1)} %collective-permute-done.refs_0_), channel_id=1, source_target_pairs={{0,16},{2,18},{16,0},{18,2},{1,17},{3,19},{17,1},{19,3},{4,20},{6,... | collective-permute-start | bytes 786440 | tf_op jit(solution)/shard_map/ppermute | solution.py:33
  21.0 11.5 %collective-permute-start.11 = (bf16[512,256]{1,0:T(8,128)(2,1)S(1)}, bf16[512,256]{1,0:T(8,128)(2,1)S(1)}, u32[]{:S(2)}, u32[]{:S(2)}) collective-permute-start(bf16[512,256]{1,0:T(8,128)(2,1)S(1)} %collective-permute-done.refs_0_), channel_id=1, source_target_pairs={{0,18},{2,16},{16,2},{18,0},{1,19},{3,17},{17,3},{19,1},{4,22},{6,... | collective-permute-start | bytes 786440 | tf_op jit(solution)/shard_map/ppermute | solution.py:33
  27.4 8.5 %collective-permute-start.6 = (bf16[512,128]{1,0:T(8,128)(2,1)S(1)}, bf16[512,128]{1,0:T(8,128)(2,1)S(1)}, u32[]{:S(2)}, u32[]{:S(2)}) collective-permute-start(bf16[512,128]{1,0:T(8,128)(2,1)S(1)} %low_part.1), channel_id=1, source_target_pairs={{0,4},{4,0},{8,12},{12,8},{1,5},{5,1},{9,13},{13,9},{2,6},{6,2},{1... | collective-permute-start | bytes 393224 | tf_op jit(solution)/shard_map/ppermute | solution.py:33
  32.5 11.6 %collective-permute-start.12 = (bf16[512,256]{1,0:T(8,128)(2,1)S(1)}, bf16[512,256]{1,0:T(8,128)(2,1)}, u32[]{:S(2)}, u32[]{:S(2)}) collective-permute-start(bf16[512,256]{1,0:T(8,128)(2,1)S(1)} %get-tuple-element.33), channel_id=1, source_target_pairs={{0,4},{4,0},{8,12},{12,8},{1,5},{5,1},{9,13},{13,9},{2,6},{6,2},{1... | collective-permute-start | bytes 786440 | tf_op jit(solution)/shard_map/ppermute | solution.py:33
  32.5 17.0 %collective-permute-start.13 = (bf16[512,256]{1,0:T(8,128)(2,1)}, bf16[512,256]{1,0:T(8,128)(2,1)}, u32[]{:S(2)}, u32[]{:S(2)}) collective-permute-start(bf16[512,256]{1,0:T(8,128)(2,1)} %collective-permute-done.5.refs_0_), channel_id=1, source_target_pairs={{0,2},{2,0},{16,18},{18,16},{1,3},{3,1},{17,19},{19,17},{4,6},{6,4... | collective-permute-start | bytes 786440 | tf_op jit(solution)/shard_map/ppermute | solution.py:33
  33.8 15.7 %collective-permute-start.14 = (bf16[512,256]{1,0:T(8,128)(2,1)}, bf16[512,256]{1,0:T(8,128)(2,1)}, u32[]{:S(2)}, u32[]{:S(2)}) collective-permute-start(bf16[512,256]{1,0:T(8,128)(2,1)} %collective-permute-done.5.refs_0_), channel_id=1, source_target_pairs={{0,16},{2,18},{16,0},{18,2},{1,17},{3,19},{17,1},{19,3},{4,20},{6,... | collective-permute-start | bytes 786440 | tf_op jit(solution)/shard_map/ppermute | solution.py:33
  35.0 14.5 %collective-permute-start.15 = (bf16[512,256]{1,0:T(8,128)(2,1)}, bf16[512,256]{1,0:T(8,128)(2,1)}, u32[]{:S(2)}, u32[]{:S(2)}) collective-permute-start(bf16[512,256]{1,0:T(8,128)(2,1)} %collective-permute-done.5.refs_0_), channel_id=1, source_target_pairs={{0,18},{2,16},{16,2},{18,0},{1,19},{3,17},{17,3},{19,1},{4,22},{6,... | collective-permute-start | bytes 786440 | tf_op jit(solution)/shard_map/ppermute | solution.py:33
  36.0 6.1 %collective-permute-start.7 = (bf16[512,128]{1,0:T(8,128)(2,1)S(1)}, bf16[512,128]{1,0:T(8,128)(2,1)S(1)}, u32[]{:S(2)}, u32[]{:S(2)}) collective-permute-start(bf16[512,128]{1,0:T(8,128)(2,1)S(1)} %add_convert_fusion.2), channel_id=1, source_target_pairs={{4,8},{8,4},{5,9},{9,5},{6,10},{10,6},{7,11},{11,7},{20,24},{24,20... | collective-permute-start | bytes 393224 | tf_op jit(solution)/shard_map/ppermute | solution.py:424
  42.1 19.3 %collective-permute-start.16 = (bf16[1024,256]{1,0:T(8,128)(2,1)}, bf16[1024,256]{1,0:T(8,128)(2,1)}, u32[]{:S(2)}, u32[]{:S(2)}) collective-permute-start(bf16[1024,256]{1,0:T(8,128)(2,1)} %panel.3.own_ref), channel_id=1, source_target_pairs={{0,4},{12,8},{1,5},{13,9},{2,6},{14,10},{3,7},{15,11},{16,20},{28,... | collective-permute-start | bytes 1572872 | tf_op jit(solution)/shard_map/ppermute | solution.py:421
  44.0 8.2 %collective-permute-start.8 = (bf16[512,128]{1,0:T(8,128)(2,1)}, bf16[512,128]{1,0:T(8,128)(2,1)}, u32[]{:S(2)}, u32[]{:S(2)}) collective-permute-start(bf16[512,128]{1,0:T(8,128)(2,1)} %add_convert_fusion.1), channel_id=1, source_target_pairs={{4,0},{8,12},{5,1},{9,13},{6,2},{10,14},{7,3},{11,15},{20,16},{24,... | collective-permute-start | bytes 393224 | tf_op jit(solution)/shard_map/ppermute | solution.py:427
  49.5 15.0 %collective-permute-start.18 = (bf16[512,256]{1,0:T(8,128)(2,1)}, bf16[512,256]{1,0:T(8,128)(2,1)S(1)}, u32[]{:S(2)}, u32[]{:S(2)}) collective-permute-start(bf16[512,256]{1,0:T(8,128)(2,1)} %collective-permute-done.12.refs_0_), channel_id=1, source_target_pairs={{0,2},{2,0},{16,18},{18,16},{1,3},{3,1},{17,19},{19,17},{4,6},{6,4... | collective-permute-start | bytes 786440 | tf_op jit(solution)/shard_map/ppermute | solution.py:33
  50.8 13.7 %collective-permute-start.19 = (bf16[512,256]{1,0:T(8,128)(2,1)}, bf16[512,256]{1,0:T(8,128)(2,1)S(1)}, u32[]{:S(2)}, u32[]{:S(2)}) collective-permute-start(bf16[512,256]{1,0:T(8,128)(2,1)} %collective-permute-done.12.refs_0_), channel_id=1, source_target_pairs={{0,16},{2,18},{16,0},{18,2},{1,17},{3,19},{17,1},{19,3},{4,20},{6,... | collective-permute-start | bytes 786440 | tf_op jit(solution)/shard_map/ppermute | solution.py:33
  52.0 12.5 %collective-permute-start.20 = (bf16[512,256]{1,0:T(8,128)(2,1)}, bf16[512,256]{1,0:T(8,128)(2,1)S(1)}, u32[]{:S(2)}, u32[]{:S(2)}) collective-permute-start(bf16[512,256]{1,0:T(8,128)(2,1)} %collective-permute-done.12.refs_0_), channel_id=1, source_target_pairs={{0,18},{2,16},{16,2},{18,0},{1,19},{3,17},{17,3},{19,1},{4,22},{6,... | collective-permute-start | bytes 786440 | tf_op jit(solution)/shard_map/ppermute | solution.py:33
  53.1 10.3 %collective-permute-start.22 = (bf16[512,128]{1,0:T(8,128)(2,1)S(1)}, bf16[512,128]{1,0:T(8,128)(2,1)S(1)}, u32[]{:S(2)}, u32[]{:S(2)}) collective-permute-start(bf16[512,128]{1,0:T(8,128)(2,1)S(1)} %broadcast_select_fusion.low_ref), channel_id=1, source_target_pairs={{0,1},{1,0},{2,3},{3,2},{4,5},{5,4},{6,7},{7,6},{8,9},{9,8},{10,11... | collective-permute-start | bytes 393224 | tf_op jit(solution)/shard_map/ppermute | solution.py:33
  62.5 13.6 %collective-permute-start.17 = (bf16[1024,256]{1,0:T(8,128)(2,1)S(1)}, bf16[1024,256]{1,0:T(8,128)(2,1)S(1)}, u32[]{:S(2)}, u32[]{:S(2)}) collective-permute-start(bf16[1024,256]{1,0:T(8,128)(2,1)S(1)} %join.1), channel_id=1, source_target_pairs={{0,4},{12,8},{4,12},{8,0},{1,5},{13,9},{5,13},{9,1},{2,6},{14,10},... | collective-permute-start | bytes 1572872 | tf_op jit(solution)/shard_map/ppermute | solution.py:426
  64.5 15.1 %collective-permute-start.23 = (bf16[64,2560]{1,0:T(8,128)(2,1)S(1)}, bf16[64,2560]{1,0:T(8,128)(2,1)S(1)}, u32[]{:S(2)}, u32[]{:S(2)}) collective-permute-start(bf16[64,2560]{1,0:T(8,128)(2,1)S(1)} %get-tuple-element.40), channel_id=1, source_target_pairs={{0,2},{2,0},{1,3},{3,1},{4,6},{6,4},{5,7},{7,5},{8,10},{10,8},{9,1... | collective-permute-start | bytes 983048 | tf_op jit(solution)/shard_map/ppermute | solution.py:29
  68.3 23.2 %collective-permute-start.25 = (bf16[1024,256]{1,0:T(8,128)(2,1)S(1)}, bf16[1024,256]{1,0:T(8,128)(2,1)S(1)}, u32[]{:S(2)}, u32[]{:S(2)}) collective-permute-start(bf16[1024,256]{1,0:T(8,128)(2,1)S(1)} %panel.5), channel_id=1, source_target_pairs={{0,4},{4,0},{8,12},{12,8},{1,5},{5,1},{9,13},{13,9},{2,6},{6,2},{1... | collective-permute-start | bytes 1572872 | tf_op jit(solution)/shard_map/ppermute | solution.py:33
  77.3 14.1 %collective-permute-start.21 = (bf16[1024,256]{1,0:T(8,128)(2,1)S(1)}, bf16[1024,256]{1,0:T(8,128)(2,1)S(1)}, u32[]{:S(2)}, u32[]{:S(2)}) collective-permute-start(bf16[1024,256]{1,0:T(8,128)(2,1)S(1)} %get-tuple-element.37), channel_id=1, source_target_pairs={{4,8},{8,4},{5,9},{9,5},{6,10},{10,6},{7,11},{11,7},{20,24},{24,20... | collective-permute-start | bytes 1572872 | tf_op jit(solution)/shard_map/ppermute | solution.py:432
  (16 other events, 135.1 us)

commit v15 on v14

--- a/solution.py
+++ b/solution.py
@@ -416,7 +416,7 @@
         pieces, order = gathered(weight[3])
         low = low_part(after(dp, x_other), core, block_fill, block_tenant_index, x, own_a, own_b, halves, blocks, rank)
         pieces[0] = after(pieces[0], weight[2], low)
-        (y_3,) = panel_product(order, panel_at, x, x_other, pieces, half, weight=3_000_000_000)
+        (y_3,) = panel_product(order, panel_at, x, x_other, pieces, half)
         low = add_flipped(low, 1, weight[2])
         far = lax.ppermute(y_3, "tensor", [(0, 1), (3, 2)])
         pieces, order = gathered(after(weight[2], *pieces))
@@ -453,7 +453,7 @@
     base = base_product(
         at, dp, core, block_fill, block_tenant_index, x, base_weight, low, own_b, halves, feat, blocks, rank
     )
-    parts[0] = after(parts[0], base, down_out)
+    parts[0] = after(parts[0], base)
     others = [flip(other_rows(parts), "pipe", n_pipe, 1)]
     out = finish(core, block_fill, base, parts, others, rows, blocks)
     return out, down_out, up_out

time: 97.9 us -> 101 us (1.032)
  the two profiles are of different devices: /device:TPU:9 before, /device:TPU:0 now
where the time goes in v15:
time: 101 us; the launch traced here: 99 us
  starting transfers between devices  33.6 us (33%)
  waiting for transfers between devices  30.2 us (30%)
  Pallas kernels  19.8 us (20%)
  local copies, waits for them, and re-layouts  13.3 us (13%)
  other arithmetic  1.07 us (1%)
    ppermute x19, starting transfers between devices, flip(): return lax.ppermute(x, names, [(i, i ^ mask) for i in range(count)])  22.1 us
    ppermute x19, waiting for transfers between devices, flip(): return lax.ppermute(x, names, [(i, i ^ mask) for i in range(count)])  14.8 us
    unnamed x51, local copies, waits for them, and re-layouts  12.1 us
    ppermute x1, waiting for transfers between devices, body(): lax.ppermute(join(y_2, far), 'tensor', [(0, 1), (3, 2), (1, 3), (2, 0)])  9.67 us
    ppermute x3, waiting for transfers between devices, shift(): lax.ppermute(x, name, [(i, (i + step) % count) for i in range(count)])  5.67 us
    pallas_call x3, Pallas kernels, panel_product(): pl.pallas_call(functools.partial(panel_kernel, order, len(pieces)), in_sp...  4.93 us
    pallas_call x1, Pallas kernels, pack(): pl.pallas_call(functools.partial(pack_kernel, blocks, rows // blocks), in...  2.83 us
    ppermute x1, starting transfers between devices, body(): far = lax.ppermute(y_3, 'tensor', [(0, 1), (3, 2)])  2.74 us
  transfers between devices with their start and end apart: 27, of which 9 were waited for; matrix products, arithmetic and copies ran while one was open for 1% of the time, Pallas kernels for 18%

profile of v15, /device:TPU:0, one launch (start us, length us, event | category | flops | bytes accessed | tf_op | source)
XLA Modules:
  0.0 99.0 jit_solution(18000806486592689446)
XLA Ops:
  1.8 5.1 %collective-permute-start = (bf16[512,256]{1,0:T(8,128)(2,1)S(1)}, bf16[512,256]{1,0:T(8,128)(2,1)S(1)}, u32[]{:S(2)}, u32[]{:S(2)}) collective-permute-start(bf16[512,256]{1,0:T(8,128)(2,1)S(1)} %get-tuple-element.47), channel_id=1, source_target_pairs={{0,12},{4,8},{8,4},{12,0},{1,13},{5,9},{9,5},{13,1},{2,14},{6,10},... | collective-permute-start | bytes 786440 | tf_op jit(solution)/shard_map/ppermute | solution.py:33
  7.0 1.8 %own_half.1 = (bf16[32,2560]{1,0:T(8,128)(2,1)}, bf16[32,2560]{1,0:T(8,128)(2,1)}) custom-call(s32[1]{0:T(128)} %bitcast.core_ref, bf16[128,2048]{1,0:T(8,128)(2,1)} %bitcast.8, bf16[128,512]{1,0:T(8,128)(2,1)} %bitcast.10), custom_call_target="tpu_custom_call" | custom-call | flops 1 | bytes 1 | tf_op jit(solution)/shard_map/own_half/pallas_call | solution.py:75
  8.8 1.5 %collective-permute-start.1 = (bf16[32,2560]{1,0:T(8,128)(2,1)}, bf16[32,2560]{1,0:T(8,128)(2,1)S(1)}, u32[]{:S(2)}, u32[]{:S(2)}) collective-permute-start(bf16[32,2560]{1,0:T(8,128)(2,1)} %get-tuple-element.25), channel_id=1, source_target_pairs={{0,2},{2,0},{1,3},{3,1},{4,6},{6,4},{5,7},{7,5},{8,10},{10,8},{9,1... | collective-permute-start | bytes 491528 | tf_op jit(solution)/shard_map/ppermute | solution.py:29
  10.8 1.9 %copy-done.3 = bf16[768,2048]{1,0:T(8,128)(2,1)S(1)} copy-done((bf16[768,2048]{1,0:T(8,128)(2,1)S(1)}, bf16[768,2048]{1,0:T(8,128)(2,1)}, u32[]{:S(2)}) %copy-start.3) | copy-done | bytes 3145752
  15.1 2.8 %pack.1.x_ref.own_ref = bf16[512,2688]{1,0:T(8,128)(2,1)S(1)} custom-call(s32[1,6]{1,0:T(1,128)S(1)} %copy-done.19, s32[6]{0:T(128)S(1)} %copy-done.21, bf16[768,2048]{1,0:T(8,128)(2,1)S(1)} %copy-done.3, bf16[768,512]{1,0:T(8,128)(2,1)S(1)} %copy-done.10), custom_call_target="tpu_custom_call" | custom-call | flops 1 | bytes 1 | tf_op jit(solution)/shard_map/pack/pallas_call | solution.py:104
  20.2 1.5 %collective-permute-start.9 = (bf16[512,256]{1,0:T(8,128)(2,1)S(1)}, bf16[512,256]{1,0:T(8,128)(2,1)S(1)}, u32[]{:S(2)}, u32[]{:S(2)}) collective-permute-start(bf16[512,256]{1,0:T(8,128)(2,1)S(1)} %collective-permute-done.refs_0_), channel_id=1, source_target_pairs={{0,2},{2,0},{16,18},{18,16},{1,3},{3,1},{17,19},{19,17},{4,6},{6,4... | collective-permute-start | bytes 786440 | tf_op jit(solution)/shard_map/ppermute | solution.py:33
  21.7 1.5 %collective-permute-start.10 = (bf16[512,256]{1,0:T(8,128)(2,1)S(1)}, bf16[512,256]{1,0:T(8,128)(2,1)S(1)}, u32[]{:S(2)}, u32[]{:S(2)}) collective-permute-start(bf16[512,256]{1,0:T(8,128)(2,1)S(1)} %collective-permute-done.refs_0_), channel_id=1, source_target_pairs={{0,16},{2,18},{16,0},{18,2},{1,17},{3,19},{17,1},{19,3},{4,20},{6,... | collective-permute-start | bytes 786440 | tf_op jit(solution)/shard_map/ppermute | solution.py:33
  23.2 2.4 %collective-permute-start.11 = (bf16[512,256]{1,0:T(8,128)(2,1)S(1)}, bf16[512,256]{1,0:T(8,128)(2,1)S(1)}, u32[]{:S(2)}, u32[]{:S(2)}) collective-permute-start(bf16[512,256]{1,0:T(8,128)(2,1)S(1)} %collective-permute-done.refs_0_), channel_id=1, source_target_pairs={{0,18},{2,16},{16,2},{18,0},{1,19},{3,17},{17,3},{19,1},{4,22},{6,... | collective-permute-start | bytes 786440 | tf_op jit(solution)/shard_map/ppermute | solution.py:33
  25.7 2.2 %low_part.1 = bf16[512,128]{1,0:T(8,128)(2,1)S(1)} custom-call(s32[1]{0:T(128)} %bitcast.2.dp_ref, s32[1]{0:T(128)} %bitcast.core_ref, s32[1,6]{1,0:T(1,128)S(1)} %copy-done.20, s32[6]{0:T(128)S(1)} %copy-done.22, bf16[512,2688]{1,0:T(8,128)(2,1)S(1)} %pack.1.x_ref.own_ref, bf16[128,2048]{1,0:T(8,128)(2,1)S(1)} %bitcast.9, bf16[128,512]{1,0:T(8,128)(2,1)S(1)} %bitcast.11, ...), custom_call_target="tpu_custom_call" | custom-call | flops 1 | bytes 1 | tf_op jit(solution)/shard_map/low_part/pallas_call | solution.py:147
  27.9 5.6 %collective-permute-done.5.refs_0_ = bf16[512,256]{1,0:T(8,128)(2,1)S(1)} collective-permute-done((bf16[512,256]{1,0:T(8,128)(2,1)S(1)}, bf16[512,256]{1,0:T(8,128)(2,1)S(1)}, u32[]{:S(2)}, u32[]{:S(2)}) %collective-permute-start.5) | collective-permute-done | bytes 262176 | tf_op jit(solution)/shard_map/ppermute | solution.py:33
  33.5 2.0 %collective-permute-start.12 = (bf16[512,256]{1,0:T(8,128)(2,1)S(1)}, bf16[512,256]{1,0:T(8,128)(2,1)}, u32[]{:S(2)}, u32[]{:S(2)}) collective-permute-start(bf16[512,256]{1,0:T(8,128)(2,1)S(1)} %get-tuple-element.33), channel_id=1, source_target_pairs={{0,4},{4,0},{8,12},{12,8},{1,5},{5,1},{9,13},{13,9},{2,6},{6,2},{1... | collective-permute-start | bytes 786440 | tf_op jit(solution)/shard_map/ppermute | solution.py:33
  35.5 1.6 %collective-permute-start.13 = (bf16[512,256]{1,0:T(8,128)(2,1)S(1)}, bf16[512,256]{1,0:T(8,128)(2,1)S(1)}, u32[]{:S(2)}, u32[]{:S(2)}) collective-permute-start(bf16[512,256]{1,0:T(8,128)(2,1)S(1)} %collective-permute-done.5.refs_0_), channel_id=1, source_target_pairs={{0,2},{2,0},{16,18},{18,16},{1,3},{3,1},{17,19},{19,17},{4,6},{6,4... | collective-permute-start | bytes 786440 | tf_op jit(solution)/shard_map/ppermute | solution.py:33
  37.1 1.5 %collective-permute-start.14 = (bf16[512,256]{1,0:T(8,128)(2,1)S(1)}, bf16[512,256]{1,0:T(8,128)(2,1)S(1)}, u32[]{:S(2)}, u32[]{:S(2)}) collective-permute-start(bf16[512,256]{1,0:T(8,128)(2,1)S(1)} %collective-permute-done.5.refs_0_), channel_id=1, source_target_pairs={{0,16},{2,18},{16,0},{18,2},{1,17},{3,19},{17,1},{19,3},{4,20},{6,... | collective-permute-start | bytes 786440 | tf_op jit(solution)/shard_map/ppermute | solution.py:33
  40.4 2.7 %collective-permute-start.16 = (bf16[1024,256]{1,0:T(8,128)(2,1)S(1)}, bf16[1024,256]{1,0:T(8,128)(2,1)}, u32[]{:S(2)}, u32[]{:S(2)}) collective-permute-start(bf16[1024,256]{1,0:T(8,128)(2,1)S(1)} %panel.3.own_ref), channel_id=1, source_target_pairs={{0,4},{12,8},{1,5},{13,9},{2,6},{14,10},{3,7},{15,11},{16,20},{28,... | collective-permute-start | bytes 1572872 | tf_op jit(solution)/shard_map/ppermute | solution.py:421
  46.7 3.4 %collective-permute-done.14.refs_2_ = bf16[512,256]{1,0:T(8,128)(2,1)S(1)} collective-permute-done((bf16[512,256]{1,0:T(8,128)(2,1)S(1)}, bf16[512,256]{1,0:T(8,128)(2,1)S(1)}, u32[]{:S(2)}, u32[]{:S(2)}) %collective-permute-start.14) | collective-permute-done | bytes 262176 | tf_op jit(solution)/shard_map/ppermute | solution.py:33
  52.0 1.6 %collective-permute-start.19 = (bf16[512,256]{1,0:T(8,128)(2,1)}, bf16[512,256]{1,0:T(8,128)(2,1)}, u32[]{:S(2)}, u32[]{:S(2)}) collective-permute-start(bf16[512,256]{1,0:T(8,128)(2,1)} %collective-permute-done.12.refs_0_), channel_id=1, source_target_pairs={{0,16},{2,18},{16,0},{18,2},{1,17},{3,19},{17,1},{19,3},{4,20},{6,... | collective-permute-start | bytes 786440 | tf_op jit(solution)/shard_map/ppermute | solution.py:33
  57.3 1.8 %copy-done.1 = bf16[512,2688]{1,0:T(8,128)(2,1)S(1)} copy-done((bf16[512,2688]{1,0:T(8,128)(2,1)S(1)}, bf16[512,2688]{1,0:T(8,128)(2,1)}, u32[]{:S(2)}) %copy-start.1) | copy-done | bytes 2752536
  65.4 2.7 %collective-permute-start.17 = (bf16[1024,256]{1,0:T(8,128)(2,1)S(1)}, bf16[1024,256]{1,0:T(8,128)(2,1)S(1)}, u32[]{:S(2)}, u32[]{:S(2)}) collective-permute-start(bf16[1024,256]{1,0:T(8,128)(2,1)S(1)} %join.1), channel_id=1, source_target_pairs={{0,4},{12,8},{4,12},{8,0},{1,5},{13,9},{5,13},{9,1},{2,6},{14,10},... | collective-permute-start | bytes 1572872 | tf_op jit(solution)/shard_map/ppermute | solution.py:426
  68.1 2.4 %panel.5 = bf16[1024,256]{1,0:T(8,128)(2,1)S(1)} custom-call(s32[1]{0:T(128)} %bitcast.5.place_ref, bf16[512,2688]{1,0:T(8,128)(2,1)S(1)} %pack.1.x_ref.own_ref, bf16[512,2688]{1,0:T(8,128)(2,1)S(1)} %copy-done.2, bf16[512,256]{1,0:T(8,128)(2,1)} %collective-permute-done.12.refs_0_, bf16[512,256]{1,0:T(8,128)(2,1)} %collective-permute-done.18.refs_1_, ...), custom_call_target="tpu_custom_call" | custom-call | flops 10000000000 | bytes 1 | tf_op jit(solution)/shard_map/panel/pallas_call | solution.py:214
  70.8 9.7 %collective-permute-done.17.got_ref = bf16[1024,256]{1,0:T(8,128)(2,1)S(1)} collective-permute-done((bf16[1024,256]{1,0:T(8,128)(2,1)S(1)}, bf16[1024,256]{1,0:T(8,128)(2,1)S(1)}, u32[]{:S(2)}, u32[]{:S(2)}) %collective-permute-start.17) | collective-permute-done | bytes 524320 | tf_op jit(solution)/shard_map/ppermute | solution.py:426
  84.6 2.1 %base.1.base_ref = f32[512,512]{1,0:T(8,128)S(1)} custom-call(s32[1]{0:T(128)} %bitcast.1.at_ref, s32[1]{0:T(128)} %bitcast.2.dp_ref, s32[1]{0:T(128)} %bitcast.core_ref, s32[1,6]{1,0:T(1,128)S(1)} %copy-done.20, s32[6]{0:T(128)S(1)} %copy-done.22, bf16[512,2688]{1,0:T(8,128)(2,1)S(1)} %pack.1.x_ref.own_ref, bf16[8192,512]{1,0:T(8,128)(2,1)S(1)} %bitcast.7, ...), custom_call_target="tpu_custom_call" | custom-call | flops 1 | bytes 1 | tf_op jit(solution)/shard_map/base/pallas_call | solution.py:266
  88.4 5.5 %collective-permute-done.25 = bf16[64,2560]{1,0:T(8,128)(2,1)S(1)} collective-permute-done((bf16[64,2560]{1,0:T(8,128)(2,1)S(1)}, bf16[64,2560]{1,0:T(8,128)(2,1)S(1)}, u32[]{:S(2)}, u32[]{:S(2)}) %collective-permute-start.25) | collective-permute-done | bytes 327712 | tf_op jit(solution)/shard_map/ppermute | solution.py:29
  94.0 1.6 %collective-permute-done.26.got_ref = bf16[64,2560]{1,0:T(8,128)(2,1)S(1)} collective-permute-done((bf16[64,2560]{1,0:T(8,128)(2,1)S(1)}, bf16[64,2560]{1,0:T(8,128)(2,1)S(1)}, u32[]{:S(2)}, u32[]{:S(2)}) %collective-permute-start.26) | collective-permute-done | bytes 327712 | tf_op jit(solution)/shard_map/ppermute | solution.py:33
  96.8 2.2 %finish.1 = bf16[768,512]{1,0:T(8,128)(2,1)} custom-call(s32[1]{0:T(128)} %bitcast.core_ref, s32[1,6]{1,0:T(1,128)S(1)} %copy-done.20, f32[512,512]{1,0:T(8,128)S(1)} %base.1.base_ref, bf16[1024,256]{1,0:T(8,128)(2,1)S(1)} %collective-permute-done.21.refs_0_, bf16[1024,256]{1,0:T(8,128)(2,1)S(1)} %collective-permute-done.22.refs_1_, ...), custom_call_target="tpu_custom_call" | custom-call | flops 1 | bytes 1 | tf_op jit(solution)/shard_map/finish/pallas_call | solution.py:363
  (101 shorter events, 30.9 us)
Async XLA Ops:
  1.8 16.3 %collective-permute-start = (bf16[512,256]{1,0:T(8,128)(2,1)S(1)}, bf16[512,256]{1,0:T(8,128)(2,1)S(1)}, u32[]{:S(2)}, u32[]{:S(2)}) collective-permute-start(bf16[512,256]{1,0:T(8,128)(2,1)S(1)} %get-tuple-element.47), channel_id=1, source_target_pairs={{0,12},{4,8},{8,4},{12,0},{1,13},{5,9},{9,5},{13,1},{2,14},{6,10},... | collective-permute-start | bytes 786440 | tf_op jit(solution)/shard_map/ppermute | solution.py:33
  8.8 9.2 %collective-permute-start.1 = (bf16[32,2560]{1,0:T(8,128)(2,1)}, bf16[32,2560]{1,0:T(8,128)(2,1)S(1)}, u32[]{:S(2)}, u32[]{:S(2)}) collective-permute-start(bf16[32,2560]{1,0:T(8,128)(2,1)} %get-tuple-element.25), channel_id=1, source_target_pairs={{0,2},{2,0},{1,3},{3,1},{4,6},{6,4},{5,7},{7,5},{8,10},{10,8},{9,1... | collective-permute-start | bytes 491528 | tf_op jit(solution)/shard_map/ppermute | solution.py:29
  10.2 7.9 %collective-permute-start.2 = (bf16[32,2560]{1,0:T(8,128)(2,1)}, bf16[32,2560]{1,0:T(8,128)(2,1)S(1)}, u32[]{:S(2)}, u32[]{:S(2)}) collective-permute-start(bf16[32,2560]{1,0:T(8,128)(2,1)} %get-tuple-element.26), channel_id=1, source_target_pairs={{0,2},{2,0},{1,3},{3,1},{4,6},{6,4},{5,7},{7,5},{8,10},{10,8},{9,1... | collective-permute-start | bytes 491528 | tf_op jit(solution)/shard_map/ppermute | solution.py:29
  18.2 7.5 %collective-permute-start.4 = (bf16[64,2560]{1,0:T(8,128)(2,1)S(1)}, bf16[64,2560]{1,0:T(8,128)(2,1)S(1)}, u32[]{:S(2)}, u32[]{:S(2)}) collective-permute-start(bf16[64,2560]{1,0:T(8,128)(2,1)S(1)} %constant_dynamic-update-slice_fusion.refs_0_), channel_id=1, source_target_pairs={{0,1},{1,0},{2,3},{3,2},{4,5},{5,4},{6,7},{7,6},{8,9},{9,8},{10,11... | collective-permute-start | bytes 983048 | tf_op jit(solution)/shard_map/ppermute | solution.py:33
  18.8 14.7 %collective-permute-start.5 = (bf16[512,256]{1,0:T(8,128)(2,1)S(1)}, bf16[512,256]{1,0:T(8,128)(2,1)S(1)}, u32[]{:S(2)}, u32[]{:S(2)}) collective-permute-start(bf16[512,256]{1,0:T(8,128)(2,1)S(1)} %get-tuple-element.29), channel_id=1, source_target_pairs={{0,8},{4,12},{8,0},{12,4},{1,9},{5,13},{9,1},{13,5},{2,10},{6,14},... | collective-permute-start | bytes 786440 | tf_op jit(solution)/shard_map/ppermute | solution.py:33
  20.2 15.3 %collective-permute-start.9 = (bf16[512,256]{1,0:T(8,128)(2,1)S(1)}, bf16[512,256]{1,0:T(8,128)(2,1)S(1)}, u32[]{:S(2)}, u32[]{:S(2)}) collective-permute-start(bf16[512,256]{1,0:T(8,128)(2,1)S(1)} %collective-permute-done.refs_0_), channel_id=1, source_target_pairs={{0,2},{2,0},{16,18},{18,16},{1,3},{3,1},{17,19},{19,17},{4,6},{6,4... | collective-permute-start | bytes 786440 | tf_op jit(solution)/shard_map/ppermute | solution.py:33
  21.7 13.8 %collective-permute-start.10 = (bf16[512,256]{1,0:T(8,128)(2,1)S(1)}, bf16[512,256]{1,0:T(8,128)(2,1)S(1)}, u32[]{:S(2)}, u32[]{:S(2)}) collective-permute-start(bf16[512,256]{1,0:T(8,128)(2,1)S(1)} %collective-permute-done.refs_0_), channel_id=1, source_target_pairs={{0,16},{2,18},{16,0},{18,2},{1,17},{3,19},{17,1},{19,3},{4,20},{6,... | collective-permute-start | bytes 786440 | tf_op jit(solution)/shard_map/ppermute | solution.py:33
  23.2 12.3 %collective-permute-start.11 = (bf16[512,256]{1,0:T(8,128)(2,1)S(1)}, bf16[512,256]{1,0:T(8,128)(2,1)S(1)}, u32[]{:S(2)}, u32[]{:S(2)}) collective-permute-start(bf16[512,256]{1,0:T(8,128)(2,1)S(1)} %collective-permute-done.refs_0_), channel_id=1, source_target_pairs={{0,18},{2,16},{16,2},{18,0},{1,19},{3,17},{17,3},{19,1},{4,22},{6,... | collective-permute-start | bytes 786440 | tf_op jit(solution)/shard_map/ppermute | solution.py:33
  33.5 6.9 %collective-permute-start.6 = (bf16[512,128]{1,0:T(8,128)(2,1)S(1)}, bf16[512,128]{1,0:T(8,128)(2,1)S(1)}, u32[]{:S(2)}, u32[]{:S(2)}) collective-permute-start(bf16[512,128]{1,0:T(8,128)(2,1)S(1)} %low_part.1), channel_id=1, source_target_pairs={{0,4},{4,0},{8,12},{12,8},{1,5},{5,1},{9,13},{13,9},{2,6},{6,2},{1... | collective-permute-start | bytes 393224 | tf_op jit(solution)/shard_map/ppermute | solution.py:33
  33.5 11.1 %collective-permute-start.12 = (bf16[512,256]{1,0:T(8,128)(2,1)S(1)}, bf16[512,256]{1,0:T(8,128)(2,1)}, u32[]{:S(2)}, u32[]{:S(2)}) collective-permute-start(bf16[512,256]{1,0:T(8,128)(2,1)S(1)} %get-tuple-element.33), channel_id=1, source_target_pairs={{0,4},{4,0},{8,12},{12,8},{1,5},{5,1},{9,13},{13,9},{2,6},{6,2},{1... | collective-permute-start | bytes 786440 | tf_op jit(solution)/shard_map/ppermute | solution.py:33
  35.5 10.5 %collective-permute-start.13 = (bf16[512,256]{1,0:T(8,128)(2,1)S(1)}, bf16[512,256]{1,0:T(8,128)(2,1)S(1)}, u32[]{:S(2)}, u32[]{:S(2)}) collective-permute-start(bf16[512,256]{1,0:T(8,128)(2,1)S(1)} %collective-permute-done.5.refs_0_), channel_id=1, source_target_pairs={{0,2},{2,0},{16,18},{18,16},{1,3},{3,1},{17,19},{19,17},{4,6},{6,4... | collective-permute-start | bytes 786440 | tf_op jit(solution)/shard_map/ppermute | solution.py:33
  37.1 13.0 %collective-permute-start.14 = (bf16[512,256]{1,0:T(8,128)(2,1)S(1)}, bf16[512,256]{1,0:T(8,128)(2,1)S(1)}, u32[]{:S(2)}, u32[]{:S(2)}) collective-permute-start(bf16[512,256]{1,0:T(8,128)(2,1)S(1)} %collective-permute-done.5.refs_0_), channel_id=1, source_target_pairs={{0,16},{2,18},{16,0},{18,2},{1,17},{3,19},{17,1},{19,3},{4,20},{6,... | collective-permute-start | bytes 786440 | tf_op jit(solution)/shard_map/ppermute | solution.py:33
  38.6 12.2 %collective-permute-start.15 = (bf16[512,256]{1,0:T(8,128)(2,1)S(1)}, bf16[512,256]{1,0:T(8,128)(2,1)S(1)}, u32[]{:S(2)}, u32[]{:S(2)}) collective-permute-start(bf16[512,256]{1,0:T(8,128)(2,1)S(1)} %collective-permute-done.5.refs_0_), channel_id=1, source_target_pairs={{0,18},{2,16},{16,2},{18,0},{1,19},{3,17},{17,3},{19,1},{4,22},{6,... | collective-permute-start | bytes 786440 | tf_op jit(solution)/shard_map/ppermute | solution.py:33
  40.4 23.8 %collective-permute-start.16 = (bf16[1024,256]{1,0:T(8,128)(2,1)S(1)}, bf16[1024,256]{1,0:T(8,128)(2,1)}, u32[]{:S(2)}, u32[]{:S(2)}) collective-permute-start(bf16[1024,256]{1,0:T(8,128)(2,1)S(1)} %panel.3.own_ref), channel_id=1, source_target_pairs={{0,4},{12,8},{1,5},{13,9},{2,6},{14,10},{3,7},{15,11},{16,20},{28,... | collective-permute-start | bytes 1572872 | tf_op jit(solution)/shard_map/ppermute | solution.py:421
  44.6 10.4 %collective-permute-start.7 = (bf16[512,128]{1,0:T(8,128)(2,1)S(1)}, bf16[512,128]{1,0:T(8,128)(2,1)}, u32[]{:S(2)}, u32[]{:S(2)}) collective-permute-start(bf16[512,128]{1,0:T(8,128)(2,1)S(1)} %add_convert_fusion.2), channel_id=1, source_target_pairs={{4,8},{8,4},{5,9},{9,5},{6,10},{10,6},{7,11},{11,7},{20,24},{24,20... | collective-permute-start | bytes 393224 | tf_op jit(solution)/shard_map/ppermute | solution.py:424
  51.5 16.6 %collective-permute-start.18 = (bf16[512,256]{1,0:T(8,128)(2,1)}, bf16[512,256]{1,0:T(8,128)(2,1)}, u32[]{:S(2)}, u32[]{:S(2)}) collective-permute-start(bf16[512,256]{1,0:T(8,128)(2,1)} %collective-permute-done.12.refs_0_), channel_id=1, source_target_pairs={{0,2},{2,0},{16,18},{18,16},{1,3},{3,1},{17,19},{19,17},{4,6},{6,4... | collective-permute-start | bytes 786440 | tf_op jit(solution)/shard_map/ppermute | solution.py:33
  52.0 16.1 %collective-permute-start.19 = (bf16[512,256]{1,0:T(8,128)(2,1)}, bf16[512,256]{1,0:T(8,128)(2,1)}, u32[]{:S(2)}, u32[]{:S(2)}) collective-permute-start(bf16[512,256]{1,0:T(8,128)(2,1)} %collective-permute-done.12.refs_0_), channel_id=1, source_target_pairs={{0,16},{2,18},{16,0},{18,2},{1,17},{3,19},{17,1},{19,3},{4,20},{6,... | collective-permute-start | bytes 786440 | tf_op jit(solution)/shard_map/ppermute | solution.py:33
  53.6 14.5 %collective-permute-start.20 = (bf16[512,256]{1,0:T(8,128)(2,1)}, bf16[512,256]{1,0:T(8,128)(2,1)}, u32[]{:S(2)}, u32[]{:S(2)}) collective-permute-start(bf16[512,256]{1,0:T(8,128)(2,1)} %collective-permute-done.12.refs_0_), channel_id=1, source_target_pairs={{0,18},{2,16},{16,2},{18,0},{1,19},{3,17},{17,3},{19,1},{4,22},{6,... | collective-permute-start | bytes 786440 | tf_op jit(solution)/shard_map/ppermute | solution.py:33
  56.0 25.6 %collective-permute-start.8 = (bf16[512,128]{1,0:T(8,128)(2,1)S(1)}, bf16[512,128]{1,0:T(8,128)(2,1)S(1)}, u32[]{:S(2)}, u32[]{:S(2)}) collective-permute-start(bf16[512,128]{1,0:T(8,128)(2,1)S(1)} %add_convert_fusion.1), channel_id=1, source_target_pairs={{4,0},{8,12},{5,1},{9,13},{6,2},{10,14},{7,3},{11,15},{20,16},{24,... | collective-permute-start | bytes 393224 | tf_op jit(solution)/shard_map/ppermute | solution.py:427
  65.4 15.1 %collective-permute-start.17 = (bf16[1024,256]{1,0:T(8,128)(2,1)S(1)}, bf16[1024,256]{1,0:T(8,128)(2,1)S(1)}, u32[]{:S(2)}, u32[]{:S(2)}) collective-permute-start(bf16[1024,256]{1,0:T(8,128)(2,1)S(1)} %join.1), channel_id=1, source_target_pairs={{0,4},{12,8},{4,12},{8,0},{1,5},{13,9},{5,13},{9,1},{2,6},{14,10},... | collective-permute-start | bytes 1572872 | tf_op jit(solution)/shard_map/ppermute | solution.py:426
  70.6 17.6 %collective-permute-start.22 = (bf16[1024,256]{1,0:T(8,128)(2,1)S(1)}, bf16[1024,256]{1,0:T(8,128)(2,1)S(1)}, u32[]{:S(2)}, u32[]{:S(2)}) collective-permute-start(bf16[1024,256]{1,0:T(8,128)(2,1)S(1)} %panel.5), channel_id=1, source_target_pairs={{0,4},{4,0},{8,12},{12,8},{1,5},{5,1},{9,13},{13,9},{2,6},{6,2},{1... | collective-permute-start | bytes 1572872 | tf_op jit(solution)/shard_map/ppermute | solution.py:33
  80.7 6.0 %collective-permute-start.21 = (bf16[1024,256]{1,0:T(8,128)(2,1)S(1)}, bf16[1024,256]{1,0:T(8,128)(2,1)S(1)}, u32[]{:S(2)}, u32[]{:S(2)}) collective-permute-start(bf16[1024,256]{1,0:T(8,128)(2,1)S(1)} %get-tuple-element.37), channel_id=1, source_target_pairs={{4,8},{8,4},{5,9},{9,5},{6,10},{10,6},{7,11},{11,7},{20,24},{24,20... | collective-permute-start | bytes 1572872 | tf_op jit(solution)/shard_map/ppermute | solution.py:432
  84.1 9.8 %collective-permute-start.25 = (bf16[64,2560]{1,0:T(8,128)(2,1)S(1)}, bf16[64,2560]{1,0:T(8,128)(2,1)S(1)}, u32[]{:S(2)}, u32[]{:S(2)}) collective-permute-start(bf16[64,2560]{1,0:T(8,128)(2,1)S(1)} %get-tuple-element.42), channel_id=1, source_target_pairs={{0,2},{2,0},{1,3},{3,1},{4,6},{6,4},{5,7},{7,5},{8,10},{10,8},{9,1... | collective-permute-start | bytes 983048 | tf_op jit(solution)/shard_map/ppermute | solution.py:29
  88.3 8.6 %collective-permute-start.23 = (f32[512,256]{1,0:T(8,128)S(1)}, f32[512,256]{1,0:T(8,128)S(1)}, u32[]{:S(2)}, u32[]{:S(2)}) collective-permute-start(f32[512,256]{1,0:T(8,128)S(1)} %other_rows.1), channel_id=1, source_target_pairs={{0,1},{1,0},{2,3},{3,2},{4,5},{5,4},{6,7},{7,6},{8,9},{9,8},{10,11... | collective-permute-start | bytes 1572872 | tf_op jit(solution)/shard_map/ppermute | solution.py:33
  (28 other events, 174.8 us)

commit v16 on v11

--- a/solution.py
+++ b/solution.py
@@ -415,9 +415,10 @@
         near = lax.ppermute(after(y_2, low), "tensor", [(0, 1), (3, 2), (1, 3), (2, 0)])
         pieces, order = gathered(after(weight[1], *pieces))
         (y_1,) = panel_product(order, panel_at, x, x_other, pieces, half)
-        part_1 = flip(y_1, "tensor", n_t, 1)
+        part_1 = lax.ppermute(y_1, "tensor", [(0, 1), (3, 2)])
         passed, kept = relay(at, y_3, near)
-        parts = [lax.ppermute(passed, "tensor", [(1, 2), (2, 1)]), part_1, kept]
+        part_end = lax.ppermute(after(y_1, passed), "tensor", [(1, 0), (2, 3)])
+        parts = [lax.ppermute(passed, "tensor", [(1, 2), (2, 1)]), part_1, part_end, kept]
     else:
         x = pack(block_fill, block_tenant_index, tokens, cotangent, blocks, 2 * rank)
         x_other = flip(x, "pipe", n_pipe, 1)

time: 88.8 us -> 92.4 us (1.041)
  starting transfers between devices: 29.7 us -> 32.5 us
  waiting for transfers between devices: 34.1 us -> 35.6 us
    ppermute x1 -> x3, waiting for transfers between devices: 0.01 us -> 9.85 us  [the longest x1 7.32 us: body(): part_end = lax.ppermute(after(y_1, passed), 'tensor', [(1, 0), (2, 3)])]
    ppermute x20 -> x19, waiting for transfers between devices: 27.6 us -> 21.3 us  [flip(): return lax.ppermute(x, names, [(i, i ^ mask) for i in range(count)])]
    ppermute x1 -> x3, starting transfers between devices: 0.69 us -> 4.56 us  [the longest x1 2.57 us: body(): part_1 = lax.ppermute(y_1, 'tensor', [(0, 1), (3, 2)])]
    ppermute x1, waiting for transfers between devices: 6.3 us -> 4.32 us  [body(): lax.ppermute(after(y_2, low), 'tensor', [(0, 1), (3, 2), (1, 3), (2, 0)])]
    ppermute x20 -> x19, starting transfers between devices: 22.5 us -> 20.9 us  [flip(): return lax.ppermute(x, names, [(i, i ^ mask) for i in range(count)])]
  transfers between devices with their start and end apart: 26 -> 27, of which waited for: 11 -> 12; matrix products, arithmetic and copies ran while one was open for 0% -> 0% of each run, Pallas kernels for 17% -> 16%
where the time goes in v16:
time: 92.4 us; the launch traced here: 92.1 us
  waiting for transfers between devices  35.6 us (39%)
  starting transfers between devices  32.5 us (35%)
  Pallas kernels  17.4 us (19%)
  local copies, waits for them, and re-layouts  5.55 us (6%)
    ppermute x19, waiting for transfers between devices, flip(): return lax.ppermute(x, names, [(i, i ^ mask) for i in range(count)])  21.3 us
    ppermute x19, starting transfers between devices, flip(): return lax.ppermute(x, names, [(i, i ^ mask) for i in range(count)])  20.9 us
    ppermute x1, waiting for transfers between devices, body(): part_end = lax.ppermute(after(y_1, passed), 'tensor', [(1, 0), (2, 3)])  7.32 us
    unnamed x21, local copies, waits for them, and re-layouts  4.36 us
    ppermute x1, waiting for transfers between devices, body(): lax.ppermute(after(y_2, low), 'tensor', [(0, 1), (3, 2), (1, 3), (2, 0)])  4.32 us
    pallas_call x3, Pallas kernels, panel_product(): pl.pallas_call(functools.partial(panel_kernel, order, len(pieces)), in_sp...  3.75 us
    pallas_call x1, Pallas kernels, pack(): pl.pallas_call(functools.partial(pack_kernel, blocks, rows // blocks), in...  2.83 us
    ppermute x3, starting transfers between devices, shift(): lax.ppermute(x, name, [(i, (i + step) % count) for i in range(count)])  2.67 us
  transfers between devices with their start and end apart: 27, of which 12 were waited for; matrix products, arithmetic and copies ran while one was open for 0% of the time, Pallas kernels for 16%

profile of v16, /device:TPU:0, one launch (start us, length us, event | category | flops | bytes accessed | tf_op | source)
XLA Modules:
  0.0 92.1 jit_solution(9186921157909707075)
XLA Ops:
  1.8 5.1 %collective-permute-start = (bf16[512,256]{1,0:T(8,128)(2,1)S(1)}, bf16[512,256]{1,0:T(8,128)(2,1)S(1)}, u32[]{:S(2)}, u32[]{:S(2)}) collective-permute-start(bf16[512,256]{1,0:T(8,128)(2,1)S(1)} %get-tuple-element.49), channel_id=1, source_target_pairs={{0,12},{4,8},{8,4},{12,0},{1,13},{5,9},{9,5},{13,1},{2,14},{6,10},... | collective-permute-start | bytes 786440 | tf_op jit(solution)/shard_map/ppermute | solution.py:33
  6.9 1.8 %own_half.1 = (bf16[32,2560]{1,0:T(8,128)(2,1)}, bf16[32,2560]{1,0:T(8,128)(2,1)}) custom-call(s32[1]{0:T(128)} %bitcast.core_ref, bf16[128,2048]{1,0:T(8,128)(2,1)} %bitcast.8, bf16[128,512]{1,0:T(8,128)(2,1)} %bitcast.10), custom_call_target="tpu_custom_call" | custom-call | flops 1 | bytes 1 | tf_op jit(solution)/shard_map/own_half/pallas_call | solution.py:75
  8.8 1.5 %collective-permute-start.1 = (bf16[32,2560]{1,0:T(8,128)(2,1)}, bf16[32,2560]{1,0:T(8,128)(2,1)S(1)}, u32[]{:S(2)}, u32[]{:S(2)}) collective-permute-start(bf16[32,2560]{1,0:T(8,128)(2,1)} %get-tuple-element.26), channel_id=1, source_target_pairs={{0,2},{2,0},{1,3},{3,1},{4,6},{6,4},{5,7},{7,5},{8,10},{10,8},{9,1... | collective-permute-start | bytes 491528 | tf_op jit(solution)/shard_map/ppermute | solution.py:29
  10.8 1.9 %copy-done = bf16[768,2048]{1,0:T(8,128)(2,1)S(1)} copy-done((bf16[768,2048]{1,0:T(8,128)(2,1)S(1)}, bf16[768,2048]{1,0:T(8,128)(2,1)}, u32[]{:S(2)}) %copy-start) | copy-done | bytes 3145752
  15.1 2.8 %pack.1.x_ref.own_ref = bf16[512,2688]{1,0:T(8,128)(2,1)S(1)} custom-call(s32[1,6]{1,0:T(1,128)S(1)} %copy-done.4, s32[6]{0:T(128)S(1)} %copy-done.6, bf16[768,2048]{1,0:T(8,128)(2,1)S(1)} %copy-done, bf16[768,512]{1,0:T(8,128)(2,1)S(1)} %copy-done.3), custom_call_target="tpu_custom_call" | custom-call | flops 1 | bytes 1 | tf_op jit(solution)/shard_map/pack/pallas_call | solution.py:104
  20.2 2.4 %collective-permute-start.10 = (bf16[512,256]{1,0:T(8,128)(2,1)S(1)}, bf16[512,256]{1,0:T(8,128)(2,1)S(1)}, u32[]{:S(2)}, u32[]{:S(2)}) collective-permute-start(bf16[512,256]{1,0:T(8,128)(2,1)S(1)} %collective-permute-done.refs_0_), channel_id=1, source_target_pairs={{0,18},{2,16},{16,2},{18,0},{1,19},{3,17},{17,3},{19,1},{4,22},{6,... | collective-permute-start | bytes 786440 | tf_op jit(solution)/shard_map/ppermute | solution.py:33
  23.2 1.5 %collective-permute-start.9 = (bf16[512,256]{1,0:T(8,128)(2,1)S(1)}, bf16[512,256]{1,0:T(8,128)(2,1)S(1)}, u32[]{:S(2)}, u32[]{:S(2)}) collective-permute-start(bf16[512,256]{1,0:T(8,128)(2,1)S(1)} %collective-permute-done.refs_0_), channel_id=1, source_target_pairs={{0,16},{2,18},{16,0},{18,2},{1,17},{3,19},{17,1},{19,3},{4,20},{6,... | collective-permute-start | bytes 786440 | tf_op jit(solution)/shard_map/ppermute | solution.py:33
  24.8 2.2 %low_part.1 = bf16[512,128]{1,0:T(8,128)(2,1)S(1)} custom-call(s32[1]{0:T(128)} %bitcast.2.dp_ref, s32[1]{0:T(128)} %bitcast.core_ref, s32[1,6]{1,0:T(1,128)S(1)} %copy-done.4, s32[6]{0:T(128)S(1)} %copy-done.6, bf16[512,2688]{1,0:T(8,128)(2,1)S(1)} %pack.1.x_ref.own_ref, bf16[128,2048]{1,0:T(8,128)(2,1)S(1)} %bitcast.9, bf16[128,512]{1,0:T(8,128)(2,1)S(1)} %bitcast.11, ...), custom_call_target="tpu_custom_call" | custom-call | flops 1 | bytes 1 | tf_op jit(solution)/shard_map/low_part/pallas_call | solution.py:147
  26.9 6.5 %collective-permute-done.5.refs_0_ = bf16[512,256]{1,0:T(8,128)(2,1)S(1)} collective-permute-done((bf16[512,256]{1,0:T(8,128)(2,1)S(1)}, bf16[512,256]{1,0:T(8,128)(2,1)S(1)}, u32[]{:S(2)}, u32[]{:S(2)}) %collective-permute-start.5) | collective-permute-done | bytes 262176 | tf_op jit(solution)/shard_map/ppermute | solution.py:33
  33.4 2.0 %collective-permute-start.11 = (bf16[512,256]{1,0:T(8,128)(2,1)S(1)}, bf16[512,256]{1,0:T(8,128)(2,1)S(1)}, u32[]{:S(2)}, u32[]{:S(2)}) collective-permute-start(bf16[512,256]{1,0:T(8,128)(2,1)S(1)} %get-tuple-element.34), channel_id=1, source_target_pairs={{0,4},{4,0},{8,12},{12,8},{1,5},{5,1},{9,13},{13,9},{2,6},{6,2},{1... | collective-permute-start | bytes 786440 | tf_op jit(solution)/shard_map/ppermute | solution.py:33
  35.5 1.6 %collective-permute-start.12 = (bf16[512,256]{1,0:T(8,128)(2,1)S(1)}, bf16[512,256]{1,0:T(8,128)(2,1)S(1)}, u32[]{:S(2)}, u32[]{:S(2)}) collective-permute-start(bf16[512,256]{1,0:T(8,128)(2,1)S(1)} %collective-permute-done.5.refs_0_), channel_id=1, source_target_pairs={{0,2},{2,0},{16,18},{18,16},{1,3},{3,1},{17,19},{19,17},{4,6},{6,4... | collective-permute-start | bytes 786440 | tf_op jit(solution)/shard_map/ppermute | solution.py:33
  37.0 1.5 %collective-permute-start.13 = (bf16[512,256]{1,0:T(8,128)(2,1)S(1)}, bf16[512,256]{1,0:T(8,128)(2,1)S(1)}, u32[]{:S(2)}, u32[]{:S(2)}) collective-permute-start(bf16[512,256]{1,0:T(8,128)(2,1)S(1)} %collective-permute-done.5.refs_0_), channel_id=1, source_target_pairs={{0,16},{2,18},{16,0},{18,2},{1,17},{3,19},{17,1},{19,3},{4,20},{6,... | collective-permute-start | bytes 786440 | tf_op jit(solution)/shard_map/ppermute | solution.py:33
  40.3 2.0 %collective-permute-start.15 = (bf16[1024,256]{1,0:T(8,128)(2,1)S(1)}, bf16[1024,256]{1,0:T(8,128)(2,1)S(1)}, u32[]{:S(2)}, u32[]{:S(2)}) collective-permute-start(bf16[1024,256]{1,0:T(8,128)(2,1)S(1)} %panel.3.own_ref), channel_id=1, source_target_pairs={{0,4},{12,8},{1,5},{13,9},{2,6},{14,10},{3,7},{15,11},{16,20},{28,... | collective-permute-start | bytes 1572872 | tf_op jit(solution)/shard_map/ppermute | solution.py:410
  42.3 2.2 %collective-permute-done.11.refs_0_ = bf16[512,256]{1,0:T(8,128)(2,1)S(1)} collective-permute-done((bf16[512,256]{1,0:T(8,128)(2,1)S(1)}, bf16[512,256]{1,0:T(8,128)(2,1)S(1)}, u32[]{:S(2)}, u32[]{:S(2)}) %collective-permute-start.11) | collective-permute-done | bytes 262176 | tf_op jit(solution)/shard_map/ppermute | solution.py:33
  44.8 5.3 %collective-permute-done.13.refs_2_ = bf16[512,256]{1,0:T(8,128)(2,1)S(1)} collective-permute-done((bf16[512,256]{1,0:T(8,128)(2,1)S(1)}, bf16[512,256]{1,0:T(8,128)(2,1)S(1)}, u32[]{:S(2)}, u32[]{:S(2)}) %collective-permute-start.13) | collective-permute-done | bytes 262176 | tf_op jit(solution)/shard_map/ppermute | solution.py:33
  53.5 2.8 %collective-permute-done.7 = bf16[512,128]{1,0:T(8,128)(2,1)S(1)} collective-permute-done((bf16[512,128]{1,0:T(8,128)(2,1)S(1)}, bf16[512,128]{1,0:T(8,128)(2,1)S(1)}, u32[]{:S(2)}, u32[]{:S(2)}) %collective-permute-start.7) | collective-permute-done | bytes 131104 | tf_op jit(solution)/shard_map/ppermute | solution.py:33
  57.6 2.4 %collective-permute-start.16 = (bf16[1024,256]{1,0:T(8,128)(2,1)S(1)}, bf16[1024,256]{1,0:T(8,128)(2,1)S(1)}, u32[]{:S(2)}, u32[]{:S(2)}) collective-permute-start(bf16[1024,256]{1,0:T(8,128)(2,1)S(1)} %panel.4), channel_id=1, source_target_pairs={{0,4},{12,8},{4,12},{8,0},{1,5},{13,9},{5,13},{9,1},{2,6},{14,10},... | collective-permute-start | bytes 1572872 | tf_op jit(solution)/shard_map/ppermute | solution.py:415
  65.3 2.6 %collective-permute-start.24 = (bf16[1024,256]{1,0:T(8,128)(2,1)S(1)}, bf16[1024,256]{1,0:T(8,128)(2,1)S(1)}, u32[]{:S(2)}, u32[]{:S(2)}) collective-permute-start(bf16[1024,256]{1,0:T(8,128)(2,1)S(1)} %panel.5), channel_id=1, source_target_pairs={{0,4},{12,8},{1,5},{13,9},{2,6},{14,10},{3,7},{15,11},{16,20},{28,... | collective-permute-start | bytes 1572872 | tf_op jit(solution)/shard_map/ppermute | solution.py:418
  67.9 4.3 %collective-permute-done.16.got_ref = bf16[1024,256]{1,0:T(8,128)(2,1)S(1)} collective-permute-done((bf16[1024,256]{1,0:T(8,128)(2,1)S(1)}, bf16[1024,256]{1,0:T(8,128)(2,1)S(1)}, u32[]{:S(2)}, u32[]{:S(2)}) %collective-permute-start.16) | collective-permute-done | bytes 524320 | tf_op jit(solution)/shard_map/ppermute | solution.py:415
  74.6 2.1 %base.1.base_ref = f32[512,512]{1,0:T(8,128)S(1)} custom-call(s32[1]{0:T(128)} %bitcast.1.at_ref, s32[1]{0:T(128)} %bitcast.2.dp_ref, s32[1]{0:T(128)} %bitcast.core_ref, s32[1,6]{1,0:T(1,128)S(1)} %copy-done.5, s32[6]{0:T(128)S(1)} %copy-done.7, bf16[512,2688]{1,0:T(8,128)(2,1)S(1)} %pack.1.x_ref.own_ref, bf16[8192,512]{1,0:T(8,128)(2,1)S(1)} %bitcast.7, ...), custom_call_target="tpu_custom_call" | custom-call | flops 1 | bytes 1 | tf_op jit(solution)/shard_map/base/pallas_call | solution.py:271
  78.0 2.5 %collective-permute-done.24.refs_1_ = bf16[1024,256]{1,0:T(8,128)(2,1)S(1)} collective-permute-done((bf16[1024,256]{1,0:T(8,128)(2,1)S(1)}, bf16[1024,256]{1,0:T(8,128)(2,1)S(1)}, u32[]{:S(2)}, u32[]{:S(2)}) %collective-permute-start.24) | collective-permute-done | bytes 524320 | tf_op jit(solution)/shard_map/ppermute | solution.py:418
  80.5 7.3 %collective-permute-done.25.refs_2_ = bf16[1024,256]{1,0:T(8,128)(2,1)S(1)} collective-permute-done((bf16[1024,256]{1,0:T(8,128)(2,1)S(1)}, bf16[1024,256]{1,0:T(8,128)(2,1)S(1)}, u32[]{:S(2)}, u32[]{:S(2)}) %collective-permute-start.25) | collective-permute-done | bytes 524320 | tf_op jit(solution)/shard_map/ppermute | solution.py:420
  88.0 1.9 %collective-permute-done.26.refs_4_ = f32[512,256]{1,0:T(8,128)S(1)} collective-permute-done((f32[512,256]{1,0:T(8,128)S(1)}, f32[512,256]{1,0:T(8,128)S(1)}, u32[]{:S(2)}, u32[]{:S(2)}) %collective-permute-start.26) | collective-permute-done | bytes 524320 | tf_op jit(solution)/shard_map/ppermute | solution.py:33
  89.9 2.2 %finish.1 = bf16[768,512]{1,0:T(8,128)(2,1)} custom-call(s32[1]{0:T(128)} %bitcast.core_ref, s32[1,6]{1,0:T(1,128)S(1)} %copy-done.5, f32[512,512]{1,0:T(8,128)S(1)} %base.1.base_ref, bf16[1024,256]{1,0:T(8,128)(2,1)S(1)} %collective-permute-done.17.refs_0_, bf16[1024,256]{1,0:T(8,128)(2,1)S(1)} %collective-permute-done.24.refs_1_, ...), custom_call_target="tpu_custom_call" | custom-call | flops 1 | bytes 1 | tf_op jit(solution)/shard_map/finish/pallas_call | solution.py:352
  (69 shorter events, 22.8 us)
Async XLA Ops:
  1.8 16.3 %collective-permute-start = (bf16[512,256]{1,0:T(8,128)(2,1)S(1)}, bf16[512,256]{1,0:T(8,128)(2,1)S(1)}, u32[]{:S(2)}, u32[]{:S(2)}) collective-permute-start(bf16[512,256]{1,0:T(8,128)(2,1)S(1)} %get-tuple-element.49), channel_id=1, source_target_pairs={{0,12},{4,8},{8,4},{12,0},{1,13},{5,9},{9,5},{13,1},{2,14},{6,10},... | collective-permute-start | bytes 786440 | tf_op jit(solution)/shard_map/ppermute | solution.py:33
  8.8 9.2 %collective-permute-start.1 = (bf16[32,2560]{1,0:T(8,128)(2,1)}, bf16[32,2560]{1,0:T(8,128)(2,1)S(1)}, u32[]{:S(2)}, u32[]{:S(2)}) collective-permute-start(bf16[32,2560]{1,0:T(8,128)(2,1)} %get-tuple-element.26), channel_id=1, source_target_pairs={{0,2},{2,0},{1,3},{3,1},{4,6},{6,4},{5,7},{7,5},{8,10},{10,8},{9,1... | collective-permute-start | bytes 491528 | tf_op jit(solution)/shard_map/ppermute | solution.py:29
  10.2 7.9 %collective-permute-start.2 = (bf16[32,2560]{1,0:T(8,128)(2,1)}, bf16[32,2560]{1,0:T(8,128)(2,1)S(1)}, u32[]{:S(2)}, u32[]{:S(2)}) collective-permute-start(bf16[32,2560]{1,0:T(8,128)(2,1)} %get-tuple-element.27), channel_id=1, source_target_pairs={{0,2},{2,0},{1,3},{3,1},{4,6},{6,4},{5,7},{7,5},{8,10},{10,8},{9,1... | collective-permute-start | bytes 491528 | tf_op jit(solution)/shard_map/ppermute | solution.py:29
  18.1 5.1 %collective-permute-start.3 = (bf16[512,2688]{1,0:T(8,128)(2,1)S(1)}, bf16[512,2688]{1,0:T(8,128)(2,1)S(1)}, u32[]{:S(2)}, u32[]{:S(2)}) collective-permute-start(bf16[512,2688]{1,0:T(8,128)(2,1)S(1)} %pack.1.x_ref.own_ref), channel_id=1, source_target_pairs={{0,1},{1,0},{2,3},{3,2},{4,5},{5,4},{6,7},{7,6},{8,9},{9,8},{10,11... | collective-permute-start | bytes 8257544 | tf_op jit(solution)/shard_map/ppermute | solution.py:33
  18.2 6.6 %collective-permute-start.4 = (bf16[64,2560]{1,0:T(8,128)(2,1)S(1)}, bf16[64,2560]{1,0:T(8,128)(2,1)S(1)}, u32[]{:S(2)}, u32[]{:S(2)}) collective-permute-start(bf16[64,2560]{1,0:T(8,128)(2,1)S(1)} %constant_dynamic-update-slice_fusion.refs_0_), channel_id=1, source_target_pairs={{0,1},{1,0},{2,3},{3,2},{4,5},{5,4},{6,7},{7,6},{8,9},{9,8},{10,11... | collective-permute-start | bytes 983048 | tf_op jit(solution)/shard_map/ppermute | solution.py:33
  18.7 14.7 %collective-permute-start.5 = (bf16[512,256]{1,0:T(8,128)(2,1)S(1)}, bf16[512,256]{1,0:T(8,128)(2,1)S(1)}, u32[]{:S(2)}, u32[]{:S(2)}) collective-permute-start(bf16[512,256]{1,0:T(8,128)(2,1)S(1)} %get-tuple-element.30), channel_id=1, source_target_pairs={{0,8},{4,12},{8,0},{12,4},{1,9},{5,13},{9,1},{13,5},{2,10},{6,14},... | collective-permute-start | bytes 786440 | tf_op jit(solution)/shard_map/ppermute | solution.py:33
  20.2 15.3 %collective-permute-start.10 = (bf16[512,256]{1,0:T(8,128)(2,1)S(1)}, bf16[512,256]{1,0:T(8,128)(2,1)S(1)}, u32[]{:S(2)}, u32[]{:S(2)}) collective-permute-start(bf16[512,256]{1,0:T(8,128)(2,1)S(1)} %collective-permute-done.refs_0_), channel_id=1, source_target_pairs={{0,18},{2,16},{16,2},{18,0},{1,19},{3,17},{17,3},{19,1},{4,22},{6,... | collective-permute-start | bytes 786440 | tf_op jit(solution)/shard_map/ppermute | solution.py:33
  22.7 12.8 %collective-permute-start.8 = (bf16[512,256]{1,0:T(8,128)(2,1)S(1)}, bf16[512,256]{1,0:T(8,128)(2,1)S(1)}, u32[]{:S(2)}, u32[]{:S(2)}) collective-permute-start(bf16[512,256]{1,0:T(8,128)(2,1)S(1)} %collective-permute-done.refs_0_), channel_id=1, source_target_pairs={{0,2},{2,0},{16,18},{18,16},{1,3},{3,1},{17,19},{19,17},{4,6},{6,4... | collective-permute-start | bytes 786440 | tf_op jit(solution)/shard_map/ppermute | solution.py:33
  23.2 12.2 %collective-permute-start.9 = (bf16[512,256]{1,0:T(8,128)(2,1)S(1)}, bf16[512,256]{1,0:T(8,128)(2,1)S(1)}, u32[]{:S(2)}, u32[]{:S(2)}) collective-permute-start(bf16[512,256]{1,0:T(8,128)(2,1)S(1)} %collective-permute-done.refs_0_), channel_id=1, source_target_pairs={{0,16},{2,18},{16,0},{18,2},{1,17},{3,19},{17,1},{19,3},{4,20},{6,... | collective-permute-start | bytes 786440 | tf_op jit(solution)/shard_map/ppermute | solution.py:33
  33.4 6.8 %collective-permute-start.6 = (bf16[512,128]{1,0:T(8,128)(2,1)S(1)}, bf16[512,128]{1,0:T(8,128)(2,1)S(1)}, u32[]{:S(2)}, u32[]{:S(2)}) collective-permute-start(bf16[512,128]{1,0:T(8,128)(2,1)S(1)} %low_part.1), channel_id=1, source_target_pairs={{0,4},{4,0},{8,12},{12,8},{1,5},{5,1},{9,13},{13,9},{2,6},{6,2},{1... | collective-permute-start | bytes 393224 | tf_op jit(solution)/shard_map/ppermute | solution.py:33
  33.4 11.0 %collective-permute-start.11 = (bf16[512,256]{1,0:T(8,128)(2,1)S(1)}, bf16[512,256]{1,0:T(8,128)(2,1)S(1)}, u32[]{:S(2)}, u32[]{:S(2)}) collective-permute-start(bf16[512,256]{1,0:T(8,128)(2,1)S(1)} %get-tuple-element.34), channel_id=1, source_target_pairs={{0,4},{4,0},{8,12},{12,8},{1,5},{5,1},{9,13},{13,9},{2,6},{6,2},{1... | collective-permute-start | bytes 786440 | tf_op jit(solution)/shard_map/ppermute | solution.py:33
  35.5 9.3 %collective-permute-start.12 = (bf16[512,256]{1,0:T(8,128)(2,1)S(1)}, bf16[512,256]{1,0:T(8,128)(2,1)S(1)}, u32[]{:S(2)}, u32[]{:S(2)}) collective-permute-start(bf16[512,256]{1,0:T(8,128)(2,1)S(1)} %collective-permute-done.5.refs_0_), channel_id=1, source_target_pairs={{0,2},{2,0},{16,18},{18,16},{1,3},{3,1},{17,19},{19,17},{4,6},{6,4... | collective-permute-start | bytes 786440 | tf_op jit(solution)/shard_map/ppermute | solution.py:33
  37.0 13.0 %collective-permute-start.13 = (bf16[512,256]{1,0:T(8,128)(2,1)S(1)}, bf16[512,256]{1,0:T(8,128)(2,1)S(1)}, u32[]{:S(2)}, u32[]{:S(2)}) collective-permute-start(bf16[512,256]{1,0:T(8,128)(2,1)S(1)} %collective-permute-done.5.refs_0_), channel_id=1, source_target_pairs={{0,16},{2,18},{16,0},{18,2},{1,17},{3,19},{17,1},{19,3},{4,20},{6,... | collective-permute-start | bytes 786440 | tf_op jit(solution)/shard_map/ppermute | solution.py:33
  38.6 11.5 %collective-permute-start.14 = (bf16[512,256]{1,0:T(8,128)(2,1)S(1)}, bf16[512,256]{1,0:T(8,128)(2,1)S(1)}, u32[]{:S(2)}, u32[]{:S(2)}) collective-permute-start(bf16[512,256]{1,0:T(8,128)(2,1)S(1)} %collective-permute-done.5.refs_0_), channel_id=1, source_target_pairs={{0,18},{2,16},{16,2},{18,0},{1,19},{3,17},{17,3},{19,1},{4,22},{6,... | collective-permute-start | bytes 786440 | tf_op jit(solution)/shard_map/ppermute | solution.py:33
  40.3 16.1 %collective-permute-start.15 = (bf16[1024,256]{1,0:T(8,128)(2,1)S(1)}, bf16[1024,256]{1,0:T(8,128)(2,1)S(1)}, u32[]{:S(2)}, u32[]{:S(2)}) collective-permute-start(bf16[1024,256]{1,0:T(8,128)(2,1)S(1)} %panel.3.own_ref), channel_id=1, source_target_pairs={{0,4},{12,8},{1,5},{13,9},{2,6},{14,10},{3,7},{15,11},{16,20},{28,... | collective-permute-start | bytes 1572872 | tf_op jit(solution)/shard_map/ppermute | solution.py:410
  44.5 11.8 %collective-permute-start.7 = (bf16[512,128]{1,0:T(8,128)(2,1)S(1)}, bf16[512,128]{1,0:T(8,128)(2,1)S(1)}, u32[]{:S(2)}, u32[]{:S(2)}) collective-permute-start(bf16[512,128]{1,0:T(8,128)(2,1)S(1)} %add_convert_fusion.2), channel_id=1, source_target_pairs={{0,8},{4,12},{8,0},{12,4},{1,9},{5,13},{9,1},{13,5},{2,10},{6,14},... | collective-permute-start | bytes 393224 | tf_op jit(solution)/shard_map/ppermute | solution.py:33
  50.1 12.4 %collective-permute-start.19 = (bf16[512,256]{1,0:T(8,128)(2,1)S(1)}, bf16[512,256]{1,0:T(8,128)(2,1)S(1)}, u32[]{:S(2)}, u32[]{:S(2)}) collective-permute-start(bf16[512,256]{1,0:T(8,128)(2,1)S(1)} %collective-permute-done.11.refs_0_), channel_id=1, source_target_pairs={{0,2},{2,0},{16,18},{18,16},{1,3},{3,1},{17,19},{19,17},{4,6},{6,4... | collective-permute-start | bytes 786440 | tf_op jit(solution)/shard_map/ppermute | solution.py:33
  51.3 12.1 %collective-permute-start.20 = (bf16[512,256]{1,0:T(8,128)(2,1)S(1)}, bf16[512,256]{1,0:T(8,128)(2,1)S(1)}, u32[]{:S(2)}, u32[]{:S(2)}) collective-permute-start(bf16[512,256]{1,0:T(8,128)(2,1)S(1)} %collective-permute-done.11.refs_0_), channel_id=1, source_target_pairs={{0,16},{2,18},{16,0},{18,2},{1,17},{3,19},{17,1},{19,3},{4,20},{6,... | collective-permute-start | bytes 786440 | tf_op jit(solution)/shard_map/ppermute | solution.py:33
  52.1 11.3 %collective-permute-start.21 = (bf16[512,256]{1,0:T(8,128)(2,1)S(1)}, bf16[512,256]{1,0:T(8,128)(2,1)S(1)}, u32[]{:S(2)}, u32[]{:S(2)}) collective-permute-start(bf16[512,256]{1,0:T(8,128)(2,1)S(1)} %collective-permute-done.11.refs_0_), channel_id=1, source_target_pairs={{0,18},{2,16},{16,2},{18,0},{1,19},{3,17},{17,3},{19,1},{4,22},{6,... | collective-permute-start | bytes 786440 | tf_op jit(solution)/shard_map/ppermute | solution.py:33
  57.6 14.6 %collective-permute-start.16 = (bf16[1024,256]{1,0:T(8,128)(2,1)S(1)}, bf16[1024,256]{1,0:T(8,128)(2,1)S(1)}, u32[]{:S(2)}, u32[]{:S(2)}) collective-permute-start(bf16[1024,256]{1,0:T(8,128)(2,1)S(1)} %panel.4), channel_id=1, source_target_pairs={{0,4},{12,8},{4,12},{8,0},{1,5},{13,9},{5,13},{9,1},{2,6},{14,10},... | collective-permute-start | bytes 1572872 | tf_op jit(solution)/shard_map/ppermute | solution.py:415
  63.4 11.0 %collective-permute-start.22 = (bf16[64,2560]{1,0:T(8,128)(2,1)S(1)}, bf16[64,2560]{1,0:T(8,128)(2,1)S(1)}, u32[]{:S(2)}, u32[]{:S(2)}) collective-permute-start(bf16[64,2560]{1,0:T(8,128)(2,1)S(1)} %get-tuple-element.41), channel_id=1, source_target_pairs={{0,2},{2,0},{1,3},{3,1},{4,6},{6,4},{5,7},{7,5},{8,10},{10,8},{9,1... | collective-permute-start | bytes 983048 | tf_op jit(solution)/shard_map/ppermute | solution.py:29
  65.3 15.2 %collective-permute-start.24 = (bf16[1024,256]{1,0:T(8,128)(2,1)S(1)}, bf16[1024,256]{1,0:T(8,128)(2,1)S(1)}, u32[]{:S(2)}, u32[]{:S(2)}) collective-permute-start(bf16[1024,256]{1,0:T(8,128)(2,1)S(1)} %panel.5), channel_id=1, source_target_pairs={{0,4},{12,8},{1,5},{13,9},{2,6},{14,10},{3,7},{15,11},{16,20},{28,... | collective-permute-start | bytes 1572872 | tf_op jit(solution)/shard_map/ppermute | solution.py:418
  72.4 5.6 %collective-permute-start.17 = (bf16[1024,256]{1,0:T(8,128)(2,1)S(1)}, bf16[1024,256]{1,0:T(8,128)(2,1)S(1)}, u32[]{:S(2)}, u32[]{:S(2)}) collective-permute-start(bf16[1024,256]{1,0:T(8,128)(2,1)S(1)} %get-tuple-element.37), channel_id=1, source_target_pairs={{4,8},{8,4},{5,9},{9,5},{6,10},{10,6},{7,11},{11,7},{20,24},{24,20... | collective-permute-start | bytes 1572872 | tf_op jit(solution)/shard_map/ppermute | solution.py:421
  73.1 14.7 %collective-permute-start.25 = (bf16[1024,256]{1,0:T(8,128)(2,1)S(1)}, bf16[1024,256]{1,0:T(8,128)(2,1)S(1)}, u32[]{:S(2)}, u32[]{:S(2)}) collective-permute-start(bf16[1024,256]{1,0:T(8,128)(2,1)S(1)} %panel.5), channel_id=1, source_target_pairs={{4,0},{8,12},{5,1},{9,13},{6,2},{10,14},{7,3},{11,15},{20,16},{24,... | collective-permute-start | bytes 1572872 | tf_op jit(solution)/shard_map/ppermute | solution.py:420
  (13 other events, 76.0 us)

commit v17 on v11

--- a/solution.py
+++ b/solution.py
@@ -83,30 +83,53 @@
     )(core, a, b)
 
 
-def pack_kernel(blocks, block, fill_ref, tenant_ref, tok_ref, cot_ref, out_ref, pick):
-    feat, cols = tok_ref.shape[1], cot_ref.shape[1]
+def pack_kernel(blocks, block, fill_hbm, tenant_hbm, tok_hbm, cot_hbm, out_ref, pick, tok, cot, fill, tenant, sems):
+    feat, cols = tok_hbm.shape[1], cot_hbm.shape[1]
+    wide = tok.shape[2]
+    small = [
+        pltpu.make_async_copy(fill_hbm, fill, sems.at[0]),
+        pltpu.make_async_copy(tenant_hbm, tenant, sems.at[1]),
+    ]
+    large = [
+        pltpu.make_async_copy(tok_hbm.at[:, i * wide : (i + 1) * wide], tok.at[i], sems.at[3 + i])
+        for i in range(tok.shape[0])
+    ]
+    last = pltpu.make_async_copy(cot_hbm, cot, sems.at[2])
+    for copy in [*small, *large, last]:
+        copy.start()
+    for copy in small:
+        copy.wait()
     row = lax.broadcasted_iota(I32, (LIVE, block), 0)
     col = lax.broadcasted_iota(I32, (LIVE, block), 1)
-    for b, start in enumerate(starts_of(fill_ref, blocks)):
-        hit = (row == col + start) & (col < fill_ref[0, b])
+    for b, start in enumerate(starts_of(fill, blocks)):
+        hit = (row == col + start) & (col < fill[0, b])
         pick[:, b * block : (b + 1) * block] = jnp.where(hit, 1.0, 0.0).astype(BF16)
-    wide = min(feat, 512)
-    for at in range(0, feat, wide):
-        out_ref[:, at : at + wide] = dot(pick[...], tok_ref[:, at : at + wide]).astype(BF16)
-    out_ref[:, feat : feat + cols] = dot(pick[...], cot_ref[...]).astype(BF16)
     lanes = out_ref.shape[1] - feat - cols
-    out_ref[:, feat + cols :] = tenant_lanes(fill_ref, tenant_ref, blocks, lanes).astype(F32).astype(BF16)
+    out_ref[:, feat + cols :] = tenant_lanes(fill, tenant, blocks, lanes).astype(F32).astype(BF16)
+    for i, copy in enumerate(large):
+        copy.wait()
+        out_ref[:, i * wide : (i + 1) * wide] = dot(pick[...], tok[i]).astype(BF16)
+    last.wait()
+    out_ref[:, feat : feat + cols] = dot(pick[...], cot[...]).astype(BF16)
 
 
 def pack(fill, tenant, tokens, cotangent, blocks, lanes):
     rows, feat = tokens.shape
     cols = cotangent.shape[1]
+    wide = min(feat, 512)
     return pl.pallas_call(
         functools.partial(pack_kernel, blocks, rows // blocks),
-        in_specs=[SMEM] * 2 + [VMEM] * 2,
+        in_specs=[pl.BlockSpec(memory_space=pltpu.HBM)] * 4,
         out_specs=VMEM,
         out_shape=shaped((LIVE, feat + cols + lanes), BF16),
-        scratch_shapes=[pltpu.VMEM((LIVE, rows), BF16)],
+        scratch_shapes=[
+            pltpu.VMEM((LIVE, rows), BF16),
+            pltpu.VMEM((feat // wide, rows, wide), BF16),
+            pltpu.VMEM((rows, cols), BF16),
+            pltpu.SMEM(fill.shape, I32),
+            pltpu.SMEM(tenant.shape, I32),
+            pltpu.SemaphoreType.DMA((3 + feat // wide,)),
+        ],
         compiler_params=params(24),
         cost_estimate=cost(2 * LIVE * rows * (feat + cols), 2 * (LIVE + rows) * (feat + cols)),
         name="pack",

time: 88.8 us -> 88.7 us (level)
  Pallas kernels: 17.3 us -> 18.3 us
    pallas_call x1, Pallas kernels: 2.83 us -> 3.78 us  [pack(): pl.pallas_call(functools.partial(pack_kernel, blocks, rows // blocks), in...]
  transfers between devices with their start and end apart: 26 -> 26, of which waited for: 11 -> 11; matrix products, arithmetic and copies ran while one was open for 0% -> 0% of each run, Pallas kernels for 17% -> 18%
where the time goes in v17:
time: 88.7 us; the launch traced here: 87.7 us
  waiting for transfers between devices  33.4 us (38%)
  starting transfers between devices  29.3 us (33%)
  Pallas kernels  18.3 us (21%)
  local copies, waits for them, and re-layouts  5.55 us (6%)
  between operations  0.93 us (1%)
    ppermute x20, waiting for transfers between devices, flip(): return lax.ppermute(x, names, [(i, i ^ mask) for i in range(count)])  27.1 us
    ppermute x20, starting transfers between devices, flip(): return lax.ppermute(x, names, [(i, i ^ mask) for i in range(count)])  21.7 us
    ppermute x1, waiting for transfers between devices, body(): lax.ppermute(after(y_2, low), 'tensor', [(0, 1), (3, 2), (1, 3), (2, 0)])  6.3 us
    unnamed x21, local copies, waits for them, and re-layouts  4.37 us
    pallas_call x1, Pallas kernels, pack(): pl.pallas_call(functools.partial(pack_kernel, blocks, rows // blocks), in...  3.78 us
    pallas_call x3, Pallas kernels, panel_product(): pl.pallas_call(functools.partial(panel_kernel, order, len(pieces)), in_sp...  3.75 us
    ppermute x3, starting transfers between devices, shift(): lax.ppermute(x, name, [(i, (i + step) % count) for i in range(count)])  2.67 us
    ppermute x1, starting transfers between devices, body(): lax.ppermute(after(y_2, low), 'tensor', [(0, 1), (3, 2), (1, 3), (2, 0)])  2.25 us
  transfers between devices with their start and end apart: 26, of which 11 were waited for; matrix products, arithmetic and copies ran while one was open for 0% of the time, Pallas kernels for 18%

profile of v17, /device:TPU:0, one launch (start us, length us, event | category | flops | bytes accessed | tf_op | source)
XLA Modules:
  0.0 87.7 jit_solution(4196640291547696803)
XLA Ops:
  1.8 5.1 %collective-permute-start = (bf16[512,256]{1,0:T(8,128)(2,1)S(1)}, bf16[512,256]{1,0:T(8,128)(2,1)S(1)}, u32[]{:S(2)}, u32[]{:S(2)}) collective-permute-start(bf16[512,256]{1,0:T(8,128)(2,1)S(1)} %get-tuple-element.47), channel_id=1, source_target_pairs={{0,12},{4,8},{8,4},{12,0},{1,13},{5,9},{9,5},{13,1},{2,14},{6,10},... | collective-permute-start | bytes 786440 | tf_op jit(solution)/shard_map/ppermute | solution.py:33
  7.0 1.8 %own_half.1 = (bf16[32,2560]{1,0:T(8,128)(2,1)}, bf16[32,2560]{1,0:T(8,128)(2,1)}) custom-call(s32[1]{0:T(128)} %bitcast.core_ref, bf16[128,2048]{1,0:T(8,128)(2,1)} %bitcast.8, bf16[128,512]{1,0:T(8,128)(2,1)} %bitcast.10), custom_call_target="tpu_custom_call" | custom-call | flops 1 | bytes 1 | tf_op jit(solution)/shard_map/own_half/pallas_call | solution.py:75
  8.8 1.5 %collective-permute-start.1 = (bf16[32,2560]{1,0:T(8,128)(2,1)}, bf16[32,2560]{1,0:T(8,128)(2,1)S(1)}, u32[]{:S(2)}, u32[]{:S(2)}) collective-permute-start(bf16[32,2560]{1,0:T(8,128)(2,1)} %get-tuple-element.25), channel_id=1, source_target_pairs={{0,2},{2,0},{1,3},{3,1},{4,6},{6,4},{5,7},{7,5},{8,10},{10,8},{9,1... | collective-permute-start | bytes 491528 | tf_op jit(solution)/shard_map/ppermute | solution.py:29
  10.8 1.9 %copy-done = bf16[768,2048]{1,0:T(8,128)(2,1)S(1)} copy-done((bf16[768,2048]{1,0:T(8,128)(2,1)S(1)}, bf16[768,2048]{1,0:T(8,128)(2,1)}, u32[]{:S(2)}) %copy-start) | copy-done | bytes 3145752
  15.1 3.8 %pack.1.x_ref.own_ref = bf16[512,2688]{1,0:T(8,128)(2,1)S(1)} custom-call(s32[1,6]{1,0:T(1,128)S(1)} %copy-done.4, s32[6]{0:T(128)S(1)} %copy-done.6, bf16[768,2048]{1,0:T(8,128)(2,1)S(1)} %copy-done, bf16[768,512]{1,0:T(8,128)(2,1)S(1)} %copy-done.3), custom_call_target="tpu_custom_call" | custom-call | flops 1 | bytes 1 | tf_op jit(solution)/shard_map/pack/pallas_call | solution.py:120
  20.2 1.5 %collective-permute-start.8 = (bf16[512,256]{1,0:T(8,128)(2,1)S(1)}, bf16[512,256]{1,0:T(8,128)(2,1)S(1)}, u32[]{:S(2)}, u32[]{:S(2)}) collective-permute-start(bf16[512,256]{1,0:T(8,128)(2,1)S(1)} %collective-permute-done.refs_0_), channel_id=1, source_target_pairs={{0,2},{2,0},{16,18},{18,16},{1,3},{3,1},{17,19},{19,17},{4,6},{6,4... | collective-permute-start | bytes 786440 | tf_op jit(solution)/shard_map/ppermute | solution.py:33
  21.7 1.5 %collective-permute-start.9 = (bf16[512,256]{1,0:T(8,128)(2,1)S(1)}, bf16[512,256]{1,0:T(8,128)(2,1)S(1)}, u32[]{:S(2)}, u32[]{:S(2)}) collective-permute-start(bf16[512,256]{1,0:T(8,128)(2,1)S(1)} %collective-permute-done.refs_0_), channel_id=1, source_target_pairs={{0,16},{2,18},{16,0},{18,2},{1,17},{3,19},{17,1},{19,3},{4,20},{6,... | collective-permute-start | bytes 786440 | tf_op jit(solution)/shard_map/ppermute | solution.py:33
  24.1 2.4 %collective-permute-start.10 = (bf16[512,256]{1,0:T(8,128)(2,1)S(1)}, bf16[512,256]{1,0:T(8,128)(2,1)S(1)}, u32[]{:S(2)}, u32[]{:S(2)}) collective-permute-start(bf16[512,256]{1,0:T(8,128)(2,1)S(1)} %collective-permute-done.refs_0_), channel_id=1, source_target_pairs={{0,18},{2,16},{16,2},{18,0},{1,19},{3,17},{17,3},{19,1},{4,22},{6,... | collective-permute-start | bytes 786440 | tf_op jit(solution)/shard_map/ppermute | solution.py:33
  26.6 2.2 %low_part.1 = bf16[512,128]{1,0:T(8,128)(2,1)S(1)} custom-call(s32[1]{0:T(128)} %bitcast.2.dp_ref, s32[1]{0:T(128)} %bitcast.core_ref, s32[1,6]{1,0:T(1,128)S(1)} %copy-done.4, s32[6]{0:T(128)S(1)} %copy-done.6, bf16[512,2688]{1,0:T(8,128)(2,1)S(1)} %pack.1.x_ref.own_ref, bf16[128,2048]{1,0:T(8,128)(2,1)S(1)} %bitcast.9, bf16[128,512]{1,0:T(8,128)(2,1)S(1)} %bitcast.11, ...), custom_call_target="tpu_custom_call" | custom-call | flops 1 | bytes 1 | tf_op jit(solution)/shard_map/low_part/pallas_call | solution.py:170
  28.7 4.7 %collective-permute-done.5.refs_0_ = bf16[512,256]{1,0:T(8,128)(2,1)S(1)} collective-permute-done((bf16[512,256]{1,0:T(8,128)(2,1)S(1)}, bf16[512,256]{1,0:T(8,128)(2,1)S(1)}, u32[]{:S(2)}, u32[]{:S(2)}) %collective-permute-start.5) | collective-permute-done | bytes 262176 | tf_op jit(solution)/shard_map/ppermute | solution.py:33
  33.5 2.0 %collective-permute-start.11 = (bf16[512,256]{1,0:T(8,128)(2,1)S(1)}, bf16[512,256]{1,0:T(8,128)(2,1)S(1)}, u32[]{:S(2)}, u32[]{:S(2)}) collective-permute-start(bf16[512,256]{1,0:T(8,128)(2,1)S(1)} %get-tuple-element.33), channel_id=1, source_target_pairs={{0,4},{4,0},{8,12},{12,8},{1,5},{5,1},{9,13},{13,9},{2,6},{6,2},{1... | collective-permute-start | bytes 786440 | tf_op jit(solution)/shard_map/ppermute | solution.py:33
  35.5 1.6 %collective-permute-start.12 = (bf16[512,256]{1,0:T(8,128)(2,1)S(1)}, bf16[512,256]{1,0:T(8,128)(2,1)S(1)}, u32[]{:S(2)}, u32[]{:S(2)}) collective-permute-start(bf16[512,256]{1,0:T(8,128)(2,1)S(1)} %collective-permute-done.5.refs_0_), channel_id=1, source_target_pairs={{0,2},{2,0},{16,18},{18,16},{1,3},{3,1},{17,19},{19,17},{4,6},{6,4... | collective-permute-start | bytes 786440 | tf_op jit(solution)/shard_map/ppermute | solution.py:33
  37.0 1.5 %collective-permute-start.13 = (bf16[512,256]{1,0:T(8,128)(2,1)S(1)}, bf16[512,256]{1,0:T(8,128)(2,1)S(1)}, u32[]{:S(2)}, u32[]{:S(2)}) collective-permute-start(bf16[512,256]{1,0:T(8,128)(2,1)S(1)} %collective-permute-done.5.refs_0_), channel_id=1, source_target_pairs={{0,16},{2,18},{16,0},{18,2},{1,17},{3,19},{17,1},{19,3},{4,20},{6,... | collective-permute-start | bytes 786440 | tf_op jit(solution)/shard_map/ppermute | solution.py:33
  40.3 2.0 %collective-permute-start.15 = (bf16[1024,256]{1,0:T(8,128)(2,1)S(1)}, bf16[1024,256]{1,0:T(8,128)(2,1)S(1)}, u32[]{:S(2)}, u32[]{:S(2)}) collective-permute-start(bf16[1024,256]{1,0:T(8,128)(2,1)S(1)} %panel.3.own_ref), channel_id=1, source_target_pairs={{0,4},{12,8},{1,5},{13,9},{2,6},{14,10},{3,7},{15,11},{16,20},{28,... | collective-permute-start | bytes 1572872 | tf_op jit(solution)/shard_map/ppermute | solution.py:433
  42.3 2.2 %collective-permute-done.11.refs_0_ = bf16[512,256]{1,0:T(8,128)(2,1)S(1)} collective-permute-done((bf16[512,256]{1,0:T(8,128)(2,1)S(1)}, bf16[512,256]{1,0:T(8,128)(2,1)S(1)}, u32[]{:S(2)}, u32[]{:S(2)}) %collective-permute-start.11) | collective-permute-done | bytes 262176 | tf_op jit(solution)/shard_map/ppermute | solution.py:33
  44.8 5.3 %collective-permute-done.13.refs_2_ = bf16[512,256]{1,0:T(8,128)(2,1)S(1)} collective-permute-done((bf16[512,256]{1,0:T(8,128)(2,1)S(1)}, bf16[512,256]{1,0:T(8,128)(2,1)S(1)}, u32[]{:S(2)}, u32[]{:S(2)}) %collective-permute-start.13) | collective-permute-done | bytes 262176 | tf_op jit(solution)/shard_map/ppermute | solution.py:33
  52.1 1.4 %collective-permute-start.21 = (bf16[512,256]{1,0:T(8,128)(2,1)S(1)}, bf16[512,256]{1,0:T(8,128)(2,1)S(1)}, u32[]{:S(2)}, u32[]{:S(2)}) collective-permute-start(bf16[512,256]{1,0:T(8,128)(2,1)S(1)} %collective-permute-done.11.refs_0_), channel_id=1, source_target_pairs={{0,18},{2,16},{16,2},{18,0},{1,19},{3,17},{17,3},{19,1},{4,22},{6,... | collective-permute-start | bytes 786440 | tf_op jit(solution)/shard_map/ppermute | solution.py:33
  53.6 2.8 %collective-permute-done.7 = bf16[512,128]{1,0:T(8,128)(2,1)S(1)} collective-permute-done((bf16[512,128]{1,0:T(8,128)(2,1)S(1)}, bf16[512,128]{1,0:T(8,128)(2,1)S(1)}, u32[]{:S(2)}, u32[]{:S(2)}) %collective-permute-start.7) | collective-permute-done | bytes 131104 | tf_op jit(solution)/shard_map/ppermute | solution.py:33
  57.7 2.3 %collective-permute-start.16 = (bf16[1024,256]{1,0:T(8,128)(2,1)S(1)}, bf16[1024,256]{1,0:T(8,128)(2,1)S(1)}, u32[]{:S(2)}, u32[]{:S(2)}) collective-permute-start(bf16[1024,256]{1,0:T(8,128)(2,1)S(1)} %panel.4), channel_id=1, source_target_pairs={{0,4},{12,8},{4,12},{8,0},{1,5},{13,9},{5,13},{9,1},{2,6},{14,10},... | collective-permute-start | bytes 1572872 | tf_op jit(solution)/shard_map/ppermute | solution.py:438
  66.0 6.3 %collective-permute-done.16.got_ref = bf16[1024,256]{1,0:T(8,128)(2,1)S(1)} collective-permute-done((bf16[1024,256]{1,0:T(8,128)(2,1)S(1)}, bf16[1024,256]{1,0:T(8,128)(2,1)S(1)}, u32[]{:S(2)}, u32[]{:S(2)}) %collective-permute-start.16) | collective-permute-done | bytes 524320 | tf_op jit(solution)/shard_map/ppermute | solution.py:438
  73.4 2.1 %base.1.base_ref = f32[512,512]{1,0:T(8,128)S(1)} custom-call(s32[1]{0:T(128)} %bitcast.1.at_ref, s32[1]{0:T(128)} %bitcast.2.dp_ref, s32[1]{0:T(128)} %bitcast.core_ref, s32[1,6]{1,0:T(1,128)S(1)} %copy-done.5, s32[6]{0:T(128)S(1)} %copy-done.7, bf16[512,2688]{1,0:T(8,128)(2,1)S(1)} %pack.1.x_ref.own_ref, bf16[8192,512]{1,0:T(8,128)(2,1)S(1)} %bitcast.7, ...), custom_call_target="tpu_custom_call" | custom-call | flops 1 | bytes 1 | tf_op jit(solution)/shard_map/base/pallas_call | solution.py:294
  76.8 6.7 %collective-permute-done.24.refs_1_ = bf16[1024,256]{1,0:T(8,128)(2,1)S(1)} collective-permute-done((bf16[1024,256]{1,0:T(8,128)(2,1)S(1)}, bf16[1024,256]{1,0:T(8,128)(2,1)S(1)}, u32[]{:S(2)}, u32[]{:S(2)}) %collective-permute-start.24) | collective-permute-done | bytes 524320 | tf_op jit(solution)/shard_map/ppermute | solution.py:33
  83.6 1.9 %collective-permute-done.25.refs_3_ = f32[512,256]{1,0:T(8,128)S(1)} collective-permute-done((f32[512,256]{1,0:T(8,128)S(1)}, f32[512,256]{1,0:T(8,128)S(1)}, u32[]{:S(2)}, u32[]{:S(2)}) %collective-permute-start.25) | collective-permute-done | bytes 524320 | tf_op jit(solution)/shard_map/ppermute | solution.py:33
  85.5 2.2 %finish.1 = bf16[768,512]{1,0:T(8,128)(2,1)} custom-call(s32[1]{0:T(128)} %bitcast.core_ref, s32[1,6]{1,0:T(1,128)S(1)} %copy-done.5, f32[512,512]{1,0:T(8,128)S(1)} %base.1.base_ref, bf16[1024,256]{1,0:T(8,128)(2,1)S(1)} %collective-permute-done.17.refs_0_, bf16[1024,256]{1,0:T(8,128)(2,1)S(1)} %collective-permute-done.24.refs_1_, ...), custom_call_target="tpu_custom_call" | custom-call | flops 1 | bytes 1 | tf_op jit(solution)/shard_map/finish/pallas_call | solution.py:375
  (67 shorter events, 20.2 us)
Async XLA Ops:
  1.8 17.1 %collective-permute-start = (bf16[512,256]{1,0:T(8,128)(2,1)S(1)}, bf16[512,256]{1,0:T(8,128)(2,1)S(1)}, u32[]{:S(2)}, u32[]{:S(2)}) collective-permute-start(bf16[512,256]{1,0:T(8,128)(2,1)S(1)} %get-tuple-element.47), channel_id=1, source_target_pairs={{0,12},{4,8},{8,4},{12,0},{1,13},{5,9},{9,5},{13,1},{2,14},{6,10},... | collective-permute-start | bytes 786440 | tf_op jit(solution)/shard_map/ppermute | solution.py:33
  8.8 10.2 %collective-permute-start.1 = (bf16[32,2560]{1,0:T(8,128)(2,1)}, bf16[32,2560]{1,0:T(8,128)(2,1)S(1)}, u32[]{:S(2)}, u32[]{:S(2)}) collective-permute-start(bf16[32,2560]{1,0:T(8,128)(2,1)} %get-tuple-element.25), channel_id=1, source_target_pairs={{0,2},{2,0},{1,3},{3,1},{4,6},{6,4},{5,7},{7,5},{8,10},{10,8},{9,1... | collective-permute-start | bytes 491528 | tf_op jit(solution)/shard_map/ppermute | solution.py:29
  10.2 8.7 %collective-permute-start.2 = (bf16[32,2560]{1,0:T(8,128)(2,1)}, bf16[32,2560]{1,0:T(8,128)(2,1)S(1)}, u32[]{:S(2)}, u32[]{:S(2)}) collective-permute-start(bf16[32,2560]{1,0:T(8,128)(2,1)} %get-tuple-element.26), channel_id=1, source_target_pairs={{0,2},{2,0},{1,3},{3,1},{4,6},{6,4},{5,7},{7,5},{8,10},{10,8},{9,1... | collective-permute-start | bytes 491528 | tf_op jit(solution)/shard_map/ppermute | solution.py:29
  18.9 5.2 %collective-permute-start.3 = (bf16[512,2688]{1,0:T(8,128)(2,1)S(1)}, bf16[512,2688]{1,0:T(8,128)(2,1)S(1)}, u32[]{:S(2)}, u32[]{:S(2)}) collective-permute-start(bf16[512,2688]{1,0:T(8,128)(2,1)S(1)} %pack.1.x_ref.own_ref), channel_id=1, source_target_pairs={{0,1},{1,0},{2,3},{3,2},{4,5},{5,4},{6,7},{7,6},{8,9},{9,8},{10,11... | collective-permute-start | bytes 8257544 | tf_op jit(solution)/shard_map/ppermute | solution.py:33
  19.1 7.5 %collective-permute-start.4 = (bf16[64,2560]{1,0:T(8,128)(2,1)S(1)}, bf16[64,2560]{1,0:T(8,128)(2,1)S(1)}, u32[]{:S(2)}, u32[]{:S(2)}) collective-permute-start(bf16[64,2560]{1,0:T(8,128)(2,1)S(1)} %constant_dynamic-update-slice_fusion.refs_0_), channel_id=1, source_target_pairs={{0,1},{1,0},{2,3},{3,2},{4,5},{5,4},{6,7},{7,6},{8,9},{9,8},{10,11... | collective-permute-start | bytes 983048 | tf_op jit(solution)/shard_map/ppermute | solution.py:33
  19.6 13.8 %collective-permute-start.5 = (bf16[512,256]{1,0:T(8,128)(2,1)S(1)}, bf16[512,256]{1,0:T(8,128)(2,1)S(1)}, u32[]{:S(2)}, u32[]{:S(2)}) collective-permute-start(bf16[512,256]{1,0:T(8,128)(2,1)S(1)} %get-tuple-element.29), channel_id=1, source_target_pairs={{0,8},{4,12},{8,0},{12,4},{1,9},{5,13},{9,1},{13,5},{2,10},{6,14},... | collective-permute-start | bytes 786440 | tf_op jit(solution)/shard_map/ppermute | solution.py:33
  20.2 15.3 %collective-permute-start.8 = (bf16[512,256]{1,0:T(8,128)(2,1)S(1)}, bf16[512,256]{1,0:T(8,128)(2,1)S(1)}, u32[]{:S(2)}, u32[]{:S(2)}) collective-permute-start(bf16[512,256]{1,0:T(8,128)(2,1)S(1)} %collective-permute-done.refs_0_), channel_id=1, source_target_pairs={{0,2},{2,0},{16,18},{18,16},{1,3},{3,1},{17,19},{19,17},{4,6},{6,4... | collective-permute-start | bytes 786440 | tf_op jit(solution)/shard_map/ppermute | solution.py:33
  21.7 13.8 %collective-permute-start.9 = (bf16[512,256]{1,0:T(8,128)(2,1)S(1)}, bf16[512,256]{1,0:T(8,128)(2,1)S(1)}, u32[]{:S(2)}, u32[]{:S(2)}) collective-permute-start(bf16[512,256]{1,0:T(8,128)(2,1)S(1)} %collective-permute-done.refs_0_), channel_id=1, source_target_pairs={{0,16},{2,18},{16,0},{18,2},{1,17},{3,19},{17,1},{19,3},{4,20},{6,... | collective-permute-start | bytes 786440 | tf_op jit(solution)/shard_map/ppermute | solution.py:33
  24.1 11.4 %collective-permute-start.10 = (bf16[512,256]{1,0:T(8,128)(2,1)S(1)}, bf16[512,256]{1,0:T(8,128)(2,1)S(1)}, u32[]{:S(2)}, u32[]{:S(2)}) collective-permute-start(bf16[512,256]{1,0:T(8,128)(2,1)S(1)} %collective-permute-done.refs_0_), channel_id=1, source_target_pairs={{0,18},{2,16},{16,2},{18,0},{1,19},{3,17},{17,3},{19,1},{4,22},{6,... | collective-permute-start | bytes 786440 | tf_op jit(solution)/shard_map/ppermute | solution.py:33
  33.4 6.8 %collective-permute-start.6 = (bf16[512,128]{1,0:T(8,128)(2,1)S(1)}, bf16[512,128]{1,0:T(8,128)(2,1)S(1)}, u32[]{:S(2)}, u32[]{:S(2)}) collective-permute-start(bf16[512,128]{1,0:T(8,128)(2,1)S(1)} %low_part.1), channel_id=1, source_target_pairs={{0,4},{4,0},{8,12},{12,8},{1,5},{5,1},{9,13},{13,9},{2,6},{6,2},{1... | collective-permute-start | bytes 393224 | tf_op jit(solution)/shard_map/ppermute | solution.py:33
  33.5 11.0 %collective-permute-start.11 = (bf16[512,256]{1,0:T(8,128)(2,1)S(1)}, bf16[512,256]{1,0:T(8,128)(2,1)S(1)}, u32[]{:S(2)}, u32[]{:S(2)}) collective-permute-start(bf16[512,256]{1,0:T(8,128)(2,1)S(1)} %get-tuple-element.33), channel_id=1, source_target_pairs={{0,4},{4,0},{8,12},{12,8},{1,5},{5,1},{9,13},{13,9},{2,6},{6,2},{1... | collective-permute-start | bytes 786440 | tf_op jit(solution)/shard_map/ppermute | solution.py:33
  35.5 9.3 %collective-permute-start.12 = (bf16[512,256]{1,0:T(8,128)(2,1)S(1)}, bf16[512,256]{1,0:T(8,128)(2,1)S(1)}, u32[]{:S(2)}, u32[]{:S(2)}) collective-permute-start(bf16[512,256]{1,0:T(8,128)(2,1)S(1)} %collective-permute-done.5.refs_0_), channel_id=1, source_target_pairs={{0,2},{2,0},{16,18},{18,16},{1,3},{3,1},{17,19},{19,17},{4,6},{6,4... | collective-permute-start | bytes 786440 | tf_op jit(solution)/shard_map/ppermute | solution.py:33
  37.0 13.0 %collective-permute-start.13 = (bf16[512,256]{1,0:T(8,128)(2,1)S(1)}, bf16[512,256]{1,0:T(8,128)(2,1)S(1)}, u32[]{:S(2)}, u32[]{:S(2)}) collective-permute-start(bf16[512,256]{1,0:T(8,128)(2,1)S(1)} %collective-permute-done.5.refs_0_), channel_id=1, source_target_pairs={{0,16},{2,18},{16,0},{18,2},{1,17},{3,19},{17,1},{19,3},{4,20},{6,... | collective-permute-start | bytes 786440 | tf_op jit(solution)/shard_map/ppermute | solution.py:33
  38.6 11.5 %collective-permute-start.14 = (bf16[512,256]{1,0:T(8,128)(2,1)S(1)}, bf16[512,256]{1,0:T(8,128)(2,1)S(1)}, u32[]{:S(2)}, u32[]{:S(2)}) collective-permute-start(bf16[512,256]{1,0:T(8,128)(2,1)S(1)} %collective-permute-done.5.refs_0_), channel_id=1, source_target_pairs={{0,18},{2,16},{16,2},{18,0},{1,19},{3,17},{17,3},{19,1},{4,22},{6,... | collective-permute-start | bytes 786440 | tf_op jit(solution)/shard_map/ppermute | solution.py:33
  40.3 16.1 %collective-permute-start.15 = (bf16[1024,256]{1,0:T(8,128)(2,1)S(1)}, bf16[1024,256]{1,0:T(8,128)(2,1)S(1)}, u32[]{:S(2)}, u32[]{:S(2)}) collective-permute-start(bf16[1024,256]{1,0:T(8,128)(2,1)S(1)} %panel.3.own_ref), channel_id=1, source_target_pairs={{0,4},{12,8},{1,5},{13,9},{2,6},{14,10},{3,7},{15,11},{16,20},{28,... | collective-permute-start | bytes 1572872 | tf_op jit(solution)/shard_map/ppermute | solution.py:433
  44.5 11.8 %collective-permute-start.7 = (bf16[512,128]{1,0:T(8,128)(2,1)S(1)}, bf16[512,128]{1,0:T(8,128)(2,1)S(1)}, u32[]{:S(2)}, u32[]{:S(2)}) collective-permute-start(bf16[512,128]{1,0:T(8,128)(2,1)S(1)} %add_convert_fusion.2), channel_id=1, source_target_pairs={{0,8},{4,12},{8,0},{12,4},{1,9},{5,13},{9,1},{13,5},{2,10},{6,14},... | collective-permute-start | bytes 393224 | tf_op jit(solution)/shard_map/ppermute | solution.py:33
  50.1 12.2 %collective-permute-start.19 = (bf16[512,256]{1,0:T(8,128)(2,1)S(1)}, bf16[512,256]{1,0:T(8,128)(2,1)S(1)}, u32[]{:S(2)}, u32[]{:S(2)}) collective-permute-start(bf16[512,256]{1,0:T(8,128)(2,1)S(1)} %collective-permute-done.11.refs_0_), channel_id=1, source_target_pairs={{0,2},{2,0},{16,18},{18,16},{1,3},{3,1},{17,19},{19,17},{4,6},{6,4... | collective-permute-start | bytes 786440 | tf_op jit(solution)/shard_map/ppermute | solution.py:33
  51.3 12.1 %collective-permute-start.20 = (bf16[512,256]{1,0:T(8,128)(2,1)S(1)}, bf16[512,256]{1,0:T(8,128)(2,1)S(1)}, u32[]{:S(2)}, u32[]{:S(2)}) collective-permute-start(bf16[512,256]{1,0:T(8,128)(2,1)S(1)} %collective-permute-done.11.refs_0_), channel_id=1, source_target_pairs={{0,16},{2,18},{16,0},{18,2},{1,17},{3,19},{17,1},{19,3},{4,20},{6,... | collective-permute-start | bytes 786440 | tf_op jit(solution)/shard_map/ppermute | solution.py:33
  52.1 11.3 %collective-permute-start.21 = (bf16[512,256]{1,0:T(8,128)(2,1)S(1)}, bf16[512,256]{1,0:T(8,128)(2,1)S(1)}, u32[]{:S(2)}, u32[]{:S(2)}) collective-permute-start(bf16[512,256]{1,0:T(8,128)(2,1)S(1)} %collective-permute-done.11.refs_0_), channel_id=1, source_target_pairs={{0,18},{2,16},{16,2},{18,0},{1,19},{3,17},{17,3},{19,1},{4,22},{6,... | collective-permute-start | bytes 786440 | tf_op jit(solution)/shard_map/ppermute | solution.py:33
  57.7 14.7 %collective-permute-start.16 = (bf16[1024,256]{1,0:T(8,128)(2,1)S(1)}, bf16[1024,256]{1,0:T(8,128)(2,1)S(1)}, u32[]{:S(2)}, u32[]{:S(2)}) collective-permute-start(bf16[1024,256]{1,0:T(8,128)(2,1)S(1)} %panel.4), channel_id=1, source_target_pairs={{0,4},{12,8},{4,12},{8,0},{1,5},{13,9},{5,13},{9,1},{2,6},{14,10},... | collective-permute-start | bytes 1572872 | tf_op jit(solution)/shard_map/ppermute | solution.py:438
  63.4 9.8 %collective-permute-start.22 = (bf16[64,2560]{1,0:T(8,128)(2,1)S(1)}, bf16[64,2560]{1,0:T(8,128)(2,1)S(1)}, u32[]{:S(2)}, u32[]{:S(2)}) collective-permute-start(bf16[64,2560]{1,0:T(8,128)(2,1)S(1)} %get-tuple-element.40), channel_id=1, source_target_pairs={{0,2},{2,0},{1,3},{3,1},{4,6},{6,4},{5,7},{7,5},{8,10},{10,8},{9,1... | collective-permute-start | bytes 983048 | tf_op jit(solution)/shard_map/ppermute | solution.py:29
  65.3 18.1 %collective-permute-start.24 = (bf16[1024,256]{1,0:T(8,128)(2,1)S(1)}, bf16[1024,256]{1,0:T(8,128)(2,1)S(1)}, u32[]{:S(2)}, u32[]{:S(2)}) collective-permute-start(bf16[1024,256]{1,0:T(8,128)(2,1)S(1)} %panel.5), channel_id=1, source_target_pairs={{0,4},{4,0},{8,12},{12,8},{1,5},{5,1},{9,13},{13,9},{2,6},{6,2},{1... | collective-permute-start | bytes 1572872 | tf_op jit(solution)/shard_map/ppermute | solution.py:33
  72.5 4.3 %collective-permute-start.17 = (bf16[1024,256]{1,0:T(8,128)(2,1)S(1)}, bf16[1024,256]{1,0:T(8,128)(2,1)S(1)}, u32[]{:S(2)}, u32[]{:S(2)}) collective-permute-start(bf16[1024,256]{1,0:T(8,128)(2,1)S(1)} %get-tuple-element.36), channel_id=1, source_target_pairs={{4,8},{8,4},{5,9},{9,5},{6,10},{10,6},{7,11},{11,7},{20,24},{24,20... | collective-permute-start | bytes 1572872 | tf_op jit(solution)/shard_map/ppermute | solution.py:443
  73.3 2.3 %collective-permute-start.23 = (bf16[64,2560]{1,0:T(8,128)(2,1)S(1)}, bf16[64,2560]{1,0:T(8,128)(2,1)S(1)}, u32[]{:S(2)}, u32[]{:S(2)}) collective-permute-start(bf16[64,2560]{1,0:T(8,128)(2,1)S(1)} %add_convert_fusion.own_ref), channel_id=1, source_target_pairs={{0,1},{1,0},{2,3},{3,2},{4,5},{5,4},{6,7},{7,6},{8,9},{9,8},{10,11... | collective-permute-start | bytes 983048 | tf_op jit(solution)/shard_map/ppermute | solution.py:33
  (12 other events, 72.7 us)

commit v18 on v11

--- a/solution.py
+++ b/solution.py
@@ -310,7 +310,7 @@
     total = ins[0][LIVE:, :].astype(F32)
     for ref in ins[1:]:
         total = total + ref[LIVE:, :].astype(F32)
-    out_ref[...] = total
+    out_ref[...] = total.astype(BF16)
 
 
 def other_rows(parts):
@@ -319,7 +319,7 @@
         swap_kernel,
         in_specs=[VMEM] * len(parts),
         out_specs=VMEM,
-        out_shape=shaped((LIVE, half), F32),
+        out_shape=shaped((LIVE, half), BF16),
         compiler_params=params(24),
         cost_estimate=cost(LIVE * half, 2 * LIVE * half * len(parts)),
         name="other_rows",
@@ -338,12 +338,14 @@
     first = core_ref[0] == 0
     held[:, :half] = (base_ref[:, :half] + jnp.where(first, own, other)).astype(BF16)
     held[:, half:] = (base_ref[:, half:] + jnp.where(first, other, own)).astype(BF16)
-    row = lax.broadcasted_iota(I32, (block, LIVE), 0)
-    col = lax.broadcasted_iota(I32, (block, LIVE), 1)
+    window = min(2 * block, LIVE)
+    row = lax.broadcasted_iota(I32, (block, window), 0)
+    col = lax.broadcasted_iota(I32, (block, window), 1)
     for b, start in enumerate(starts_of(fill_ref, blocks)):
-        hit = (col == row + start) & (row < fill_ref[0, b])
+        at = pl.multiple_of(jnp.minimum(start // 16 * 16, LIVE - window), 16)
+        hit = (col + at == row + start) & (row < fill_ref[0, b])
         pick = jnp.where(hit, 1.0, 0.0).astype(BF16)
-        out_ref[b * block : (b + 1) * block, :] = dot(pick, held[...]).astype(BF16)
+        out_ref[b * block : (b + 1) * block, :] = dot(pick, held[pl.ds(at, window), :]).astype(BF16)
 
 
 def finish(core, fill, base, parts, others, rows, blocks):

time: 88.8 us -> 88.3 us (level)
  no operation moved by 1% of the time
where the time goes in v18:
time: 88.3 us; the launch traced here: 87.2 us
  waiting for transfers between devices  33.7 us (38%)
  starting transfers between devices  29.7 us (34%)
  Pallas kernels  17.2 us (19%)
  local copies, waits for them, and re-layouts  5.55 us (6%)
  between operations  0.9 us (1%)
    ppermute x20, waiting for transfers between devices, flip(): return lax.ppermute(x, names, [(i, i ^ mask) for i in range(count)])  27.2 us
    ppermute x20, starting transfers between devices, flip(): return lax.ppermute(x, names, [(i, i ^ mask) for i in range(count)])  22.5 us
    ppermute x1, waiting for transfers between devices, body(): lax.ppermute(after(y_2, low), 'tensor', [(0, 1), (3, 2), (1, 3), (2, 0)])  6.3 us
    unnamed x21, local copies, waits for them, and re-layouts  4.36 us
    pallas_call x3, Pallas kernels, panel_product(): pl.pallas_call(functools.partial(panel_kernel, order, len(pieces)), in_sp...  3.75 us
    pallas_call x1, Pallas kernels, pack(): pl.pallas_call(functools.partial(pack_kernel, blocks, rows // blocks), in...  2.83 us
    ppermute x3, starting transfers between devices, shift(): lax.ppermute(x, name, [(i, (i + step) % count) for i in range(count)])  2.67 us
    pallas_call x1, Pallas kernels, low_part(): pl.pallas_call(functools.partial(low_kernel, n_dp, rank, blocks), in_spec...  2.17 us
  transfers between devices with their start and end apart: 26, of which 11 were waited for; matrix products, arithmetic and copies ran while one was open for 0% of the time, Pallas kernels for 17%

profile of v18, /device:TPU:0, one launch (start us, length us, event | category | flops | bytes accessed | tf_op | source)
XLA Modules:
  0.0 87.2 jit_solution(2732727836465338091)
XLA Ops:
  1.8 5.1 %collective-permute-start = (bf16[512,256]{1,0:T(8,128)(2,1)S(1)}, bf16[512,256]{1,0:T(8,128)(2,1)S(1)}, u32[]{:S(2)}, u32[]{:S(2)}) collective-permute-start(bf16[512,256]{1,0:T(8,128)(2,1)S(1)} %get-tuple-element.47), channel_id=1, source_target_pairs={{0,12},{4,8},{8,4},{12,0},{1,13},{5,9},{9,5},{13,1},{2,14},{6,10},... | collective-permute-start | bytes 786440 | tf_op jit(solution)/shard_map/ppermute | solution.py:33
  7.0 1.8 %own_half.1 = (bf16[32,2560]{1,0:T(8,128)(2,1)}, bf16[32,2560]{1,0:T(8,128)(2,1)}) custom-call(s32[1]{0:T(128)} %bitcast.core_ref, bf16[128,2048]{1,0:T(8,128)(2,1)} %bitcast.8, bf16[128,512]{1,0:T(8,128)(2,1)} %bitcast.10), custom_call_target="tpu_custom_call" | custom-call | flops 1 | bytes 1 | tf_op jit(solution)/shard_map/own_half/pallas_call | solution.py:75
  8.8 1.5 %collective-permute-start.1 = (bf16[32,2560]{1,0:T(8,128)(2,1)}, bf16[32,2560]{1,0:T(8,128)(2,1)S(1)}, u32[]{:S(2)}, u32[]{:S(2)}) collective-permute-start(bf16[32,2560]{1,0:T(8,128)(2,1)} %get-tuple-element.25), channel_id=1, source_target_pairs={{0,2},{2,0},{1,3},{3,1},{4,6},{6,4},{5,7},{7,5},{8,10},{10,8},{9,1... | collective-permute-start | bytes 491528 | tf_op jit(solution)/shard_map/ppermute | solution.py:29
  10.8 1.9 %copy-done = bf16[768,2048]{1,0:T(8,128)(2,1)S(1)} copy-done((bf16[768,2048]{1,0:T(8,128)(2,1)S(1)}, bf16[768,2048]{1,0:T(8,128)(2,1)}, u32[]{:S(2)}) %copy-start) | copy-done | bytes 3145752
  15.1 2.8 %pack.1.x_ref.own_ref = bf16[512,2688]{1,0:T(8,128)(2,1)S(1)} custom-call(s32[1,6]{1,0:T(1,128)S(1)} %copy-done.4, s32[6]{0:T(128)S(1)} %copy-done.6, bf16[768,2048]{1,0:T(8,128)(2,1)S(1)} %copy-done, bf16[768,512]{1,0:T(8,128)(2,1)S(1)} %copy-done.3), custom_call_target="tpu_custom_call" | custom-call | flops 1 | bytes 1 | tf_op jit(solution)/shard_map/pack/pallas_call | solution.py:104
  20.2 1.5 %collective-permute-start.8 = (bf16[512,256]{1,0:T(8,128)(2,1)S(1)}, bf16[512,256]{1,0:T(8,128)(2,1)S(1)}, u32[]{:S(2)}, u32[]{:S(2)}) collective-permute-start(bf16[512,256]{1,0:T(8,128)(2,1)S(1)} %collective-permute-done.refs_0_), channel_id=1, source_target_pairs={{0,2},{2,0},{16,18},{18,16},{1,3},{3,1},{17,19},{19,17},{4,6},{6,4... | collective-permute-start | bytes 786440 | tf_op jit(solution)/shard_map/ppermute | solution.py:33
  21.7 1.5 %collective-permute-start.9 = (bf16[512,256]{1,0:T(8,128)(2,1)S(1)}, bf16[512,256]{1,0:T(8,128)(2,1)S(1)}, u32[]{:S(2)}, u32[]{:S(2)}) collective-permute-start(bf16[512,256]{1,0:T(8,128)(2,1)S(1)} %collective-permute-done.refs_0_), channel_id=1, source_target_pairs={{0,16},{2,18},{16,0},{18,2},{1,17},{3,19},{17,1},{19,3},{4,20},{6,... | collective-permute-start | bytes 786440 | tf_op jit(solution)/shard_map/ppermute | solution.py:33
  23.2 2.4 %collective-permute-start.10 = (bf16[512,256]{1,0:T(8,128)(2,1)S(1)}, bf16[512,256]{1,0:T(8,128)(2,1)S(1)}, u32[]{:S(2)}, u32[]{:S(2)}) collective-permute-start(bf16[512,256]{1,0:T(8,128)(2,1)S(1)} %collective-permute-done.refs_0_), channel_id=1, source_target_pairs={{0,18},{2,16},{16,2},{18,0},{1,19},{3,17},{17,3},{19,1},{4,22},{6,... | collective-permute-start | bytes 786440 | tf_op jit(solution)/shard_map/ppermute | solution.py:33
  25.7 2.2 %low_part.1 = bf16[512,128]{1,0:T(8,128)(2,1)S(1)} custom-call(s32[1]{0:T(128)} %bitcast.2.dp_ref, s32[1]{0:T(128)} %bitcast.core_ref, s32[1,6]{1,0:T(1,128)S(1)} %copy-done.4, s32[6]{0:T(128)S(1)} %copy-done.6, bf16[512,2688]{1,0:T(8,128)(2,1)S(1)} %pack.1.x_ref.own_ref, bf16[128,2048]{1,0:T(8,128)(2,1)S(1)} %bitcast.9, bf16[128,512]{1,0:T(8,128)(2,1)S(1)} %bitcast.11, ...), custom_call_target="tpu_custom_call" | custom-call | flops 1 | bytes 1 | tf_op jit(solution)/shard_map/low_part/pallas_call | solution.py:147
  27.9 5.6 %collective-permute-done.5.refs_0_ = bf16[512,256]{1,0:T(8,128)(2,1)S(1)} collective-permute-done((bf16[512,256]{1,0:T(8,128)(2,1)S(1)}, bf16[512,256]{1,0:T(8,128)(2,1)S(1)}, u32[]{:S(2)}, u32[]{:S(2)}) %collective-permute-start.5) | collective-permute-done | bytes 262176 | tf_op jit(solution)/shard_map/ppermute | solution.py:33
  33.5 2.0 %collective-permute-start.11 = (bf16[512,256]{1,0:T(8,128)(2,1)S(1)}, bf16[512,256]{1,0:T(8,128)(2,1)S(1)}, u32[]{:S(2)}, u32[]{:S(2)}) collective-permute-start(bf16[512,256]{1,0:T(8,128)(2,1)S(1)} %get-tuple-element.33), channel_id=1, source_target_pairs={{0,4},{4,0},{8,12},{12,8},{1,5},{5,1},{9,13},{13,9},{2,6},{6,2},{1... | collective-permute-start | bytes 786440 | tf_op jit(solution)/shard_map/ppermute | solution.py:33
  35.5 1.6 %collective-permute-start.12 = (bf16[512,256]{1,0:T(8,128)(2,1)S(1)}, bf16[512,256]{1,0:T(8,128)(2,1)S(1)}, u32[]{:S(2)}, u32[]{:S(2)}) collective-permute-start(bf16[512,256]{1,0:T(8,128)(2,1)S(1)} %collective-permute-done.5.refs_0_), channel_id=1, source_target_pairs={{0,2},{2,0},{16,18},{18,16},{1,3},{3,1},{17,19},{19,17},{4,6},{6,4... | collective-permute-start | bytes 786440 | tf_op jit(solution)/shard_map/ppermute | solution.py:33
  37.0 1.5 %collective-permute-start.13 = (bf16[512,256]{1,0:T(8,128)(2,1)S(1)}, bf16[512,256]{1,0:T(8,128)(2,1)S(1)}, u32[]{:S(2)}, u32[]{:S(2)}) collective-permute-start(bf16[512,256]{1,0:T(8,128)(2,1)S(1)} %collective-permute-done.5.refs_0_), channel_id=1, source_target_pairs={{0,16},{2,18},{16,0},{18,2},{1,17},{3,19},{17,1},{19,3},{4,20},{6,... | collective-permute-start | bytes 786440 | tf_op jit(solution)/shard_map/ppermute | solution.py:33
  40.3 2.0 %collective-permute-start.15 = (bf16[1024,256]{1,0:T(8,128)(2,1)S(1)}, bf16[1024,256]{1,0:T(8,128)(2,1)S(1)}, u32[]{:S(2)}, u32[]{:S(2)}) collective-permute-start(bf16[1024,256]{1,0:T(8,128)(2,1)S(1)} %panel.3.own_ref), channel_id=1, source_target_pairs={{0,4},{12,8},{1,5},{13,9},{2,6},{14,10},{3,7},{15,11},{16,20},{28,... | collective-permute-start | bytes 1572872 | tf_op jit(solution)/shard_map/ppermute | solution.py:412
  42.3 2.2 %collective-permute-done.11.refs_0_ = bf16[512,256]{1,0:T(8,128)(2,1)S(1)} collective-permute-done((bf16[512,256]{1,0:T(8,128)(2,1)S(1)}, bf16[512,256]{1,0:T(8,128)(2,1)S(1)}, u32[]{:S(2)}, u32[]{:S(2)}) %collective-permute-start.11) | collective-permute-done | bytes 262176 | tf_op jit(solution)/shard_map/ppermute | solution.py:33
  44.8 5.3 %collective-permute-done.13.refs_2_ = bf16[512,256]{1,0:T(8,128)(2,1)S(1)} collective-permute-done((bf16[512,256]{1,0:T(8,128)(2,1)S(1)}, bf16[512,256]{1,0:T(8,128)(2,1)S(1)}, u32[]{:S(2)}, u32[]{:S(2)}) %collective-permute-start.13) | collective-permute-done | bytes 262176 | tf_op jit(solution)/shard_map/ppermute | solution.py:33
  53.6 2.8 %collective-permute-done.7 = bf16[512,128]{1,0:T(8,128)(2,1)S(1)} collective-permute-done((bf16[512,128]{1,0:T(8,128)(2,1)S(1)}, bf16[512,128]{1,0:T(8,128)(2,1)S(1)}, u32[]{:S(2)}, u32[]{:S(2)}) %collective-permute-start.7) | collective-permute-done | bytes 131104 | tf_op jit(solution)/shard_map/ppermute | solution.py:33
  57.7 1.8 %collective-permute-start.16 = (bf16[1024,256]{1,0:T(8,128)(2,1)S(1)}, bf16[1024,256]{1,0:T(8,128)(2,1)S(1)}, u32[]{:S(2)}, u32[]{:S(2)}) collective-permute-start(bf16[1024,256]{1,0:T(8,128)(2,1)S(1)} %panel.4), channel_id=1, source_target_pairs={{0,4},{12,8},{4,12},{8,0},{1,5},{13,9},{5,13},{9,1},{2,6},{14,10},... | collective-permute-start | bytes 1572872 | tf_op jit(solution)/shard_map/ppermute | solution.py:417
  61.8 1.6 %collective-permute-done.20.refs_2_ = bf16[512,256]{1,0:T(8,128)(2,1)S(1)} collective-permute-done((bf16[512,256]{1,0:T(8,128)(2,1)S(1)}, bf16[512,256]{1,0:T(8,128)(2,1)S(1)}, u32[]{:S(2)}, u32[]{:S(2)}) %collective-permute-start.20) | collective-permute-done | bytes 262176 | tf_op jit(solution)/shard_map/ppermute | solution.py:33
  66.0 6.3 %collective-permute-done.16.got_ref = bf16[1024,256]{1,0:T(8,128)(2,1)S(1)} collective-permute-done((bf16[1024,256]{1,0:T(8,128)(2,1)S(1)}, bf16[1024,256]{1,0:T(8,128)(2,1)S(1)}, u32[]{:S(2)}, u32[]{:S(2)}) %collective-permute-start.16) | collective-permute-done | bytes 524320 | tf_op jit(solution)/shard_map/ppermute | solution.py:417
  73.4 2.1 %base.1.base_ref = f32[512,512]{1,0:T(8,128)S(1)} custom-call(s32[1]{0:T(128)} %bitcast.1.at_ref, s32[1]{0:T(128)} %bitcast.2.dp_ref, s32[1]{0:T(128)} %bitcast.core_ref, s32[1,6]{1,0:T(1,128)S(1)} %copy-done.5, s32[6]{0:T(128)S(1)} %copy-done.7, bf16[512,2688]{1,0:T(8,128)(2,1)S(1)} %pack.1.x_ref.own_ref, bf16[8192,512]{1,0:T(8,128)(2,1)S(1)} %bitcast.7, ...), custom_call_target="tpu_custom_call" | custom-call | flops 1 | bytes 1 | tf_op jit(solution)/shard_map/base/pallas_call | solution.py:271
  76.8 6.7 %collective-permute-done.24.refs_1_ = bf16[1024,256]{1,0:T(8,128)(2,1)S(1)} collective-permute-done((bf16[1024,256]{1,0:T(8,128)(2,1)S(1)}, bf16[1024,256]{1,0:T(8,128)(2,1)S(1)}, u32[]{:S(2)}, u32[]{:S(2)}) %collective-permute-start.24) | collective-permute-done | bytes 524320 | tf_op jit(solution)/shard_map/ppermute | solution.py:33
  83.6 1.5 %collective-permute-done.25.refs_3_ = bf16[512,256]{1,0:T(8,128)(2,1)S(1)} collective-permute-done((bf16[512,256]{1,0:T(8,128)(2,1)S(1)}, bf16[512,256]{1,0:T(8,128)(2,1)S(1)}, u32[]{:S(2)}, u32[]{:S(2)}) %collective-permute-start.25) | collective-permute-done | bytes 262176 | tf_op jit(solution)/shard_map/ppermute | solution.py:33
  85.1 2.0 %finish.1 = bf16[768,512]{1,0:T(8,128)(2,1)} custom-call(s32[1]{0:T(128)} %bitcast.core_ref, s32[1,6]{1,0:T(1,128)S(1)} %copy-done.5, f32[512,512]{1,0:T(8,128)S(1)} %base.1.base_ref, bf16[1024,256]{1,0:T(8,128)(2,1)S(1)} %collective-permute-done.17.refs_0_, bf16[1024,256]{1,0:T(8,128)(2,1)S(1)} %collective-permute-done.24.refs_1_, ...), custom_call_target="tpu_custom_call" | custom-call | flops 1 | bytes 1 | tf_op jit(solution)/shard_map/finish/pallas_call | solution.py:354
  (67 shorter events, 20.7 us)
Async XLA Ops:
  1.8 16.3 %collective-permute-start = (bf16[512,256]{1,0:T(8,128)(2,1)S(1)}, bf16[512,256]{1,0:T(8,128)(2,1)S(1)}, u32[]{:S(2)}, u32[]{:S(2)}) collective-permute-start(bf16[512,256]{1,0:T(8,128)(2,1)S(1)} %get-tuple-element.47), channel_id=1, source_target_pairs={{0,12},{4,8},{8,4},{12,0},{1,13},{5,9},{9,5},{13,1},{2,14},{6,10},... | collective-permute-start | bytes 786440 | tf_op jit(solution)/shard_map/ppermute | solution.py:33
  8.8 9.2 %collective-permute-start.1 = (bf16[32,2560]{1,0:T(8,128)(2,1)}, bf16[32,2560]{1,0:T(8,128)(2,1)S(1)}, u32[]{:S(2)}, u32[]{:S(2)}) collective-permute-start(bf16[32,2560]{1,0:T(8,128)(2,1)} %get-tuple-element.25), channel_id=1, source_target_pairs={{0,2},{2,0},{1,3},{3,1},{4,6},{6,4},{5,7},{7,5},{8,10},{10,8},{9,1... | collective-permute-start | bytes 491528 | tf_op jit(solution)/shard_map/ppermute | solution.py:29
  10.2 7.9 %collective-permute-start.2 = (bf16[32,2560]{1,0:T(8,128)(2,1)}, bf16[32,2560]{1,0:T(8,128)(2,1)S(1)}, u32[]{:S(2)}, u32[]{:S(2)}) collective-permute-start(bf16[32,2560]{1,0:T(8,128)(2,1)} %get-tuple-element.26), channel_id=1, source_target_pairs={{0,2},{2,0},{1,3},{3,1},{4,6},{6,4},{5,7},{7,5},{8,10},{10,8},{9,1... | collective-permute-start | bytes 491528 | tf_op jit(solution)/shard_map/ppermute | solution.py:29
  18.1 5.1 %collective-permute-start.3 = (bf16[512,2688]{1,0:T(8,128)(2,1)S(1)}, bf16[512,2688]{1,0:T(8,128)(2,1)S(1)}, u32[]{:S(2)}, u32[]{:S(2)}) collective-permute-start(bf16[512,2688]{1,0:T(8,128)(2,1)S(1)} %pack.1.x_ref.own_ref), channel_id=1, source_target_pairs={{0,1},{1,0},{2,3},{3,2},{4,5},{5,4},{6,7},{7,6},{8,9},{9,8},{10,11... | collective-permute-start | bytes 8257544 | tf_op jit(solution)/shard_map/ppermute | solution.py:33
  18.2 7.5 %collective-permute-start.4 = (bf16[64,2560]{1,0:T(8,128)(2,1)S(1)}, bf16[64,2560]{1,0:T(8,128)(2,1)S(1)}, u32[]{:S(2)}, u32[]{:S(2)}) collective-permute-start(bf16[64,2560]{1,0:T(8,128)(2,1)S(1)} %constant_dynamic-update-slice_fusion.refs_0_), channel_id=1, source_target_pairs={{0,1},{1,0},{2,3},{3,2},{4,5},{5,4},{6,7},{7,6},{8,9},{9,8},{10,11... | collective-permute-start | bytes 983048 | tf_op jit(solution)/shard_map/ppermute | solution.py:33
  18.8 14.7 %collective-permute-start.5 = (bf16[512,256]{1,0:T(8,128)(2,1)S(1)}, bf16[512,256]{1,0:T(8,128)(2,1)S(1)}, u32[]{:S(2)}, u32[]{:S(2)}) collective-permute-start(bf16[512,256]{1,0:T(8,128)(2,1)S(1)} %get-tuple-element.29), channel_id=1, source_target_pairs={{0,8},{4,12},{8,0},{12,4},{1,9},{5,13},{9,1},{13,5},{2,10},{6,14},... | collective-permute-start | bytes 786440 | tf_op jit(solution)/shard_map/ppermute | solution.py:33
  20.2 15.3 %collective-permute-start.8 = (bf16[512,256]{1,0:T(8,128)(2,1)S(1)}, bf16[512,256]{1,0:T(8,128)(2,1)S(1)}, u32[]{:S(2)}, u32[]{:S(2)}) collective-permute-start(bf16[512,256]{1,0:T(8,128)(2,1)S(1)} %collective-permute-done.refs_0_), channel_id=1, source_target_pairs={{0,2},{2,0},{16,18},{18,16},{1,3},{3,1},{17,19},{19,17},{4,6},{6,4... | collective-permute-start | bytes 786440 | tf_op jit(solution)/shard_map/ppermute | solution.py:33
  21.7 13.8 %collective-permute-start.9 = (bf16[512,256]{1,0:T(8,128)(2,1)S(1)}, bf16[512,256]{1,0:T(8,128)(2,1)S(1)}, u32[]{:S(2)}, u32[]{:S(2)}) collective-permute-start(bf16[512,256]{1,0:T(8,128)(2,1)S(1)} %collective-permute-done.refs_0_), channel_id=1, source_target_pairs={{0,16},{2,18},{16,0},{18,2},{1,17},{3,19},{17,1},{19,3},{4,20},{6,... | collective-permute-start | bytes 786440 | tf_op jit(solution)/shard_map/ppermute | solution.py:33
  23.2 12.2 %collective-permute-start.10 = (bf16[512,256]{1,0:T(8,128)(2,1)S(1)}, bf16[512,256]{1,0:T(8,128)(2,1)S(1)}, u32[]{:S(2)}, u32[]{:S(2)}) collective-permute-start(bf16[512,256]{1,0:T(8,128)(2,1)S(1)} %collective-permute-done.refs_0_), channel_id=1, source_target_pairs={{0,18},{2,16},{16,2},{18,0},{1,19},{3,17},{17,3},{19,1},{4,22},{6,... | collective-permute-start | bytes 786440 | tf_op jit(solution)/shard_map/ppermute | solution.py:33
  33.4 6.8 %collective-permute-start.6 = (bf16[512,128]{1,0:T(8,128)(2,1)S(1)}, bf16[512,128]{1,0:T(8,128)(2,1)S(1)}, u32[]{:S(2)}, u32[]{:S(2)}) collective-permute-start(bf16[512,128]{1,0:T(8,128)(2,1)S(1)} %low_part.1), channel_id=1, source_target_pairs={{0,4},{4,0},{8,12},{12,8},{1,5},{5,1},{9,13},{13,9},{2,6},{6,2},{1... | collective-permute-start | bytes 393224 | tf_op jit(solution)/shard_map/ppermute | solution.py:33
  33.5 11.0 %collective-permute-start.11 = (bf16[512,256]{1,0:T(8,128)(2,1)S(1)}, bf16[512,256]{1,0:T(8,128)(2,1)S(1)}, u32[]{:S(2)}, u32[]{:S(2)}) collective-permute-start(bf16[512,256]{1,0:T(8,128)(2,1)S(1)} %get-tuple-element.33), channel_id=1, source_target_pairs={{0,4},{4,0},{8,12},{12,8},{1,5},{5,1},{9,13},{13,9},{2,6},{6,2},{1... | collective-permute-start | bytes 786440 | tf_op jit(solution)/shard_map/ppermute | solution.py:33
  35.5 9.3 %collective-permute-start.12 = (bf16[512,256]{1,0:T(8,128)(2,1)S(1)}, bf16[512,256]{1,0:T(8,128)(2,1)S(1)}, u32[]{:S(2)}, u32[]{:S(2)}) collective-permute-start(bf16[512,256]{1,0:T(8,128)(2,1)S(1)} %collective-permute-done.5.refs_0_), channel_id=1, source_target_pairs={{0,2},{2,0},{16,18},{18,16},{1,3},{3,1},{17,19},{19,17},{4,6},{6,4... | collective-permute-start | bytes 786440 | tf_op jit(solution)/shard_map/ppermute | solution.py:33
  37.0 13.0 %collective-permute-start.13 = (bf16[512,256]{1,0:T(8,128)(2,1)S(1)}, bf16[512,256]{1,0:T(8,128)(2,1)S(1)}, u32[]{:S(2)}, u32[]{:S(2)}) collective-permute-start(bf16[512,256]{1,0:T(8,128)(2,1)S(1)} %collective-permute-done.5.refs_0_), channel_id=1, source_target_pairs={{0,16},{2,18},{16,0},{18,2},{1,17},{3,19},{17,1},{19,3},{4,20},{6,... | collective-permute-start | bytes 786440 | tf_op jit(solution)/shard_map/ppermute | solution.py:33
  38.6 11.5 %collective-permute-start.14 = (bf16[512,256]{1,0:T(8,128)(2,1)S(1)}, bf16[512,256]{1,0:T(8,128)(2,1)S(1)}, u32[]{:S(2)}, u32[]{:S(2)}) collective-permute-start(bf16[512,256]{1,0:T(8,128)(2,1)S(1)} %collective-permute-done.5.refs_0_), channel_id=1, source_target_pairs={{0,18},{2,16},{16,2},{18,0},{1,19},{3,17},{17,3},{19,1},{4,22},{6,... | collective-permute-start | bytes 786440 | tf_op jit(solution)/shard_map/ppermute | solution.py:33
  40.3 16.1 %collective-permute-start.15 = (bf16[1024,256]{1,0:T(8,128)(2,1)S(1)}, bf16[1024,256]{1,0:T(8,128)(2,1)S(1)}, u32[]{:S(2)}, u32[]{:S(2)}) collective-permute-start(bf16[1024,256]{1,0:T(8,128)(2,1)S(1)} %panel.3.own_ref), channel_id=1, source_target_pairs={{0,4},{12,8},{1,5},{13,9},{2,6},{14,10},{3,7},{15,11},{16,20},{28,... | collective-permute-start | bytes 1572872 | tf_op jit(solution)/shard_map/ppermute | solution.py:412
  44.5 11.8 %collective-permute-start.7 = (bf16[512,128]{1,0:T(8,128)(2,1)S(1)}, bf16[512,128]{1,0:T(8,128)(2,1)S(1)}, u32[]{:S(2)}, u32[]{:S(2)}) collective-permute-start(bf16[512,128]{1,0:T(8,128)(2,1)S(1)} %add_convert_fusion.2), channel_id=1, source_target_pairs={{0,8},{4,12},{8,0},{12,4},{1,9},{5,13},{9,1},{13,5},{2,10},{6,14},... | collective-permute-start | bytes 393224 | tf_op jit(solution)/shard_map/ppermute | solution.py:33
  50.1 11.8 %collective-permute-start.19 = (bf16[512,256]{1,0:T(8,128)(2,1)S(1)}, bf16[512,256]{1,0:T(8,128)(2,1)S(1)}, u32[]{:S(2)}, u32[]{:S(2)}) collective-permute-start(bf16[512,256]{1,0:T(8,128)(2,1)S(1)} %collective-permute-done.11.refs_0_), channel_id=1, source_target_pairs={{0,2},{2,0},{16,18},{18,16},{1,3},{3,1},{17,19},{19,17},{4,6},{6,4... | collective-permute-start | bytes 786440 | tf_op jit(solution)/shard_map/ppermute | solution.py:33
  51.3 12.1 %collective-permute-start.20 = (bf16[512,256]{1,0:T(8,128)(2,1)S(1)}, bf16[512,256]{1,0:T(8,128)(2,1)S(1)}, u32[]{:S(2)}, u32[]{:S(2)}) collective-permute-start(bf16[512,256]{1,0:T(8,128)(2,1)S(1)} %collective-permute-done.11.refs_0_), channel_id=1, source_target_pairs={{0,16},{2,18},{16,0},{18,2},{1,17},{3,19},{17,1},{19,3},{4,20},{6,... | collective-permute-start | bytes 786440 | tf_op jit(solution)/shard_map/ppermute | solution.py:33
  52.1 11.3 %collective-permute-start.21 = (bf16[512,256]{1,0:T(8,128)(2,1)S(1)}, bf16[512,256]{1,0:T(8,128)(2,1)S(1)}, u32[]{:S(2)}, u32[]{:S(2)}) collective-permute-start(bf16[512,256]{1,0:T(8,128)(2,1)S(1)} %collective-permute-done.11.refs_0_), channel_id=1, source_target_pairs={{0,18},{2,16},{16,2},{18,0},{1,19},{3,17},{17,3},{19,1},{4,22},{6,... | collective-permute-start | bytes 786440 | tf_op jit(solution)/shard_map/ppermute | solution.py:33
  57.7 14.7 %collective-permute-start.16 = (bf16[1024,256]{1,0:T(8,128)(2,1)S(1)}, bf16[1024,256]{1,0:T(8,128)(2,1)S(1)}, u32[]{:S(2)}, u32[]{:S(2)}) collective-permute-start(bf16[1024,256]{1,0:T(8,128)(2,1)S(1)} %panel.4), channel_id=1, source_target_pairs={{0,4},{12,8},{4,12},{8,0},{1,5},{13,9},{5,13},{9,1},{2,6},{14,10},... | collective-permute-start | bytes 1572872 | tf_op jit(solution)/shard_map/ppermute | solution.py:417
  63.4 9.8 %collective-permute-start.22 = (bf16[64,2560]{1,0:T(8,128)(2,1)S(1)}, bf16[64,2560]{1,0:T(8,128)(2,1)S(1)}, u32[]{:S(2)}, u32[]{:S(2)}) collective-permute-start(bf16[64,2560]{1,0:T(8,128)(2,1)S(1)} %get-tuple-element.40), channel_id=1, source_target_pairs={{0,2},{2,0},{1,3},{3,1},{4,6},{6,4},{5,7},{7,5},{8,10},{10,8},{9,1... | collective-permute-start | bytes 983048 | tf_op jit(solution)/shard_map/ppermute | solution.py:29
  65.3 18.1 %collective-permute-start.24 = (bf16[1024,256]{1,0:T(8,128)(2,1)S(1)}, bf16[1024,256]{1,0:T(8,128)(2,1)S(1)}, u32[]{:S(2)}, u32[]{:S(2)}) collective-permute-start(bf16[1024,256]{1,0:T(8,128)(2,1)S(1)} %panel.5), channel_id=1, source_target_pairs={{0,4},{4,0},{8,12},{12,8},{1,5},{5,1},{9,13},{13,9},{2,6},{6,2},{1... | collective-permute-start | bytes 1572872 | tf_op jit(solution)/shard_map/ppermute | solution.py:33
  72.5 4.3 %collective-permute-start.17 = (bf16[1024,256]{1,0:T(8,128)(2,1)S(1)}, bf16[1024,256]{1,0:T(8,128)(2,1)S(1)}, u32[]{:S(2)}, u32[]{:S(2)}) collective-permute-start(bf16[1024,256]{1,0:T(8,128)(2,1)S(1)} %get-tuple-element.36), channel_id=1, source_target_pairs={{4,8},{8,4},{5,9},{9,5},{6,10},{10,6},{7,11},{11,7},{20,24},{24,20... | collective-permute-start | bytes 1572872 | tf_op jit(solution)/shard_map/ppermute | solution.py:422
  73.3 2.3 %collective-permute-start.23 = (bf16[64,2560]{1,0:T(8,128)(2,1)S(1)}, bf16[64,2560]{1,0:T(8,128)(2,1)S(1)}, u32[]{:S(2)}, u32[]{:S(2)}) collective-permute-start(bf16[64,2560]{1,0:T(8,128)(2,1)S(1)} %add_convert_fusion.own_ref), channel_id=1, source_target_pairs={{0,1},{1,0},{2,3},{3,2},{4,5},{5,4},{6,7},{7,6},{8,9},{9,8},{10,11... | collective-permute-start | bytes 983048 | tf_op jit(solution)/shard_map/ppermute | solution.py:33
  (12 other events, 71.0 us)

commit v19 on v18

--- a/solution.py
+++ b/solution.py
@@ -408,7 +408,7 @@
         low = low_part(after(dp, x_other), core, block_fill, block_tenant_index, x, own_a, own_b, halves, blocks, rank)
         pieces[0] = after(pieces[0], weight[2], low)
         (y_3,) = panel_product(order, panel_at, x, x_other, pieces, half)
-        low = add_flipped(low, 1, weight[2])
+        low = add_flipped(low, 1)
         far = lax.ppermute(y_3, "tensor", [(0, 1), (3, 2)])
         pieces, order = gathered(after(weight[2], *pieces))
         pieces[0] = after(pieces[0], weight[1])

time: 88.3 us -> 86.8 us (0.983)
  the two profiles are of different devices: /device:TPU:0 before, /device:TPU:23 now
where the time goes in v19:
time: 86.8 us; the launch traced here: 86.5 us
  starting transfers between devices  34.4 us (40%)
  waiting for transfers between devices  28.3 us (33%)
  Pallas kernels  17.2 us (20%)
  local copies, waits for them, and re-layouts  5.56 us (6%)
  between operations  0.91 us (1%)
    ppermute x20, starting transfers between devices, flip(): return lax.ppermute(x, names, [(i, i ^ mask) for i in range(count)])  29.4 us
    ppermute x20, waiting for transfers between devices, flip(): return lax.ppermute(x, names, [(i, i ^ mask) for i in range(count)])  24.7 us
    unnamed x21, local copies, waits for them, and re-layouts  4.37 us
    pallas_call x3, Pallas kernels, panel_product(): pl.pallas_call(functools.partial(panel_kernel, order, len(pieces)), in_sp...  3.74 us
    pallas_call x1, Pallas kernels, pack(): pl.pallas_call(functools.partial(pack_kernel, blocks, rows // blocks), in...  2.83 us
    pallas_call x1, Pallas kernels, low_part(): pl.pallas_call(functools.partial(low_kernel, n_dp, rank, blocks), in_spec...  2.17 us
    pallas_call x1, Pallas kernels, base_product(): pl.pallas_call(functools.partial(base_kernel, n_dp, rank, blocks), grid_s...  2.14 us
    ppermute x3, waiting for transfers between devices, shift(): lax.ppermute(x, name, [(i, (i + step) % count) for i in range(count)])  2.08 us
  transfers between devices with their start and end apart: 26, of which 12 were waited for; matrix products, arithmetic and copies ran while one was open for 0% of the time, Pallas kernels for 17%

profile of v19, /device:TPU:23, one launch (start us, length us, event | category | flops | bytes accessed | tf_op | source)
XLA Modules:
  0.0 86.5 jit_solution(6113672959561217895)
XLA Ops:
  2.1 1.8 %own_half.1 = (bf16[32,2560]{1,0:T(8,128)(2,1)}, bf16[32,2560]{1,0:T(8,128)(2,1)}) custom-call(s32[1]{0:T(128)} %bitcast.core_ref, bf16[128,2048]{1,0:T(8,128)(2,1)} %bitcast.8, bf16[128,512]{1,0:T(8,128)(2,1)} %bitcast.10), custom_call_target="tpu_custom_call" | custom-call | flops 1 | bytes 1 | tf_op jit(solution)/shard_map/own_half/pallas_call | solution.py:75
  5.3 1.9 %copy-done = bf16[768,2048]{1,0:T(8,128)(2,1)S(1)} copy-done((bf16[768,2048]{1,0:T(8,128)(2,1)S(1)}, bf16[768,2048]{1,0:T(8,128)(2,1)}, u32[]{:S(2)}) %copy-start) | copy-done | bytes 3145752
  9.7 2.8 %pack.1.x_ref.own_ref = bf16[512,2688]{1,0:T(8,128)(2,1)S(1)} custom-call(s32[1,6]{1,0:T(1,128)S(1)} %copy-done.4, s32[6]{0:T(128)S(1)} %copy-done.6, bf16[768,2048]{1,0:T(8,128)(2,1)S(1)} %copy-done, bf16[768,512]{1,0:T(8,128)(2,1)S(1)} %copy-done.3), custom_call_target="tpu_custom_call" | custom-call | flops 1 | bytes 1 | tf_op jit(solution)/shard_map/pack/pallas_call | solution.py:104
  12.5 2.2 %collective-permute-done.refs_0_ = bf16[512,256]{1,0:T(8,128)(2,1)S(1)} collective-permute-done((bf16[512,256]{1,0:T(8,128)(2,1)S(1)}, bf16[512,256]{1,0:T(8,128)(2,1)S(1)}, u32[]{:S(2)}, u32[]{:S(2)}) %collective-permute-start) | collective-permute-done | bytes 262176 | tf_op jit(solution)/shard_map/ppermute | solution.py:33
  14.7 1.5 %collective-permute-start.3 = (bf16[512,2688]{1,0:T(8,128)(2,1)S(1)}, bf16[512,2688]{1,0:T(8,128)(2,1)S(1)}, u32[]{:S(2)}, u32[]{:S(2)}) collective-permute-start(bf16[512,2688]{1,0:T(8,128)(2,1)S(1)} %pack.1.x_ref.own_ref), channel_id=1, source_target_pairs={{0,1},{1,0},{2,3},{3,2},{4,5},{5,4},{6,7},{7,6},{8,9},{9,8},{10,11... | collective-permute-start | bytes 8257544 | tf_op jit(solution)/shard_map/ppermute | solution.py:33
  16.4 1.2 %collective-permute-start.7 = (bf16[512,256]{1,0:T(8,128)(2,1)S(1)}, bf16[512,256]{1,0:T(8,128)(2,1)S(1)}, u32[]{:S(2)}, u32[]{:S(2)}) collective-permute-start(bf16[512,256]{1,0:T(8,128)(2,1)S(1)} %get-tuple-element.28), channel_id=1, source_target_pairs={{0,8},{4,12},{8,0},{12,4},{1,9},{5,13},{9,1},{13,5},{2,10},{6,14},... | collective-permute-start | bytes 786440 | tf_op jit(solution)/shard_map/ppermute | solution.py:33
  18.1 2.9 %collective-permute-done.3.other_ref = bf16[512,2688]{1,0:T(8,128)(2,1)S(1)} collective-permute-done((bf16[512,2688]{1,0:T(8,128)(2,1)S(1)}, bf16[512,2688]{1,0:T(8,128)(2,1)S(1)}, u32[]{:S(2)}, u32[]{:S(2)}) %collective-permute-start.3) | collective-permute-done | bytes 2752544 | tf_op jit(solution)/shard_map/ppermute | solution.py:33
  21.4 2.2 %low_part.1 = bf16[512,128]{1,0:T(8,128)(2,1)S(1)} custom-call(s32[1]{0:T(128)} %bitcast.2.dp_ref, s32[1]{0:T(128)} %bitcast.core_ref, s32[1,6]{1,0:T(1,128)S(1)} %copy-done.4, s32[6]{0:T(128)S(1)} %copy-done.6, bf16[512,2688]{1,0:T(8,128)(2,1)S(1)} %pack.1.x_ref.own_ref, bf16[128,2048]{1,0:T(8,128)(2,1)S(1)} %bitcast.9, bf16[128,512]{1,0:T(8,128)(2,1)S(1)} %bitcast.11, ...), custom_call_target="tpu_custom_call" | custom-call | flops 1 | bytes 1 | tf_op jit(solution)/shard_map/low_part/pallas_call | solution.py:147
  23.7 5.5 %collective-permute-done.7.refs_0_ = bf16[512,256]{1,0:T(8,128)(2,1)S(1)} collective-permute-done((bf16[512,256]{1,0:T(8,128)(2,1)S(1)}, bf16[512,256]{1,0:T(8,128)(2,1)S(1)}, u32[]{:S(2)}, u32[]{:S(2)}) %collective-permute-start.7) | collective-permute-done | bytes 262176 | tf_op jit(solution)/shard_map/ppermute | solution.py:33
  34.3 1.3 %collective-permute-start.15 = (bf16[1024,256]{1,0:T(8,128)(2,1)S(1)}, bf16[1024,256]{1,0:T(8,128)(2,1)S(1)}, u32[]{:S(2)}, u32[]{:S(2)}) collective-permute-start(bf16[1024,256]{1,0:T(8,128)(2,1)S(1)} %panel.3.own_ref), channel_id=1, source_target_pairs={{0,4},{12,8},{1,5},{13,9},{2,6},{14,10},{3,7},{15,11},{16,20},{28,... | collective-permute-start | bytes 1572872 | tf_op jit(solution)/shard_map/ppermute | solution.py:412
  36.6 3.2 %collective-permute-start.6 = (bf16[512,128]{1,0:T(8,128)(2,1)S(1)}, bf16[512,128]{1,0:T(8,128)(2,1)S(1)}, u32[]{:S(2)}, u32[]{:S(2)}) collective-permute-start(bf16[512,128]{1,0:T(8,128)(2,1)S(1)} %add_convert_fusion.2), channel_id=1, source_target_pairs={{0,8},{4,12},{8,0},{12,4},{1,9},{5,13},{9,1},{13,5},{2,10},{6,14},... | collective-permute-start | bytes 393224 | tf_op jit(solution)/shard_map/ppermute | solution.py:33
  39.8 3.3 %collective-permute-done.14.refs_3_ = bf16[512,256]{1,0:T(8,128)(2,1)S(1)} collective-permute-done((bf16[512,256]{1,0:T(8,128)(2,1)S(1)}, bf16[512,256]{1,0:T(8,128)(2,1)S(1)}, u32[]{:S(2)}, u32[]{:S(2)}) %collective-permute-start.14) | collective-permute-done | bytes 262176 | tf_op jit(solution)/shard_map/ppermute | solution.py:33
  43.2 2.6 %collective-permute-start.21 = (bf16[512,256]{1,0:T(8,128)(2,1)S(1)}, bf16[512,256]{1,0:T(8,128)(2,1)S(1)}, u32[]{:S(2)}, u32[]{:S(2)}) collective-permute-start(bf16[512,256]{1,0:T(8,128)(2,1)S(1)} %collective-permute-done.11.refs_0_), channel_id=1, source_target_pairs={{0,18},{2,16},{16,2},{18,0},{1,19},{3,17},{17,3},{19,1},{4,22},{6,... | collective-permute-start | bytes 786440 | tf_op jit(solution)/shard_map/ppermute | solution.py:33
  45.8 6.7 %collective-permute-done.6 = bf16[512,128]{1,0:T(8,128)(2,1)S(1)} collective-permute-done((bf16[512,128]{1,0:T(8,128)(2,1)S(1)}, bf16[512,128]{1,0:T(8,128)(2,1)S(1)}, u32[]{:S(2)}, u32[]{:S(2)}) %collective-permute-start.6) | collective-permute-done | bytes 131104 | tf_op jit(solution)/shard_map/ppermute | solution.py:33
  52.5 1.3 %panel.4 = bf16[1024,256]{1,0:T(8,128)(2,1)S(1)} custom-call(s32[1]{0:T(128)} %bitcast.5.place_ref, bf16[512,2688]{1,0:T(8,128)(2,1)S(1)} %pack.1.x_ref.own_ref, bf16[512,2688]{1,0:T(8,128)(2,1)S(1)} %collective-permute-done.3.other_ref, bf16[512,256]{1,0:T(8,128)(2,1)S(1)} %collective-permute-done.7.refs_0_, ...), custom_call_target="tpu_custom_call" | custom-call | flops 1 | bytes 1 | tf_op jit(solution)/shard_map/panel/pallas_call | solution.py:219
  53.8 3.3 %collective-permute-start.18 = (bf16[512,128]{1,0:T(8,128)(2,1)S(1)}, bf16[512,128]{1,0:T(8,128)(2,1)S(1)}, u32[]{:S(2)}, u32[]{:S(2)}) collective-permute-start(bf16[512,128]{1,0:T(8,128)(2,1)S(1)} %add_convert_fusion.1.low_ref), channel_id=1, source_target_pairs={{0,1},{1,0},{2,3},{3,2},{4,5},{5,4},{6,7},{7,6},{8,9},{9,8},{10,11... | collective-permute-start | bytes 393224 | tf_op jit(solution)/shard_map/ppermute | solution.py:33
  60.8 1.7 %collective-permute-start.24 = (bf16[1024,256]{1,0:T(8,128)(2,1)S(1)}, bf16[1024,256]{1,0:T(8,128)(2,1)S(1)}, u32[]{:S(2)}, u32[]{:S(2)}) collective-permute-start(bf16[1024,256]{1,0:T(8,128)(2,1)S(1)} %panel.5), channel_id=1, source_target_pairs={{0,4},{4,0},{8,12},{12,8},{1,5},{5,1},{9,13},{13,9},{2,6},{6,2},{1... | collective-permute-start | bytes 1572872 | tf_op jit(solution)/shard_map/ppermute | solution.py:33
  62.5 1.5 %collective-permute-done.16.got_ref = bf16[1024,256]{1,0:T(8,128)(2,1)S(1)} collective-permute-done((bf16[1024,256]{1,0:T(8,128)(2,1)S(1)}, bf16[1024,256]{1,0:T(8,128)(2,1)S(1)}, u32[]{:S(2)}, u32[]{:S(2)}) %collective-permute-start.16) | collective-permute-done | bytes 524320 | tf_op jit(solution)/shard_map/ppermute | solution.py:417
  64.2 1.9 %collective-permute-start.17 = (bf16[1024,256]{1,0:T(8,128)(2,1)S(1)}, bf16[1024,256]{1,0:T(8,128)(2,1)S(1)}, u32[]{:S(2)}, u32[]{:S(2)}) collective-permute-start(bf16[1024,256]{1,0:T(8,128)(2,1)S(1)} %get-tuple-element.34), channel_id=1, source_target_pairs={{4,8},{8,4},{5,9},{9,5},{6,10},{10,6},{7,11},{11,7},{20,24},{24,20... | collective-permute-start | bytes 1572872 | tf_op jit(solution)/shard_map/ppermute | solution.py:422
  66.1 2.1 %collective-permute-done.22 = bf16[64,2560]{1,0:T(8,128)(2,1)S(1)} collective-permute-done((bf16[64,2560]{1,0:T(8,128)(2,1)S(1)}, bf16[64,2560]{1,0:T(8,128)(2,1)S(1)}, u32[]{:S(2)}, u32[]{:S(2)}) %collective-permute-start.22) | collective-permute-done | bytes 327712 | tf_op jit(solution)/shard_map/ppermute | solution.py:29
  68.3 5.9 %collective-permute-start.23 = (bf16[64,2560]{1,0:T(8,128)(2,1)S(1)}, bf16[64,2560]{1,0:T(8,128)(2,1)S(1)}, u32[]{:S(2)}, u32[]{:S(2)}) collective-permute-start(bf16[64,2560]{1,0:T(8,128)(2,1)S(1)} %add_convert_fusion.own_ref), channel_id=1, source_target_pairs={{0,1},{1,0},{2,3},{3,2},{4,5},{5,4},{6,7},{7,6},{8,9},{9,8},{10,11... | collective-permute-start | bytes 983048 | tf_op jit(solution)/shard_map/ppermute | solution.py:33
  74.2 2.1 %base.1.base_ref = f32[512,512]{1,0:T(8,128)S(1)} custom-call(s32[1]{0:T(128)} %bitcast.1.at_ref, s32[1]{0:T(128)} %bitcast.2.dp_ref, s32[1]{0:T(128)} %bitcast.core_ref, s32[1,6]{1,0:T(1,128)S(1)} %copy-done.5, s32[6]{0:T(128)S(1)} %copy-done.7, bf16[512,2688]{1,0:T(8,128)(2,1)S(1)} %pack.1.x_ref.own_ref, bf16[8192,512]{1,0:T(8,128)(2,1)S(1)} %bitcast.7, ...), custom_call_target="tpu_custom_call" | custom-call | flops 1 | bytes 1 | tf_op jit(solution)/shard_map/base/pallas_call | solution.py:271
  77.6 5.7 %collective-permute-start.25 = (bf16[512,256]{1,0:T(8,128)(2,1)S(1)}, bf16[512,256]{1,0:T(8,128)(2,1)S(1)}, u32[]{:S(2)}, u32[]{:S(2)}) collective-permute-start(bf16[512,256]{1,0:T(8,128)(2,1)S(1)} %other_rows.1), channel_id=1, source_target_pairs={{0,1},{1,0},{2,3},{3,2},{4,5},{5,4},{6,7},{7,6},{8,9},{9,8},{10,11... | collective-permute-start | bytes 786440 | tf_op jit(solution)/shard_map/ppermute | solution.py:33
  84.5 2.0 %finish.1 = bf16[768,512]{1,0:T(8,128)(2,1)} custom-call(s32[1]{0:T(128)} %bitcast.core_ref, s32[1,6]{1,0:T(1,128)S(1)} %copy-done.5, f32[512,512]{1,0:T(8,128)S(1)} %base.1.base_ref, bf16[1024,256]{1,0:T(8,128)(2,1)S(1)} %collective-permute-done.17.refs_0_, bf16[1024,256]{1,0:T(8,128)(2,1)S(1)} %collective-permute-done.24.refs_1_, ...), custom_call_target="tpu_custom_call" | custom-call | flops 1 | bytes 1 | tf_op jit(solution)/shard_map/finish/pallas_call | solution.py:354
  (67 shorter events, 19.0 us)
Async XLA Ops:
  1.8 12.9 %collective-permute-start = (bf16[512,256]{1,0:T(8,128)(2,1)S(1)}, bf16[512,256]{1,0:T(8,128)(2,1)S(1)}, u32[]{:S(2)}, u32[]{:S(2)}) collective-permute-start(bf16[512,256]{1,0:T(8,128)(2,1)S(1)} %get-tuple-element.44), channel_id=1, source_target_pairs={{0,12},{4,8},{8,4},{12,0},{1,13},{5,9},{9,5},{13,1},{2,14},{6,10},... | collective-permute-start | bytes 786440 | tf_op jit(solution)/shard_map/ppermute | solution.py:33
  3.9 8.6 %collective-permute-start.1 = (bf16[32,2560]{1,0:T(8,128)(2,1)}, bf16[32,2560]{1,0:T(8,128)(2,1)S(1)}, u32[]{:S(2)}, u32[]{:S(2)}) collective-permute-start(bf16[32,2560]{1,0:T(8,128)(2,1)} %get-tuple-element.24), channel_id=1, source_target_pairs={{0,2},{2,0},{1,3},{3,1},{4,6},{6,4},{5,7},{7,5},{8,10},{10,8},{9,1... | collective-permute-start | bytes 491528 | tf_op jit(solution)/shard_map/ppermute | solution.py:29
  4.1 8.4 %collective-permute-start.2 = (bf16[32,2560]{1,0:T(8,128)(2,1)}, bf16[32,2560]{1,0:T(8,128)(2,1)S(1)}, u32[]{:S(2)}, u32[]{:S(2)}) collective-permute-start(bf16[32,2560]{1,0:T(8,128)(2,1)} %get-tuple-element.25), channel_id=1, source_target_pairs={{0,2},{2,0},{1,3},{3,1},{4,6},{6,4},{5,7},{7,5},{8,10},{10,8},{9,1... | collective-permute-start | bytes 491528 | tf_op jit(solution)/shard_map/ppermute | solution.py:29
  14.7 6.3 %collective-permute-start.3 = (bf16[512,2688]{1,0:T(8,128)(2,1)S(1)}, bf16[512,2688]{1,0:T(8,128)(2,1)S(1)}, u32[]{:S(2)}, u32[]{:S(2)}) collective-permute-start(bf16[512,2688]{1,0:T(8,128)(2,1)S(1)} %pack.1.x_ref.own_ref), channel_id=1, source_target_pairs={{0,1},{1,0},{2,3},{3,2},{4,5},{5,4},{6,7},{7,6},{8,9},{9,8},{10,11... | collective-permute-start | bytes 8257544 | tf_op jit(solution)/shard_map/ppermute | solution.py:33
  16.4 12.8 %collective-permute-start.7 = (bf16[512,256]{1,0:T(8,128)(2,1)S(1)}, bf16[512,256]{1,0:T(8,128)(2,1)S(1)}, u32[]{:S(2)}, u32[]{:S(2)}) collective-permute-start(bf16[512,256]{1,0:T(8,128)(2,1)S(1)} %get-tuple-element.28), channel_id=1, source_target_pairs={{0,8},{4,12},{8,0},{12,4},{1,9},{5,13},{9,1},{13,5},{2,10},{6,14},... | collective-permute-start | bytes 786440 | tf_op jit(solution)/shard_map/ppermute | solution.py:33
  17.6 12.0 %collective-permute-start.8 = (bf16[512,256]{1,0:T(8,128)(2,1)S(1)}, bf16[512,256]{1,0:T(8,128)(2,1)S(1)}, u32[]{:S(2)}, u32[]{:S(2)}) collective-permute-start(bf16[512,256]{1,0:T(8,128)(2,1)S(1)} %collective-permute-done.refs_0_), channel_id=1, source_target_pairs={{0,2},{2,0},{16,18},{18,16},{1,3},{3,1},{17,19},{19,17},{4,6},{6,4... | collective-permute-start | bytes 786440 | tf_op jit(solution)/shard_map/ppermute | solution.py:33
  17.9 11.7 %collective-permute-start.9 = (bf16[512,256]{1,0:T(8,128)(2,1)S(1)}, bf16[512,256]{1,0:T(8,128)(2,1)S(1)}, u32[]{:S(2)}, u32[]{:S(2)}) collective-permute-start(bf16[512,256]{1,0:T(8,128)(2,1)S(1)} %collective-permute-done.refs_0_), channel_id=1, source_target_pairs={{0,16},{2,18},{16,0},{18,2},{1,17},{3,19},{17,1},{19,3},{4,20},{6,... | collective-permute-start | bytes 786440 | tf_op jit(solution)/shard_map/ppermute | solution.py:33
  21.0 9.4 %collective-permute-start.10 = (bf16[512,256]{1,0:T(8,128)(2,1)S(1)}, bf16[512,256]{1,0:T(8,128)(2,1)S(1)}, u32[]{:S(2)}, u32[]{:S(2)}) collective-permute-start(bf16[512,256]{1,0:T(8,128)(2,1)S(1)} %collective-permute-done.refs_0_), channel_id=1, source_target_pairs={{0,18},{2,16},{16,2},{18,0},{1,19},{3,17},{17,3},{19,1},{4,22},{6,... | collective-permute-start | bytes 786440 | tf_op jit(solution)/shard_map/ppermute | solution.py:33
  23.6 10.6 %collective-permute-start.5 = (bf16[512,128]{1,0:T(8,128)(2,1)S(1)}, bf16[512,128]{1,0:T(8,128)(2,1)S(1)}, u32[]{:S(2)}, u32[]{:S(2)}) collective-permute-start(bf16[512,128]{1,0:T(8,128)(2,1)S(1)} %low_part.1), channel_id=1, source_target_pairs={{0,4},{4,0},{8,12},{12,8},{1,5},{5,1},{9,13},{13,9},{2,6},{6,2},{1... | collective-permute-start | bytes 393224 | tf_op jit(solution)/shard_map/ppermute | solution.py:33
  29.2 7.4 %collective-permute-start.11 = (bf16[512,256]{1,0:T(8,128)(2,1)S(1)}, bf16[512,256]{1,0:T(8,128)(2,1)S(1)}, u32[]{:S(2)}, u32[]{:S(2)}) collective-permute-start(bf16[512,256]{1,0:T(8,128)(2,1)S(1)} %get-tuple-element.31), channel_id=1, source_target_pairs={{0,4},{4,0},{8,12},{12,8},{1,5},{5,1},{9,13},{13,9},{2,6},{6,2},{1... | collective-permute-start | bytes 786440 | tf_op jit(solution)/shard_map/ppermute | solution.py:33
  30.3 9.5 %collective-permute-start.12 = (bf16[512,256]{1,0:T(8,128)(2,1)S(1)}, bf16[512,256]{1,0:T(8,128)(2,1)S(1)}, u32[]{:S(2)}, u32[]{:S(2)}) collective-permute-start(bf16[512,256]{1,0:T(8,128)(2,1)S(1)} %collective-permute-done.7.refs_0_), channel_id=1, source_target_pairs={{0,2},{2,0},{16,18},{18,16},{1,3},{3,1},{17,19},{19,17},{4,6},{6,4... | collective-permute-start | bytes 786440 | tf_op jit(solution)/shard_map/ppermute | solution.py:33
  30.6 9.2 %collective-permute-start.13 = (bf16[512,256]{1,0:T(8,128)(2,1)S(1)}, bf16[512,256]{1,0:T(8,128)(2,1)S(1)}, u32[]{:S(2)}, u32[]{:S(2)}) collective-permute-start(bf16[512,256]{1,0:T(8,128)(2,1)S(1)} %collective-permute-done.7.refs_0_), channel_id=1, source_target_pairs={{0,16},{2,18},{16,0},{18,2},{1,17},{3,19},{17,1},{19,3},{4,20},{6,... | collective-permute-start | bytes 786440 | tf_op jit(solution)/shard_map/ppermute | solution.py:33
  31.8 11.3 %collective-permute-start.14 = (bf16[512,256]{1,0:T(8,128)(2,1)S(1)}, bf16[512,256]{1,0:T(8,128)(2,1)S(1)}, u32[]{:S(2)}, u32[]{:S(2)}) collective-permute-start(bf16[512,256]{1,0:T(8,128)(2,1)S(1)} %collective-permute-done.7.refs_0_), channel_id=1, source_target_pairs={{0,18},{2,16},{16,2},{18,0},{1,19},{3,17},{17,3},{19,1},{4,22},{6,... | collective-permute-start | bytes 786440 | tf_op jit(solution)/shard_map/ppermute | solution.py:33
  34.3 18.2 %collective-permute-start.15 = (bf16[1024,256]{1,0:T(8,128)(2,1)S(1)}, bf16[1024,256]{1,0:T(8,128)(2,1)S(1)}, u32[]{:S(2)}, u32[]{:S(2)}) collective-permute-start(bf16[1024,256]{1,0:T(8,128)(2,1)S(1)} %panel.3.own_ref), channel_id=1, source_target_pairs={{0,4},{12,8},{1,5},{13,9},{2,6},{14,10},{3,7},{15,11},{16,20},{28,... | collective-permute-start | bytes 1572872 | tf_op jit(solution)/shard_map/ppermute | solution.py:412
  36.6 15.8 %collective-permute-start.6 = (bf16[512,128]{1,0:T(8,128)(2,1)S(1)}, bf16[512,128]{1,0:T(8,128)(2,1)S(1)}, u32[]{:S(2)}, u32[]{:S(2)}) collective-permute-start(bf16[512,128]{1,0:T(8,128)(2,1)S(1)} %add_convert_fusion.2), channel_id=1, source_target_pairs={{0,8},{4,12},{8,0},{12,4},{1,9},{5,13},{9,1},{13,5},{2,10},{6,14},... | collective-permute-start | bytes 393224 | tf_op jit(solution)/shard_map/ppermute | solution.py:33
  43.1 16.0 %collective-permute-start.19 = (bf16[512,256]{1,0:T(8,128)(2,1)S(1)}, bf16[512,256]{1,0:T(8,128)(2,1)S(1)}, u32[]{:S(2)}, u32[]{:S(2)}) collective-permute-start(bf16[512,256]{1,0:T(8,128)(2,1)S(1)} %collective-permute-done.11.refs_0_), channel_id=1, source_target_pairs={{0,2},{2,0},{16,18},{18,16},{1,3},{3,1},{17,19},{19,17},{4,6},{6,4... | collective-permute-start | bytes 786440 | tf_op jit(solution)/shard_map/ppermute | solution.py:33
  43.2 16.0 %collective-permute-start.20 = (bf16[512,256]{1,0:T(8,128)(2,1)S(1)}, bf16[512,256]{1,0:T(8,128)(2,1)S(1)}, u32[]{:S(2)}, u32[]{:S(2)}) collective-permute-start(bf16[512,256]{1,0:T(8,128)(2,1)S(1)} %collective-permute-done.11.refs_0_), channel_id=1, source_target_pairs={{0,16},{2,18},{16,0},{18,2},{1,17},{3,19},{17,1},{19,3},{4,20},{6,... | collective-permute-start | bytes 786440 | tf_op jit(solution)/shard_map/ppermute | solution.py:33
  43.2 16.0 %collective-permute-start.21 = (bf16[512,256]{1,0:T(8,128)(2,1)S(1)}, bf16[512,256]{1,0:T(8,128)(2,1)S(1)}, u32[]{:S(2)}, u32[]{:S(2)}) collective-permute-start(bf16[512,256]{1,0:T(8,128)(2,1)S(1)} %collective-permute-done.11.refs_0_), channel_id=1, source_target_pairs={{0,18},{2,16},{16,2},{18,0},{1,19},{3,17},{17,3},{19,1},{4,22},{6,... | collective-permute-start | bytes 786440 | tf_op jit(solution)/shard_map/ppermute | solution.py:33
  53.7 10.2 %collective-permute-start.16 = (bf16[1024,256]{1,0:T(8,128)(2,1)S(1)}, bf16[1024,256]{1,0:T(8,128)(2,1)S(1)}, u32[]{:S(2)}, u32[]{:S(2)}) collective-permute-start(bf16[1024,256]{1,0:T(8,128)(2,1)S(1)} %panel.4), channel_id=1, source_target_pairs={{0,4},{12,8},{4,12},{8,0},{1,5},{13,9},{5,13},{9,1},{2,6},{14,10},... | collective-permute-start | bytes 1572872 | tf_op jit(solution)/shard_map/ppermute | solution.py:417
  59.2 9.0 %collective-permute-start.22 = (bf16[64,2560]{1,0:T(8,128)(2,1)S(1)}, bf16[64,2560]{1,0:T(8,128)(2,1)S(1)}, u32[]{:S(2)}, u32[]{:S(2)}) collective-permute-start(bf16[64,2560]{1,0:T(8,128)(2,1)S(1)} %get-tuple-element.38), channel_id=1, source_target_pairs={{0,2},{2,0},{1,3},{3,1},{4,6},{6,4},{5,7},{7,5},{8,10},{10,8},{9,1... | collective-permute-start | bytes 983048 | tf_op jit(solution)/shard_map/ppermute | solution.py:29
  60.8 16.8 %collective-permute-start.24 = (bf16[1024,256]{1,0:T(8,128)(2,1)S(1)}, bf16[1024,256]{1,0:T(8,128)(2,1)S(1)}, u32[]{:S(2)}, u32[]{:S(2)}) collective-permute-start(bf16[1024,256]{1,0:T(8,128)(2,1)S(1)} %panel.5), channel_id=1, source_target_pairs={{0,4},{4,0},{8,12},{12,8},{1,5},{5,1},{9,13},{13,9},{2,6},{6,2},{1... | collective-permute-start | bytes 1572872 | tf_op jit(solution)/shard_map/ppermute | solution.py:33
  64.2 13.4 %collective-permute-start.17 = (bf16[1024,256]{1,0:T(8,128)(2,1)S(1)}, bf16[1024,256]{1,0:T(8,128)(2,1)S(1)}, u32[]{:S(2)}, u32[]{:S(2)}) collective-permute-start(bf16[1024,256]{1,0:T(8,128)(2,1)S(1)} %get-tuple-element.34), channel_id=1, source_target_pairs={{4,8},{8,4},{5,9},{9,5},{6,10},{10,6},{7,11},{11,7},{20,24},{24,20... | collective-permute-start | bytes 1572872 | tf_op jit(solution)/shard_map/ppermute | solution.py:422
  68.3 8.1 %collective-permute-start.23 = (bf16[64,2560]{1,0:T(8,128)(2,1)S(1)}, bf16[64,2560]{1,0:T(8,128)(2,1)S(1)}, u32[]{:S(2)}, u32[]{:S(2)}) collective-permute-start(bf16[64,2560]{1,0:T(8,128)(2,1)S(1)} %add_convert_fusion.own_ref), channel_id=1, source_target_pairs={{0,1},{1,0},{2,3},{3,2},{4,5},{5,4},{6,7},{7,6},{8,9},{9,8},{10,11... | collective-permute-start | bytes 983048 | tf_op jit(solution)/shard_map/ppermute | solution.py:33
  77.6 6.9 %collective-permute-start.25 = (bf16[512,256]{1,0:T(8,128)(2,1)S(1)}, bf16[512,256]{1,0:T(8,128)(2,1)S(1)}, u32[]{:S(2)}, u32[]{:S(2)}) collective-permute-start(bf16[512,256]{1,0:T(8,128)(2,1)S(1)} %other_rows.1), channel_id=1, source_target_pairs={{0,1},{1,0},{2,3},{3,2},{4,5},{5,4},{6,7},{7,6},{8,9},{9,8},{10,11... | collective-permute-start | bytes 786440 | tf_op jit(solution)/shard_map/ppermute | solution.py:33
  (12 other events, 98.4 us)

commit v20 on v19

--- a/solution.py
+++ b/solution.py
@@ -62,23 +62,29 @@
 
 
 def half_kernel(core_ref, a_ref, b_ref, *outs):
-    rank, feat, rows = a_ref.shape[0] // 2, a_ref.shape[1], outs[0].shape[0]
-    first = core_ref[0] == 0
+    feat, rows = a_ref.shape[1], outs[0].shape[0]
     for n, out in enumerate(outs):
-        one, other = slice(n * rows, (n + 1) * rows), slice(rank + n * rows, rank + (n + 1) * rows)
-        out[:, :feat] = jnp.where(first, a_ref[one, :], a_ref[other, :])
-        out[:, feat:] = jnp.where(first, b_ref[one, :], b_ref[other, :])
+        out[:, :feat] = a_ref[n * rows : (n + 1) * rows, :]
+        out[:, feat:] = b_ref[n * rows : (n + 1) * rows, :]
 
 
 def own_half(core, a, b, rank):
-    width = a.shape[1] + b.shape[1]
+    feat, cols = a.shape[1], b.shape[1]
+    part = pl.BlockSpec((rank // 2, feat + cols), lambda i, core: (0, 0))
     return pl.pallas_call(
         half_kernel,
-        in_specs=[SMEM] + [VMEM] * 2,
-        out_specs=[VMEM] * 2,
-        out_shape=[shaped((rank // 2, width), BF16)] * 2,
+        grid_spec=pltpu.PrefetchScalarGridSpec(
+            num_scalar_prefetch=1,
+            grid=(1,),
+            in_specs=[
+                pl.BlockSpec((rank, feat), lambda i, core: (core[0], 0)),
+                pl.BlockSpec((rank, cols), lambda i, core: (core[0], 0)),
+            ],
+            out_specs=[part] * 2,
+        ),
+        out_shape=[shaped((rank // 2, feat + cols), BF16)] * 2,
         compiler_params=params(56),
-        cost_estimate=cost(rank * width, 6 * rank * width),
+        cost_estimate=cost(rank * feat, 4 * rank * (feat + cols)),
         name="own_half",
     )(core, a, b)
 

time: 86.8 us -> 86.8 us (level)
  no operation moved by 1% of the time
where the time goes in v20:
time: 86.8 us; the launch traced here: 86.5 us
  starting transfers between devices  34.3 us (40%)
  waiting for transfers between devices  28.5 us (33%)
  Pallas kernels  17.1 us (20%)
  local copies, waits for them, and re-layouts  5.56 us (6%)
  between operations  0.91 us (1%)
    ppermute x20, starting transfers between devices, flip(): return lax.ppermute(x, names, [(i, i ^ mask) for i in range(count)])  29.2 us
    ppermute x20, waiting for transfers between devices, flip(): return lax.ppermute(x, names, [(i, i ^ mask) for i in range(count)])  24.9 us
    unnamed x21, local copies, waits for them, and re-layouts  4.37 us
    pallas_call x3, Pallas kernels, panel_product(): pl.pallas_call(functools.partial(panel_kernel, order, len(pieces)), in_sp...  3.74 us
    pallas_call x1, Pallas kernels, pack(): pl.pallas_call(functools.partial(pack_kernel, blocks, rows // blocks), in...  2.83 us
    pallas_call x1, Pallas kernels, low_part(): pl.pallas_call(functools.partial(low_kernel, n_dp, rank, blocks), in_spec...  2.17 us
    pallas_call x1, Pallas kernels, base_product(): pl.pallas_call(functools.partial(base_kernel, n_dp, rank, blocks), grid_s...  2.14 us
    ppermute x3, waiting for transfers between devices, shift(): lax.ppermute(x, name, [(i, (i + step) % count) for i in range(count)])  2.13 us
  transfers between devices with their start and end apart: 26, of which 12 were waited for; matrix products, arithmetic and copies ran while one was open for 0% of the time, Pallas kernels for 17%

profile of v20, /device:TPU:23, one launch (start us, length us, event | category | flops | bytes accessed | tf_op | source)
XLA Modules:
  0.0 86.5 jit_solution(693217964102128436)
XLA Ops:
  2.1 1.7 %own_half.1 = (bf16[32,2560]{1,0:T(8,128)(2,1)}, bf16[32,2560]{1,0:T(8,128)(2,1)}) custom-call(s32[1]{0:T(128)} %bitcast.core_ref, bf16[128,2048]{1,0:T(8,128)(2,1)} %bitcast.8, bf16[128,512]{1,0:T(8,128)(2,1)} %bitcast.10), custom_call_target="tpu_custom_call" | custom-call | flops 1 | bytes 1 | tf_op jit(solution)/shard_map/own_half/pallas_call | solution.py:74
  5.2 1.9 %copy-done = bf16[768,2048]{1,0:T(8,128)(2,1)S(1)} copy-done((bf16[768,2048]{1,0:T(8,128)(2,1)S(1)}, bf16[768,2048]{1,0:T(8,128)(2,1)}, u32[]{:S(2)}) %copy-start) | copy-done | bytes 3145752
  9.6 2.8 %pack.1.x_ref.own_ref = bf16[512,2688]{1,0:T(8,128)(2,1)S(1)} custom-call(s32[1,6]{1,0:T(1,128)S(1)} %copy-done.4, s32[6]{0:T(128)S(1)} %copy-done.6, bf16[768,2048]{1,0:T(8,128)(2,1)S(1)} %copy-done, bf16[768,512]{1,0:T(8,128)(2,1)S(1)} %copy-done.3), custom_call_target="tpu_custom_call" | custom-call | flops 1 | bytes 1 | tf_op jit(solution)/shard_map/pack/pallas_call | solution.py:110
  12.4 2.3 %collective-permute-done.refs_0_ = bf16[512,256]{1,0:T(8,128)(2,1)S(1)} collective-permute-done((bf16[512,256]{1,0:T(8,128)(2,1)S(1)}, bf16[512,256]{1,0:T(8,128)(2,1)S(1)}, u32[]{:S(2)}, u32[]{:S(2)}) %collective-permute-start) | collective-permute-done | bytes 262176 | tf_op jit(solution)/shard_map/ppermute | solution.py:33
  14.7 1.5 %collective-permute-start.3 = (bf16[512,2688]{1,0:T(8,128)(2,1)S(1)}, bf16[512,2688]{1,0:T(8,128)(2,1)S(1)}, u32[]{:S(2)}, u32[]{:S(2)}) collective-permute-start(bf16[512,2688]{1,0:T(8,128)(2,1)S(1)} %pack.1.x_ref.own_ref), channel_id=1, source_target_pairs={{0,1},{1,0},{2,3},{3,2},{4,5},{5,4},{6,7},{7,6},{8,9},{9,8},{10,11... | collective-permute-start | bytes 8257544 | tf_op jit(solution)/shard_map/ppermute | solution.py:33
  18.0 3.0 %collective-permute-done.3.other_ref = bf16[512,2688]{1,0:T(8,128)(2,1)S(1)} collective-permute-done((bf16[512,2688]{1,0:T(8,128)(2,1)S(1)}, bf16[512,2688]{1,0:T(8,128)(2,1)S(1)}, u32[]{:S(2)}, u32[]{:S(2)}) %collective-permute-start.3) | collective-permute-done | bytes 2752544 | tf_op jit(solution)/shard_map/ppermute | solution.py:33
  21.4 2.2 %low_part.1 = bf16[512,128]{1,0:T(8,128)(2,1)S(1)} custom-call(s32[1]{0:T(128)} %bitcast.2.dp_ref, s32[1]{0:T(128)} %bitcast.core_ref, s32[1,6]{1,0:T(1,128)S(1)} %copy-done.4, s32[6]{0:T(128)S(1)} %copy-done.6, bf16[512,2688]{1,0:T(8,128)(2,1)S(1)} %pack.1.x_ref.own_ref, bf16[128,2048]{1,0:T(8,128)(2,1)S(1)} %bitcast.9, bf16[128,512]{1,0:T(8,128)(2,1)S(1)} %bitcast.11, ...), custom_call_target="tpu_custom_call" | custom-call | flops 1 | bytes 1 | tf_op jit(solution)/shard_map/low_part/pallas_call | solution.py:153
  23.7 5.5 %collective-permute-done.7.refs_0_ = bf16[512,256]{1,0:T(8,128)(2,1)S(1)} collective-permute-done((bf16[512,256]{1,0:T(8,128)(2,1)S(1)}, bf16[512,256]{1,0:T(8,128)(2,1)S(1)}, u32[]{:S(2)}, u32[]{:S(2)}) %collective-permute-start.7) | collective-permute-done | bytes 262176 | tf_op jit(solution)/shard_map/ppermute | solution.py:33
  33.0 1.2 %panel.3.own_ref = bf16[1024,256]{1,0:T(8,128)(2,1)S(1)} custom-call(s32[1]{0:T(128)} %bitcast.5.place_ref, bf16[512,2688]{1,0:T(8,128)(2,1)S(1)} %pack.1.x_ref.own_ref, bf16[512,2688]{1,0:T(8,128)(2,1)S(1)} %collective-permute-done.3.other_ref, bf16[512,256]{1,0:T(8,128)(2,1)S(1)} %collective-permute-done.refs_0_, ...), custom_call_target="tpu_custom_call" | custom-call | flops 1 | bytes 1 | tf_op jit(solution)/shard_map/panel/pallas_call | solution.py:225
  34.2 1.3 %collective-permute-start.15 = (bf16[1024,256]{1,0:T(8,128)(2,1)S(1)}, bf16[1024,256]{1,0:T(8,128)(2,1)S(1)}, u32[]{:S(2)}, u32[]{:S(2)}) collective-permute-start(bf16[1024,256]{1,0:T(8,128)(2,1)S(1)} %panel.3.own_ref), channel_id=1, source_target_pairs={{0,4},{12,8},{1,5},{13,9},{2,6},{14,10},{3,7},{15,11},{16,20},{28,... | collective-permute-start | bytes 1572872 | tf_op jit(solution)/shard_map/ppermute | solution.py:418
  36.5 3.3 %collective-permute-start.6 = (bf16[512,128]{1,0:T(8,128)(2,1)S(1)}, bf16[512,128]{1,0:T(8,128)(2,1)S(1)}, u32[]{:S(2)}, u32[]{:S(2)}) collective-permute-start(bf16[512,128]{1,0:T(8,128)(2,1)S(1)} %add_convert_fusion.2), channel_id=1, source_target_pairs={{0,8},{4,12},{8,0},{12,4},{1,9},{5,13},{9,1},{13,5},{2,10},{6,14},... | collective-permute-start | bytes 393224 | tf_op jit(solution)/shard_map/ppermute | solution.py:33
  39.8 3.2 %collective-permute-done.14.refs_3_ = bf16[512,256]{1,0:T(8,128)(2,1)S(1)} collective-permute-done((bf16[512,256]{1,0:T(8,128)(2,1)S(1)}, bf16[512,256]{1,0:T(8,128)(2,1)S(1)}, u32[]{:S(2)}, u32[]{:S(2)}) %collective-permute-start.14) | collective-permute-done | bytes 262176 | tf_op jit(solution)/shard_map/ppermute | solution.py:33
  43.2 2.5 %collective-permute-start.21 = (bf16[512,256]{1,0:T(8,128)(2,1)S(1)}, bf16[512,256]{1,0:T(8,128)(2,1)S(1)}, u32[]{:S(2)}, u32[]{:S(2)}) collective-permute-start(bf16[512,256]{1,0:T(8,128)(2,1)S(1)} %collective-permute-done.11.refs_0_), channel_id=1, source_target_pairs={{0,18},{2,16},{16,2},{18,0},{1,19},{3,17},{17,3},{19,1},{4,22},{6,... | collective-permute-start | bytes 786440 | tf_op jit(solution)/shard_map/ppermute | solution.py:33
  45.6 6.7 %collective-permute-done.6 = bf16[512,128]{1,0:T(8,128)(2,1)S(1)} collective-permute-done((bf16[512,128]{1,0:T(8,128)(2,1)S(1)}, bf16[512,128]{1,0:T(8,128)(2,1)S(1)}, u32[]{:S(2)}, u32[]{:S(2)}) %collective-permute-start.6) | collective-permute-done | bytes 131104 | tf_op jit(solution)/shard_map/ppermute | solution.py:33
  52.4 1.3 %panel.4 = bf16[1024,256]{1,0:T(8,128)(2,1)S(1)} custom-call(s32[1]{0:T(128)} %bitcast.5.place_ref, bf16[512,2688]{1,0:T(8,128)(2,1)S(1)} %pack.1.x_ref.own_ref, bf16[512,2688]{1,0:T(8,128)(2,1)S(1)} %collective-permute-done.3.other_ref, bf16[512,256]{1,0:T(8,128)(2,1)S(1)} %collective-permute-done.7.refs_0_, ...), custom_call_target="tpu_custom_call" | custom-call | flops 1 | bytes 1 | tf_op jit(solution)/shard_map/panel/pallas_call | solution.py:225
  53.8 3.3 %collective-permute-start.18 = (bf16[512,128]{1,0:T(8,128)(2,1)S(1)}, bf16[512,128]{1,0:T(8,128)(2,1)S(1)}, u32[]{:S(2)}, u32[]{:S(2)}) collective-permute-start(bf16[512,128]{1,0:T(8,128)(2,1)S(1)} %add_convert_fusion.1.low_ref), channel_id=1, source_target_pairs={{0,1},{1,0},{2,3},{3,2},{4,5},{5,4},{6,7},{7,6},{8,9},{9,8},{10,11... | collective-permute-start | bytes 393224 | tf_op jit(solution)/shard_map/ppermute | solution.py:33
  60.8 1.7 %collective-permute-start.24 = (bf16[1024,256]{1,0:T(8,128)(2,1)S(1)}, bf16[1024,256]{1,0:T(8,128)(2,1)S(1)}, u32[]{:S(2)}, u32[]{:S(2)}) collective-permute-start(bf16[1024,256]{1,0:T(8,128)(2,1)S(1)} %panel.5), channel_id=1, source_target_pairs={{0,4},{4,0},{8,12},{12,8},{1,5},{5,1},{9,13},{13,9},{2,6},{6,2},{1... | collective-permute-start | bytes 1572872 | tf_op jit(solution)/shard_map/ppermute | solution.py:33
  62.5 1.4 %collective-permute-done.16.got_ref = bf16[1024,256]{1,0:T(8,128)(2,1)S(1)} collective-permute-done((bf16[1024,256]{1,0:T(8,128)(2,1)S(1)}, bf16[1024,256]{1,0:T(8,128)(2,1)S(1)}, u32[]{:S(2)}, u32[]{:S(2)}) %collective-permute-start.16) | collective-permute-done | bytes 524320 | tf_op jit(solution)/shard_map/ppermute | solution.py:423
  64.1 1.9 %collective-permute-start.17 = (bf16[1024,256]{1,0:T(8,128)(2,1)S(1)}, bf16[1024,256]{1,0:T(8,128)(2,1)S(1)}, u32[]{:S(2)}, u32[]{:S(2)}) collective-permute-start(bf16[1024,256]{1,0:T(8,128)(2,1)S(1)} %get-tuple-element.34), channel_id=1, source_target_pairs={{4,8},{8,4},{5,9},{9,5},{6,10},{10,6},{7,11},{11,7},{20,24},{24,20... | collective-permute-start | bytes 1572872 | tf_op jit(solution)/shard_map/ppermute | solution.py:428
  66.1 2.1 %collective-permute-done.22 = bf16[64,2560]{1,0:T(8,128)(2,1)S(1)} collective-permute-done((bf16[64,2560]{1,0:T(8,128)(2,1)S(1)}, bf16[64,2560]{1,0:T(8,128)(2,1)S(1)}, u32[]{:S(2)}, u32[]{:S(2)}) %collective-permute-start.22) | collective-permute-done | bytes 327712 | tf_op jit(solution)/shard_map/ppermute | solution.py:29
  68.2 5.9 %collective-permute-start.23 = (bf16[64,2560]{1,0:T(8,128)(2,1)S(1)}, bf16[64,2560]{1,0:T(8,128)(2,1)S(1)}, u32[]{:S(2)}, u32[]{:S(2)}) collective-permute-start(bf16[64,2560]{1,0:T(8,128)(2,1)S(1)} %add_convert_fusion.own_ref), channel_id=1, source_target_pairs={{0,1},{1,0},{2,3},{3,2},{4,5},{5,4},{6,7},{7,6},{8,9},{9,8},{10,11... | collective-permute-start | bytes 983048 | tf_op jit(solution)/shard_map/ppermute | solution.py:33
  74.2 2.1 %base.1.base_ref = f32[512,512]{1,0:T(8,128)S(1)} custom-call(s32[1]{0:T(128)} %bitcast.1.at_ref, s32[1]{0:T(128)} %bitcast.2.dp_ref, s32[1]{0:T(128)} %bitcast.core_ref, s32[1,6]{1,0:T(1,128)S(1)} %copy-done.5, s32[6]{0:T(128)S(1)} %copy-done.7, bf16[512,2688]{1,0:T(8,128)(2,1)S(1)} %pack.1.x_ref.own_ref, bf16[8192,512]{1,0:T(8,128)(2,1)S(1)} %bitcast.7, ...), custom_call_target="tpu_custom_call" | custom-call | flops 1 | bytes 1 | tf_op jit(solution)/shard_map/base/pallas_call | solution.py:277
  77.6 5.7 %collective-permute-start.25 = (bf16[512,256]{1,0:T(8,128)(2,1)S(1)}, bf16[512,256]{1,0:T(8,128)(2,1)S(1)}, u32[]{:S(2)}, u32[]{:S(2)}) collective-permute-start(bf16[512,256]{1,0:T(8,128)(2,1)S(1)} %other_rows.1), channel_id=1, source_target_pairs={{0,1},{1,0},{2,3},{3,2},{4,5},{5,4},{6,7},{7,6},{8,9},{9,8},{10,11... | collective-permute-start | bytes 786440 | tf_op jit(solution)/shard_map/ppermute | solution.py:33
  84.5 2.0 %finish.1 = bf16[768,512]{1,0:T(8,128)(2,1)} custom-call(s32[1]{0:T(128)} %bitcast.core_ref, s32[1,6]{1,0:T(1,128)S(1)} %copy-done.5, f32[512,512]{1,0:T(8,128)S(1)} %base.1.base_ref, bf16[1024,256]{1,0:T(8,128)(2,1)S(1)} %collective-permute-done.17.refs_0_, bf16[1024,256]{1,0:T(8,128)(2,1)S(1)} %collective-permute-done.24.refs_1_, ...), custom_call_target="tpu_custom_call" | custom-call | flops 1 | bytes 1 | tf_op jit(solution)/shard_map/finish/pallas_call | solution.py:360
  (67 shorter events, 19.0 us)
Async XLA Ops:
  1.8 12.9 %collective-permute-start = (bf16[512,256]{1,0:T(8,128)(2,1)S(1)}, bf16[512,256]{1,0:T(8,128)(2,1)S(1)}, u32[]{:S(2)}, u32[]{:S(2)}) collective-permute-start(bf16[512,256]{1,0:T(8,128)(2,1)S(1)} %get-tuple-element.44), channel_id=1, source_target_pairs={{0,12},{4,8},{8,4},{12,0},{1,13},{5,9},{9,5},{13,1},{2,14},{6,10},... | collective-permute-start | bytes 786440 | tf_op jit(solution)/shard_map/ppermute | solution.py:33
  3.8 8.6 %collective-permute-start.1 = (bf16[32,2560]{1,0:T(8,128)(2,1)}, bf16[32,2560]{1,0:T(8,128)(2,1)S(1)}, u32[]{:S(2)}, u32[]{:S(2)}) collective-permute-start(bf16[32,2560]{1,0:T(8,128)(2,1)} %get-tuple-element.24), channel_id=1, source_target_pairs={{0,2},{2,0},{1,3},{3,1},{4,6},{6,4},{5,7},{7,5},{8,10},{10,8},{9,1... | collective-permute-start | bytes 491528 | tf_op jit(solution)/shard_map/ppermute | solution.py:29
  4.0 8.4 %collective-permute-start.2 = (bf16[32,2560]{1,0:T(8,128)(2,1)}, bf16[32,2560]{1,0:T(8,128)(2,1)S(1)}, u32[]{:S(2)}, u32[]{:S(2)}) collective-permute-start(bf16[32,2560]{1,0:T(8,128)(2,1)} %get-tuple-element.25), channel_id=1, source_target_pairs={{0,2},{2,0},{1,3},{3,1},{4,6},{6,4},{5,7},{7,5},{8,10},{10,8},{9,1... | collective-permute-start | bytes 491528 | tf_op jit(solution)/shard_map/ppermute | solution.py:29
  14.7 6.3 %collective-permute-start.3 = (bf16[512,2688]{1,0:T(8,128)(2,1)S(1)}, bf16[512,2688]{1,0:T(8,128)(2,1)S(1)}, u32[]{:S(2)}, u32[]{:S(2)}) collective-permute-start(bf16[512,2688]{1,0:T(8,128)(2,1)S(1)} %pack.1.x_ref.own_ref), channel_id=1, source_target_pairs={{0,1},{1,0},{2,3},{3,2},{4,5},{5,4},{6,7},{7,6},{8,9},{9,8},{10,11... | collective-permute-start | bytes 8257544 | tf_op jit(solution)/shard_map/ppermute | solution.py:33
  16.4 12.8 %collective-permute-start.7 = (bf16[512,256]{1,0:T(8,128)(2,1)S(1)}, bf16[512,256]{1,0:T(8,128)(2,1)S(1)}, u32[]{:S(2)}, u32[]{:S(2)}) collective-permute-start(bf16[512,256]{1,0:T(8,128)(2,1)S(1)} %get-tuple-element.28), channel_id=1, source_target_pairs={{0,8},{4,12},{8,0},{12,4},{1,9},{5,13},{9,1},{13,5},{2,10},{6,14},... | collective-permute-start | bytes 786440 | tf_op jit(solution)/shard_map/ppermute | solution.py:33
  17.5 12.0 %collective-permute-start.8 = (bf16[512,256]{1,0:T(8,128)(2,1)S(1)}, bf16[512,256]{1,0:T(8,128)(2,1)S(1)}, u32[]{:S(2)}, u32[]{:S(2)}) collective-permute-start(bf16[512,256]{1,0:T(8,128)(2,1)S(1)} %collective-permute-done.refs_0_), channel_id=1, source_target_pairs={{0,2},{2,0},{16,18},{18,16},{1,3},{3,1},{17,19},{19,17},{4,6},{6,4... | collective-permute-start | bytes 786440 | tf_op jit(solution)/shard_map/ppermute | solution.py:33
  17.7 11.7 %collective-permute-start.9 = (bf16[512,256]{1,0:T(8,128)(2,1)S(1)}, bf16[512,256]{1,0:T(8,128)(2,1)S(1)}, u32[]{:S(2)}, u32[]{:S(2)}) collective-permute-start(bf16[512,256]{1,0:T(8,128)(2,1)S(1)} %collective-permute-done.refs_0_), channel_id=1, source_target_pairs={{0,16},{2,18},{16,0},{18,2},{1,17},{3,19},{17,1},{19,3},{4,20},{6,... | collective-permute-start | bytes 786440 | tf_op jit(solution)/shard_map/ppermute | solution.py:33
  21.0 9.3 %collective-permute-start.10 = (bf16[512,256]{1,0:T(8,128)(2,1)S(1)}, bf16[512,256]{1,0:T(8,128)(2,1)S(1)}, u32[]{:S(2)}, u32[]{:S(2)}) collective-permute-start(bf16[512,256]{1,0:T(8,128)(2,1)S(1)} %collective-permute-done.refs_0_), channel_id=1, source_target_pairs={{0,18},{2,16},{16,2},{18,0},{1,19},{3,17},{17,3},{19,1},{4,22},{6,... | collective-permute-start | bytes 786440 | tf_op jit(solution)/shard_map/ppermute | solution.py:33
  23.6 10.6 %collective-permute-start.5 = (bf16[512,128]{1,0:T(8,128)(2,1)S(1)}, bf16[512,128]{1,0:T(8,128)(2,1)S(1)}, u32[]{:S(2)}, u32[]{:S(2)}) collective-permute-start(bf16[512,128]{1,0:T(8,128)(2,1)S(1)} %low_part.1), channel_id=1, source_target_pairs={{0,4},{4,0},{8,12},{12,8},{1,5},{5,1},{9,13},{13,9},{2,6},{6,2},{1... | collective-permute-start | bytes 393224 | tf_op jit(solution)/shard_map/ppermute | solution.py:33
  29.2 7.4 %collective-permute-start.11 = (bf16[512,256]{1,0:T(8,128)(2,1)S(1)}, bf16[512,256]{1,0:T(8,128)(2,1)S(1)}, u32[]{:S(2)}, u32[]{:S(2)}) collective-permute-start(bf16[512,256]{1,0:T(8,128)(2,1)S(1)} %get-tuple-element.31), channel_id=1, source_target_pairs={{0,4},{4,0},{8,12},{12,8},{1,5},{5,1},{9,13},{13,9},{2,6},{6,2},{1... | collective-permute-start | bytes 786440 | tf_op jit(solution)/shard_map/ppermute | solution.py:33
  30.3 9.5 %collective-permute-start.12 = (bf16[512,256]{1,0:T(8,128)(2,1)S(1)}, bf16[512,256]{1,0:T(8,128)(2,1)S(1)}, u32[]{:S(2)}, u32[]{:S(2)}) collective-permute-start(bf16[512,256]{1,0:T(8,128)(2,1)S(1)} %collective-permute-done.7.refs_0_), channel_id=1, source_target_pairs={{0,2},{2,0},{16,18},{18,16},{1,3},{3,1},{17,19},{19,17},{4,6},{6,4... | collective-permute-start | bytes 786440 | tf_op jit(solution)/shard_map/ppermute | solution.py:33
  30.6 9.3 %collective-permute-start.13 = (bf16[512,256]{1,0:T(8,128)(2,1)S(1)}, bf16[512,256]{1,0:T(8,128)(2,1)S(1)}, u32[]{:S(2)}, u32[]{:S(2)}) collective-permute-start(bf16[512,256]{1,0:T(8,128)(2,1)S(1)} %collective-permute-done.7.refs_0_), channel_id=1, source_target_pairs={{0,16},{2,18},{16,0},{18,2},{1,17},{3,19},{17,1},{19,3},{4,20},{6,... | collective-permute-start | bytes 786440 | tf_op jit(solution)/shard_map/ppermute | solution.py:33
  31.7 11.3 %collective-permute-start.14 = (bf16[512,256]{1,0:T(8,128)(2,1)S(1)}, bf16[512,256]{1,0:T(8,128)(2,1)S(1)}, u32[]{:S(2)}, u32[]{:S(2)}) collective-permute-start(bf16[512,256]{1,0:T(8,128)(2,1)S(1)} %collective-permute-done.7.refs_0_), channel_id=1, source_target_pairs={{0,18},{2,16},{16,2},{18,0},{1,19},{3,17},{17,3},{19,1},{4,22},{6,... | collective-permute-start | bytes 786440 | tf_op jit(solution)/shard_map/ppermute | solution.py:33
  34.2 18.2 %collective-permute-start.15 = (bf16[1024,256]{1,0:T(8,128)(2,1)S(1)}, bf16[1024,256]{1,0:T(8,128)(2,1)S(1)}, u32[]{:S(2)}, u32[]{:S(2)}) collective-permute-start(bf16[1024,256]{1,0:T(8,128)(2,1)S(1)} %panel.3.own_ref), channel_id=1, source_target_pairs={{0,4},{12,8},{1,5},{13,9},{2,6},{14,10},{3,7},{15,11},{16,20},{28,... | collective-permute-start | bytes 1572872 | tf_op jit(solution)/shard_map/ppermute | solution.py:418
  36.5 15.9 %collective-permute-start.6 = (bf16[512,128]{1,0:T(8,128)(2,1)S(1)}, bf16[512,128]{1,0:T(8,128)(2,1)S(1)}, u32[]{:S(2)}, u32[]{:S(2)}) collective-permute-start(bf16[512,128]{1,0:T(8,128)(2,1)S(1)} %add_convert_fusion.2), channel_id=1, source_target_pairs={{0,8},{4,12},{8,0},{12,4},{1,9},{5,13},{9,1},{13,5},{2,10},{6,14},... | collective-permute-start | bytes 393224 | tf_op jit(solution)/shard_map/ppermute | solution.py:33
  43.0 16.1 %collective-permute-start.19 = (bf16[512,256]{1,0:T(8,128)(2,1)S(1)}, bf16[512,256]{1,0:T(8,128)(2,1)S(1)}, u32[]{:S(2)}, u32[]{:S(2)}) collective-permute-start(bf16[512,256]{1,0:T(8,128)(2,1)S(1)} %collective-permute-done.11.refs_0_), channel_id=1, source_target_pairs={{0,2},{2,0},{16,18},{18,16},{1,3},{3,1},{17,19},{19,17},{4,6},{6,4... | collective-permute-start | bytes 786440 | tf_op jit(solution)/shard_map/ppermute | solution.py:33
  43.0 16.1 %collective-permute-start.20 = (bf16[512,256]{1,0:T(8,128)(2,1)S(1)}, bf16[512,256]{1,0:T(8,128)(2,1)S(1)}, u32[]{:S(2)}, u32[]{:S(2)}) collective-permute-start(bf16[512,256]{1,0:T(8,128)(2,1)S(1)} %collective-permute-done.11.refs_0_), channel_id=1, source_target_pairs={{0,16},{2,18},{16,0},{18,2},{1,17},{3,19},{17,1},{19,3},{4,20},{6,... | collective-permute-start | bytes 786440 | tf_op jit(solution)/shard_map/ppermute | solution.py:33
  43.2 16.0 %collective-permute-start.21 = (bf16[512,256]{1,0:T(8,128)(2,1)S(1)}, bf16[512,256]{1,0:T(8,128)(2,1)S(1)}, u32[]{:S(2)}, u32[]{:S(2)}) collective-permute-start(bf16[512,256]{1,0:T(8,128)(2,1)S(1)} %collective-permute-done.11.refs_0_), channel_id=1, source_target_pairs={{0,18},{2,16},{16,2},{18,0},{1,19},{3,17},{17,3},{19,1},{4,22},{6,... | collective-permute-start | bytes 786440 | tf_op jit(solution)/shard_map/ppermute | solution.py:33
  53.7 10.2 %collective-permute-start.16 = (bf16[1024,256]{1,0:T(8,128)(2,1)S(1)}, bf16[1024,256]{1,0:T(8,128)(2,1)S(1)}, u32[]{:S(2)}, u32[]{:S(2)}) collective-permute-start(bf16[1024,256]{1,0:T(8,128)(2,1)S(1)} %panel.4), channel_id=1, source_target_pairs={{0,4},{12,8},{4,12},{8,0},{1,5},{13,9},{5,13},{9,1},{2,6},{14,10},... | collective-permute-start | bytes 1572872 | tf_op jit(solution)/shard_map/ppermute | solution.py:423
  59.2 9.0 %collective-permute-start.22 = (bf16[64,2560]{1,0:T(8,128)(2,1)S(1)}, bf16[64,2560]{1,0:T(8,128)(2,1)S(1)}, u32[]{:S(2)}, u32[]{:S(2)}) collective-permute-start(bf16[64,2560]{1,0:T(8,128)(2,1)S(1)} %get-tuple-element.38), channel_id=1, source_target_pairs={{0,2},{2,0},{1,3},{3,1},{4,6},{6,4},{5,7},{7,5},{8,10},{10,8},{9,1... | collective-permute-start | bytes 983048 | tf_op jit(solution)/shard_map/ppermute | solution.py:29
  60.8 16.8 %collective-permute-start.24 = (bf16[1024,256]{1,0:T(8,128)(2,1)S(1)}, bf16[1024,256]{1,0:T(8,128)(2,1)S(1)}, u32[]{:S(2)}, u32[]{:S(2)}) collective-permute-start(bf16[1024,256]{1,0:T(8,128)(2,1)S(1)} %panel.5), channel_id=1, source_target_pairs={{0,4},{4,0},{8,12},{12,8},{1,5},{5,1},{9,13},{13,9},{2,6},{6,2},{1... | collective-permute-start | bytes 1572872 | tf_op jit(solution)/shard_map/ppermute | solution.py:33
  64.1 13.4 %collective-permute-start.17 = (bf16[1024,256]{1,0:T(8,128)(2,1)S(1)}, bf16[1024,256]{1,0:T(8,128)(2,1)S(1)}, u32[]{:S(2)}, u32[]{:S(2)}) collective-permute-start(bf16[1024,256]{1,0:T(8,128)(2,1)S(1)} %get-tuple-element.34), channel_id=1, source_target_pairs={{4,8},{8,4},{5,9},{9,5},{6,10},{10,6},{7,11},{11,7},{20,24},{24,20... | collective-permute-start | bytes 1572872 | tf_op jit(solution)/shard_map/ppermute | solution.py:428
  68.2 8.1 %collective-permute-start.23 = (bf16[64,2560]{1,0:T(8,128)(2,1)S(1)}, bf16[64,2560]{1,0:T(8,128)(2,1)S(1)}, u32[]{:S(2)}, u32[]{:S(2)}) collective-permute-start(bf16[64,2560]{1,0:T(8,128)(2,1)S(1)} %add_convert_fusion.own_ref), channel_id=1, source_target_pairs={{0,1},{1,0},{2,3},{3,2},{4,5},{5,4},{6,7},{7,6},{8,9},{9,8},{10,11... | collective-permute-start | bytes 983048 | tf_op jit(solution)/shard_map/ppermute | solution.py:33
  77.6 6.9 %collective-permute-start.25 = (bf16[512,256]{1,0:T(8,128)(2,1)S(1)}, bf16[512,256]{1,0:T(8,128)(2,1)S(1)}, u32[]{:S(2)}, u32[]{:S(2)}) collective-permute-start(bf16[512,256]{1,0:T(8,128)(2,1)S(1)} %other_rows.1), channel_id=1, source_target_pairs={{0,1},{1,0},{2,3},{3,2},{4,5},{5,4},{6,7},{7,6},{8,9},{9,8},{10,11... | collective-permute-start | bytes 786440 | tf_op jit(solution)/shard_map/ppermute | solution.py:33
  (12 other events, 98.7 us)
